TPU v7x, 32 devices: a whole 2x2x4 slice. The times are simulated.
32 devices in a mesh: cfg: 2 (over x), blk: 4 (over z), uly: 4 (over y, core).
Axes of the slice: x: 2, y: 2, z: 4, core: 2. Of those that a mesh axis runs over, the one named last changes fastest.
Arguments:
- new_queries: bfloat16 [4096, 6144], P(('cfg', 'blk', 'uly')), parts along dimension 0, may hold values from -15 to 15
- new_keys: bfloat16 [4096, 6144], P(('cfg', 'blk', 'uly')), parts along dimension 0, may hold values from -6 to 6
- new_values: bfloat16 [4096, 6144], P(('cfg', 'blk', 'uly')), parts along dimension 0, may hold values from -6 to 6
- context_keys: bfloat16 [8192, 6144], P(('cfg', 'blk'), 'uly'), parts along dimension 0, may hold values from -6 to 6
- context_values: bfloat16 [8192, 6144], P(('cfg', 'blk'), 'uly'), parts along dimension 0, may hold values from -6 to 6
- keep_flags: int32 [16, 48], replicated, may hold values from 0 to 1, as said below
Outputs:
- attended: bfloat16 [4096, 6144], P(('cfg', 'blk', 'uly')), parts along dimension 0
There are 2 independent parts, one for each index of `cfg`. A program takes and returns all parts, laid end to end along the dimension named above; an argument that names none is the same for every part. Nothing has to cross between parts.
Inputs may be any that keep to these rules, and one draw needn't show every extreme that they name: keep_flags[i, 0] and keep_flags[i, 32 + i] are 1 for every query block i; at least one query block keeps every key block.
All inputs are finite; a program needn't handle non-finite values.
Results may differ from a plain program's by a relative error of at most 0.017.
Values may be sent and summed in bfloat16 or wider, within the bound.
No kernel may reach another device: no remote copies, remote signals or barrier semaphores. Data moves between devices by JAX's collectives and lax.ppermute only.
A program may use at most 128 MiB of HBM per device.

v0:
```python
import jax
import jax.numpy as jnp
from jax import lax
from jax.sharding import PartitionSpec as P

DH = 128
TILE = 128


masked_score = -1e30


def tile_numbers(row_count, context_rows, span_rows, cycle_size):
    row_index = jnp.arange(row_count, dtype=jnp.int32)
    local_rows = context_rows + span_rows
    holder = row_index // local_rows
    within = row_index % local_rows
    context_tile = (holder * context_rows + within) // TILE
    span_tile = (context_rows * cycle_size + holder * span_rows + within - context_rows) // TILE
    return jnp.where(within < context_rows, context_tile, span_tile)


def allowed_pairs(keep_rows, tile_ids):
    columns = jnp.take(keep_rows, tile_ids, axis=1)
    return jnp.repeat(columns, TILE, axis=0) > 0


def partial_softmax(queries, key_rows, value_rows, allowed):
    heads_here = queries.shape[1] // DH
    high_list = []
    total_list = []
    weighted_list = []
    for head in range(heads_here):
        query_head = queries[:, head * DH : (head + 1) * DH]
        key_head = key_rows[:, head * DH : (head + 1) * DH]
        value_head = value_rows[:, head * DH : (head + 1) * DH]
        scores = lax.dot_general(
            query_head, key_head, (((1,), (1,)), ((), ())), preferred_element_type=jnp.float32
        ) * DH ** (-0.5)
        scores = jnp.where(allowed, scores, masked_score)
        highest = jnp.max(scores, axis=1)
        weights = jnp.where(allowed, jnp.exp(scores - highest[:, None]), 0.0)
        high_list.append(highest)
        total_list.append(jnp.sum(weights, axis=1))
        weighted_list.append(
            jnp.dot(weights.astype(jnp.bfloat16), value_head, preferred_element_type=jnp.float32)
        )
    return (
        jnp.stack(high_list, axis=1),
        jnp.stack(total_list, axis=1),
        jnp.concatenate(weighted_list, axis=1),
    )


def join_states(earlier, later):
    highest = jnp.maximum(earlier[0], later[0])
    first_scale = jnp.exp(earlier[0] - highest)
    second_scale = jnp.exp(later[0] - highest)
    totals = earlier[1] * first_scale + later[1] * second_scale
    weighted = earlier[2] * jnp.repeat(first_scale, DH, axis=1) + later[2] * jnp.repeat(
        second_scale, DH, axis=1
    )
    return (highest, totals, weighted)


def shards(new_queries, new_keys, new_values, context_keys, context_values, keep_flags):
    span_queries, span_keys, span_values = (
        lax.all_to_all(new_queries, "uly", split_axis=1, concat_axis=0, tiled=True),
        lax.all_to_all(new_keys, "uly", split_axis=1, concat_axis=0, tiled=True),
        lax.all_to_all(new_values, "uly", split_axis=1, concat_axis=0, tiled=True),
    )
    span_rows = span_queries.shape[0]
    head_width = span_queries.shape[1]
    heads_here = head_width // DH
    context_rows = context_keys.shape[0]
    cycle_size = lax.axis_size("blk")
    cycle_index = lax.axis_index("blk")
    query_tiles = span_rows // TILE
    local_keys = jnp.concatenate([context_keys, span_keys], axis=0)
    local_values = jnp.concatenate([context_values, span_values], axis=0)
    keep_rows = lax.dynamic_slice_in_dim(keep_flags, cycle_index * query_tiles, query_tiles, 0)
    start_state = (
        jnp.full((span_rows, heads_here), masked_score, jnp.float32),
        jnp.zeros((span_rows, heads_here), jnp.float32),
        jnp.zeros((span_rows, head_width), jnp.float32),
    )
    carried_state = start_state
    key_piece = lax.all_gather(local_keys, "blk", axis=0, tiled=True)
    value_piece = lax.all_gather(local_values, "blk", axis=0, tiled=True)
    row_count = key_piece.shape[0]
    allowed = allowed_pairs(keep_rows, tile_numbers(row_count, context_rows, span_rows, cycle_size))
    block_width = 512
    blocks = row_count // block_width

    def advance(running, block_number):
        start = block_number * block_width
        key_block = lax.dynamic_slice_in_dim(key_piece, start, block_width, 0)
        value_block = lax.dynamic_slice_in_dim(value_piece, start, block_width, 0)
        mask_block = lax.dynamic_slice_in_dim(allowed, start, block_width, 1)
        found = partial_softmax(span_queries, key_block, value_block, mask_block)
        return (join_states(running, found), None)

    carried_state, unused = lax.scan(advance, carried_state, jnp.arange(blocks, dtype=jnp.int32))
    highest, totals, weighted = carried_state
    attended = (weighted / jnp.repeat(totals, DH, axis=1)).astype(jnp.bfloat16)
    return lax.all_to_all(attended, "uly", split_axis=0, concat_axis=1, tiled=True)


def solution(mesh):
    in_specs = (
        P(("cfg", "blk", "uly"), None),
        P(("cfg", "blk", "uly"), None),
        P(("cfg", "blk", "uly"), None),
        P(("cfg", "blk"), "uly"),
        P(("cfg", "blk"), "uly"),
        P(),
    )
    out_specs = P(("cfg", "blk", "uly"), None)
    return jax.shard_map(shards, mesh=mesh, in_specs=in_specs, out_specs=out_specs, check_vma=False)
```

profile of v0, /device:TPU:0, one launch (start us, length us, event | category | flops | bytes accessed | tf_op | source)
XLA Modules:
  0.0 1234.3 jit_solution(10397931738747198527)
XLA Ops:
  8.2 24.1 %all_to_all.76 = bf16[128,4,1536]{2,0,1:T(8,128)(2,1)S(1)} all-to-all(bf16[128,4,1536]{2,0,1:T(8,128)(2,1)S(1)} %bitcast.179), channel_id=1, replica_groups=mesh['cfg'=2,'blk'=4,'uly'=4] {'uly'}, dimensions={1} | all-to-all | bytes 3145728 | tf_op jit(solution)/shard_map/all_to_all | solution.py:70
  32.3 2.5 pad_maximum_fusion.1
  36.3 22.8 %all_to_all.77 = bf16[128,4,1536]{2,0,1:T(8,128)(2,1)S(1)} all-to-all(bf16[128,4,1536]{2,0,1:T(8,128)(2,1)S(1)} %bitcast.180), channel_id=1, replica_groups=mesh['cfg'=2,'blk'=4,'uly'=4] {'uly'}, dimensions={1} | all-to-all | bytes 3145728 | tf_op jit(solution)/shard_map/all_to_all | solution.py:69
  59.1 2.5 pad_maximum_fusion
  64.3 4.3 all-to-all-start.1
  69.2 16.1 %gather_fusion = s32[6144,4]{1,0:T(8,128)S(1)} fusion(s32[4,48]{0,1:T(8,128)S(1)} %copy.29, s32[6144]{0:T(1024)S(1)} %broadcast_clamp_fusion), kind=kCustom, calls=%fused_computation | custom fusion | bytes 221184 | tf_op jit(solution)/shard_map/jit(_take)/gather | solution.py:24
  85.4 3.3 fusion.137
  88.7 8.9 broadcast_in_dim.77
  100.3 257.6 %all-gather.5.cloned.1.call-done = bf16[6144,1536]{1,0:T(8,128)(2,1)} async-done(((bf16[1536,1536]{1,0:T(8,128)(2,1)}), bf16[6144,1536]{1,0:T(8,128)(2,1)}) %all-gather.5.cloned.1.call-update) | async-done | bytes 18874384 | tf_op jit(solution)/shard_map/all_gather | solution.py:89
  357.9 323.1 %all-gather.3.cloned.1.call-done = bf16[6144,1536]{1,0:T(8,128)(2,1)} async-done(((bf16[1536,1536]{1,0:T(8,128)(2,1)}), bf16[6144,1536]{1,0:T(8,128)(2,1)}) %all-gather.3.cloned.1.call-update) | async-done | bytes 18874384 | tf_op jit(solution)/shard_map/all_gather | solution.py:88
  680.9 518.4 %while.15 = (s32[]{:T(128)}, f32[512,12]{0,1:T(8,128)S(1)}, f32[512,12]{0,1:T(8,128)S(1)}, f32[512,1536]{0,1:T(8,128)}, s32[12]{0:T(128)S(1)}, /*index=5*/pred[5...) while((s32[]{:T(128)}, f32[512,12]{0,1:T(8,128)S(1)}, ...), condition=%wide.region_25.26_spmd.clone, body=%wide.region_0.25_spmd.clone.sunk | while | flops 1642106880 | bytes 179785872 | solution.py:103
  704.0 1.8 convolution_dynamic-update-slice_fusion.24
  747.2 1.8 convolution_dynamic-update-slice_fusion.24
  790.4 1.8 convolution_dynamic-update-slice_fusion.24
  833.6 1.8 convolution_dynamic-update-slice_fusion.24
  876.8 1.8 convolution_dynamic-update-slice_fusion.24
  920.0 1.8 convolution_dynamic-update-slice_fusion.24
  963.2 1.8 convolution_dynamic-update-slice_fusion.24
  1006.4 1.8 convolution_dynamic-update-slice_fusion.24
  1049.6 1.8 convolution_dynamic-update-slice_fusion.24
  1092.8 1.8 convolution_dynamic-update-slice_fusion.24
  1136.0 1.8 convolution_dynamic-update-slice_fusion.24
  1199.3 2.3 fusion.136
  1202.3 22.6 %all_to_all.78 = bf16[4,128,1536]{2,1,0:T(8,128)(2,1)S(1)} all-to-all(bf16[4,128,1536]{2,1,0:T(8,128)(2,1)S(1)} %bitcast.177), channel_id=1, replica_groups=mesh['cfg'=2,'blk'=4,'uly'=4] {'uly'}, dimensions={0} | all-to-all | bytes 3145728 | tf_op jit(solution)/shard_map/all_to_all | solution.py:106
  (971 shorter events, 497.1 us)
Async XLA Ops:
  6.5 62.2 %copy-start = (s32[16,48]{1,0:T(8,128)S(1)}, s32[16,48]{1,0:T(8,128)}, u32[]{:S(2)}) copy-start(s32[16,48]{1,0:T(8,128)} %param.13) | copy-start | bytes 9220
  6.5 351.3 %all-gather.5.cloned.1.call-start = ((), (), s32[]{:S(2)}) async-start(), calls=%async_computation.5 | async-start | bytes 23592960 | tf_op jit(solution)/shard_map/all_gather | solution.py:89
  6.5 25.8 %copy-start.26 = (bf16[1024,1536]{1,0:T(8,128)(2,1)S(1)}, bf16[1024,1536]{1,0:T(8,128)(2,1)}, u32[]{:S(2)}) copy-start(bf16[1024,1536]{1,0:T(8,128)(2,1)} %param.12) | copy-start | bytes 9437188
  34.8 646.1 %all-gather.3.cloned.1.call-start = ((), (), s32[]{:S(2)}) async-start(), calls=%async_computation.4 | async-start | bytes 23592960 | tf_op jit(solution)/shard_map/all_gather | solution.py:88
  36.2 22.9 %copy-start.27 = (bf16[1024,1536]{1,0:T(8,128)(2,1)S(1)}, bf16[1024,1536]{1,0:T(8,128)(2,1)}, u32[]{:S(2)}) copy-start(bf16[1024,1536]{1,0:T(8,128)(2,1)} %param.11) | copy-start | bytes 9437188
  64.3 35.9 %all-to-all-start.1 = ((bf16[128,4,1536]{2,0,1:T(8,128)(2,1)}), bf16[128,4,1536]{2,0,1:T(8,128)(2,1)}, u32[]{:S(2)}, u32[]{:S(2)}) async-start(bf16[128,4,1536]{2,0,1:T(8,128)(2,1)} %bitcast.117), calls=%async_computation.1 | async-start | bytes 3145728 | tf_op jit(solution)/shard_map/all_to_all | solution.py:68
  690.6 11.7 copy-start.10
  692.3 10.0 copy-start.14
  733.8 11.7 copy-start.10
  735.5 10.0 copy-start.14
  777.0 11.7 copy-start.10
  778.7 10.0 copy-start.14
  820.2 11.7 copy-start.10
  821.9 10.0 copy-start.14
  863.4 11.7 copy-start.10
  865.1 10.0 copy-start.14
  906.6 11.7 copy-start.10
  949.8 11.7 copy-start.10
  993.0 11.7 copy-start.10
  1036.2 11.7 copy-start.10
  1079.4 11.7 copy-start.10
  1122.6 11.7 copy-start.10
  1165.8 11.7 copy-start.10
  1202.3 25.1 %copy-start.1 = (s32[16,48]{1,0:T(8,128)S(1)}, s32[16,48]{1,0:T(8,128)}, u32[]{:S(2)}) copy-start(s32[16,48]{1,0:T(8,128)} %param.13) | copy-start | bytes 9220
  (273 other events, 1390.6 us)
Sparse Core Ops, SparseCore 0:
  34.9 322.8 all-gather.4
  359.5 321.4 all-gather.2
where the time goes:
time: 1240 us; the launch traced here: 1230 us
  waiting for transfers between devices  581 us (47%)
  matrix products  433 us (35%)
  blocking collectives  69.5 us (6%)
  local copies, waits for them, and re-layouts  65.9 us (5%)
  other arithmetic  53.3 us (4%)
  loops' own time  14.2 us (1%)
  between operations  13.6 us (1%)
    all_gather x1, waiting for transfers between devices, shards(): key_piece = lax.all_gather(local_keys, 'blk', axis=0, tiled=True)  323 us
    all_gather x1, waiting for transfers between devices, shards(): value_piece = lax.all_gather(local_values, 'blk', axis=0, tiled=True)  258 us
    dot_general x144, matrix products, partial_softmax(): lax.dot_general(query_head, key_head, (((1,), (1,)), ((), ())), preferred...  229 us
    dot_general x144, matrix products, partial_softmax(): jnp.dot(weights.astype(jnp.bfloat16), value_head, preferred_element_type=...  203 us
    reduce_sum x24, other arithmetic, partial_softmax(): total_list.append(jnp.sum(weights, axis=1))  27.3 us
  transfers between devices with their start and end apart: 3, of which 2 were waited for; matrix products, arithmetic and copies ran while one was open for 3% of the time, Pallas kernels for 0%

commit v1 on v0

v1 whole, which is shorter than its diff:
```python
import functools

import jax
import jax.numpy as jnp
from jax import lax
from jax.experimental import pallas as pl
from jax.experimental.pallas import tpu as pltpu
from jax.sharding import PartitionSpec as P

DH = 128
TILE = 128
PIECES = ((0, 1), (1, 1), (2, 1))
PIECE_UNITS = 3
HALF = 256
CHUNK = 256
LOG2E = 1.4426950408889634
TINY = 1.0e-30
ONES = 16
SCALE2 = DH ** (-0.5) * LOG2E
MASKED = -1.0e30
MIB = 1024 * 1024
QUICK = pl.CostEstimate(flops=1024, bytes_accessed=1024, transcendentals=0)


def split3(x):
    hi = x.astype(jnp.bfloat16).astype(jnp.float32)
    rest = x - hi
    mid = rest.astype(jnp.bfloat16).astype(jnp.float32)
    lo = (rest - mid).astype(jnp.bfloat16).astype(jnp.float32)
    return hi, mid, lo


def stat_rows(width):
    return -(-3 * (width // DH) // 16) * 16


def attend_kernel(deltas, table_ref, kept_ref, *refs):
    count = len(deltas)
    q_refs = refs[:count]
    ck_ref, nk_ref, cv_ref, nv_ref = refs[count : count + 4]
    out_ref, q_s, s0, s1, m0, m1, stat_s = refs[-7:]
    rows = q_s.shape[0]
    width = q_s.shape[1] // 2
    heads = width // DH
    ctx, new = ck_ref.shape[0], nk_ref.shape[0]
    subs = HALF // TILE
    halves = rows // HALF
    slots = ((s0, m0), (s1, m1))
    nt = (((1,), (1,)), ((), ()))
    target = table_ref[1 + pl.program_id(0)]
    first_tile = target * (rows // TILE)
    stat_s[...] = jnp.zeros_like(stat_s)
    for delta, q_ref in zip(deltas, q_refs):

        @pl.when(target - table_ref[0] == delta)
        def _():
            for head in range(heads):
                scaled = q_ref[:, head * DH : (head + 1) * DH].astype(jnp.float32) * SCALE2
                hi = scaled.astype(jnp.bfloat16)
                q_s[:, 2 * head * DH : (2 * head + 1) * DH] = hi
                q_s[:, (2 * head + 1) * DH : (2 * head + 2) * DH] = (scaled - hi.astype(jnp.float32)).astype(jnp.bfloat16)

    def columns(head, size=DH):
        return pl.ds(pl.multiple_of(head * size, size), size)

    chunks = [(k, v, at, base) for k, v, size, base in ((ck_ref, cv_ref, ctx, 0), (nk_ref, nv_ref, new, ctx))
              for at in range(0, size, CHUNK)]

    def kept(half, sub, row):
        return kept_ref[first_tile + half * subs + sub, row // TILE] > 0

    def score(head, half, chunk, q, tops):
        s_ref = slots[half % 2][0]
        k_ref, _, at, base = chunk
        size = min(CHUNK, k_ref.shape[0] - at)
        k = k_ref[at : at + size, columns(head)]
        scores = lax.dot_general(jnp.concatenate([k, k], axis=1), q, nt, preferred_element_type=jnp.float32)
        s_ref[base + at : base + at + size, :] = scores
        for j in range(0, size, TILE):
            for sub in range(subs):
                piece = scores[j : j + TILE, sub * TILE : (sub + 1) * TILE]
                top = jnp.max(piece.reshape(TILE // 8, 8, TILE), axis=0)
                top = jnp.where(kept(half, sub, base + at + j), top, MASKED)
                tops[sub] = top if tops[sub] is None else jnp.maximum(tops[sub], top)

    def weigh(head, half, chunk, high):
        s_ref = slots[half % 2][0]
        _, v_ref, at, base = chunk
        size = min(CHUNK, v_ref.shape[1] - at)
        lows = []
        for j in range(0, size, TILE):
            row = base + at + j
            pieces = []
            for sub in range(subs):
                lanes = slice(sub * TILE, (sub + 1) * TILE)
                less = jnp.where(kept(half, sub, row), high[:, lanes], -MASKED)
                pieces.append(jnp.exp2(s_ref[row : row + TILE, lanes] - less).astype(jnp.bfloat16))
            lows.append(jnp.concatenate(pieces, axis=1))
        low = jnp.concatenate(lows, axis=0)
        values = jnp.concatenate([v_ref[columns(head), at : at + size], jnp.ones((ONES, size), jnp.bfloat16)], axis=0)
        return jnp.dot(values, low, preferred_element_type=jnp.float32)

    def step(head, half, next_head, next_half, both=True):
        q = q_s[next_half * HALF : (next_half + 1) * HALF, columns(next_head, 2 * DH)]
        tops = [None] * subs
        if both:
            high = jnp.max(slots[half % 2][1][...], axis=0, keepdims=True)
            acc = None
        for chunk in chunks:
            score(next_head, next_half, chunk, q, tops)
            if both:
                found = weigh(head, half, chunk, high)
                acc = found if acc is None else acc + found
        for sub in range(subs):
            slots[next_half % 2][1][:, sub * TILE : (sub + 1) * TILE] = tops[sub]
        if both:
            total = jnp.maximum(acc[DH : DH + 1, :], TINY)
            lanes = slice(half * HALF, (half + 1) * HALF)
            out_ref[0, columns(head), lanes] = (acc[:DH, :] * (1.0 / total)).astype(jnp.bfloat16)
            for part, value in enumerate(split3(high + jnp.log2(total))):
                stat_s[pl.ds(3 * head + part, 1), lanes] = value

    step(0, 1, 0, 0, both=False)

    @pl.loop(0, heads)
    def _(head):
        for half in range(halves):
            if half + 1 < halves:
                step(head, half, head, half + 1)
            else:
                step(head, half, jnp.minimum(head + 1, heads - 1), 0)

    out_ref[0, width:, :] = stat_s[...].astype(jnp.bfloat16)


def attend(order, kept, queries, ctx_k, new_k, ctx_v, new_v, piece, blocks, out_blocks, dep):
    deltas = sorted(queries)
    rows, width = queries[deltas[0]].shape
    ctx, new = ctx_k.shape[0], new_k.shape[0]
    heads = width // DH
    keys = ctx + new
    across = lambda i, t, b: (0, piece)
    down = lambda i, t, b: (piece, 0)
    at = (lambda i, t, b: (0, 0, 0)) if out_blocks == 1 else (lambda i, t, b: (t[1 + i], 0, 0))
    prow = width + stat_rows(width)
    return pl.pallas_call(
        functools.partial(attend_kernel, deltas),
        out_shape=jax.ShapeDtypeStruct((out_blocks, prow, rows), jnp.bfloat16),
        grid_spec=pltpu.PrefetchScalarGridSpec(
            num_scalar_prefetch=2,
            grid=(blocks,),
            in_specs=[pl.BlockSpec((rows, width), lambda i, t, b: (0, 0))] * len(deltas)
            + [
                pl.BlockSpec((ctx, width), across),
                pl.BlockSpec((new, width), across),
                pl.BlockSpec((width, ctx), down),
                pl.BlockSpec((width, new), down),
                pl.BlockSpec(memory_space=pl.ANY),
            ],
            out_specs=pl.BlockSpec((1, prow, rows), at),
            scratch_shapes=[
                pltpu.VMEM((rows, 2 * width), jnp.bfloat16),
                pltpu.VMEM((keys, HALF), jnp.float32),
                pltpu.VMEM((keys, HALF), jnp.float32),
                pltpu.VMEM((8, HALF), jnp.float32),
                pltpu.VMEM((8, HALF), jnp.float32),
                pltpu.VMEM((stat_rows(width), rows), jnp.float32),
            ],
        ),
        compiler_params=pltpu.CompilerParams(vmem_limit_bytes=28 * MIB),
        cost_estimate=pl.CostEstimate(
            flops=8 * blocks * rows * keys * DH * heads,
            bytes_accessed=4 * blocks * rows * width + 4 * keys * width,
            transcendentals=blocks * rows * keys * heads,
        ),
        name="attend",
    )(order, kept, *[queries[d] for d in deltas], ctx_k, new_k, ctx_v, new_v, dep)


def load_stats(ref, lead, width):
    terms = ref[lead + (slice(width, None), slice(None))].astype(jnp.float32)
    return [
        terms[3 * h : 3 * h + 1, :] + terms[3 * h + 1 : 3 * h + 2, :] + terms[3 * h + 2 : 3 * h + 3, :]
        for h in range(width // DH)
    ]


def merge_one(own_ref, far_ref, got_ref, out_ref, stat_ref, use_far, got_ok):
    width = out_ref.shape[0] - stat_ref.shape[0]
    own_stats = load_stats(own_ref, (0,), width)
    far_stats = load_stats(far_ref, (0,), width)
    got_stats = load_stats(got_ref, (), width)
    stat_ref[...] = jnp.zeros_like(stat_ref)
    for head in range(width // DH):
        at = slice(head * DH, (head + 1) * DH)
        a = jnp.where(use_far, far_stats[head], own_stats[head])
        g = jnp.where(got_ok, got_stats[head], MASKED)
        top = jnp.maximum(a, g)
        wa = jnp.exp2(a - top)
        wg = jnp.exp2(g - top)
        total = wa + wg
        share = wg / total
        mine = jnp.where(use_far, far_ref[0, at, :], own_ref[0, at, :]).astype(jnp.float32)
        theirs = got_ref[at, :].astype(jnp.float32)
        out_ref[at, :] = (mine + share * (theirs - mine)).astype(jnp.bfloat16)
        for part, value in enumerate(split3(top + jnp.log2(total))):
            stat_ref[3 * head + part : 3 * head + part + 1, :] = value
    out_ref[width:, :] = stat_ref[...].astype(jnp.bfloat16)


def merge_kernel(n, info_ref, own_r, own_l, far_ref, got_r, got_l, dep, out_r, out_l, stat_ref):
    place, ahead, far = info_ref[0], info_ref[1], info_ref[2]

    @pl.when(place + ahead <= n - 1)
    def _():
        merge_one(own_r, far_ref, got_r, out_r, stat_ref, place + ahead == far, place > 0)

    @pl.when(place - ahead >= 0)
    def _():
        merge_one(own_l, far_ref, got_l, out_l, stat_ref, place - ahead == far, place < n - 1)


def merge(info, n, width, own, far, got_r, got_l, dep):
    _, prow, rows = own.shape
    whole = pl.BlockSpec((prow, rows), lambda i, t: (0, 0))
    return pl.pallas_call(
        functools.partial(merge_kernel, n),
        out_shape=[jax.ShapeDtypeStruct((prow, rows), jnp.bfloat16)] * 2,
        grid_spec=pltpu.PrefetchScalarGridSpec(
            num_scalar_prefetch=1,
            grid=(1,),
            in_specs=[
                pl.BlockSpec((1, prow, rows), lambda i, t: (jnp.minimum(t[0] + t[1], n - 1), 0, 0)),
                pl.BlockSpec((1, prow, rows), lambda i, t: (jnp.maximum(t[0] - t[1], 0), 0, 0)),
                pl.BlockSpec((1, prow, rows), lambda i, t: (0, 0, 0)),
                whole,
                whole,
                pl.BlockSpec(memory_space=pl.ANY),
            ],
            out_specs=[whole, whole],
            scratch_shapes=[pltpu.VMEM((prow - width, rows), jnp.float32)],
        ),
        compiler_params=pltpu.CompilerParams(vmem_limit_bytes=16 * MIB),
        cost_estimate=QUICK,
        name="merge",
    )(info, own, own, far, got_r, got_l, dep)


def finish_kernel(n, info_ref, own_ref, got_r, got_l, dep, out_ref):
    place = info_ref[0]
    rows, width = out_ref.shape
    own_stats = load_stats(own_ref, (0,), width)
    r_stats = load_stats(got_r, (), width)
    l_stats = load_stats(got_l, (), width)
    for head in range(width // DH):
        at = slice(head * DH, (head + 1) * DH)
        a = own_stats[head]
        r = jnp.where(place > 0, r_stats[head], MASKED)
        l = jnp.where(place < n - 1, l_stats[head], MASKED)
        top = jnp.maximum(jnp.maximum(a, r), l)
        wa, wr, wl = jnp.exp2(a - top), jnp.exp2(r - top), jnp.exp2(l - top)
        total = wa + wr + wl
        mine = own_ref[0, at, :].astype(jnp.float32)
        from_r = got_r[at, :].astype(jnp.float32)
        from_l = got_l[at, :].astype(jnp.float32)
        value = mine + (wr / total) * (from_r - mine) + (wl / total) * (from_l - mine)
        out_ref[:, at] = jnp.transpose(value).astype(jnp.bfloat16)


def finish(info, n, width, own, got_r, got_l, dep):
    _, prow, rows = own.shape
    whole = pl.BlockSpec((prow, rows), lambda i, t: (0, 0))
    return pl.pallas_call(
        functools.partial(finish_kernel, n),
        out_shape=jax.ShapeDtypeStruct((rows, width), jnp.bfloat16),
        grid_spec=pltpu.PrefetchScalarGridSpec(
            num_scalar_prefetch=1,
            grid=(1,),
            in_specs=[
                pl.BlockSpec((1, prow, rows), lambda i, t: (t[0], 0, 0)),
                whole,
                whole,
                pl.BlockSpec(memory_space=pl.ANY),
            ],
            out_specs=pl.BlockSpec((rows, width), lambda i, t: (0, 0)),
        ),
        compiler_params=pltpu.CompilerParams(vmem_limit_bytes=16 * MIB),
        cost_estimate=QUICK,
        name="finish",
    )(info, own, got_r, got_l, dep)


def part_kernel(peers, peer_ref, *refs):
    rows = refs[0].shape[0]
    for k in range(peers):
        target = refs[k - peers]
        target[:rows, :] = refs[k][...]
        target[rows:, :] = refs[peers + k][...]


def parts_for_peers(peer, upper, lower, peers, dep):
    rows, group = upper.shape[0], upper.shape[1] // peers
    specs = [pl.BlockSpec((rows, group), functools.partial(lambda k, i, t: (0, t[0] ^ k), k)) for k in range(peers)]
    return pl.pallas_call(
        functools.partial(part_kernel, peers),
        out_shape=[jax.ShapeDtypeStruct((2 * rows, group), jnp.bfloat16)] * peers,
        grid_spec=pltpu.PrefetchScalarGridSpec(
            num_scalar_prefetch=1,
            grid=(1,),
            in_specs=specs * 2 + [pl.BlockSpec(memory_space=pl.ANY)],
            out_specs=[pl.BlockSpec((2 * rows, group), lambda i, t: (0, 0))] * peers,
        ),
        compiler_params=pltpu.CompilerParams(vmem_limit_bytes=24 * MIB),
        cost_estimate=QUICK,
        name="parts",
    )(peer.reshape(1), *[upper] * peers, *[lower] * peers, dep)


def join_kernel(*refs):
    pieces, (k_ref, v_ref, v_s) = refs[:-4], refs[-3:]
    rows = pieces[0].shape[0] // 2
    for i, piece in enumerate(pieces):
        k_ref[i * rows : (i + 1) * rows, :] = piece[:rows, :]
        v_s[i * rows : (i + 1) * rows, :] = piece[rows:, :]
    for at in range(0, v_s.shape[0], TILE):
        v_ref[:, at : at + TILE] = jnp.transpose(v_s[at : at + TILE, :])


def joined(pieces, dep):
    rows, group = pieces[0].shape[0] // 2 * len(pieces), pieces[0].shape[1]
    return pl.pallas_call(
        join_kernel,
        out_shape=[
            jax.ShapeDtypeStruct((rows, group), jnp.bfloat16),
            jax.ShapeDtypeStruct((group, rows), jnp.bfloat16),
        ],
        in_specs=[pl.BlockSpec(memory_space=pltpu.VMEM)] * len(pieces) + [pl.BlockSpec(memory_space=pl.ANY)],
        scratch_shapes=[pltpu.VMEM((rows, group), jnp.bfloat16)],
        compiler_params=pltpu.CompilerParams(vmem_limit_bytes=24 * MIB),
        cost_estimate=QUICK,
        name="join",
    )(*pieces, dep)


def hold_kernel(*refs):
    pass


def hold(arrays, dep):
    anywhere = pl.BlockSpec(memory_space=pl.ANY)
    return pl.pallas_call(
        hold_kernel,
        out_shape=[jax.ShapeDtypeStruct(a.shape, a.dtype) for a in arrays],
        in_specs=[anywhere] * (len(arrays) + 1),
        out_specs=[anywhere] * len(arrays),
        input_output_aliases={i: i for i in range(len(arrays))},
        cost_estimate=QUICK,
        name="hold",
    )(*arrays, dep)


def later_kernel(start, x_ref, dep, out_ref):
    out_ref[0] = x_ref[:, start:]


def later_columns(x, peers, start, dep):
    rows, group = x.shape[0], x.shape[1] // peers
    return pl.pallas_call(
        functools.partial(later_kernel, start),
        out_shape=jax.ShapeDtypeStruct((peers, rows, group - start), jnp.bfloat16),
        grid=(peers,),
        in_specs=[pl.BlockSpec((rows, group), lambda p: (0, p)), pl.BlockSpec(memory_space=pl.ANY)],
        out_specs=pl.BlockSpec((1, rows, group - start), lambda p: (p, 0, 0)),
        compiler_params=pltpu.CompilerParams(vmem_limit_bytes=16 * MIB),
        cost_estimate=QUICK,
        name="later",
    )(x, dep)


def shards(new_queries, new_keys, new_values, context_keys, context_values, keep_flags):
    n = lax.axis_size("blk")
    place = lax.axis_index("blk").astype(jnp.int32)
    peers = lax.axis_size("uly")
    own_rows = new_queries.shape[0]
    group = context_keys.shape[1]
    unit = group // PIECE_UNITS
    span_rows = own_rows * peers
    ctx_tiles, new_tiles = context_keys.shape[0] // TILE, span_rows // TILE

    peer = lax.axis_index("uly").astype(jnp.int32)
    new_order = jnp.arange(new_tiles, dtype=jnp.int32) ^ (peer * own_rows // TILE)
    new_kept = lax.dynamic_slice_in_dim(keep_flags, n * ctx_tiles + place * new_tiles, new_tiles, 1)
    kept = jnp.concatenate(
        [
            lax.dynamic_slice_in_dim(keep_flags, place * ctx_tiles, ctx_tiles, 1),
            jnp.sum(jnp.where(new_order[:, None] == jnp.arange(new_tiles), new_kept[:, None, :], 0), axis=2),
        ],
        axis=1,
    )
    kept = (kept == 1).astype(jnp.int32)
    far = jnp.where(place < n // 2, n - 1, 0).astype(jnp.int32)
    others = jnp.arange(n - 1, dtype=jnp.int32)
    others = jnp.where(far == 0, others + 1, n - 2 - others)
    far_order = jnp.stack([place, far])
    others = jnp.concatenate([place.reshape(1), others])

    count = len(PIECES)
    widths = [units * unit for _, units in PIECES]
    found = [None] * count
    fars, owns, got, backs = [None] * count, [None] * count, [None] * count, [None] * count

    def to_heads(pieces):
        moved = lax.all_to_all(pieces, "uly", split_axis=0, concat_axis=0, tiled=False)
        return moved.reshape(span_rows, pieces.shape[2])

    def pass_on(c, step):
        found[c][-step] = lax.ppermute(found[c][1 - step], "blk", [(i, i + 1) for i in range(step - 1, n - 1)])
        found[c][step] = lax.ppermute(found[c][step - 1], "blk", [(i, i - 1) for i in range(n - step, 0, -1)])

    early = widths[0]
    first_span = to_heads(jnp.stack([new_queries[:, p * group : p * group + early] for p in range(peers)]))
    found[0] = {0: first_span}
    pass_on(0, 1)
    rest = to_heads(later_columns(new_queries, peers, early, first_span))
    spans = [rest[:, first * unit - early : (first + units) * unit - early] for first, units in PIECES[1:]]
    spans = dict(zip(range(1, count), spans))
    pieces = parts_for_peers(peer, new_keys, new_values, peers, rest)
    moved = [lax.ppermute(p, "uly", [(i, i ^ k) for i in range(peers)]) if k else p for k, p in enumerate(pieces)]
    context_values_t = context_values.T
    last = [pieces[0]]
    new_kv = []

    def run_forward(*hops):
        keys, arrays = [], []
        for c, step in hops:
            for d in [0] if step == 1 else [1 - step, step - 1]:
                keys.append((c, d))
                arrays.append(spans[c] if step == 1 else found[c][d])
        held = hold(arrays, last[0])
        last[0] = held[0]
        for (c, d), array in zip(keys, held):
            if d == 0:
                found[c] = {}
            found[c][d] = array
        for c, step in hops:
            pass_on(c, step)

    def run_join():
        new_kv.extend(joined(moved, last[0]))
        last[0] = new_kv[0]

    def run_far(c):
        distant = {d: q for d, q in found[c].items() if abs(d) >= n // 2}
        fars[c] = attend(far_order, kept, distant, *work(c), 1, 1, last[0])
        last[0] = fars[c]
        both = lax.ppermute(fars[c][0], "blk", [(0, 1), (n - 1, n - 2)])
        got[c] = (both, both)

    def work(c):
        return context_keys, new_kv[0], context_values_t, new_kv[1], PIECES[c][0] // PIECES[c][1]

    def run_rest(c):
        nearer = {d: q for d, q in found[c].items() if abs(d) < n - 1}
        owns[c] = attend(others, kept, nearer, *work(c), n - 1, n, last[0])
        last[0] = owns[c]

    def run_merge(c, step):
        info = jnp.stack([place, jnp.int32(n - step), far])
        out_r, out_l = merge(info, n, widths[c], owns[c], fars[c], got[c][0], got[c][1], last[0])
        last[0] = out_r
        got[c] = (
            lax.ppermute(out_r, "blk", [(i, i + 1) for i in range(step)]),
            lax.ppermute(out_l, "blk", [(n - 1 - i, n - 2 - i) for i in range(step)]),
        )

    def run_finish(c):
        info = jnp.stack([place, jnp.int32(0), far])
        done = finish(info, n, widths[c], owns[c], got[c][0], got[c][1], last[0])
        last[0] = done
        done = done.reshape(peers, own_rows, widths[c])
        backs[c] = lax.all_to_all(done, "uly", split_axis=0, concat_axis=0, tiled=False)

    if n == 4 and count == 3:
        run_forward((0, 2), (1, 1))
        run_forward((0, 3), (1, 2))
        run_join()
        run_far(0)
        run_forward((1, 3), (2, 1))
        run_rest(0)
        run_merge(0, 2)
        run_forward((2, 2))
        run_far(1)
        run_forward((2, 3))
        run_merge(0, 3)
        run_rest(1)
        run_merge(1, 2)
        run_far(2)
        run_finish(0)
        run_merge(1, 3)
        run_rest(2)
        run_merge(2, 2)
        run_finish(1)
        run_merge(2, 3)
        run_finish(2)
    else:
        run_join()
        for c in range(count):
            for step in range(2 if c == 0 else 1, n):
                run_forward((c, step))
            run_far(c)
            run_rest(c)
            for step in range(2, n):
                run_merge(c, step)
            run_finish(c)

    in_order = [backs[c] for c in sorted(range(count), key=lambda c: PIECES[c][0])]
    together = jnp.concatenate(in_order, axis=2)
    return together.transpose(1, 0, 2).reshape(own_rows, peers * group)


def solution(mesh):
    in_specs = (
        P(("cfg", "blk", "uly"), None),
        P(("cfg", "blk", "uly"), None),
        P(("cfg", "blk", "uly"), None),
        P(("cfg", "blk"), "uly"),
        P(("cfg", "blk"), "uly"),
        P(),
    )
    out_specs = P(("cfg", "blk", "uly"), None)
    return jax.shard_map(shards, mesh=mesh, in_specs=in_specs, out_specs=out_specs, check_vma=False)
```

time: 1240 us -> 323 us (0.26)
  waiting for transfers between devices: 581 us -> 46.2 us
  matrix products: 433 us -> 0 us
  starting transfers between devices: 4.39 us -> 110 us
  Pallas kernels: 0 us -> 95.7 us
  other arithmetic: 53.3 us -> 2.01 us
  blocking collectives: 69.5 us -> 24.5 us
  local copies, waits for them, and re-layouts: 65.9 us -> 40.8 us
  loops' own time: 14.2 us -> 0 us
  between operations: 13.6 us -> 0.78 us
    all_gather x2 -> x0, waiting for transfers between devices: 581 us -> none  [the longest x1 323 us: shards(): key_piece = lax.all_gather(local_keys, 'blk', axis=0, tiled=True)]
    dot_general x288 -> x0, matrix products: 433 us -> none  [the longest x144 229 us: partial_softmax(): lax.dot_general(query_head, key_head, (((1,), (1,)), ((), ())), preferred...]
    ppermute x0 -> x36, starting transfers between devices: none -> 97.7 us  [the longest x6 36.9 us: run_merge(): lax.ppermute(out_r, 'blk', [(i, i + 1) for i in range(step)])]
    pallas_call x0 -> x23, Pallas kernels: none -> 95.7 us  [the longest x6 71.6 us: attend(): pl.pallas_call(functools.partial(attend_kernel, deltas), out_shape=jax.Sh...]
    all_to_all x3 -> x2, blocking collectives: 69.5 us -> 24.5 us  [the longest x1 12.9 us: to_heads(): lax.all_to_all(pieces, 'uly', split_axis=0, concat_axis=0, tiled=False)]
    ppermute x0 -> x36, waiting for transfers between devices: none -> 37.2 us  [the longest x9 14.3 us: pass_on(): lax.ppermute(found[c][step - 1], 'blk', [(i, i - 1) for i in range(n - st...]
    unnamed x15 -> x103, local copies, waits for them, and re-layouts: 5.43 us -> 35.7 us
    reduce_sum x24 -> x1, other arithmetic: 27.3 us -> 0.09 us  [shards(): jnp.sum(jnp.where(new_order[:, None] == jnp.arange(new_tiles), new_kept[:...]
  transfers between devices with their start and end apart: 3 -> 39, of which waited for: 2 -> 10; matrix products, arithmetic and copies ran while one was open for 3% -> 2% of each run, Pallas kernels for 0% -> 30%
where the time goes in v1:
time: 323 us; the launch traced here: 320 us
  starting transfers between devices  110 us (34%)
  Pallas kernels  95.7 us (30%)
  waiting for transfers between devices  46.2 us (14%)
  local copies, waits for them, and re-layouts  40.8 us (13%)
  blocking collectives  24.5 us (8%)
    pallas_call x6, Pallas kernels, attend(): pl.pallas_call(functools.partial(attend_kernel, deltas), out_shape=jax.Sh...  71.6 us
    ppermute x6, starting transfers between devices, run_merge(): lax.ppermute(out_r, 'blk', [(i, i + 1) for i in range(step)])  36.9 us
    unnamed x103, local copies, waits for them, and re-layouts  35.7 us
    ppermute x9, starting transfers between devices, pass_on(): lax.ppermute(found[c][1 - step], 'blk', [(i, i + 1) for i in range(step -...  21.8 us
    ppermute x3, starting transfers between devices, run_far(): both = lax.ppermute(fars[c][0], 'blk', [(0, 1), (n - 1, n - 2)])  17.4 us
    ppermute x9, waiting for transfers between devices, pass_on(): lax.ppermute(found[c][step - 1], 'blk', [(i, i - 1) for i in range(n - st...  14.3 us
    pallas_call x6, Pallas kernels, merge(): pl.pallas_call(functools.partial(merge_kernel, n), out_shape=[jax.ShapeDt...  13.2 us
    all_to_all x1, blocking collectives, to_heads(): lax.all_to_all(pieces, 'uly', split_axis=0, concat_axis=0, tiled=False)  12.9 us
  transfers between devices with their start and end apart: 39, of which 10 were waited for; matrix products, arithmetic and copies ran while one was open for 2% of the time, Pallas kernels for 30%

profile of v1, /device:TPU:0, one launch (start us, length us, event | category | flops | bytes accessed | tf_op | source)
XLA Modules:
  0.0 320.3 jit_solution(10044777881896590106)
XLA Ops:
  1.3 12.9 %all_to_all.25 = bf16[4,128,512]{2,1,0:T(8,128)(2,1)S(1)} all-to-all(bf16[4,128,512]{2,1,0:T(8,128)(2,1)S(1)} %pad_maximum_fusion), channel_id=1, replica_groups=mesh['cfg'=2,'blk'=4,'uly'=4] {'uly'}, dimensions={0} | all-to-all | bytes 1048576 | tf_op jit(solution)/shard_map/all_to_all | solution.py:413
  26.2 8.9 %all-to-all-done.1 = bf16[4,128,1024]{2,1,0:T(8,128)(2,1)} async-done(((bf16[4,128,1024]{2,1,0:T(8,128)(2,1)}), bf16[4,128,1024]{2,1,0:T(8,128)(2,1)}, u32[]{:S(2)}, u32[]{:S(2)}) %all-to-all-start.1) | async-done | bytes 1048608 | tf_op jit(solution)/shard_map/all_to_all | solution.py:413
  41.8 6.3 %collective-permute-start.4 = (bf16[512,512]{1,0:T(8,128)(2,1)}, bf16[512,512]{1,0:T(8,128)(2,1)}, u32[]{:S(2)}, u32[]{:S(2)}) collective-permute-start(bf16[512,512]{1,0:T(8,128)(2,1)} %get-tuple-element.40.refs_2_), channel_id=1, source_target_pairs={{0,4},{4,8},{8,12},{1,5},{5,9},{9,13},{2,6},{6,10},{10,14},{3,7},{... | collective-permute-start | bytes 1572872 | tf_op jit(solution)/shard_map/ppermute | solution.py:417
  52.8 5.2 %collective-permute-done.4.refs_2_ = bf16[512,512]{1,0:T(8,128)(2,1)} collective-permute-done((bf16[512,512]{1,0:T(8,128)(2,1)}, bf16[512,512]{1,0:T(8,128)(2,1)}, u32[]{:S(2)}, u32[]{:S(2)}) %collective-permute-start.4) | collective-permute-done | bytes 524320 | tf_op jit(solution)/shard_map/ppermute | solution.py:417
  65.4 9.0 %collective-permute-done.3.refs_1_ = bf16[512,512]{1,0:T(8,128)(2,1)} collective-permute-done((bf16[512,512]{1,0:T(8,128)(2,1)}, bf16[512,512]{1,0:T(8,128)(2,1)}, u32[]{:S(2)}, u32[]{:S(2)}) %collective-permute-start.3) | collective-permute-done | bytes 524320 | tf_op jit(solution)/shard_map/ppermute | solution.py:418
  78.7 8.9 %collective-permute-done.8.refs_3_ = bf16[256,1536]{1,0:T(8,128)(2,1)} collective-permute-done((bf16[256,1536]{1,0:T(8,128)(2,1)}, bf16[256,1536]{1,0:T(8,128)(2,1)}, u32[]{:S(2)}, u32[]{:S(2)}) %collective-permute-start.8) | collective-permute-done | bytes 786464 | tf_op jit(solution)/shard_map/ppermute | solution.py:428
  92.1 7.0 %attend.6.refs_3_.far_ref = bf16[1,528,512]{2,1,0:T(8,128)(2,1)S(1)} custom-call(s32[2]{0:T(128)S(1)} %pad_add_fusion.1.table_ref, s32[16,12]{1,0:T(8,128)S(1)} %fusion.kept_ref, bf16[512,512]{1,0:T(8,128)(2,1)S(1)} %collective-permute-done.11.refs_0_, bf16[512,512]{1,0:T(8,128)(2,1)S(1)} %copy-done.32, bf16[512,512]{1,0:T(8,128)(2,1)} %get-tuple-element.42.refs_2_.refs_4_, ...), custom_call_target="tpu_custom_call" | custom-call | flops 3221225472 | bytes 4194304 | tf_op jit(solution)/shard_map/attend/pallas_call | solution.py:146
  101.7 5.5 %collective-permute-start.16 = (bf16[512,512]{1,0:T(8,128)(2,1)}, bf16[512,512]{1,0:T(8,128)(2,1)}, u32[]{:S(2)}, u32[]{:S(2)}) collective-permute-start(bf16[512,512]{1,0:T(8,128)(2,1)} %get-tuple-element.53.refs_2_), channel_id=1, source_target_pairs={{0,4},{4,8},{8,12},{1,5},{5,9},{9,13},{2,6},{6,10},{10,14},{3,7},{... | collective-permute-start | bytes 1572872 | tf_op jit(solution)/shard_map/ppermute | solution.py:417
  108.5 4.6 %collective-permute-start.13 = (bf16[528,512]{1,0:T(8,128)(2,1)S(1)}, bf16[528,512]{1,0:T(8,128)(2,1)S(1)}, u32[]{:S(2)}, u32[]{:S(2)}) collective-permute-start(bf16[528,512]{1,0:T(8,128)(2,1)S(1)} %bitcast.32), channel_id=1, source_target_pairs={{0,4},{12,8},{1,5},{13,9},{2,6},{14,10},{3,7},{15,11},{16,20},{28,... | collective-permute-start | bytes 1622024 | tf_op jit(solution)/shard_map/ppermute | solution.py:456
  124.5 16.9 %attend.7.own_r.own_l.dep.own_ref = bf16[4,528,512]{2,1,0:T(8,128)(2,1)S(1)} custom-call(s32[4]{0:T(128)S(1)} %pad_add_fusion.table_ref, s32[16,12]{1,0:T(8,128)S(1)} %fusion.kept_ref, bf16[512,512]{1,0:T(8,128)(2,1)S(1)} %copy-done.33, bf16[512,512]{1,0:T(8,128)(2,1)} %get-tuple-element.38.refs_4_.refs_1_, bf16[512,512]{1,0:T(8,128)(2,1)S(1)} %bitcast.37, ...), custom_call_target="tpu_custom_call" | custom-call | flops 9663676416 | bytes 6291456 | tf_op jit(solution)/shard_map/attend/pallas_call | solution.py:146
  143.4 6.1 %collective-permute-start.14 = (bf16[528,512]{1,0:T(8,128)(2,1)}, bf16[528,512]{1,0:T(8,128)(2,1)}, u32[]{:S(2)}, u32[]{:S(2)}) collective-permute-start(bf16[528,512]{1,0:T(8,128)(2,1)} %get-tuple-element.51.refs_2_), channel_id=1, source_target_pairs={{0,4},{4,8},{1,5},{5,9},{2,6},{6,10},{3,7},{7,11},{16,20},{20,24},... | collective-permute-start | bytes 1622024 | tf_op jit(solution)/shard_map/ppermute | solution.py:472
  162.6 7.0 %attend.8.refs_2_.far_ref = bf16[1,528,512]{2,1,0:T(8,128)(2,1)S(1)} custom-call(s32[2]{0:T(128)S(1)} %pad_add_fusion.1.table_ref, s32[16,12]{1,0:T(8,128)S(1)} %fusion.kept_ref, bf16[512,512]{1,0:T(8,128)(2,1)} %collective-permute-done.20.refs_0_, bf16[512,512]{1,0:T(8,128)(2,1)S(1)} %copy-done.43, bf16[512,512]{1,0:T(8,128)(2,1)S(1)} %copy-done.39, ...), custom_call_target="tpu_custom_call" | custom-call | flops 3221225472 | bytes 4194304 | tf_op jit(solution)/shard_map/attend/pallas_call | solution.py:146
  169.6 8.3 %collective-permute-start.26 = (bf16[528,512]{1,0:T(8,128)(2,1)S(1)}, bf16[528,512]{1,0:T(8,128)(2,1)}, u32[]{:S(2)}, u32[]{:S(2)}) collective-permute-start(bf16[528,512]{1,0:T(8,128)(2,1)S(1)} %bitcast.30), channel_id=1, source_target_pairs={{0,4},{12,8},{1,5},{13,9},{2,6},{14,10},{3,7},{15,11},{16,20},{28,... | collective-permute-start | bytes 1622024 | tf_op jit(solution)/shard_map/ppermute | solution.py:456
  188.3 16.8 %attend.9.own_r.own_l.dep.own_ref = bf16[4,528,512]{2,1,0:T(8,128)(2,1)S(1)} custom-call(s32[4]{0:T(128)S(1)} %pad_add_fusion.table_ref, s32[16,12]{1,0:T(8,128)S(1)} %fusion.kept_ref, bf16[512,512]{1,0:T(8,128)(2,1)S(1)} %copy-done.44, bf16[512,512]{1,0:T(8,128)(2,1)} %get-tuple-element.48.refs_1_, bf16[512,512]{1,0:T(8,128)(2,1)S(1)} %copy-done.48, ...), custom_call_target="tpu_custom_call" | custom-call | flops 9663676416 | bytes 6291456 | tf_op jit(solution)/shard_map/attend/pallas_call | solution.py:146
  205.1 5.0 %collective-permute-start.22 = (bf16[528,512]{1,0:T(8,128)(2,1)S(1)}, bf16[528,512]{1,0:T(8,128)(2,1)S(1)}, u32[]{:S(2)}, u32[]{:S(2)}) collective-permute-start(bf16[528,512]{1,0:T(8,128)(2,1)S(1)} %get-tuple-element.58.refs_9_), channel_id=1, source_target_pairs={{0,4},{4,8},{8,12},{1,5},{5,9},{9,13},{2,6},{6,10},{10,14},{3,7},{... | collective-permute-start | bytes 1622024 | tf_op jit(solution)/shard_map/ppermute | solution.py:472
  213.9 5.7 %collective-permute-start.27 = (bf16[528,512]{1,0:T(8,128)(2,1)S(1)}, bf16[528,512]{1,0:T(8,128)(2,1)S(1)}, u32[]{:S(2)}, u32[]{:S(2)}) collective-permute-start(bf16[528,512]{1,0:T(8,128)(2,1)S(1)} %get-tuple-element.61.refs_8_), channel_id=1, source_target_pairs={{0,4},{4,8},{1,5},{5,9},{2,6},{6,10},{3,7},{7,11},{16,20},{20,24},... | collective-permute-start | bytes 1622024 | tf_op jit(solution)/shard_map/ppermute | solution.py:472
  220.4 6.8 %attend.10.dep.far_ref = bf16[1,528,512]{2,1,0:T(8,128)(2,1)S(1)} custom-call(s32[2]{0:T(128)S(1)} %pad_add_fusion.1.table_ref, s32[16,12]{1,0:T(8,128)S(1)} %fusion.kept_ref, bf16[512,512]{1,0:T(8,128)(2,1)S(1)} %collective-permute-done.24.refs_0_, bf16[512,512]{1,0:T(8,128)(2,1)} %get-tuple-element.57.dep.refs_1_.refs_0_, ...), custom_call_target="tpu_custom_call" | custom-call | flops 3221225472 | bytes 4194304 | tf_op jit(solution)/shard_map/attend/pallas_call | solution.py:146
  227.2 4.5 %collective-permute-start.31 = (bf16[528,512]{1,0:T(8,128)(2,1)S(1)}, bf16[528,512]{1,0:T(8,128)(2,1)S(1)}, u32[]{:S(2)}, u32[]{:S(2)}) collective-permute-start(bf16[528,512]{1,0:T(8,128)(2,1)S(1)} %bitcast.31), channel_id=1, source_target_pairs={{0,4},{12,8},{1,5},{13,9},{2,6},{14,10},{3,7},{15,11},{16,20},{28,... | collective-permute-start | bytes 1622024 | tf_op jit(solution)/shard_map/ppermute | solution.py:456
  236.2 6.9 %collective-permute-start.29 = (bf16[528,512]{1,0:T(8,128)(2,1)}, bf16[528,512]{1,0:T(8,128)(2,1)S(1)}, u32[]{:S(2)}, u32[]{:S(2)}) collective-permute-start(bf16[528,512]{1,0:T(8,128)(2,1)} %get-tuple-element.63.refs_9_), channel_id=1, source_target_pairs={{0,4},{4,8},{8,12},{1,5},{5,9},{9,13},{2,6},{6,10},{10,14},{3,7},{... | collective-permute-start | bytes 1622024 | tf_op jit(solution)/shard_map/ppermute | solution.py:472
  244.7 17.1 %attend.11.own_r.own_l.dep.own_ref = bf16[4,528,512]{2,1,0:T(8,128)(2,1)S(1)} custom-call(s32[4]{0:T(128)S(1)} %pad_add_fusion.table_ref, s32[16,12]{1,0:T(8,128)S(1)} %fusion.kept_ref, bf16[512,512]{1,0:T(8,128)(2,1)} %get-tuple-element.57.dep.refs_1_.refs_0_, bf16[512,512]{1,0:T(8,128)(2,1)} %get-tuple-element.54.refs_8_.refs_1_, ...), custom_call_target="tpu_custom_call" | custom-call | flops 9663676416 | bytes 6291456 | tf_op jit(solution)/shard_map/attend/pallas_call | solution.py:146
  263.8 6.6 %collective-permute-start.32 = (bf16[528,512]{1,0:T(8,128)(2,1)}, bf16[528,512]{1,0:T(8,128)(2,1)}, u32[]{:S(2)}, u32[]{:S(2)}) collective-permute-start(bf16[528,512]{1,0:T(8,128)(2,1)} %get-tuple-element.65.dep), channel_id=1, source_target_pairs={{0,4},{4,8},{1,5},{5,9},{2,6},{6,10},{3,7},{7,11},{16,20},{20,24},... | collective-permute-start | bytes 1622024 | tf_op jit(solution)/shard_map/ppermute | solution.py:472
  282.1 6.5 %collective-permute-start.34 = (bf16[528,512]{1,0:T(8,128)(2,1)S(1)}, bf16[528,512]{1,0:T(8,128)(2,1)S(1)}, u32[]{:S(2)}, u32[]{:S(2)}) collective-permute-start(bf16[528,512]{1,0:T(8,128)(2,1)S(1)} %get-tuple-element.67.dep), channel_id=1, source_target_pairs={{0,4},{4,8},{8,12},{1,5},{5,9},{9,13},{2,6},{6,10},{10,14},{3,7},{... | collective-permute-start | bytes 1622024 | tf_op jit(solution)/shard_map/ppermute | solution.py:472
  298.4 4.5 %collective-permute-done.35.got_l = bf16[528,512]{1,0:T(8,128)(2,1)} collective-permute-done((bf16[528,512]{1,0:T(8,128)(2,1)}, bf16[528,512]{1,0:T(8,128)(2,1)}, u32[]{:S(2)}, u32[]{:S(2)}) %collective-permute-start.35) | collective-permute-done | bytes 540704 | tf_op jit(solution)/shard_map/ppermute | solution.py:473
  306.1 11.6 %all_to_all.26 = bf16[4,128,512]{2,1,0:T(8,128)(2,1)S(1)} all-to-all(bf16[4,128,512]{2,1,0:T(8,128)(2,1)S(1)} %bitcast.33), channel_id=1, replica_groups=mesh['cfg'=2,'blk'=4,'uly'=4] {'uly'}, dimensions={0} | all-to-all | bytes 1048576 | tf_op jit(solution)/shard_map/all_to_all | solution.py:481
  (201 shorter events, 120.7 us)
Async XLA Ops:
  49.6 24.8 %collective-permute-start.3 = (bf16[512,512]{1,0:T(8,128)(2,1)}, bf16[512,512]{1,0:T(8,128)(2,1)}, u32[]{:S(2)}, u32[]{:S(2)}) collective-permute-start(bf16[512,512]{1,0:T(8,128)(2,1)} %get-tuple-element.39.refs_3_), channel_id=1, source_target_pairs={{8,4},{4,0},{9,5},{5,1},{10,6},{6,2},{11,7},{7,3},{24,20},{20,16},... | collective-permute-start | bytes 1572872 | tf_op jit(solution)/shard_map/ppermute | solution.py:418
  50.9 25.7 %collective-permute-start.6 = (bf16[256,1536]{1,0:T(8,128)(2,1)}, bf16[256,1536]{1,0:T(8,128)(2,1)}, u32[]{:S(2)}, u32[]{:S(2)}) collective-permute-start(bf16[256,1536]{1,0:T(8,128)(2,1)} %get-tuple-element.43), channel_id=1, source_target_pairs={{0,1},{1,0},{2,3},{3,2},{4,5},{5,4},{6,7},{7,6},{8,9},{9,8},{10,11... | collective-permute-start | bytes 2359304 | tf_op jit(solution)/shard_map/ppermute | solution.py:428
  51.0 26.9 %collective-permute-start.7 = (bf16[256,1536]{1,0:T(8,128)(2,1)}, bf16[256,1536]{1,0:T(8,128)(2,1)}, u32[]{:S(2)}, u32[]{:S(2)}) collective-permute-start(bf16[256,1536]{1,0:T(8,128)(2,1)} %get-tuple-element.44), channel_id=1, source_target_pairs={{0,2},{1,3},{2,0},{3,1},{4,6},{5,7},{6,4},{7,5},{8,10},{9,11},{10,... | collective-permute-start | bytes 2359304 | tf_op jit(solution)/shard_map/ppermute | solution.py:428
  58.1 29.6 %collective-permute-start.8 = (bf16[256,1536]{1,0:T(8,128)(2,1)}, bf16[256,1536]{1,0:T(8,128)(2,1)}, u32[]{:S(2)}, u32[]{:S(2)}) collective-permute-start(bf16[256,1536]{1,0:T(8,128)(2,1)} %get-tuple-element.45), channel_id=1, source_target_pairs={{0,3},{1,2},{2,1},{3,0},{4,7},{5,6},{6,5},{7,4},{8,11},{9,10},{10,... | collective-permute-start | bytes 2359304 | tf_op jit(solution)/shard_map/ppermute | solution.py:428
  76.6 23.5 %collective-permute-start.10 = (bf16[512,512]{1,0:T(8,128)(2,1)}, bf16[512,512]{1,0:T(8,128)(2,1)S(1)}, u32[]{:S(2)}, u32[]{:S(2)}) collective-permute-start(bf16[512,512]{1,0:T(8,128)(2,1)} %get-tuple-element.49.refs_3_), channel_id=1, source_target_pairs={{8,4},{4,0},{9,5},{5,1},{10,6},{6,2},{11,7},{7,3},{24,20},{20,16},... | collective-permute-start | bytes 1572872 | tf_op jit(solution)/shard_map/ppermute | solution.py:418
  77.9 23.0 %collective-permute-start.9 = (bf16[512,512]{1,0:T(8,128)(2,1)}, bf16[512,512]{1,0:T(8,128)(2,1)S(1)}, u32[]{:S(2)}, u32[]{:S(2)}) collective-permute-start(bf16[512,512]{1,0:T(8,128)(2,1)} %get-tuple-element.48.refs_1_), channel_id=1, source_target_pairs={{4,8},{8,12},{5,9},{9,13},{6,10},{10,14},{7,11},{11,15},{20,24},{2... | collective-permute-start | bytes 1572872 | tf_op jit(solution)/shard_map/ppermute | solution.py:417
  101.7 47.9 %collective-permute-start.16 = (bf16[512,512]{1,0:T(8,128)(2,1)}, bf16[512,512]{1,0:T(8,128)(2,1)}, u32[]{:S(2)}, u32[]{:S(2)}) collective-permute-start(bf16[512,512]{1,0:T(8,128)(2,1)} %get-tuple-element.53.refs_2_), channel_id=1, source_target_pairs={{0,4},{4,8},{8,12},{1,5},{5,9},{9,13},{2,6},{6,10},{10,14},{3,7},{... | collective-permute-start | bytes 1572872 | tf_op jit(solution)/shard_map/ppermute | solution.py:417
  107.2 43.9 %collective-permute-start.17 = (bf16[512,512]{1,0:T(8,128)(2,1)}, bf16[512,512]{1,0:T(8,128)(2,1)}, u32[]{:S(2)}, u32[]{:S(2)}) collective-permute-start(bf16[512,512]{1,0:T(8,128)(2,1)} %get-tuple-element.53.refs_2_), channel_id=1, source_target_pairs={{12,8},{8,4},{4,0},{13,9},{9,5},{5,1},{14,10},{10,6},{6,2},{15,11}... | collective-permute-start | bytes 1572872 | tf_op jit(solution)/shard_map/ppermute | solution.py:418
  108.5 33.0 %collective-permute-start.13 = (bf16[528,512]{1,0:T(8,128)(2,1)S(1)}, bf16[528,512]{1,0:T(8,128)(2,1)S(1)}, u32[]{:S(2)}, u32[]{:S(2)}) collective-permute-start(bf16[528,512]{1,0:T(8,128)(2,1)S(1)} %bitcast.32), channel_id=1, source_target_pairs={{0,4},{12,8},{1,5},{13,9},{2,6},{14,10},{3,7},{15,11},{16,20},{28,... | collective-permute-start | bytes 1622024 | tf_op jit(solution)/shard_map/ppermute | solution.py:456
  113.1 39.5 %collective-permute-start.20 = (bf16[512,512]{1,0:T(8,128)(2,1)}, bf16[512,512]{1,0:T(8,128)(2,1)}, u32[]{:S(2)}, u32[]{:S(2)}) collective-permute-start(bf16[512,512]{1,0:T(8,128)(2,1)} %get-tuple-element.50.refs_9_.refs_1_.refs_0_), channel_id=1, source_target_pairs={{8,12},{9,13},{10,14},{11,15},{24,28},{25,29},{26,30},{27,31}} | collective-permute-start | bytes 1572872 | tf_op jit(solution)/shard_map/ppermute | solution.py:417
  114.5 39.4 %collective-permute-start.21 = (bf16[512,512]{1,0:T(8,128)(2,1)}, bf16[512,512]{1,0:T(8,128)(2,1)}, u32[]{:S(2)}, u32[]{:S(2)}) collective-permute-start(bf16[512,512]{1,0:T(8,128)(2,1)} %get-tuple-element.56.refs_2_.refs_4_), channel_id=1, source_target_pairs={{4,0},{5,1},{6,2},{7,3},{20,16},{21,17},{22,18},{23,19}} | collective-permute-start | bytes 1572872 | tf_op jit(solution)/shard_map/ppermute | solution.py:418
  143.4 36.7 %collective-permute-start.14 = (bf16[528,512]{1,0:T(8,128)(2,1)}, bf16[528,512]{1,0:T(8,128)(2,1)}, u32[]{:S(2)}, u32[]{:S(2)}) collective-permute-start(bf16[528,512]{1,0:T(8,128)(2,1)} %get-tuple-element.51.refs_2_), channel_id=1, source_target_pairs={{0,4},{4,8},{1,5},{5,9},{2,6},{6,10},{3,7},{7,11},{16,20},{20,24},... | collective-permute-start | bytes 1622024 | tf_op jit(solution)/shard_map/ppermute | solution.py:472
  149.6 30.6 %collective-permute-start.15 = (bf16[528,512]{1,0:T(8,128)(2,1)}, bf16[528,512]{1,0:T(8,128)(2,1)}, u32[]{:S(2)}, u32[]{:S(2)}) collective-permute-start(bf16[528,512]{1,0:T(8,128)(2,1)} %get-tuple-element.52), channel_id=1, source_target_pairs={{12,8},{8,4},{13,9},{9,5},{14,10},{10,6},{15,11},{11,7},{28,24},{2... | collective-permute-start | bytes 1622024 | tf_op jit(solution)/shard_map/ppermute | solution.py:473
  151.1 26.8 %collective-permute-start.18 = (bf16[512,512]{1,0:T(8,128)(2,1)}, bf16[512,512]{1,0:T(8,128)(2,1)}, u32[]{:S(2)}, u32[]{:S(2)}) collective-permute-start(bf16[512,512]{1,0:T(8,128)(2,1)} %get-tuple-element.54.refs_8_.refs_1_), channel_id=1, source_target_pairs={{4,8},{8,12},{5,9},{9,13},{6,10},{10,14},{7,11},{11,15},{20,24},{2... | collective-permute-start | bytes 1572872 | tf_op jit(solution)/shard_map/ppermute | solution.py:417
  152.5 25.3 %collective-permute-start.19 = (bf16[512,512]{1,0:T(8,128)(2,1)}, bf16[512,512]{1,0:T(8,128)(2,1)}, u32[]{:S(2)}, u32[]{:S(2)}) collective-permute-start(bf16[512,512]{1,0:T(8,128)(2,1)} %get-tuple-element.55.refs_3_), channel_id=1, source_target_pairs={{8,4},{4,0},{9,5},{5,1},{10,6},{6,2},{11,7},{7,3},{24,20},{20,16},... | collective-permute-start | bytes 1572872 | tf_op jit(solution)/shard_map/ppermute | solution.py:418
  169.6 42.1 %collective-permute-start.26 = (bf16[528,512]{1,0:T(8,128)(2,1)S(1)}, bf16[528,512]{1,0:T(8,128)(2,1)}, u32[]{:S(2)}, u32[]{:S(2)}) collective-permute-start(bf16[528,512]{1,0:T(8,128)(2,1)S(1)} %bitcast.30), channel_id=1, source_target_pairs={{0,4},{12,8},{1,5},{13,9},{2,6},{14,10},{3,7},{15,11},{16,20},{28,... | collective-permute-start | bytes 1622024 | tf_op jit(solution)/shard_map/ppermute | solution.py:456
  177.9 41.7 %collective-permute-start.24 = (bf16[512,512]{1,0:T(8,128)(2,1)}, bf16[512,512]{1,0:T(8,128)(2,1)S(1)}, u32[]{:S(2)}, u32[]{:S(2)}) collective-permute-start(bf16[512,512]{1,0:T(8,128)(2,1)} %get-tuple-element.57.dep.refs_1_.refs_0_), channel_id=1, source_target_pairs={{8,12},{9,13},{10,14},{11,15},{24,28},{25,29},{26,30},{27,31}} | collective-permute-start | bytes 1572872 | tf_op jit(solution)/shard_map/ppermute | solution.py:417
  178.6 41.8 %collective-permute-start.25 = (bf16[512,512]{1,0:T(8,128)(2,1)}, bf16[512,512]{1,0:T(8,128)(2,1)S(1)}, u32[]{:S(2)}, u32[]{:S(2)}) collective-permute-start(bf16[512,512]{1,0:T(8,128)(2,1)} %get-tuple-element.60.refs_2_.refs_4_), channel_id=1, source_target_pairs={{4,0},{5,1},{6,2},{7,3},{20,16},{21,17},{22,18},{23,19}} | collective-permute-start | bytes 1572872 | tf_op jit(solution)/shard_map/ppermute | solution.py:418
  205.1 26.6 %collective-permute-start.22 = (bf16[528,512]{1,0:T(8,128)(2,1)S(1)}, bf16[528,512]{1,0:T(8,128)(2,1)S(1)}, u32[]{:S(2)}, u32[]{:S(2)}) collective-permute-start(bf16[528,512]{1,0:T(8,128)(2,1)S(1)} %get-tuple-element.58.refs_9_), channel_id=1, source_target_pairs={{0,4},{4,8},{8,12},{1,5},{5,9},{9,13},{2,6},{6,10},{10,14},{3,7},{... | collective-permute-start | bytes 1622024 | tf_op jit(solution)/shard_map/ppermute | solution.py:472
  210.1 21.6 %collective-permute-start.23 = (bf16[528,512]{1,0:T(8,128)(2,1)S(1)}, bf16[528,512]{1,0:T(8,128)(2,1)S(1)}, u32[]{:S(2)}, u32[]{:S(2)}) collective-permute-start(bf16[528,512]{1,0:T(8,128)(2,1)S(1)} %get-tuple-element.59), channel_id=1, source_target_pairs={{12,8},{8,4},{4,0},{13,9},{9,5},{5,1},{14,10},{10,6},{6,2},{15,11}... | collective-permute-start | bytes 1622024 | tf_op jit(solution)/shard_map/ppermute | solution.py:473
  213.9 20.4 %collective-permute-start.27 = (bf16[528,512]{1,0:T(8,128)(2,1)S(1)}, bf16[528,512]{1,0:T(8,128)(2,1)S(1)}, u32[]{:S(2)}, u32[]{:S(2)}) collective-permute-start(bf16[528,512]{1,0:T(8,128)(2,1)S(1)} %get-tuple-element.61.refs_8_), channel_id=1, source_target_pairs={{0,4},{4,8},{1,5},{5,9},{2,6},{6,10},{3,7},{7,11},{16,20},{20,24},... | collective-permute-start | bytes 1622024 | tf_op jit(solution)/shard_map/ppermute | solution.py:472
  227.2 34.7 %collective-permute-start.31 = (bf16[528,512]{1,0:T(8,128)(2,1)S(1)}, bf16[528,512]{1,0:T(8,128)(2,1)S(1)}, u32[]{:S(2)}, u32[]{:S(2)}) collective-permute-start(bf16[528,512]{1,0:T(8,128)(2,1)S(1)} %bitcast.31), channel_id=1, source_target_pairs={{0,4},{12,8},{1,5},{13,9},{2,6},{14,10},{3,7},{15,11},{16,20},{28,... | collective-permute-start | bytes 1622024 | tf_op jit(solution)/shard_map/ppermute | solution.py:456
  236.2 39.8 %collective-permute-start.29 = (bf16[528,512]{1,0:T(8,128)(2,1)}, bf16[528,512]{1,0:T(8,128)(2,1)S(1)}, u32[]{:S(2)}, u32[]{:S(2)}) collective-permute-start(bf16[528,512]{1,0:T(8,128)(2,1)} %get-tuple-element.63.refs_9_), channel_id=1, source_target_pairs={{0,4},{4,8},{8,12},{1,5},{5,9},{9,13},{2,6},{6,10},{10,14},{3,7},{... | collective-permute-start | bytes 1622024 | tf_op jit(solution)/shard_map/ppermute | solution.py:472
  243.2 32.9 %collective-permute-start.30 = (bf16[528,512]{1,0:T(8,128)(2,1)}, bf16[528,512]{1,0:T(8,128)(2,1)}, u32[]{:S(2)}, u32[]{:S(2)}) collective-permute-start(bf16[528,512]{1,0:T(8,128)(2,1)} %get-tuple-element.64), channel_id=1, source_target_pairs={{12,8},{8,4},{4,0},{13,9},{9,5},{5,1},{14,10},{10,6},{6,2},{15,11}... | collective-permute-start | bytes 1622024 | tf_op jit(solution)/shard_map/ppermute | solution.py:473
  (66 other events, 603.7 us)

commit v2 on v1

v2 whole, which is shorter than its diff:
```python
import functools

import jax
import jax.numpy as jnp
from jax import lax
from jax.experimental import pallas as pl
from jax.experimental.pallas import tpu as pltpu
from jax.sharding import PartitionSpec as P

DH = 128
TILE = 128
PIECES = ((0, 1), (1, 1), (2, 1))
PIECE_UNITS = 3
HALF = 256
CHUNK = 256
LOG2E = 1.4426950408889634
TINY = 1.0e-30
ONES = 16
SCALE2 = DH ** (-0.5) * LOG2E
MASKED = -1.0e30
MIB = 1024 * 1024
QUICK = pl.CostEstimate(flops=1024, bytes_accessed=1024, transcendentals=0)


def split3(x):
    hi = x.astype(jnp.bfloat16).astype(jnp.float32)
    rest = x - hi
    mid = rest.astype(jnp.bfloat16).astype(jnp.float32)
    lo = (rest - mid).astype(jnp.bfloat16).astype(jnp.float32)
    return hi, mid, lo


def stat_rows(width):
    return -(-3 * (width // DH) // 16) * 16


def attend_kernel(distances, place_ref, kept_ref, *refs):
    count = len(distances)
    q_refs = refs[:count]
    ck_ref, nk_ref, cv_ref, nv_ref = refs[count : count + 4]
    out_ref, q_s, s0, s1, m0, m1, stat_s = refs[-7:]
    rows = q_s.shape[0]
    width = q_s.shape[1] // 2
    heads = width // DH
    ctx, new = ck_ref.shape[0], nk_ref.shape[0]
    subs = HALF // TILE
    halves = rows // HALF
    slots = ((s0, m0), (s1, m1))
    nt = (((1,), (1,)), ((), ()))
    distance = distances[0]
    for i in range(1, count):
        distance = jnp.where(pl.program_id(0) == i, distances[i], distance)
    first_tile = (place_ref[0] ^ distance) * (rows // TILE)
    stat_s[...] = jnp.zeros_like(stat_s)
    for i, q_ref in enumerate(q_refs):

        @pl.when(pl.program_id(0) == i)
        def _():
            for head in range(heads):
                scaled = q_ref[:, head * DH : (head + 1) * DH].astype(jnp.float32) * SCALE2
                hi = scaled.astype(jnp.bfloat16)
                q_s[:, 2 * head * DH : (2 * head + 1) * DH] = hi
                q_s[:, (2 * head + 1) * DH : (2 * head + 2) * DH] = (scaled - hi.astype(jnp.float32)).astype(jnp.bfloat16)

    def columns(head, size=DH):
        return pl.ds(pl.multiple_of(head * size, size), size)

    chunks = [(k, v, at, base) for k, v, size, base in ((ck_ref, cv_ref, ctx, 0), (nk_ref, nv_ref, new, ctx))
              for at in range(0, size, CHUNK)]

    def kept(half, sub, row):
        return kept_ref[first_tile + half * subs + sub, row // TILE] > 0

    def score(head, half, chunk, q, tops):
        s_ref = slots[half % 2][0]
        k_ref, _, at, base = chunk
        size = min(CHUNK, k_ref.shape[0] - at)
        k = k_ref[at : at + size, columns(head)]
        scores = lax.dot_general(jnp.concatenate([k, k], axis=1), q, nt, preferred_element_type=jnp.float32)
        s_ref[base + at : base + at + size, :] = scores
        for j in range(0, size, TILE):
            for sub in range(subs):
                piece = scores[j : j + TILE, sub * TILE : (sub + 1) * TILE]
                top = jnp.max(piece.reshape(TILE // 8, 8, TILE), axis=0)
                top = jnp.where(kept(half, sub, base + at + j), top, MASKED)
                tops[sub] = top if tops[sub] is None else jnp.maximum(tops[sub], top)

    def weigh(head, half, chunk, high):
        s_ref = slots[half % 2][0]
        _, v_ref, at, base = chunk
        size = min(CHUNK, v_ref.shape[1] - at)
        lows = []
        for j in range(0, size, TILE):
            row = base + at + j
            pieces = []
            for sub in range(subs):
                lanes = slice(sub * TILE, (sub + 1) * TILE)
                less = jnp.where(kept(half, sub, row), high[:, lanes], -MASKED)
                pieces.append(jnp.exp2(s_ref[row : row + TILE, lanes] - less).astype(jnp.bfloat16))
            lows.append(jnp.concatenate(pieces, axis=1))
        low = jnp.concatenate(lows, axis=0)
        values = jnp.concatenate([v_ref[columns(head), at : at + size], jnp.ones((ONES, size), jnp.bfloat16)], axis=0)
        return jnp.dot(values, low, preferred_element_type=jnp.float32)

    def step(head, half, next_head, next_half, both=True):
        q = q_s[next_half * HALF : (next_half + 1) * HALF, columns(next_head, 2 * DH)]
        tops = [None] * subs
        if both:
            high = jnp.max(slots[half % 2][1][...], axis=0, keepdims=True)
            acc = None
        for chunk in chunks:
            score(next_head, next_half, chunk, q, tops)
            if both:
                found = weigh(head, half, chunk, high)
                acc = found if acc is None else acc + found
        for sub in range(subs):
            slots[next_half % 2][1][:, sub * TILE : (sub + 1) * TILE] = tops[sub]
        if both:
            total = jnp.maximum(acc[DH : DH + 1, :], TINY)
            lanes = slice(half * HALF, (half + 1) * HALF)
            out_ref[0, columns(head), lanes] = (acc[:DH, :] * (1.0 / total)).astype(jnp.bfloat16)
            for part, value in enumerate(split3(high + jnp.log2(total))):
                stat_s[pl.ds(3 * head + part, 1), lanes] = value

    step(0, 1, 0, 0, both=False)

    @pl.loop(0, heads)
    def _(head):
        for half in range(halves):
            if half + 1 < halves:
                step(head, half, head, half + 1)
            else:
                step(head, half, jnp.minimum(head + 1, heads - 1), 0)

    out_ref[0, width:, :] = stat_s[...].astype(jnp.bfloat16)


def attend(place, kept, queries, distances, ctx_k, new_k, ctx_v, new_v, piece, dep):
    rows, width = queries[distances[0]].shape
    ctx, new = ctx_k.shape[0], new_k.shape[0]
    heads = width // DH
    keys = ctx + new
    blocks = len(distances)
    across = lambda i, t, b: (0, piece)
    down = lambda i, t, b: (piece, 0)
    prow = width + stat_rows(width)
    return pl.pallas_call(
        functools.partial(attend_kernel, distances),
        out_shape=jax.ShapeDtypeStruct((blocks, prow, rows), jnp.bfloat16),
        grid_spec=pltpu.PrefetchScalarGridSpec(
            num_scalar_prefetch=2,
            grid=(blocks,),
            in_specs=[pl.BlockSpec((rows, width), lambda i, t, b: (0, 0))] * blocks
            + [
                pl.BlockSpec((ctx, width), across),
                pl.BlockSpec((new, width), across),
                pl.BlockSpec((width, ctx), down),
                pl.BlockSpec((width, new), down),
                pl.BlockSpec(memory_space=pl.ANY),
            ],
            out_specs=pl.BlockSpec((1, prow, rows), lambda i, t, b: (i, 0, 0)),
            scratch_shapes=[
                pltpu.VMEM((rows, 2 * width), jnp.bfloat16),
                pltpu.VMEM((keys, HALF), jnp.float32),
                pltpu.VMEM((keys, HALF), jnp.float32),
                pltpu.VMEM((8, HALF), jnp.float32),
                pltpu.VMEM((8, HALF), jnp.float32),
                pltpu.VMEM((stat_rows(width), rows), jnp.float32),
            ],
        ),
        compiler_params=pltpu.CompilerParams(vmem_limit_bytes=28 * MIB),
        cost_estimate=pl.CostEstimate(
            flops=8 * blocks * rows * keys * DH * heads,
            bytes_accessed=4 * blocks * rows * width + 4 * keys * width,
            transcendentals=blocks * rows * keys * heads,
        ),
        name="attend",
    )(place, kept, *[queries[d] for d in distances], ctx_k, new_k, ctx_v, new_v, dep)


def combine(refs, width, emit):
    stats = []
    for ref in refs:
        terms = ref[0, width:, :].astype(jnp.float32)
        stats.append([terms[3 * h : 3 * h + 1] + terms[3 * h + 1 : 3 * h + 2] + terms[3 * h + 2 : 3 * h + 3]
                      for h in range(width // DH)])
    for head in range(width // DH):
        logs = [s[head] for s in stats]
        top = functools.reduce(jnp.maximum, logs)
        weights = [jnp.exp2(l - top) for l in logs]
        total = functools.reduce(jnp.add, weights)
        value = None
        for ref, weight in zip(refs, weights):
            part = ref[0, head * DH : (head + 1) * DH, :].astype(jnp.float32) * (weight / total)
            value = part if value is None else value + part
        emit(head, value, top + jnp.log2(total))


def merge_kernel(*refs):
    sources, (out_ref, stat_ref) = refs[:-3], refs[-2:]
    width = out_ref.shape[1] - stat_ref.shape[0]
    stat_ref[...] = jnp.zeros_like(stat_ref)

    def emit(head, value, log):
        out_ref[0, head * DH : (head + 1) * DH, :] = value.astype(jnp.bfloat16)
        for part, term in enumerate(split3(log)):
            stat_ref[3 * head + part : 3 * head + part + 1, :] = term

    combine(sources, width, emit)
    out_ref[0, width:, :] = stat_ref[...].astype(jnp.bfloat16)


def finish_kernel(*refs):
    sources, out_ref = refs[:-2], refs[-1]

    def emit(head, value, log):
        out_ref[:, head * DH : (head + 1) * DH] = jnp.transpose(value).astype(jnp.bfloat16)

    combine(sources, out_ref.shape[1], emit)


def join_parts(parts, width, dep, final):
    _, prow, rows = parts[0][0].shape
    specs = [pl.BlockSpec((1, prow, rows), functools.partial(lambda slot, i: (slot, 0, 0), slot)) for _, slot in parts]
    shape = (rows, width) if final else (1, prow, rows)
    return pl.pallas_call(
        finish_kernel if final else merge_kernel,
        out_shape=jax.ShapeDtypeStruct(shape, jnp.bfloat16),
        grid=(1,),
        in_specs=specs + [pl.BlockSpec(memory_space=pl.ANY)],
        out_specs=pl.BlockSpec(shape, lambda i: (0,) * len(shape)),
        scratch_shapes=[] if final else [pltpu.VMEM((prow - width, rows), jnp.float32)],
        compiler_params=pltpu.CompilerParams(vmem_limit_bytes=16 * MIB),
        cost_estimate=QUICK,
        name="finish" if final else "merge",
    )(*[array for array, _ in parts], dep)


def part_kernel(peers, count, start, peer_ref, *refs):
    rows = refs[0].shape[0]
    outs = refs[-peers:]
    for i, ref in enumerate(refs[: count * peers]):
        outs[i % peers][i // peers * rows : (i // peers + 1) * rows, :] = ref[:, start:]


def parts_for_peers(peer, arrays, start, peers, deps):
    rows, group = arrays[0].shape[0], arrays[0].shape[1] // peers
    specs = [pl.BlockSpec((rows, group), functools.partial(lambda k, i, t: (0, t[0] ^ k), k)) for k in range(peers)]
    shape = (len(arrays) * rows, group - start)
    return pl.pallas_call(
        functools.partial(part_kernel, peers, len(arrays), start),
        out_shape=[jax.ShapeDtypeStruct(shape, jnp.bfloat16)] * peers,
        grid_spec=pltpu.PrefetchScalarGridSpec(
            num_scalar_prefetch=1,
            grid=(1,),
            in_specs=specs * len(arrays) + [pl.BlockSpec(memory_space=pl.ANY)] * len(deps),
            out_specs=[pl.BlockSpec(shape, lambda i, t: (0, 0))] * peers,
        ),
        compiler_params=pltpu.CompilerParams(vmem_limit_bytes=28 * MIB),
        cost_estimate=QUICK,
        name="parts",
    )(peer.reshape(1), *[a for a in arrays for _ in range(peers)], *deps)


def regroup_kernel(peers, peer_ref, *refs):
    rows = refs[0].shape[0]
    for k in range(peers):
        here = pl.ds(pl.multiple_of((peer_ref[0] ^ k) * rows, rows), rows)
        start = 0
        for out_ref in refs[peers + 1 :]:
            width = out_ref.shape[1]
            out_ref[here, :] = refs[k][:, start : start + width]
            start += width


def regrouped(peer, pieces, widths, dep):
    peers, rows = len(pieces), pieces[0].shape[0]
    whole = lambda i, t: (0, 0)
    shapes = [(peers * rows, width) for width in widths]
    return pl.pallas_call(
        functools.partial(regroup_kernel, peers),
        out_shape=[jax.ShapeDtypeStruct(shape, jnp.bfloat16) for shape in shapes],
        grid_spec=pltpu.PrefetchScalarGridSpec(
            num_scalar_prefetch=1,
            grid=(1,),
            in_specs=[pl.BlockSpec(p.shape, whole) for p in pieces] + [pl.BlockSpec(memory_space=pl.ANY)],
            out_specs=[pl.BlockSpec(shape, whole) for shape in shapes],
        ),
        compiler_params=pltpu.CompilerParams(vmem_limit_bytes=16 * MIB),
        cost_estimate=QUICK,
        name="regroup",
    )(peer.reshape(1), *pieces, dep)


def join_kernel(*refs):
    pieces, (k_ref, v_ref, v_s) = refs[:-4], refs[-3:]
    rows = pieces[0].shape[0] // 2
    for i, piece in enumerate(pieces):
        k_ref[i * rows : (i + 1) * rows, :] = piece[:rows, :]
        v_s[i * rows : (i + 1) * rows, :] = piece[rows:, :]
    for at in range(0, v_s.shape[0], TILE):
        v_ref[:, at : at + TILE] = jnp.transpose(v_s[at : at + TILE, :])


def joined(pieces, dep):
    rows, group = pieces[0].shape[0] // 2 * len(pieces), pieces[0].shape[1]
    return pl.pallas_call(
        join_kernel,
        out_shape=[
            jax.ShapeDtypeStruct((rows, group), jnp.bfloat16),
            jax.ShapeDtypeStruct((group, rows), jnp.bfloat16),
        ],
        in_specs=[pl.BlockSpec(memory_space=pltpu.VMEM)] * len(pieces) + [pl.BlockSpec(memory_space=pl.ANY)],
        scratch_shapes=[pltpu.VMEM((rows, group), jnp.bfloat16)],
        compiler_params=pltpu.CompilerParams(vmem_limit_bytes=24 * MIB),
        cost_estimate=QUICK,
        name="join",
    )(*pieces, dep)


def shards(new_queries, new_keys, new_values, context_keys, context_values, keep_flags):
    n = lax.axis_size("blk")
    place = lax.axis_index("blk").astype(jnp.int32)
    peers = lax.axis_size("uly")
    own_rows = new_queries.shape[0]
    group = context_keys.shape[1]
    unit = group // PIECE_UNITS
    span_rows = own_rows * peers
    ctx_tiles, new_tiles = context_keys.shape[0] // TILE, span_rows // TILE

    peer = lax.axis_index("uly").astype(jnp.int32)
    new_order = jnp.arange(new_tiles, dtype=jnp.int32) ^ (peer * own_rows // TILE)
    new_kept = lax.dynamic_slice_in_dim(keep_flags, n * ctx_tiles + place * new_tiles, new_tiles, 1)
    kept = jnp.concatenate(
        [
            lax.dynamic_slice_in_dim(keep_flags, place * ctx_tiles, ctx_tiles, 1),
            jnp.sum(jnp.where(new_order[:, None] == jnp.arange(new_tiles), new_kept[:, None, :], 0), axis=2),
        ],
        axis=1,
    )
    kept = (kept == 1).astype(jnp.int32)
    count = len(PIECES)
    widths = [units * unit for _, units in PIECES]
    bits = [1 << k for k in range((n - 1).bit_length())]
    where = place.reshape(1)
    parts = [{d: [] for d in range(n)} for _ in range(count)]
    sent, backs = [None] * count, [None] * count

    def to_heads(pieces):
        moved = lax.all_to_all(pieces, "uly", split_axis=0, concat_axis=0, tiled=False)
        return moved.reshape(span_rows, pieces.shape[2])

    def to_peers(pieces):
        return [lax.ppermute(p, "uly", [(i, i ^ k) for i in range(peers)]) if k else p for k, p in enumerate(pieces)]

    def across(x, bit):
        return lax.ppermute(x, "blk", [(i, i ^ bit) for i in range(n)])

    def spread(span):
        found = {0: span}
        for bit in reversed(bits):
            for d in list(found):
                found[d ^ bit] = across(found[d], bit)
        return found

    early = widths[0]
    first_span = to_heads(jnp.stack([new_queries[:, p * group : p * group + early] for p in range(peers)]))
    found = [spread(first_span)]
    both = parts_for_peers(peer, [new_keys, new_values], 0, peers, [first_span])
    span_k, span_v_t = joined(to_peers(both), first_span)
    later = parts_for_peers(peer, [new_queries], early, peers, [both[0]])
    found += [spread(span) for span in regrouped(peer, to_peers(later), widths[1:], span_k)]
    context_values_t = context_values.T
    last = [span_k]

    def run_attend(c, distances):
        own = attend(
            where, kept, found[c], distances, context_keys, span_k, context_values_t, span_v_t,
            PIECES[c][0] // PIECES[c][1], last[0],
        )
        last[0] = own
        for slot, d in enumerate(distances):
            parts[c][d] = [(own, slot)]
        return own

    def run_sent(c):
        sent[c] = across(run_attend(c, list(range(1, n, 2))), 1)

    def run_kept(c):
        run_attend(c, list(range(0, n, 2)))
        for d in range(0, n, 2):
            parts[c][d].append((sent[c], d // 2))

    def run_merge(c):
        for bit in bits[1:]:
            for d in range(bit, n, 2 * bit):
                joint = join_parts(parts[c][d], widths[c], last[0], False)
                last[0] = joint
                parts[c][d ^ bit].append((across(joint, bit), 0))

    def run_finish(c):
        done = join_parts(parts[c][0], widths[c], last[0], True)
        last[0] = done
        done = done.reshape(peers, own_rows, widths[c])
        backs[c] = lax.all_to_all(done, "uly", split_axis=0, concat_axis=0, tiled=False)

    for c in range(count):
        run_sent(c)
        if c > 0:
            run_merge(c - 1)
        run_kept(c)
        if c > 0:
            run_finish(c - 1)
    run_merge(count - 1)
    run_finish(count - 1)

    in_order = [backs[c] for c in sorted(range(count), key=lambda c: PIECES[c][0])]
    together = jnp.concatenate(in_order, axis=2)
    return together.transpose(1, 0, 2).reshape(own_rows, peers * group)


def solution(mesh):
    in_specs = (
        P(("cfg", "blk", "uly"), None),
        P(("cfg", "blk", "uly"), None),
        P(("cfg", "blk", "uly"), None),
        P(("cfg", "blk"), "uly"),
        P(("cfg", "blk"), "uly"),
        P(),
    )
    out_specs = P(("cfg", "blk", "uly"), None)
    return jax.shard_map(shards, mesh=mesh, in_specs=in_specs, out_specs=out_specs, check_vma=False)
```

time: 323 us -> 290 us (0.90)
  waiting for transfers between devices: 46.2 us -> 140 us
  starting transfers between devices: 110 us -> 39.9 us
  local copies, waits for them, and re-layouts: 40.8 us -> 19.7 us
  Pallas kernels: 95.7 us -> 75.9 us
  blocking collectives: 24.5 us -> 11.2 us
    ppermute x36 -> x21, waiting for transfers between devices: 37.2 us -> 130 us  [the longest x15 122 us: across(): return lax.ppermute(x, 'blk', [(i, i ^ bit) for i in range(n)])]
    ppermute x36 -> x21, starting transfers between devices: 97.7 us -> 27.4 us  [the longest x15 24.5 us: across(): return lax.ppermute(x, 'blk', [(i, i ^ bit) for i in range(n)])]
    pallas_call x22 -> x15, Pallas kernels: 93.5 us -> 74.1 us  [the longest x6 68.2 us: attend(): pl.pallas_call(functools.partial(attend_kernel, distances), out_shape=jax...]
    unnamed x103 -> x49, local copies, waits for them, and re-layouts: 35.7 us -> 16.8 us
    all_to_all x1 -> x0, blocking collectives: 12.9 us -> none  [to_heads(): lax.all_to_all(pieces, 'uly', split_axis=0, concat_axis=0, tiled=False)]
  transfers between devices with their start and end apart: 39 -> 24, of which waited for: 10 -> 10; matrix products, arithmetic and copies ran while one was open for 2% -> 2% of each run, Pallas kernels for 30% -> 26%
where the time goes in v2:
time: 290 us; the launch traced here: 289 us
  waiting for transfers between devices  140 us (48%)
  Pallas kernels  75.9 us (26%)
  starting transfers between devices  39.9 us (14%)
  local copies, waits for them, and re-layouts  19.7 us (7%)
  blocking collectives  11.2 us (4%)
    ppermute x15, waiting for transfers between devices, across(): return lax.ppermute(x, 'blk', [(i, i ^ bit) for i in range(n)])  122 us
    pallas_call x6, Pallas kernels, attend(): pl.pallas_call(functools.partial(attend_kernel, distances), out_shape=jax...  68.2 us
    ppermute x15, starting transfers between devices, across(): return lax.ppermute(x, 'blk', [(i, i ^ bit) for i in range(n)])  24.5 us
    unnamed x49, local copies, waits for them, and re-layouts  16.8 us
    all_to_all x1, blocking collectives, run_finish(): lax.all_to_all(done, 'uly', split_axis=0, concat_axis=0, tiled=False)  11.2 us
    all_to_all x1, waiting for transfers between devices, to_heads(): lax.all_to_all(pieces, 'uly', split_axis=0, concat_axis=0, tiled=False)  9.45 us
    all_to_all x2, starting transfers between devices, run_finish(): lax.all_to_all(done, 'uly', split_axis=0, concat_axis=0, tiled=False)  8.27 us
    ppermute x6, waiting for transfers between devices, to_peers(): lax.ppermute(p, 'uly', [(i, i ^ k) for i in range(peers)])  7.81 us
  transfers between devices with their start and end apart: 24, of which 10 were waited for; matrix products, arithmetic and copies ran while one was open for 2% of the time, Pallas kernels for 26%

profile of v2, /device:TPU:0, one launch (start us, length us, event | category | flops | bytes accessed | tf_op | source)
XLA Modules:
  0.0 289.1 jit_solution(7519417888031082065)
XLA Ops:
  2.1 4.2 %all-to-all-start = ((bf16[4,128,512]{2,1,0:T(8,128)(2,1)}), bf16[4,128,512]{2,1,0:T(8,128)(2,1)}, u32[]{:S(2)}, u32[]{:S(2)}) async-start(bf16[4,128,512]{2,1,0:T(8,128)(2,1)} %pad_maximum_fusion), calls=%async_computation | async-start | bytes 1048576 | tf_op jit(solution)/shard_map/all_to_all | solution.py:350
  6.4 9.4 %all-to-all-done = bf16[4,128,512]{2,1,0:T(8,128)(2,1)} async-done(((bf16[4,128,512]{2,1,0:T(8,128)(2,1)}), bf16[4,128,512]{2,1,0:T(8,128)(2,1)}, u32[]{:S(2)}, u32[]{:S(2)}) %all-to-all-start) | async-done | bytes 524320 | tf_op jit(solution)/shard_map/all_to_all | solution.py:350
  21.5 3.4 %collective-permute-start = (bf16[512,512]{1,0:T(8,128)(2,1)}, bf16[512,512]{1,0:T(8,128)(2,1)}, u32[]{:S(2)}, u32[]{:S(2)}) collective-permute-start(bf16[512,512]{1,0:T(8,128)(2,1)} %bitcast.5.refs_8_.refs_4_.refs_0_), channel_id=1, source_target_pairs={{0,8},{4,12},{8,0},{12,4},{1,9},{5,13},{9,1},{13,5},{2,10},{6,14},... | collective-permute-start | bytes 1572872 | tf_op jit(solution)/shard_map/ppermute | solution.py:357
  26.7 22.3 %collective-permute-done.refs_1_ = bf16[512,512]{1,0:T(8,128)(2,1)} collective-permute-done((bf16[512,512]{1,0:T(8,128)(2,1)}, bf16[512,512]{1,0:T(8,128)(2,1)}, u32[]{:S(2)}, u32[]{:S(2)}) %collective-permute-start) | collective-permute-done | bytes 524320 | tf_op jit(solution)/shard_map/ppermute | solution.py:357
  52.2 4.2 %collective-permute-done.3.refs_3_ = bf16[256,1536]{1,0:T(8,128)(2,1)} collective-permute-done((bf16[256,1536]{1,0:T(8,128)(2,1)}, bf16[256,1536]{1,0:T(8,128)(2,1)}, u32[]{:S(2)}, u32[]{:S(2)}) %collective-permute-start.3) | collective-permute-done | bytes 786464 | tf_op jit(solution)/shard_map/ppermute | solution.py:354
  57.3 4.7 %copy.11 = bf16[1024,1536]{0,1:T(8,128)(2,1)} copy(bf16[1024,1536]{1,0:T(8,128)(2,1)} %param.10) | data formatting | bytes 6291456 | tf_op args[4]
  63.9 3.6 %collective-permute-done.9.refs_3_ = bf16[128,1024]{1,0:T(8,128)(2,1)S(1)} collective-permute-done((bf16[128,1024]{1,0:T(8,128)(2,1)}, bf16[128,1024]{1,0:T(8,128)(2,1)S(1)}, u32[]{:S(2)}, u32[]{:S(2)}) %collective-permute-start.9) | collective-permute-done | bytes 262176 | tf_op jit(solution)/shard_map/ppermute | solution.py:354
  67.6 3.5 %collective-permute-start.11 = (bf16[512,512]{1,0:T(8,128)(2,1)S(1)}, bf16[512,512]{1,0:T(8,128)(2,1)S(1)}, u32[]{:S(2)}, u32[]{:S(2)}) collective-permute-start(bf16[512,512]{1,0:T(8,128)(2,1)S(1)} %get-tuple-element.27.refs_0_), channel_id=1, source_target_pairs={{0,8},{4,12},{8,0},{12,4},{1,9},{5,13},{9,1},{13,5},{2,10},{6,14},... | collective-permute-start | bytes 1572872 | tf_op jit(solution)/shard_map/ppermute | solution.py:357
  73.2 11.8 %attend.6.refs_6_ = bf16[2,528,512]{2,1,0:T(8,128)(2,1)S(1)} custom-call(s32[1]{0:T(128)} %bitcast.place_ref, s32[16,12]{1,0:T(8,128)S(1)} %fusion.kept_ref, bf16[512,512]{1,0:T(8,128)(2,1)} %collective-permute-done.4.refs_0_, bf16[512,512]{1,0:T(8,128)(2,1)} %collective-permute-done.5.refs_1_, bf16[1024,1536]{1,0:T(8,128)(2,1)S(1)} %copy-done.16, ...), custom_call_target="tpu_custom_call" | custom-call | flops 6442450944 | bytes 5242880 | tf_op jit(solution)/shard_map/attend/pallas_call | solution.py:147
  87.0 8.2 %collective-permute-done.11.refs_1_ = bf16[512,512]{1,0:T(8,128)(2,1)S(1)} collective-permute-done((bf16[512,512]{1,0:T(8,128)(2,1)S(1)}, bf16[512,512]{1,0:T(8,128)(2,1)S(1)}, u32[]{:S(2)}, u32[]{:S(2)}) %collective-permute-start.11) | collective-permute-done | bytes 524320 | tf_op jit(solution)/shard_map/ppermute | solution.py:357
  96.0 11.8 %attend.7.refs_6_.refs_0_ = bf16[2,528,512]{2,1,0:T(8,128)(2,1)S(1)} custom-call(s32[1]{0:T(128)} %bitcast.place_ref, s32[16,12]{1,0:T(8,128)S(1)} %fusion.kept_ref, bf16[512,512]{1,0:T(8,128)(2,1)} %bitcast.5.refs_8_.refs_4_.refs_0_, bf16[512,512]{1,0:T(8,128)(2,1)} %collective-permute-done.refs_1_, bf16[1024,1536]{1,0:T(8,128)(2,1)S(1)} %copy-done.16, ...), custom_call_target="tpu_custom_call" | custom-call | flops 6442450944 | bytes 5242880 | tf_op jit(solution)/shard_map/attend/pallas_call | solution.py:147
  107.8 9.5 %collective-permute-done.16.refs_1_ = bf16[512,512]{1,0:T(8,128)(2,1)S(1)} collective-permute-done((bf16[512,512]{1,0:T(8,128)(2,1)S(1)}, bf16[512,512]{1,0:T(8,128)(2,1)S(1)}, u32[]{:S(2)}, u32[]{:S(2)}) %collective-permute-start.16) | collective-permute-done | bytes 524320 | tf_op jit(solution)/shard_map/ppermute | solution.py:357
  117.9 34.9 %collective-permute-done.12.refs_1_ = bf16[512,512]{1,0:T(8,128)(2,1)S(1)} collective-permute-done((bf16[512,512]{1,0:T(8,128)(2,1)S(1)}, bf16[512,512]{1,0:T(8,128)(2,1)S(1)}, u32[]{:S(2)}, u32[]{:S(2)}) %collective-permute-start.12) | collective-permute-done | bytes 524320 | tf_op jit(solution)/shard_map/ppermute | solution.py:357
  152.9 11.5 %attend.8.refs_2_ = bf16[2,528,512]{2,1,0:T(8,128)(2,1)} custom-call(s32[1]{0:T(128)} %bitcast.place_ref, s32[16,12]{1,0:T(8,128)S(1)} %fusion.kept_ref, bf16[512,512]{1,0:T(8,128)(2,1)S(1)} %collective-permute-done.10.refs_0_, bf16[512,512]{1,0:T(8,128)(2,1)S(1)} %collective-permute-done.12.refs_1_, bf16[1024,1536]{1,0:T(8,128)(2,1)S(1)} %copy-done.16, ...), custom_call_target="tpu_custom_call" | custom-call | flops 6442450944 | bytes 5242880 | tf_op jit(solution)/shard_map/attend/pallas_call | solution.py:147
  167.8 10.7 %attend.9.refs_3_.refs_0_ = bf16[2,528,512]{2,1,0:T(8,128)(2,1)S(1)} custom-call(s32[1]{0:T(128)} %bitcast.place_ref, s32[16,12]{1,0:T(8,128)S(1)} %fusion.kept_ref, bf16[512,512]{1,0:T(8,128)(2,1)S(1)} %get-tuple-element.27.refs_0_, bf16[512,512]{1,0:T(8,128)(2,1)S(1)} %collective-permute-done.11.refs_1_, bf16[1024,1536]{1,0:T(8,128)(2,1)S(1)} %copy-done.16, ...), custom_call_target="tpu_custom_call" | custom-call | flops 6442450944 | bytes 5242880 | tf_op jit(solution)/shard_map/attend/pallas_call | solution.py:147
  178.5 20.8 %collective-permute-done.13.refs_2_ = bf16[1,528,512]{2,1,0:T(8,128)(2,1)S(1)} collective-permute-done((bf16[1,528,512]{2,1,0:T(8,128)(2,1)S(1)}, bf16[1,528,512]{2,1,0:T(8,128)(2,1)S(1)}, u32[]{:S(2)}, u32[]{:S(2)}) %collective-permute-start.13) | collective-permute-done | bytes 540704 | tf_op jit(solution)/shard_map/ppermute | solution.py:357
  199.9 11.7 %attend.10.refs_2_ = bf16[2,528,512]{2,1,0:T(8,128)(2,1)} custom-call(s32[1]{0:T(128)} %bitcast.place_ref, s32[16,12]{1,0:T(8,128)S(1)} %fusion.kept_ref, bf16[512,512]{1,0:T(8,128)(2,1)S(1)} %collective-permute-done.15.refs_0_, bf16[512,512]{1,0:T(8,128)(2,1)S(1)} %collective-permute-done.17.refs_1_, bf16[1024,1536]{1,0:T(8,128)(2,1)S(1)} %copy-done.16, ...), custom_call_target="tpu_custom_call" | custom-call | flops 6442450944 | bytes 5242880 | tf_op jit(solution)/shard_map/attend/pallas_call | solution.py:147
  214.0 4.1 %all-to-all-start.1 = ((bf16[4,128,512]{2,1,0:T(8,128)(2,1)}), bf16[4,128,512]{2,1,0:T(8,128)(2,1)}, u32[]{:S(2)}, u32[]{:S(2)}) async-start(bf16[4,128,512]{2,1,0:T(8,128)(2,1)} %bitcast.25), calls=%async_computation.1 | async-start | bytes 1048576 | tf_op jit(solution)/shard_map/all_to_all | solution.py:405
  226.2 10.7 %attend.11.refs_3_.refs_0_ = bf16[2,528,512]{2,1,0:T(8,128)(2,1)S(1)} custom-call(s32[1]{0:T(128)} %bitcast.place_ref, s32[16,12]{1,0:T(8,128)S(1)} %fusion.kept_ref, bf16[512,512]{1,0:T(8,128)(2,1)S(1)} %copy-done.21, bf16[512,512]{1,0:T(8,128)(2,1)S(1)} %copy-done.23, bf16[1024,1536]{1,0:T(8,128)(2,1)S(1)} %copy-done.17, bf16[512,1536]{1,0:T(8,128)(2,1)S(1)} %copy-done.13, ...), custom_call_target="tpu_custom_call" | custom-call | flops 6442450944 | bytes 5242880 | tf_op jit(solution)/shard_map/attend/pallas_call | solution.py:147
  236.9 9.8 %collective-permute-done.18.refs_2_ = bf16[1,528,512]{2,1,0:T(8,128)(2,1)S(1)} collective-permute-done((bf16[1,528,512]{2,1,0:T(8,128)(2,1)S(1)}, bf16[1,528,512]{2,1,0:T(8,128)(2,1)S(1)}, u32[]{:S(2)}, u32[]{:S(2)}) %collective-permute-start.18) | collective-permute-done | bytes 540704 | tf_op jit(solution)/shard_map/ppermute | solution.py:357
  248.4 3.4 %collective-permute-start.20 = (bf16[1,528,512]{2,1,0:T(8,128)(2,1)S(1)}, bf16[1,528,512]{2,1,0:T(8,128)(2,1)S(1)}, u32[]{:S(2)}, u32[]{:S(2)}) collective-permute-start(bf16[1,528,512]{2,1,0:T(8,128)(2,1)S(1)} %merge.5.refs_3_), channel_id=1, source_target_pairs={{0,8},{4,12},{8,0},{12,4},{1,9},{5,13},{9,1},{13,5},{2,10},{6,14},... | collective-permute-start | bytes 1622024 | tf_op jit(solution)/shard_map/ppermute | solution.py:357
  251.9 4.1 %all-to-all-start.2 = ((bf16[4,128,512]{2,1,0:T(8,128)(2,1)}), bf16[4,128,512]{2,1,0:T(8,128)(2,1)}, u32[]{:S(2)}, u32[]{:S(2)}) async-start(bf16[4,128,512]{2,1,0:T(8,128)(2,1)} %bitcast.9), calls=%async_computation.2 | async-start | bytes 1048576 | tf_op jit(solution)/shard_map/all_to_all | solution.py:405
  256.0 16.9 %collective-permute-done.20.refs_2_ = bf16[1,528,512]{2,1,0:T(8,128)(2,1)S(1)} collective-permute-done((bf16[1,528,512]{2,1,0:T(8,128)(2,1)S(1)}, bf16[1,528,512]{2,1,0:T(8,128)(2,1)S(1)}, u32[]{:S(2)}, u32[]{:S(2)}) %collective-permute-start.20) | collective-permute-done | bytes 540704 | tf_op jit(solution)/shard_map/ppermute | solution.py:357
  275.2 11.2 %all_to_all.20 = bf16[4,128,512]{2,1,0:T(8,128)(2,1)S(1)} all-to-all(bf16[4,128,512]{2,1,0:T(8,128)(2,1)S(1)} %bitcast.26), channel_id=1, replica_groups=mesh['cfg'=2,'blk'=4,'uly'=4] {'uly'}, dimensions={0} | all-to-all | bytes 1048576 | tf_op jit(solution)/shard_map/all_to_all | solution.py:405
  (102 shorter events, 42.2 us)
Async XLA Ops:
  2.1 13.7 %all-to-all-start = ((bf16[4,128,512]{2,1,0:T(8,128)(2,1)}), bf16[4,128,512]{2,1,0:T(8,128)(2,1)}, u32[]{:S(2)}, u32[]{:S(2)}) async-start(bf16[4,128,512]{2,1,0:T(8,128)(2,1)} %pad_maximum_fusion), calls=%async_computation | async-start | bytes 1048576 | tf_op jit(solution)/shard_map/all_to_all | solution.py:350
  19.7 32.1 %collective-permute-start.1 = (bf16[256,1536]{1,0:T(8,128)(2,1)}, bf16[256,1536]{1,0:T(8,128)(2,1)S(1)}, u32[]{:S(2)}, u32[]{:S(2)}) collective-permute-start(bf16[256,1536]{1,0:T(8,128)(2,1)} %get-tuple-element.18), channel_id=1, source_target_pairs={{0,1},{1,0},{2,3},{3,2},{4,5},{5,4},{6,7},{7,6},{8,9},{9,8},{10,11... | collective-permute-start | bytes 2359304 | tf_op jit(solution)/shard_map/ppermute | solution.py:354
  19.7 32.1 %collective-permute-start.2 = (bf16[256,1536]{1,0:T(8,128)(2,1)}, bf16[256,1536]{1,0:T(8,128)(2,1)S(1)}, u32[]{:S(2)}, u32[]{:S(2)}) collective-permute-start(bf16[256,1536]{1,0:T(8,128)(2,1)} %get-tuple-element.19), channel_id=1, source_target_pairs={{0,2},{1,3},{2,0},{3,1},{4,6},{5,7},{6,4},{7,5},{8,10},{9,11},{10,... | collective-permute-start | bytes 2359304 | tf_op jit(solution)/shard_map/ppermute | solution.py:354
  19.7 36.7 %collective-permute-start.3 = (bf16[256,1536]{1,0:T(8,128)(2,1)}, bf16[256,1536]{1,0:T(8,128)(2,1)}, u32[]{:S(2)}, u32[]{:S(2)}) collective-permute-start(bf16[256,1536]{1,0:T(8,128)(2,1)} %get-tuple-element.20), channel_id=1, source_target_pairs={{0,3},{1,2},{2,1},{3,0},{4,7},{5,6},{6,5},{7,4},{8,11},{9,10},{10,... | collective-permute-start | bytes 2359304 | tf_op jit(solution)/shard_map/ppermute | solution.py:354
  21.5 27.4 %collective-permute-start = (bf16[512,512]{1,0:T(8,128)(2,1)}, bf16[512,512]{1,0:T(8,128)(2,1)}, u32[]{:S(2)}, u32[]{:S(2)}) collective-permute-start(bf16[512,512]{1,0:T(8,128)(2,1)} %bitcast.5.refs_8_.refs_4_.refs_0_), channel_id=1, source_target_pairs={{0,8},{4,12},{8,0},{12,4},{1,9},{5,13},{9,1},{13,5},{2,10},{6,14},... | collective-permute-start | bytes 1572872 | tf_op jit(solution)/shard_map/ppermute | solution.py:357
  25.1 47.9 %collective-permute-start.4 = (bf16[512,512]{1,0:T(8,128)(2,1)}, bf16[512,512]{1,0:T(8,128)(2,1)}, u32[]{:S(2)}, u32[]{:S(2)}) collective-permute-start(bf16[512,512]{1,0:T(8,128)(2,1)} %bitcast.5.refs_8_.refs_4_.refs_0_), channel_id=1, source_target_pairs={{0,4},{4,0},{8,12},{12,8},{1,5},{5,1},{9,13},{13,9},{2,6},{6,2},{1... | collective-permute-start | bytes 1572872 | tf_op jit(solution)/shard_map/ppermute | solution.py:357
  49.0 24.2 %collective-permute-start.5 = (bf16[512,512]{1,0:T(8,128)(2,1)}, bf16[512,512]{1,0:T(8,128)(2,1)}, u32[]{:S(2)}, u32[]{:S(2)}) collective-permute-start(bf16[512,512]{1,0:T(8,128)(2,1)} %collective-permute-done.refs_1_), channel_id=1, source_target_pairs={{0,4},{4,0},{8,12},{12,8},{1,5},{5,1},{9,13},{13,9},{2,6},{6,2},{1... | collective-permute-start | bytes 1572872 | tf_op jit(solution)/shard_map/ppermute | solution.py:357
  51.8 12.1 %collective-permute-start.7 = (bf16[128,1024]{1,0:T(8,128)(2,1)}, bf16[128,1024]{1,0:T(8,128)(2,1)S(1)}, u32[]{:S(2)}, u32[]{:S(2)}) collective-permute-start(bf16[128,1024]{1,0:T(8,128)(2,1)} %get-tuple-element.24), channel_id=1, source_target_pairs={{0,1},{1,0},{2,3},{3,2},{4,5},{5,4},{6,7},{7,6},{8,9},{9,8},{10,11... | collective-permute-start | bytes 786440 | tf_op jit(solution)/shard_map/ppermute | solution.py:354
  51.8 12.1 %collective-permute-start.8 = (bf16[128,1024]{1,0:T(8,128)(2,1)}, bf16[128,1024]{1,0:T(8,128)(2,1)S(1)}, u32[]{:S(2)}, u32[]{:S(2)}) collective-permute-start(bf16[128,1024]{1,0:T(8,128)(2,1)} %get-tuple-element.25), channel_id=1, source_target_pairs={{0,2},{1,3},{2,0},{3,1},{4,6},{5,7},{6,4},{7,5},{8,10},{9,11},{10,... | collective-permute-start | bytes 786440 | tf_op jit(solution)/shard_map/ppermute | solution.py:354
  56.4 11.1 %collective-permute-start.9 = (bf16[128,1024]{1,0:T(8,128)(2,1)}, bf16[128,1024]{1,0:T(8,128)(2,1)S(1)}, u32[]{:S(2)}, u32[]{:S(2)}) collective-permute-start(bf16[128,1024]{1,0:T(8,128)(2,1)} %get-tuple-element.26), channel_id=1, source_target_pairs={{0,3},{1,2},{2,1},{3,0},{4,7},{5,6},{6,5},{7,4},{8,11},{9,10},{10,... | collective-permute-start | bytes 786440 | tf_op jit(solution)/shard_map/ppermute | solution.py:354
  67.6 27.5 %collective-permute-start.11 = (bf16[512,512]{1,0:T(8,128)(2,1)S(1)}, bf16[512,512]{1,0:T(8,128)(2,1)S(1)}, u32[]{:S(2)}, u32[]{:S(2)}) collective-permute-start(bf16[512,512]{1,0:T(8,128)(2,1)S(1)} %get-tuple-element.27.refs_0_), channel_id=1, source_target_pairs={{0,8},{4,12},{8,0},{12,4},{1,9},{5,13},{9,1},{13,5},{2,10},{6,14},... | collective-permute-start | bytes 1572872 | tf_op jit(solution)/shard_map/ppermute | solution.py:357
  71.1 46.8 %collective-permute-start.10 = (bf16[512,512]{1,0:T(8,128)(2,1)S(1)}, bf16[512,512]{1,0:T(8,128)(2,1)S(1)}, u32[]{:S(2)}, u32[]{:S(2)}) collective-permute-start(bf16[512,512]{1,0:T(8,128)(2,1)S(1)} %get-tuple-element.27.refs_0_), channel_id=1, source_target_pairs={{0,4},{4,0},{8,12},{12,8},{1,5},{5,1},{9,13},{13,9},{2,6},{6,2},{1... | collective-permute-start | bytes 1572872 | tf_op jit(solution)/shard_map/ppermute | solution.py:357
  72.7 44.6 %collective-permute-start.16 = (bf16[512,512]{1,0:T(8,128)(2,1)S(1)}, bf16[512,512]{1,0:T(8,128)(2,1)S(1)}, u32[]{:S(2)}, u32[]{:S(2)}) collective-permute-start(bf16[512,512]{1,0:T(8,128)(2,1)S(1)} %get-tuple-element.28.refs_0_), channel_id=1, source_target_pairs={{0,8},{4,12},{8,0},{12,4},{1,9},{5,13},{9,1},{13,5},{2,10},{6,14},... | collective-permute-start | bytes 1572872 | tf_op jit(solution)/shard_map/ppermute | solution.py:357
  73.0 126.8 %collective-permute-start.15 = (bf16[512,512]{1,0:T(8,128)(2,1)S(1)}, bf16[512,512]{1,0:T(8,128)(2,1)S(1)}, u32[]{:S(2)}, u32[]{:S(2)}) collective-permute-start(bf16[512,512]{1,0:T(8,128)(2,1)S(1)} %get-tuple-element.28.refs_0_), channel_id=1, source_target_pairs={{0,4},{4,0},{8,12},{12,8},{1,5},{5,1},{9,13},{13,9},{2,6},{6,2},{1... | collective-permute-start | bytes 1572872 | tf_op jit(solution)/shard_map/ppermute | solution.py:357
  85.1 80.5 %collective-permute-start.6 = (bf16[2,528,512]{2,1,0:T(8,128)(2,1)S(1)}, bf16[2,528,512]{2,1,0:T(8,128)(2,1)S(1)}, u32[]{:S(2)}, u32[]{:S(2)}) collective-permute-start(bf16[2,528,512]{2,1,0:T(8,128)(2,1)S(1)} %attend.6.refs_6_), channel_id=1, source_target_pairs={{0,4},{4,0},{8,12},{12,8},{1,5},{5,1},{9,13},{13,9},{2,6},{6,2},{1... | collective-permute-start | bytes 3244040 | tf_op jit(solution)/shard_map/ppermute | solution.py:357
  95.2 57.7 %collective-permute-start.12 = (bf16[512,512]{1,0:T(8,128)(2,1)S(1)}, bf16[512,512]{1,0:T(8,128)(2,1)S(1)}, u32[]{:S(2)}, u32[]{:S(2)}) collective-permute-start(bf16[512,512]{1,0:T(8,128)(2,1)S(1)} %collective-permute-done.11.refs_1_), channel_id=1, source_target_pairs={{0,4},{4,0},{8,12},{12,8},{1,5},{5,1},{9,13},{13,9},{2,6},{6,2},{1... | collective-permute-start | bytes 1572872 | tf_op jit(solution)/shard_map/ppermute | solution.py:357
  117.3 82.6 %collective-permute-start.17 = (bf16[512,512]{1,0:T(8,128)(2,1)S(1)}, bf16[512,512]{1,0:T(8,128)(2,1)S(1)}, u32[]{:S(2)}, u32[]{:S(2)}) collective-permute-start(bf16[512,512]{1,0:T(8,128)(2,1)S(1)} %collective-permute-done.16.refs_1_), channel_id=1, source_target_pairs={{0,4},{4,0},{8,12},{12,8},{1,5},{5,1},{9,13},{13,9},{2,6},{6,2},{1... | collective-permute-start | bytes 1572872 | tf_op jit(solution)/shard_map/ppermute | solution.py:357
  164.4 53.7 %collective-permute-start.14 = (bf16[2,528,512]{2,1,0:T(8,128)(2,1)}, bf16[2,528,512]{2,1,0:T(8,128)(2,1)S(1)}, u32[]{:S(2)}, u32[]{:S(2)}) collective-permute-start(bf16[2,528,512]{2,1,0:T(8,128)(2,1)} %attend.8.refs_2_), channel_id=1, source_target_pairs={{0,4},{4,0},{8,12},{12,8},{1,5},{5,1},{9,13},{13,9},{2,6},{6,2},{1... | collective-permute-start | bytes 3244040 | tf_op jit(solution)/shard_map/ppermute | solution.py:357
  165.9 33.4 %collective-permute-start.13 = (bf16[1,528,512]{2,1,0:T(8,128)(2,1)S(1)}, bf16[1,528,512]{2,1,0:T(8,128)(2,1)S(1)}, u32[]{:S(2)}, u32[]{:S(2)}) collective-permute-start(bf16[1,528,512]{2,1,0:T(8,128)(2,1)S(1)} %merge.3.refs_6_), channel_id=1, source_target_pairs={{0,8},{4,12},{8,0},{12,4},{1,9},{5,13},{9,1},{13,5},{2,10},{6,14},... | collective-permute-start | bytes 1622024 | tf_op jit(solution)/shard_map/ppermute | solution.py:357
  211.6 36.5 %collective-permute-start.19 = (bf16[2,528,512]{2,1,0:T(8,128)(2,1)}, bf16[2,528,512]{2,1,0:T(8,128)(2,1)S(1)}, u32[]{:S(2)}, u32[]{:S(2)}) collective-permute-start(bf16[2,528,512]{2,1,0:T(8,128)(2,1)} %attend.10.refs_2_), channel_id=1, source_target_pairs={{0,4},{4,0},{8,12},{12,8},{1,5},{5,1},{9,13},{13,9},{2,6},{6,2},{1... | collective-permute-start | bytes 3244040 | tf_op jit(solution)/shard_map/ppermute | solution.py:357
  214.0 37.9 %all-to-all-start.1 = ((bf16[4,128,512]{2,1,0:T(8,128)(2,1)}), bf16[4,128,512]{2,1,0:T(8,128)(2,1)}, u32[]{:S(2)}, u32[]{:S(2)}) async-start(bf16[4,128,512]{2,1,0:T(8,128)(2,1)} %bitcast.25), calls=%async_computation.1 | async-start | bytes 1048576 | tf_op jit(solution)/shard_map/all_to_all | solution.py:405
  219.1 27.7 %collective-permute-start.18 = (bf16[1,528,512]{2,1,0:T(8,128)(2,1)S(1)}, bf16[1,528,512]{2,1,0:T(8,128)(2,1)S(1)}, u32[]{:S(2)}, u32[]{:S(2)}) collective-permute-start(bf16[1,528,512]{2,1,0:T(8,128)(2,1)S(1)} %merge.4.refs_6_), channel_id=1, source_target_pairs={{0,8},{4,12},{8,0},{12,4},{1,9},{5,13},{9,1},{13,5},{2,10},{6,14},... | collective-permute-start | bytes 1622024 | tf_op jit(solution)/shard_map/ppermute | solution.py:357
  248.4 24.5 %collective-permute-start.20 = (bf16[1,528,512]{2,1,0:T(8,128)(2,1)S(1)}, bf16[1,528,512]{2,1,0:T(8,128)(2,1)S(1)}, u32[]{:S(2)}, u32[]{:S(2)}) collective-permute-start(bf16[1,528,512]{2,1,0:T(8,128)(2,1)S(1)} %merge.5.refs_3_), channel_id=1, source_target_pairs={{0,8},{4,12},{8,0},{12,4},{1,9},{5,13},{9,1},{13,5},{2,10},{6,14},... | collective-permute-start | bytes 1622024 | tf_op jit(solution)/shard_map/ppermute | solution.py:357
  251.9 23.3 %all-to-all-start.2 = ((bf16[4,128,512]{2,1,0:T(8,128)(2,1)}), bf16[4,128,512]{2,1,0:T(8,128)(2,1)}, u32[]{:S(2)}, u32[]{:S(2)}) async-start(bf16[4,128,512]{2,1,0:T(8,128)(2,1)} %bitcast.9), calls=%async_computation.2 | async-start | bytes 1048576 | tf_op jit(solution)/shard_map/all_to_all | solution.py:405
  (24 other events, 485.7 us)

commit v3 on v2

--- a/solution.py
+++ b/solution.py
@@ -262,34 +262,31 @@
     )(peer.reshape(1), *[a for a in arrays for _ in range(peers)], *deps)
 
 
-def regroup_kernel(peers, peer_ref, *refs):
-    rows = refs[0].shape[0]
+def regroup_kernel(peers, start, peer_ref, *refs):
+    out_ref = refs[-1]
+    rows, width = refs[0].shape[0], out_ref.shape[1]
     for k in range(peers):
         here = pl.ds(pl.multiple_of((peer_ref[0] ^ k) * rows, rows), rows)
-        start = 0
-        for out_ref in refs[peers + 1 :]:
-            width = out_ref.shape[1]
-            out_ref[here, :] = refs[k][:, start : start + width]
-            start += width
-
-
-def regrouped(peer, pieces, widths, dep):
+        out_ref[here, :] = refs[k][:, start : start + width]
+
+
+def regrouped(peer, pieces, start, width, deps):
     peers, rows = len(pieces), pieces[0].shape[0]
     whole = lambda i, t: (0, 0)
-    shapes = [(peers * rows, width) for width in widths]
+    shape = (peers * rows, width)
     return pl.pallas_call(
-        functools.partial(regroup_kernel, peers),
-        out_shape=[jax.ShapeDtypeStruct(shape, jnp.bfloat16) for shape in shapes],
+        functools.partial(regroup_kernel, peers, start),
+        out_shape=jax.ShapeDtypeStruct(shape, jnp.bfloat16),
         grid_spec=pltpu.PrefetchScalarGridSpec(
             num_scalar_prefetch=1,
             grid=(1,),
-            in_specs=[pl.BlockSpec(p.shape, whole) for p in pieces] + [pl.BlockSpec(memory_space=pl.ANY)],
-            out_specs=[pl.BlockSpec(shape, whole) for shape in shapes],
+            in_specs=[pl.BlockSpec(p.shape, whole) for p in pieces] + [pl.BlockSpec(memory_space=pl.ANY)] * len(deps),
+            out_specs=pl.BlockSpec(shape, whole),
         ),
         compiler_params=pltpu.CompilerParams(vmem_limit_bytes=16 * MIB),
         cost_estimate=QUICK,
         name="regroup",
-    )(peer.reshape(1), *pieces, dep)
+    )(peer.reshape(1), *pieces, *deps)
 
 
 def join_kernel(*refs):
@@ -366,10 +363,18 @@
     early = widths[0]
     first_span = to_heads(jnp.stack([new_queries[:, p * group : p * group + early] for p in range(peers)]))
     found = [spread(first_span)]
-    both = parts_for_peers(peer, [new_keys, new_values], 0, peers, [first_span])
-    span_k, span_v_t = joined(to_peers(both), first_span)
-    later = parts_for_peers(peer, [new_queries], early, peers, [both[0]])
-    found += [spread(span) for span in regrouped(peer, to_peers(later), widths[1:], span_k)]
+    parts_q = parts_for_peers(peer, [new_queries], early, peers, [first_span])
+    later = to_peers(parts_q)
+    parts_kv = parts_for_peers(peer, [new_keys, new_values], 0, peers, [*later, found[0][n // 2]])
+
+    def run_spread(c, deps):
+        span = regrouped(peer, later, PIECES[c][0] * unit - early, widths[c], deps)
+        found.append(spread(span))
+        return span
+
+    for c in range(1, count):
+        latest = run_spread(c, [found[c - 1][n // 2]])
+    span_k, span_v_t = joined(to_peers(parts_kv), latest)
     context_values_t = context_values.T
     last = [span_k]
 
@@ -409,9 +414,10 @@
         if c > 0:
             run_merge(c - 1)
         run_kept(c)
-        if c > 0:
+        if 0 < c < count - 1:
             run_finish(c - 1)
     run_merge(count - 1)
+    run_finish(count - 2)
     run_finish(count - 1)
 
     in_order = [backs[c] for c in sorted(range(count), key=lambda c: PIECES[c][0])]

time: 290 us -> 294 us (1.014)
  blocking collectives: 11.2 us -> 24.2 us
  waiting for transfers between devices: 140 us -> 127 us
  Pallas kernels: 75.9 us -> 82.1 us
  starting transfers between devices: 39.9 us -> 33.9 us
  local copies, waits for them, and re-layouts: 19.7 us -> 23.9 us
    ppermute x15, waiting for transfers between devices: 122 us -> 107 us  [across(): return lax.ppermute(x, 'blk', [(i, i ^ bit) for i in range(n)])]
    all_to_all x0 -> x1, blocking collectives: none -> 13 us  [to_heads(): lax.all_to_all(pieces, 'uly', split_axis=0, concat_axis=0, tiled=False)]
    ppermute x6, waiting for transfers between devices: 7.81 us -> 20.2 us  [to_peers(): lax.ppermute(p, 'uly', [(i, i ^ k) for i in range(peers)])]
    all_to_all x1 -> x0, waiting for transfers between devices: 9.45 us -> none  [to_heads(): lax.all_to_all(pieces, 'uly', split_axis=0, concat_axis=0, tiled=False)]
    pallas_call x6, Pallas kernels: 3.24 us -> 8.93 us  [join_parts(): pl.pallas_call(finish_kernel if final else merge_kernel, out_shape=jax.Sh...]
    unnamed x49 -> x59, local copies, waits for them, and re-layouts: 16.8 us -> 21.1 us
    all_to_all x1 -> x0, starting transfers between devices: 4.24 us -> none  [to_heads(): lax.all_to_all(pieces, 'uly', split_axis=0, concat_axis=0, tiled=False)]
  transfers between devices with their start and end apart: 24 -> 23, of which waited for: 10 -> 12; matrix products, arithmetic and copies ran while one was open for 2% -> 1% of each run, Pallas kernels for 26% -> 28%
where the time goes in v3:
time: 294 us; the launch traced here: 293 us
  waiting for transfers between devices  127 us (43%)
  Pallas kernels  82.1 us (28%)
  starting transfers between devices  33.9 us (12%)
  blocking collectives  24.2 us (8%)
  local copies, waits for them, and re-layouts  23.9 us (8%)
    ppermute x15, waiting for transfers between devices, across(): return lax.ppermute(x, 'blk', [(i, i ^ bit) for i in range(n)])  107 us
    pallas_call x6, Pallas kernels, attend(): pl.pallas_call(functools.partial(attend_kernel, distances), out_shape=jax...  68.3 us
    ppermute x15, starting transfers between devices, across(): return lax.ppermute(x, 'blk', [(i, i ^ bit) for i in range(n)])  21.9 us
    unnamed x59, local copies, waits for them, and re-layouts  21.1 us
    ppermute x6, waiting for transfers between devices, to_peers(): lax.ppermute(p, 'uly', [(i, i ^ k) for i in range(peers)])  20.2 us
    all_to_all x1, blocking collectives, to_heads(): lax.all_to_all(pieces, 'uly', split_axis=0, concat_axis=0, tiled=False)  13 us
    all_to_all x1, blocking collectives, run_finish(): lax.all_to_all(done, 'uly', split_axis=0, concat_axis=0, tiled=False)  11.2 us
    pallas_call x6, Pallas kernels, join_parts(): pl.pallas_call(finish_kernel if final else merge_kernel, out_shape=jax.Sh...  8.93 us
  transfers between devices with their start and end apart: 23, of which 12 were waited for; matrix products, arithmetic and copies ran while one was open for 1% of the time, Pallas kernels for 28%

profile of v3, /device:TPU:0, one launch (start us, length us, event | category | flops | bytes accessed | tf_op | source)
XLA Modules:
  0.0 293.1 jit_solution(5483023446327936909)
XLA Ops:
  1.3 13.0 %all_to_all.20 = bf16[4,128,512]{2,1,0:T(8,128)(2,1)} all-to-all(bf16[4,128,512]{2,1,0:T(8,128)(2,1)S(1)} %pad_maximum_fusion), channel_id=1, replica_groups=mesh['cfg'=2,'blk'=4,'uly'=4] {'uly'}, dimensions={0} | all-to-all | bytes 1048576 | tf_op jit(solution)/shard_map/all_to_all | solution.py:347
  19.3 7.3 %collective-permute-done.2.refs_10_.refs_2_ = bf16[128,1024]{1,0:T(8,128)(2,1)S(1)} collective-permute-done((bf16[128,1024]{1,0:T(8,128)(2,1)S(1)}, bf16[128,1024]{1,0:T(8,128)(2,1)S(1)}, u32[]{:S(2)}, u32[]{:S(2)}) %collective-permute-start.2) | collective-permute-done | bytes 262176 | tf_op jit(solution)/shard_map/ppermute | solution.py:351
  26.6 4.7 %collective-permute-done.3.refs_11_.refs_3_ = bf16[128,1024]{1,0:T(8,128)(2,1)S(1)} collective-permute-done((bf16[128,1024]{1,0:T(8,128)(2,1)S(1)}, bf16[128,1024]{1,0:T(8,128)(2,1)S(1)}, u32[]{:S(2)}, u32[]{:S(2)}) %collective-permute-start.3) | collective-permute-done | bytes 262176 | tf_op jit(solution)/shard_map/ppermute | solution.py:351
  31.4 9.1 %collective-permute-done.refs_12_.refs_4_.refs_1_ = bf16[512,512]{1,0:T(8,128)(2,1)} collective-permute-done((bf16[512,512]{1,0:T(8,128)(2,1)}, bf16[512,512]{1,0:T(8,128)(2,1)}, u32[]{:S(2)}, u32[]{:S(2)}) %collective-permute-start) | collective-permute-done | bytes 524320 | tf_op jit(solution)/shard_map/ppermute | solution.py:354
  49.3 4.1 %collective-permute-start.8 = (bf16[512,512]{1,0:T(8,128)(2,1)}, bf16[512,512]{1,0:T(8,128)(2,1)}, u32[]{:S(2)}, u32[]{:S(2)}) collective-permute-start(bf16[512,512]{1,0:T(8,128)(2,1)} %bitcast.5.refs_4_.refs_0_), channel_id=1, source_target_pairs={{0,4},{4,0},{8,12},{12,8},{1,5},{5,1},{9,13},{13,9},{2,6},{6,2},{1... | collective-permute-start | bytes 1572872 | tf_op jit(solution)/shard_map/ppermute | solution.py:354
  53.4 13.8 %collective-permute-done.7.refs_4_.refs_1_ = bf16[512,512]{1,0:T(8,128)(2,1)} collective-permute-done((bf16[512,512]{1,0:T(8,128)(2,1)}, bf16[512,512]{1,0:T(8,128)(2,1)}, u32[]{:S(2)}, u32[]{:S(2)}) %collective-permute-start.7) | collective-permute-done | bytes 524320 | tf_op jit(solution)/shard_map/ppermute | solution.py:354
  75.9 8.2 %collective-permute-done.6.refs_3_ = bf16[256,1536]{1,0:T(8,128)(2,1)} collective-permute-done((bf16[256,1536]{1,0:T(8,128)(2,1)}, bf16[256,1536]{1,0:T(8,128)(2,1)}, u32[]{:S(2)}, u32[]{:S(2)}) %collective-permute-start.6) | collective-permute-done | bytes 786464 | tf_op jit(solution)/shard_map/ppermute | solution.py:351
  84.0 4.1 %collective-permute-start.15 = (bf16[512,512]{1,0:T(8,128)(2,1)S(1)}, bf16[512,512]{1,0:T(8,128)(2,1)S(1)}, u32[]{:S(2)}, u32[]{:S(2)}) collective-permute-start(bf16[512,512]{1,0:T(8,128)(2,1)S(1)} %regroup.3.refs_4_.refs_0_), channel_id=1, source_target_pairs={{0,4},{4,0},{8,12},{12,8},{1,5},{5,1},{9,13},{13,9},{2,6},{6,2},{1... | collective-permute-start | bytes 1572872 | tf_op jit(solution)/shard_map/ppermute | solution.py:354
  90.5 7.5 %collective-permute-done.9.refs_1_ = bf16[512,512]{1,0:T(8,128)(2,1)} collective-permute-done((bf16[512,512]{1,0:T(8,128)(2,1)}, bf16[512,512]{1,0:T(8,128)(2,1)}, u32[]{:S(2)}, u32[]{:S(2)}) %collective-permute-start.9) | collective-permute-done | bytes 524320 | tf_op jit(solution)/shard_map/ppermute | solution.py:354
  98.0 11.7 %attend.6.refs_6_ = bf16[2,528,512]{2,1,0:T(8,128)(2,1)S(1)} custom-call(s32[1]{0:T(128)} %bitcast.place_ref, s32[16,12]{1,0:T(8,128)S(1)} %fusion.kept_ref, bf16[512,512]{1,0:T(8,128)(2,1)} %collective-permute-done.8.refs_0_, bf16[512,512]{1,0:T(8,128)(2,1)} %collective-permute-done.9.refs_1_, bf16[1024,1536]{1,0:T(8,128)(2,1)S(1)} %copy-done.21, ...), custom_call_target="tpu_custom_call" | custom-call | flops 6442450944 | bytes 5242880 | tf_op jit(solution)/shard_map/attend/pallas_call | solution.py:147
  111.7 11.8 %attend.7.refs_6_.refs_0_ = bf16[2,528,512]{2,1,0:T(8,128)(2,1)S(1)} custom-call(s32[1]{0:T(128)} %bitcast.place_ref, s32[16,12]{1,0:T(8,128)S(1)} %fusion.kept_ref, bf16[512,512]{1,0:T(8,128)(2,1)} %bitcast.5.refs_4_.refs_0_, bf16[512,512]{1,0:T(8,128)(2,1)} %collective-permute-done.refs_12_.refs_4_.refs_1_, bf16[1024,1536]{1,0:T(8,128)(2,1)S(1)} %copy-done.21, ...), custom_call_target="tpu_custom_call" | custom-call | flops 6442450944 | bytes 5242880 | tf_op jit(solution)/shard_map/attend/pallas_call | solution.py:147
  123.5 8.1 %collective-permute-done.12.refs_1_ = bf16[512,512]{1,0:T(8,128)(2,1)S(1)} collective-permute-done((bf16[512,512]{1,0:T(8,128)(2,1)}, bf16[512,512]{1,0:T(8,128)(2,1)S(1)}, u32[]{:S(2)}, u32[]{:S(2)}) %collective-permute-start.12) | collective-permute-done | bytes 524320 | tf_op jit(solution)/shard_map/ppermute | solution.py:354
  131.6 10.7 %attend.8.refs_2_ = bf16[2,528,512]{2,1,0:T(8,128)(2,1)S(1)} custom-call(s32[1]{0:T(128)} %bitcast.place_ref, s32[16,12]{1,0:T(8,128)S(1)} %fusion.kept_ref, bf16[512,512]{1,0:T(8,128)(2,1)S(1)} %collective-permute-done.11.refs_0_, bf16[512,512]{1,0:T(8,128)(2,1)S(1)} %collective-permute-done.12.refs_1_, bf16[1024,1536]{1,0:T(8,128)(2,1)S(1)} %copy-done.21, ...), custom_call_target="tpu_custom_call" | custom-call | flops 6442450944 | bytes 5242880 | tf_op jit(solution)/shard_map/attend/pallas_call | solution.py:147
  144.4 10.4 %collective-permute-done.10.refs_1_ = bf16[2,528,512]{2,1,0:T(8,128)(2,1)S(1)} collective-permute-done((bf16[2,528,512]{2,1,0:T(8,128)(2,1)S(1)}, bf16[2,528,512]{2,1,0:T(8,128)(2,1)S(1)}, u32[]{:S(2)}, u32[]{:S(2)}) %collective-permute-start.10) | collective-permute-done | bytes 1081376 | tf_op jit(solution)/shard_map/ppermute | solution.py:354
  156.8 11.8 %attend.9.refs_3_.refs_0_ = bf16[2,528,512]{2,1,0:T(8,128)(2,1)S(1)} custom-call(s32[1]{0:T(128)} %bitcast.place_ref, s32[16,12]{1,0:T(8,128)S(1)} %fusion.kept_ref, bf16[512,512]{1,0:T(8,128)(2,1)} %regroup.2.refs_0_, bf16[512,512]{1,0:T(8,128)(2,1)} %collective-permute-done.7.refs_4_.refs_1_, bf16[1024,1536]{1,0:T(8,128)(2,1)S(1)} %copy-done.21, ...), custom_call_target="tpu_custom_call" | custom-call | flops 6442450944 | bytes 5242880 | tf_op jit(solution)/shard_map/attend/pallas_call | solution.py:147
  168.6 22.7 %collective-permute-done.13.refs_2_ = bf16[1,528,512]{2,1,0:T(8,128)(2,1)S(1)} collective-permute-done((bf16[1,528,512]{2,1,0:T(8,128)(2,1)S(1)}, bf16[1,528,512]{2,1,0:T(8,128)(2,1)S(1)}, u32[]{:S(2)}, u32[]{:S(2)}) %collective-permute-start.13) | collective-permute-done | bytes 540704 | tf_op jit(solution)/shard_map/ppermute | solution.py:354
  192.5 8.0 %collective-permute-done.17.refs_1_ = bf16[512,512]{1,0:T(8,128)(2,1)S(1)} collective-permute-done((bf16[512,512]{1,0:T(8,128)(2,1)S(1)}, bf16[512,512]{1,0:T(8,128)(2,1)S(1)}, u32[]{:S(2)}, u32[]{:S(2)}) %collective-permute-start.17) | collective-permute-done | bytes 524320 | tf_op jit(solution)/shard_map/ppermute | solution.py:354
  200.5 11.7 %attend.10.refs_2_ = bf16[2,528,512]{2,1,0:T(8,128)(2,1)} custom-call(s32[1]{0:T(128)} %bitcast.place_ref, s32[16,12]{1,0:T(8,128)S(1)} %fusion.kept_ref, bf16[512,512]{1,0:T(8,128)(2,1)S(1)} %collective-permute-done.15.refs_0_, bf16[512,512]{1,0:T(8,128)(2,1)S(1)} %collective-permute-done.17.refs_1_, bf16[1024,1536]{1,0:T(8,128)(2,1)S(1)} %copy-done.21, ...), custom_call_target="tpu_custom_call" | custom-call | flops 6442450944 | bytes 5242880 | tf_op jit(solution)/shard_map/attend/pallas_call | solution.py:147
  217.1 4.1 %all-to-all-start.1 = ((bf16[4,128,512]{2,1,0:T(8,128)(2,1)}), bf16[4,128,512]{2,1,0:T(8,128)(2,1)}, u32[]{:S(2)}, u32[]{:S(2)}) async-start(bf16[4,128,512]{2,1,0:T(8,128)(2,1)} %bitcast.8), calls=%async_computation.1 | async-start | bytes 1048576 | tf_op jit(solution)/shard_map/all_to_all | solution.py:410
  229.9 10.7 %attend.11.refs_0_.refs_2_ = bf16[2,528,512]{2,1,0:T(8,128)(2,1)S(1)} custom-call(s32[1]{0:T(128)} %bitcast.place_ref, s32[16,12]{1,0:T(8,128)S(1)} %fusion.kept_ref, bf16[512,512]{1,0:T(8,128)(2,1)S(1)} %copy-done.18, bf16[512,512]{1,0:T(8,128)(2,1)S(1)} %copy-done.28, bf16[1024,1536]{1,0:T(8,128)(2,1)S(1)} %copy-done.22, bf16[512,1536]{1,0:T(8,128)(2,1)S(1)} %copy-done.24, ...), custom_call_target="tpu_custom_call" | custom-call | flops 6442450944 | bytes 5242880 | tf_op jit(solution)/shard_map/attend/pallas_call | solution.py:147
  240.6 9.0 %collective-permute-done.19.refs_1_ = bf16[2,528,512]{2,1,0:T(8,128)(2,1)} collective-permute-done((bf16[2,528,512]{2,1,0:T(8,128)(2,1)}, bf16[2,528,512]{2,1,0:T(8,128)(2,1)}, u32[]{:S(2)}, u32[]{:S(2)}) %collective-permute-start.19) | collective-permute-done | bytes 1081376 | tf_op jit(solution)/shard_map/ppermute | solution.py:354
  255.1 4.1 %all-to-all-start.2 = ((bf16[4,128,512]{2,1,0:T(8,128)(2,1)}), bf16[4,128,512]{2,1,0:T(8,128)(2,1)}, u32[]{:S(2)}, u32[]{:S(2)}) async-start(bf16[4,128,512]{2,1,0:T(8,128)(2,1)} %bitcast.9), calls=%async_computation.2 | async-start | bytes 1048576 | tf_op jit(solution)/shard_map/all_to_all | solution.py:410
  259.2 18.4 %collective-permute-done.20.refs_2_ = bf16[1,528,512]{2,1,0:T(8,128)(2,1)} collective-permute-done((bf16[1,528,512]{2,1,0:T(8,128)(2,1)}, bf16[1,528,512]{2,1,0:T(8,128)(2,1)}, u32[]{:S(2)}, u32[]{:S(2)}) %collective-permute-start.20) | collective-permute-done | bytes 540704 | tf_op jit(solution)/shard_map/ppermute | solution.py:354
  279.3 11.2 %all_to_all.21 = bf16[4,128,512]{2,1,0:T(8,128)(2,1)S(1)} all-to-all(bf16[4,128,512]{2,1,0:T(8,128)(2,1)S(1)} %bitcast.25), channel_id=1, replica_groups=mesh['cfg'=2,'blk'=4,'uly'=4] {'uly'}, dimensions={0} | all-to-all | bytes 1048576 | tf_op jit(solution)/shard_map/all_to_all | solution.py:410
  (112 shorter events, 56.8 us)
Async XLA Ops:
  14.3 26.1 %collective-permute-start = (bf16[512,512]{1,0:T(8,128)(2,1)}, bf16[512,512]{1,0:T(8,128)(2,1)}, u32[]{:S(2)}, u32[]{:S(2)}) collective-permute-start(bf16[512,512]{1,0:T(8,128)(2,1)} %bitcast.5.refs_4_.refs_0_), channel_id=1, source_target_pairs={{0,8},{4,12},{8,0},{12,4},{1,9},{5,13},{9,1},{13,5},{2,10},{6,14},... | collective-permute-start | bytes 1572872 | tf_op jit(solution)/shard_map/ppermute | solution.py:354
  17.4 1.9 collective-permute-start.1
  17.5 9.2 %collective-permute-start.2 = (bf16[128,1024]{1,0:T(8,128)(2,1)S(1)}, bf16[128,1024]{1,0:T(8,128)(2,1)S(1)}, u32[]{:S(2)}, u32[]{:S(2)}) collective-permute-start(bf16[128,1024]{1,0:T(8,128)(2,1)S(1)} %get-tuple-element.17), channel_id=1, source_target_pairs={{0,2},{1,3},{2,0},{3,1},{4,6},{5,7},{6,4},{7,5},{8,10},{9,11},{10,... | collective-permute-start | bytes 786440 | tf_op jit(solution)/shard_map/ppermute | solution.py:351
  17.9 13.5 %collective-permute-start.3 = (bf16[128,1024]{1,0:T(8,128)(2,1)S(1)}, bf16[128,1024]{1,0:T(8,128)(2,1)S(1)}, u32[]{:S(2)}, u32[]{:S(2)}) collective-permute-start(bf16[128,1024]{1,0:T(8,128)(2,1)S(1)} %get-tuple-element.18), channel_id=1, source_target_pairs={{0,3},{1,2},{2,1},{3,0},{4,7},{5,6},{6,5},{7,4},{8,11},{9,10},{10,... | collective-permute-start | bytes 786440 | tf_op jit(solution)/shard_map/ppermute | solution.py:351
  41.9 25.3 %collective-permute-start.7 = (bf16[512,512]{1,0:T(8,128)(2,1)}, bf16[512,512]{1,0:T(8,128)(2,1)}, u32[]{:S(2)}, u32[]{:S(2)}) collective-permute-start(bf16[512,512]{1,0:T(8,128)(2,1)} %regroup.2.refs_0_), channel_id=1, source_target_pairs={{0,8},{4,12},{8,0},{12,4},{1,9},{5,13},{9,1},{13,5},{2,10},{6,14},... | collective-permute-start | bytes 1572872 | tf_op jit(solution)/shard_map/ppermute | solution.py:354
  47.3 26.5 %collective-permute-start.4 = (bf16[256,1536]{1,0:T(8,128)(2,1)}, bf16[256,1536]{1,0:T(8,128)(2,1)}, u32[]{:S(2)}, u32[]{:S(2)}) collective-permute-start(bf16[256,1536]{1,0:T(8,128)(2,1)} %get-tuple-element.20), channel_id=1, source_target_pairs={{0,1},{1,0},{2,3},{3,2},{4,5},{5,4},{6,7},{7,6},{8,9},{9,8},{10,11... | collective-permute-start | bytes 2359304 | tf_op jit(solution)/shard_map/ppermute | solution.py:351
  47.3 28.6 %collective-permute-start.5 = (bf16[256,1536]{1,0:T(8,128)(2,1)}, bf16[256,1536]{1,0:T(8,128)(2,1)}, u32[]{:S(2)}, u32[]{:S(2)}) collective-permute-start(bf16[256,1536]{1,0:T(8,128)(2,1)} %get-tuple-element.21), channel_id=1, source_target_pairs={{0,2},{1,3},{2,0},{3,1},{4,6},{5,7},{6,4},{7,5},{8,10},{9,11},{10,... | collective-permute-start | bytes 2359304 | tf_op jit(solution)/shard_map/ppermute | solution.py:351
  48.1 36.0 %collective-permute-start.6 = (bf16[256,1536]{1,0:T(8,128)(2,1)}, bf16[256,1536]{1,0:T(8,128)(2,1)}, u32[]{:S(2)}, u32[]{:S(2)}) collective-permute-start(bf16[256,1536]{1,0:T(8,128)(2,1)} %get-tuple-element.22), channel_id=1, source_target_pairs={{0,3},{1,2},{2,1},{3,0},{4,7},{5,6},{6,5},{7,4},{8,11},{9,10},{10,... | collective-permute-start | bytes 2359304 | tf_op jit(solution)/shard_map/ppermute | solution.py:351
  49.3 41.2 %collective-permute-start.8 = (bf16[512,512]{1,0:T(8,128)(2,1)}, bf16[512,512]{1,0:T(8,128)(2,1)}, u32[]{:S(2)}, u32[]{:S(2)}) collective-permute-start(bf16[512,512]{1,0:T(8,128)(2,1)} %bitcast.5.refs_4_.refs_0_), channel_id=1, source_target_pairs={{0,4},{4,0},{8,12},{12,8},{1,5},{5,1},{9,13},{13,9},{2,6},{6,2},{1... | collective-permute-start | bytes 1572872 | tf_op jit(solution)/shard_map/ppermute | solution.py:354
  67.2 30.8 %collective-permute-start.9 = (bf16[512,512]{1,0:T(8,128)(2,1)}, bf16[512,512]{1,0:T(8,128)(2,1)}, u32[]{:S(2)}, u32[]{:S(2)}) collective-permute-start(bf16[512,512]{1,0:T(8,128)(2,1)} %collective-permute-done.refs_12_.refs_4_.refs_1_), channel_id=1, source_target_pairs={{0,4},{4,0},{8,12},{12,8},{1,5},{5,1},{9,13},{13,9},{2,6},{6,2},{1... | collective-permute-start | bytes 1572872 | tf_op jit(solution)/shard_map/ppermute | solution.py:354
  73.8 49.7 %collective-permute-start.11 = (bf16[512,512]{1,0:T(8,128)(2,1)}, bf16[512,512]{1,0:T(8,128)(2,1)S(1)}, u32[]{:S(2)}, u32[]{:S(2)}) collective-permute-start(bf16[512,512]{1,0:T(8,128)(2,1)} %regroup.2.refs_0_), channel_id=1, source_target_pairs={{0,4},{4,0},{8,12},{12,8},{1,5},{5,1},{9,13},{13,9},{2,6},{6,2},{1... | collective-permute-start | bytes 1572872 | tf_op jit(solution)/shard_map/ppermute | solution.py:354
  75.9 66.5 %collective-permute-start.16 = (bf16[512,512]{1,0:T(8,128)(2,1)S(1)}, bf16[512,512]{1,0:T(8,128)(2,1)S(1)}, u32[]{:S(2)}, u32[]{:S(2)}) collective-permute-start(bf16[512,512]{1,0:T(8,128)(2,1)S(1)} %regroup.3.refs_4_.refs_0_), channel_id=1, source_target_pairs={{0,8},{4,12},{8,0},{12,4},{1,9},{5,13},{9,1},{13,5},{2,10},{6,14},... | collective-permute-start | bytes 1572872 | tf_op jit(solution)/shard_map/ppermute | solution.py:354
  84.0 108.5 %collective-permute-start.15 = (bf16[512,512]{1,0:T(8,128)(2,1)S(1)}, bf16[512,512]{1,0:T(8,128)(2,1)S(1)}, u32[]{:S(2)}, u32[]{:S(2)}) collective-permute-start(bf16[512,512]{1,0:T(8,128)(2,1)S(1)} %regroup.3.refs_4_.refs_0_), channel_id=1, source_target_pairs={{0,4},{4,0},{8,12},{12,8},{1,5},{5,1},{9,13},{13,9},{2,6},{6,2},{1... | collective-permute-start | bytes 1572872 | tf_op jit(solution)/shard_map/ppermute | solution.py:354
  90.4 110.0 %copy-start.23 = (bf16[512,1536]{1,0:T(8,128)(2,1)}, bf16[512,1536]{1,0:T(8,128)(2,1)S(1)}, u32[]{:S(2)}) copy-start(bf16[512,1536]{1,0:T(8,128)(2,1)S(1)} %get-tuple-element.23.refs_3_.refs_6_) | copy-start | bytes 4718596
  90.5 41.1 %collective-permute-start.12 = (bf16[512,512]{1,0:T(8,128)(2,1)}, bf16[512,512]{1,0:T(8,128)(2,1)S(1)}, u32[]{:S(2)}, u32[]{:S(2)}) collective-permute-start(bf16[512,512]{1,0:T(8,128)(2,1)} %collective-permute-done.7.refs_4_.refs_1_), channel_id=1, source_target_pairs={{0,4},{4,0},{8,12},{12,8},{1,5},{5,1},{9,13},{13,9},{2,6},{6,2},{1... | collective-permute-start | bytes 1572872 | tf_op jit(solution)/shard_map/ppermute | solution.py:354
  109.7 45.1 %collective-permute-start.10 = (bf16[2,528,512]{2,1,0:T(8,128)(2,1)S(1)}, bf16[2,528,512]{2,1,0:T(8,128)(2,1)S(1)}, u32[]{:S(2)}, u32[]{:S(2)}) collective-permute-start(bf16[2,528,512]{2,1,0:T(8,128)(2,1)S(1)} %attend.6.refs_6_), channel_id=1, source_target_pairs={{0,4},{4,0},{8,12},{12,8},{1,5},{5,1},{9,13},{13,9},{2,6},{6,2},{1... | collective-permute-start | bytes 3244040 | tf_op jit(solution)/shard_map/ppermute | solution.py:354
  142.3 69.8 %collective-permute-start.14 = (bf16[2,528,512]{2,1,0:T(8,128)(2,1)S(1)}, bf16[2,528,512]{2,1,0:T(8,128)(2,1)S(1)}, u32[]{:S(2)}, u32[]{:S(2)}) collective-permute-start(bf16[2,528,512]{2,1,0:T(8,128)(2,1)S(1)} %attend.8.refs_2_), channel_id=1, source_target_pairs={{0,4},{4,0},{8,12},{12,8},{1,5},{5,1},{9,13},{13,9},{2,6},{6,2},{1... | collective-permute-start | bytes 3244040 | tf_op jit(solution)/shard_map/ppermute | solution.py:354
  142.4 58.0 %collective-permute-start.17 = (bf16[512,512]{1,0:T(8,128)(2,1)S(1)}, bf16[512,512]{1,0:T(8,128)(2,1)S(1)}, u32[]{:S(2)}, u32[]{:S(2)}) collective-permute-start(bf16[512,512]{1,0:T(8,128)(2,1)S(1)} %collective-permute-done.16.refs_1_), channel_id=1, source_target_pairs={{0,4},{4,0},{8,12},{12,8},{1,5},{5,1},{9,13},{13,9},{2,6},{6,2},{1... | collective-permute-start | bytes 1572872 | tf_op jit(solution)/shard_map/ppermute | solution.py:354
  155.1 36.1 %collective-permute-start.13 = (bf16[1,528,512]{2,1,0:T(8,128)(2,1)S(1)}, bf16[1,528,512]{2,1,0:T(8,128)(2,1)S(1)}, u32[]{:S(2)}, u32[]{:S(2)}) collective-permute-start(bf16[1,528,512]{2,1,0:T(8,128)(2,1)S(1)} %merge.3.refs_6_), channel_id=1, source_target_pairs={{0,8},{4,12},{8,0},{12,4},{1,9},{5,13},{9,1},{13,5},{2,10},{6,14},... | collective-permute-start | bytes 1622024 | tf_op jit(solution)/shard_map/ppermute | solution.py:354
  212.2 37.5 %collective-permute-start.19 = (bf16[2,528,512]{2,1,0:T(8,128)(2,1)}, bf16[2,528,512]{2,1,0:T(8,128)(2,1)}, u32[]{:S(2)}, u32[]{:S(2)}) collective-permute-start(bf16[2,528,512]{2,1,0:T(8,128)(2,1)} %attend.10.refs_2_), channel_id=1, source_target_pairs={{0,4},{4,0},{8,12},{12,8},{1,5},{5,1},{9,13},{13,9},{2,6},{6,2},{1... | collective-permute-start | bytes 3244040 | tf_op jit(solution)/shard_map/ppermute | solution.py:354
  213.4 39.4 %collective-permute-start.18 = (bf16[1,528,512]{2,1,0:T(8,128)(2,1)}, bf16[1,528,512]{2,1,0:T(8,128)(2,1)}, u32[]{:S(2)}, u32[]{:S(2)}) collective-permute-start(bf16[1,528,512]{2,1,0:T(8,128)(2,1)} %merge.4.refs_6_), channel_id=1, source_target_pairs={{0,8},{4,12},{8,0},{12,4},{1,9},{5,13},{9,1},{13,5},{2,10},{6,14},... | collective-permute-start | bytes 1622024 | tf_op jit(solution)/shard_map/ppermute | solution.py:354
  217.1 38.0 %all-to-all-start.1 = ((bf16[4,128,512]{2,1,0:T(8,128)(2,1)}), bf16[4,128,512]{2,1,0:T(8,128)(2,1)}, u32[]{:S(2)}, u32[]{:S(2)}) async-start(bf16[4,128,512]{2,1,0:T(8,128)(2,1)} %bitcast.8), calls=%async_computation.1 | async-start | bytes 1048576 | tf_op jit(solution)/shard_map/all_to_all | solution.py:410
  251.8 25.8 %collective-permute-start.20 = (bf16[1,528,512]{2,1,0:T(8,128)(2,1)}, bf16[1,528,512]{2,1,0:T(8,128)(2,1)}, u32[]{:S(2)}, u32[]{:S(2)}) collective-permute-start(bf16[1,528,512]{2,1,0:T(8,128)(2,1)} %merge.5.refs_3_), channel_id=1, source_target_pairs={{0,8},{4,12},{8,0},{12,4},{1,9},{5,13},{9,1},{13,5},{2,10},{6,14},... | collective-permute-start | bytes 1622024 | tf_op jit(solution)/shard_map/ppermute | solution.py:354
  255.1 24.2 %all-to-all-start.2 = ((bf16[4,128,512]{2,1,0:T(8,128)(2,1)}), bf16[4,128,512]{2,1,0:T(8,128)(2,1)}, u32[]{:S(2)}, u32[]{:S(2)}) async-start(bf16[4,128,512]{2,1,0:T(8,128)(2,1)} %bitcast.9), calls=%async_computation.2 | async-start | bytes 1048576 | tf_op jit(solution)/shard_map/all_to_all | solution.py:410
  (28 other events, 378.0 us)

commit v4 on v3

--- a/solution.py
+++ b/solution.py
@@ -34,9 +34,12 @@
     return -(-3 * (width // DH) // 16) * 16
 
 
-def attend_kernel(distances, place_ref, kept_ref, *refs):
-    count = len(distances)
-    q_refs = refs[:count]
+def attend_kernel(choices, table_ref, kept_ref, *refs):
+    count = sum(len(c) for c in choices)
+    sources, at = [], 0
+    for c in choices:
+        sources.append(refs[at : at + len(c)])
+        at += len(c)
     ck_ref, nk_ref, cv_ref, nv_ref = refs[count : count + 4]
     out_ref, q_s, s0, s1, m0, m1, stat_s = refs[-7:]
     rows = q_s.shape[0]
@@ -47,20 +50,20 @@
     halves = rows // HALF
     slots = ((s0, m0), (s1, m1))
     nt = (((1,), (1,)), ((), ()))
-    distance = distances[0]
-    for i in range(1, count):
-        distance = jnp.where(pl.program_id(0) == i, distances[i], distance)
-    first_tile = (place_ref[0] ^ distance) * (rows // TILE)
+    step_no = pl.program_id(0)
+    first_tile = table_ref[1 + step_no] * (rows // TILE)
     stat_s[...] = jnp.zeros_like(stat_s)
-    for i, q_ref in enumerate(q_refs):
-
-        @pl.when(pl.program_id(0) == i)
-        def _():
-            for head in range(heads):
-                scaled = q_ref[:, head * DH : (head + 1) * DH].astype(jnp.float32) * SCALE2
-                hi = scaled.astype(jnp.bfloat16)
-                q_s[:, 2 * head * DH : (2 * head + 1) * DH] = hi
-                q_s[:, (2 * head + 1) * DH : (2 * head + 2) * DH] = (scaled - hi.astype(jnp.float32)).astype(jnp.bfloat16)
+    for c, q_refs in enumerate(sources):
+        for i, q_ref in enumerate(q_refs):
+
+            @pl.when((step_no == i) & (table_ref[0] == c))
+            def _():
+                for head in range(heads):
+                    scaled = q_ref[:, head * DH : (head + 1) * DH].astype(jnp.float32) * SCALE2
+                    hi = scaled.astype(jnp.bfloat16)
+                    lo = (scaled - hi.astype(jnp.float32)).astype(jnp.bfloat16)
+                    q_s[:, 2 * head * DH : (2 * head + 1) * DH] = hi
+                    q_s[:, (2 * head + 1) * DH : (2 * head + 2) * DH] = lo
 
     def columns(head, size=DH):
         return pl.ds(pl.multiple_of(head * size, size), size)
@@ -135,22 +138,23 @@
     out_ref[0, width:, :] = stat_s[...].astype(jnp.bfloat16)
 
 
-def attend(place, kept, queries, distances, ctx_k, new_k, ctx_v, new_v, piece, dep):
-    rows, width = queries[distances[0]].shape
+def attend(table, kept, choices, ctx_k, new_k, ctx_v, new_v, piece, dep):
+    queries = [q for choice in choices for q in choice]
+    rows, width = queries[0].shape
     ctx, new = ctx_k.shape[0], new_k.shape[0]
     heads = width // DH
     keys = ctx + new
-    blocks = len(distances)
+    blocks = len(choices[0])
     across = lambda i, t, b: (0, piece)
     down = lambda i, t, b: (piece, 0)
     prow = width + stat_rows(width)
     return pl.pallas_call(
-        functools.partial(attend_kernel, distances),
+        functools.partial(attend_kernel, [[None] * len(c) for c in choices]),
         out_shape=jax.ShapeDtypeStruct((blocks, prow, rows), jnp.bfloat16),
         grid_spec=pltpu.PrefetchScalarGridSpec(
             num_scalar_prefetch=2,
             grid=(blocks,),
-            in_specs=[pl.BlockSpec((rows, width), lambda i, t, b: (0, 0))] * blocks
+            in_specs=[pl.BlockSpec((rows, width), lambda i, t, b: (0, 0))] * len(queries)
             + [
                 pl.BlockSpec((ctx, width), across),
                 pl.BlockSpec((new, width), across),
@@ -175,7 +179,7 @@
             transcendentals=blocks * rows * keys * heads,
         ),
         name="attend",
-    )(place, kept, *[queries[d] for d in distances], ctx_k, new_k, ctx_v, new_v, dep)
+    )(table, kept, *queries, ctx_k, new_k, ctx_v, new_v, dep)
 
 
 def combine(refs, width, emit):
@@ -196,44 +200,61 @@
         emit(head, value, top + jnp.log2(total))
 
 
-def merge_kernel(*refs):
-    sources, (out_ref, stat_ref) = refs[:-3], refs[-2:]
-    width = out_ref.shape[1] - stat_ref.shape[0]
-    stat_ref[...] = jnp.zeros_like(stat_ref)
+def join_kernel_of(sizes, final, table_ref, *refs):
+    sources, at = [], 0
+    for size in sizes:
+        sources.append(refs[at : at + size])
+        at += size
+    if final:
+        out_ref = refs[-1]
+        width = out_ref.shape[1]
+    else:
+        out_ref, stat_ref = refs[-2:]
+        width = out_ref.shape[1] - stat_ref.shape[0]
 
     def emit(head, value, log):
-        out_ref[0, head * DH : (head + 1) * DH, :] = value.astype(jnp.bfloat16)
+        at = slice(head * DH, (head + 1) * DH)
+        if final:
+            out_ref[:, at] = jnp.transpose(value).astype(jnp.bfloat16)
+            return
+        out_ref[0, at, :] = value.astype(jnp.bfloat16)
         for part, term in enumerate(split3(log)):
             stat_ref[3 * head + part : 3 * head + part + 1, :] = term
 
-    combine(sources, width, emit)
-    out_ref[0, width:, :] = stat_ref[...].astype(jnp.bfloat16)
-
-
-def finish_kernel(*refs):
-    sources, out_ref = refs[:-2], refs[-1]
-
-    def emit(head, value, log):
-        out_ref[:, head * DH : (head + 1) * DH] = jnp.transpose(value).astype(jnp.bfloat16)
-
-    combine(sources, out_ref.shape[1], emit)
-
-
-def join_parts(parts, width, dep, final):
+    for c, chosen in enumerate(sources):
+        if chosen:
+
+            @pl.when(table_ref[0] == c)
+            def _():
+                if not final:
+                    stat_ref[...] = jnp.zeros_like(stat_ref)
+                combine(chosen, width, emit)
+                if not final:
+                    out_ref[0, width:, :] = stat_ref[...].astype(jnp.bfloat16)
+
+
+def join_parts(table, choices, width, dep, final, blocks=1):
+    parts = [part for choice in choices for part in choice]
     _, prow, rows = parts[0][0].shape
-    specs = [pl.BlockSpec((1, prow, rows), functools.partial(lambda slot, i: (slot, 0, 0), slot)) for _, slot in parts]
-    shape = (rows, width) if final else (1, prow, rows)
+    specs = [
+        pl.BlockSpec((1, prow, rows), functools.partial(lambda slot, i, t: (slot + i, 0, 0), slot)) for _, slot in parts
+    ]
+    shape = (rows, width) if final else (blocks, prow, rows)
+    out_spec = pl.BlockSpec(shape, lambda i, t: (0, 0)) if final else pl.BlockSpec((1, prow, rows), lambda i, t: (i, 0, 0))
     return pl.pallas_call(
-        finish_kernel if final else merge_kernel,
+        functools.partial(join_kernel_of, [len(c) for c in choices], final),
         out_shape=jax.ShapeDtypeStruct(shape, jnp.bfloat16),
-        grid=(1,),
-        in_specs=specs + [pl.BlockSpec(memory_space=pl.ANY)],
-        out_specs=pl.BlockSpec(shape, lambda i: (0,) * len(shape)),
-        scratch_shapes=[] if final else [pltpu.VMEM((prow - width, rows), jnp.float32)],
+        grid_spec=pltpu.PrefetchScalarGridSpec(
+            num_scalar_prefetch=1,
+            grid=(blocks,),
+            in_specs=specs + [pl.BlockSpec(memory_space=pl.ANY)],
+            out_specs=out_spec,
+            scratch_shapes=[] if final else [pltpu.VMEM((prow - width, rows), jnp.float32)],
+        ),
         compiler_params=pltpu.CompilerParams(vmem_limit_bytes=16 * MIB),
         cost_estimate=QUICK,
         name="finish" if final else "merge",
-    )(*[array for array, _ in parts], dep)
+    )(table, *[array for array, _ in parts], dep)
 
 
 def part_kernel(peers, count, start, peer_ref, *refs):
@@ -338,10 +359,7 @@
     kept = (kept == 1).astype(jnp.int32)
     count = len(PIECES)
     widths = [units * unit for _, units in PIECES]
-    bits = [1 << k for k in range((n - 1).bit_length())]
-    where = place.reshape(1)
-    parts = [{d: [] for d in range(n)} for _ in range(count)]
-    sent, backs = [None] * count, [None] * count
+    backs = [None] * count
 
     def to_heads(pieces):
         moved = lax.all_to_all(pieces, "uly", split_axis=0, concat_axis=0, tiled=False)
@@ -350,75 +368,120 @@
     def to_peers(pieces):
         return [lax.ppermute(p, "uly", [(i, i ^ k) for i in range(peers)]) if k else p for k, p in enumerate(pieces)]
 
-    def across(x, bit):
-        return lax.ppermute(x, "blk", [(i, i ^ bit) for i in range(n)])
-
-    def spread(span):
+    def send(x, *pairs):
+        return lax.ppermute(x, "blk", pairs)
+
+    def spread_line(span):
+        near = send(span, (0, 1), (1, 0), (2, 3), (3, 2))
+        third = send(span, (1, 2), (2, 1))
+        far = send(near, (1, 2), (2, 1))
+        third_out = send(third, (1, 0), (2, 3))
+        far_out = send(far, (1, 0), (2, 3))
+        return dict(own=span, near=near, sent=[[far, third], [far_out, third_out]], early=third, mid=third_out)
+
+    def spread_cube(span):
         found = {0: span}
         for bit in reversed(bits):
             for d in list(found):
-                found[d ^ bit] = across(found[d], bit)
-        return found
-
+                found[d ^ bit] = send(found[d], *[(i, i ^ bit) for i in range(n)])
+        return dict(found=found, early=found[n // 2], mid=found[n // 2])
+
+    bits = [1 << k for k in range((n - 1).bit_length())]
+    line = n == 4
+    spread = spread_line if line else spread_cube
     early = widths[0]
     first_span = to_heads(jnp.stack([new_queries[:, p * group : p * group + early] for p in range(peers)]))
     found = [spread(first_span)]
     parts_q = parts_for_peers(peer, [new_queries], early, peers, [first_span])
     later = to_peers(parts_q)
-    parts_kv = parts_for_peers(peer, [new_keys, new_values], 0, peers, [*later, found[0][n // 2]])
+    parts_kv = parts_for_peers(peer, [new_keys, new_values], 0, peers, [*later, found[0]["early"]])
 
     def run_spread(c, deps):
         span = regrouped(peer, later, PIECES[c][0] * unit - early, widths[c], deps)
         found.append(spread(span))
         return span
 
+    latest = parts_kv[0]
     for c in range(1, count):
-        latest = run_spread(c, [found[c - 1][n // 2]])
+        latest = run_spread(c, [found[c - 1]["early"], latest])
     span_k, span_v_t = joined(to_peers(parts_kv), latest)
     context_values_t = context_values.T
     last = [span_k]
-
-    def run_attend(c, distances):
+    outer = ((place == 0) | (place == n - 1)).astype(jnp.int32)
+    low = place < n // 2
+
+    def run_attend(c, choices, targets):
+        table = jnp.stack([outer, *targets]).astype(jnp.int32)
         own = attend(
-            where, kept, found[c], distances, context_keys, span_k, context_values_t, span_v_t,
-            PIECES[c][0] // PIECES[c][1], last[0],
+            table, kept, choices, context_keys, span_k, context_values_t, span_v_t, PIECES[c][0] // PIECES[c][1], last[0]
         )
         last[0] = own
-        for slot, d in enumerate(distances):
-            parts[c][d] = [(own, slot)]
         return own
 
+    def run_join(c, choices, final=False, blocks=1):
+        last[0] = join_parts(outer.reshape(1), choices, widths[c], last[0], final, blocks)
+        return last[0]
+
+    def run_back(c, choices):
+        done = run_join(c, choices, True).reshape(peers, own_rows, widths[c])
+        backs[c] = lax.all_to_all(done, "uly", split_axis=0, concat_axis=0, tiled=False)
+
+    state = [dict() for _ in range(count)]
+
     def run_sent(c):
-        sent[c] = across(run_attend(c, list(range(1, n, 2))), 1)
+        mine = run_attend(c, found[c]["sent"], [jnp.where(low, 3, 0), jnp.where(low, 2, 1)])
+        state[c].update(far=mine, edge=send(mine, (0, 1), (3, 2)))
 
     def run_kept(c):
-        run_attend(c, list(range(0, n, 2)))
-        for d in range(0, n, 2):
-            parts[c][d].append((sent[c], d // 2))
-
-    def run_merge(c):
-        for bit in bits[1:]:
-            for d in range(bit, n, 2 * bit):
-                joint = join_parts(parts[c][d], widths[c], last[0], False)
-                last[0] = joint
-                parts[c][d ^ bit].append((across(joint, bit), 0))
+        blocks = [found[c]["near"], found[c]["own"]]
+        mine = run_attend(c, [blocks, blocks], [place ^ 1, place])
+        state[c].update(kept=mine, edge_near=send(mine[:1], (0, 1), (3, 2)))
+
+    def run_cross(c):
+        joint = run_join(c, [[(state[c]["far"], 0), (state[c]["edge"], 0)], []], blocks=2)
+        state[c]["cross"] = send(joint, (1, 2), (2, 1))
+
+    def run_outward(c):
+        joint = run_join(c, [[(state[c]["kept"], 0), (state[c]["cross"], 0)], []])
+        state[c]["outward"] = send(joint, (1, 0), (2, 3))
 
     def run_finish(c):
-        done = join_parts(parts[c][0], widths[c], last[0], True)
-        last[0] = done
-        done = done.reshape(peers, own_rows, widths[c])
-        backs[c] = lax.all_to_all(done, "uly", split_axis=0, concat_axis=0, tiled=False)
-
-    for c in range(count):
-        run_sent(c)
-        if c > 0:
-            run_merge(c - 1)
-        run_kept(c)
-        if 0 < c < count - 1:
-            run_finish(c - 1)
-    run_merge(count - 1)
-    run_finish(count - 2)
-    run_finish(count - 1)
+        inner = [(state[c]["kept"], 1), (state[c]["edge_near"], 0), (state[c]["cross"], 1)]
+        run_back(c, [inner, [(state[c]["kept"], 1), (state[c]["outward"], 0)]])
+
+    if line:
+        run_sent(0)
+        run_kept(0)
+        run_sent(1)
+        run_cross(0)
+        run_kept(1)
+        run_sent(2)
+        run_outward(0)
+        run_cross(1)
+        run_kept(2)
+        run_cross(2)
+        run_finish(0)
+        run_outward(1)
+        run_outward(2)
+        run_finish(1)
+        run_finish(2)
+    else:
+        for c in range(count):
+            parts = {d: [] for d in range(n)}
+            for distances in (range(1, n, 2), range(0, n, 2)):
+                blocks = [found[c]["found"][d] for d in distances]
+                mine = run_attend(c, [blocks, blocks], [place ^ d for d in distances])
+                for slot, d in enumerate(distances):
+                    parts[d].append((mine, slot))
+                if 1 in distances:
+                    moved = send(mine, *[(i, i ^ 1) for i in range(n)])
+            for slot, d in enumerate(range(0, n, 2)):
+                parts[d].append((moved, slot))
+            for bit in bits[1:]:
+                for d in range(bit, n, 2 * bit):
+                    joint = run_join(c, [parts[d], parts[d]])
+                    parts[d ^ bit].append((send(joint, *[(i, i ^ bit) for i in range(n)]), 0))
+            run_back(c, [parts[0], parts[0]])
 
     in_order = [backs[c] for c in sorted(range(count), key=lambda c: PIECES[c][0])]
     together = jnp.concatenate(in_order, axis=2)

time: 294 us -> 269 us (0.915)
  waiting for transfers between devices: 127 us -> 45.5 us
  starting transfers between devices: 33.9 us -> 88 us
  blocking collectives: 24.2 us -> 35.4 us
  Pallas kernels: 82.1 us -> 77.1 us
  local copies, waits for them, and re-layouts: 23.9 us -> 19.4 us
    ppermute x15 -> x27, waiting for transfers between devices: 107 us -> 37.1 us  [send(): return lax.ppermute(x, 'blk', pairs)]
    ppermute x15 -> x27, starting transfers between devices: 21.9 us -> 79.9 us  [send(): return lax.ppermute(x, 'blk', pairs)]
    ppermute x6, waiting for transfers between devices: 20.2 us -> 8.39 us  [to_peers(): lax.ppermute(p, 'uly', [(i, i ^ k) for i in range(peers)])]
    all_to_all x1 -> x2, blocking collectives: 11.2 us -> 22.5 us  [run_back(): lax.all_to_all(done, 'uly', split_axis=0, concat_axis=0, tiled=False)]
    unnamed x59 -> x55, local copies, waits for them, and re-layouts: 21.1 us -> 14.8 us
    pallas_call x12 -> x15, Pallas kernels: 77.3 us -> 72.9 us  [the longest x6 68.4 us: attend(): pl.pallas_call(functools.partial(attend_kernel, [[None] * len(c) for c in...]
    all_to_all x2 -> x1, starting transfers between devices: 8.27 us -> 4.15 us  [run_back(): lax.all_to_all(done, 'uly', split_axis=0, concat_axis=0, tiled=False)]
  transfers between devices with their start and end apart: 23 -> 34, of which waited for: 12 -> 9; matrix products, arithmetic and copies ran while one was open for 1% -> 2% of each run, Pallas kernels for 28% -> 29%
where the time goes in v4:
time: 269 us; the launch traced here: 268 us
  starting transfers between devices  88 us (33%)
  Pallas kernels  77.1 us (29%)
  waiting for transfers between devices  45.5 us (17%)
  blocking collectives  35.4 us (13%)
  local copies, waits for them, and re-layouts  19.4 us (7%)
    ppermute x27, starting transfers between devices, send(): return lax.ppermute(x, 'blk', pairs)  79.9 us
    pallas_call x6, Pallas kernels, attend(): pl.pallas_call(functools.partial(attend_kernel, [[None] * len(c) for c in...  68.4 us
    ppermute x27, waiting for transfers between devices, send(): return lax.ppermute(x, 'blk', pairs)  37.1 us
    all_to_all x2, blocking collectives, run_back(): lax.all_to_all(done, 'uly', split_axis=0, concat_axis=0, tiled=False)  22.5 us
    unnamed x55, local copies, waits for them, and re-layouts  14.8 us
    all_to_all x1, blocking collectives, to_heads(): lax.all_to_all(pieces, 'uly', split_axis=0, concat_axis=0, tiled=False)  12.9 us
    ppermute x6, waiting for transfers between devices, to_peers(): lax.ppermute(p, 'uly', [(i, i ^ k) for i in range(peers)])  8.39 us
  transfers between devices with their start and end apart: 34, of which 9 were waited for; matrix products, arithmetic and copies ran while one was open for 2% of the time, Pallas kernels for 29%

profile of v4, /device:TPU:0, one launch (start us, length us, event | category | flops | bytes accessed | tf_op | source)
XLA Modules:
  0.0 267.7 jit_solution(2253833468253909288)
XLA Ops:
  1.3 12.9 %all_to_all.20 = bf16[4,128,512]{2,1,0:T(8,128)(2,1)S(1)} all-to-all(bf16[4,128,512]{2,1,0:T(8,128)(2,1)S(1)} %pad_maximum_fusion), channel_id=1, replica_groups=mesh['cfg'=2,'blk'=4,'uly'=4] {'uly'}, dimensions={0} | all-to-all | bytes 1048576 | tf_op jit(solution)/shard_map/all_to_all | solution.py:365
  17.7 3.6 %collective-permute-start = (bf16[512,512]{1,0:T(8,128)(2,1)S(1)}, bf16[512,512]{1,0:T(8,128)(2,1)}, u32[]{:S(2)}, u32[]{:S(2)}) collective-permute-start(bf16[512,512]{1,0:T(8,128)(2,1)S(1)} %bitcast.32), channel_id=1, source_target_pairs={{0,4},{4,0},{8,12},{12,8},{1,5},{5,1},{9,13},{13,9},{2,6},{6,2},{1... | collective-permute-start | bytes 1572872 | tf_op jit(solution)/shard_map/ppermute | solution.py:372
  21.4 3.7 %collective-permute-done.2.refs_10_.refs_2_ = bf16[128,1024]{1,0:T(8,128)(2,1)S(1)} collective-permute-done((bf16[128,1024]{1,0:T(8,128)(2,1)S(1)}, bf16[128,1024]{1,0:T(8,128)(2,1)S(1)}, u32[]{:S(2)}, u32[]{:S(2)}) %collective-permute-start.2) | collective-permute-done | bytes 262176 | tf_op jit(solution)/shard_map/ppermute | solution.py:369
  25.0 4.7 %collective-permute-done.3.refs_11_.refs_3_ = bf16[128,1024]{1,0:T(8,128)(2,1)S(1)} collective-permute-done((bf16[128,1024]{1,0:T(8,128)(2,1)S(1)}, bf16[128,1024]{1,0:T(8,128)(2,1)S(1)}, u32[]{:S(2)}, u32[]{:S(2)}) %collective-permute-start.3) | collective-permute-done | bytes 262176 | tf_op jit(solution)/shard_map/ppermute | solution.py:369
  38.2 16.7 %collective-permute-start.14 = (bf16[512,512]{1,0:T(8,128)(2,1)}, bf16[512,512]{1,0:T(8,128)(2,1)}, u32[]{:S(2)}, u32[]{:S(2)}) collective-permute-start(bf16[512,512]{1,0:T(8,128)(2,1)} %regroup.2.refs_5_.refs_1_.refs_3_), channel_id=1, source_target_pairs={{0,4},{4,0},{8,12},{12,8},{1,5},{5,1},{9,13},{13,9},{2,6},{6,2},{1... | collective-permute-start | bytes 1572872 | tf_op jit(solution)/shard_map/ppermute | solution.py:372
  66.0 11.2 %collective-permute-start.19 = (bf16[512,512]{1,0:T(8,128)(2,1)S(1)}, bf16[512,512]{1,0:T(8,128)(2,1)S(1)}, u32[]{:S(2)}, u32[]{:S(2)}) collective-permute-start(bf16[512,512]{1,0:T(8,128)(2,1)S(1)} %regroup.3.refs_4_.refs_1_.refs_3_), channel_id=1, source_target_pairs={{0,4},{4,0},{8,12},{12,8},{1,5},{5,1},{9,13},{13,9},{2,6},{6,2},{1... | collective-permute-start | bytes 1572872 | tf_op jit(solution)/shard_map/ppermute | solution.py:372
  81.9 8.2 %collective-permute-done.10.refs_2_ = bf16[512,512]{1,0:T(8,128)(2,1)} collective-permute-done((bf16[512,512]{1,0:T(8,128)(2,1)}, bf16[512,512]{1,0:T(8,128)(2,1)}, u32[]{:S(2)}, u32[]{:S(2)}) %collective-permute-start.10) | collective-permute-done | bytes 524320 | tf_op jit(solution)/shard_map/ppermute | solution.py:372
  90.1 12.1 %attend.6.refs_8_.refs_0_ = bf16[2,528,512]{2,1,0:T(8,128)(2,1)S(1)} custom-call(s32[3]{0:T(128)S(1)} %pad_add_fusion.1.table_ref, s32[16,12]{1,0:T(8,128)S(1)} %fusion.kept_ref, bf16[512,512]{1,0:T(8,128)(2,1)} %collective-permute-done.9.refs_0_, bf16[512,512]{1,0:T(8,128)(2,1)} %collective-permute-done.4.refs_12_.refs_4_.refs_1_, ...), custom_call_target="tpu_custom_call" | custom-call | flops 6442450944 | bytes 5242880 | tf_op jit(solution)/shard_map/attend/pallas_call | solution.py:151
  107.2 11.8 %attend.7.refs_8_.refs_0_.refs_3_ = bf16[2,528,512]{2,1,0:T(8,128)(2,1)S(1)} custom-call(s32[3]{0:T(128)S(1)} %pad_add_fusion.table_ref, s32[16,12]{1,0:T(8,128)S(1)} %fusion.kept_ref, bf16[512,512]{1,0:T(8,128)(2,1)} %collective-permute-done.refs_0_.refs_2_, bf16[512,512]{1,0:T(8,128)(2,1)S(1)} %bitcast.33, ...), custom_call_target="tpu_custom_call" | custom-call | flops 6442450944 | bytes 5242880 | tf_op jit(solution)/shard_map/attend/pallas_call | solution.py:151
  119.0 4.7 %collective-permute-done.16.refs_2_ = bf16[512,512]{1,0:T(8,128)(2,1)S(1)} collective-permute-done((bf16[512,512]{1,0:T(8,128)(2,1)S(1)}, bf16[512,512]{1,0:T(8,128)(2,1)S(1)}, u32[]{:S(2)}, u32[]{:S(2)}) %collective-permute-start.16) | collective-permute-done | bytes 524320 | tf_op jit(solution)/shard_map/ppermute | solution.py:372
  125.6 10.7 %attend.8.refs_2_.refs_0_ = bf16[2,528,512]{2,1,0:T(8,128)(2,1)S(1)} custom-call(s32[3]{0:T(128)S(1)} %pad_add_fusion.1.table_ref, s32[16,12]{1,0:T(8,128)S(1)} %fusion.kept_ref, bf16[512,512]{1,0:T(8,128)(2,1)S(1)} %collective-permute-done.15.refs_0_, bf16[512,512]{1,0:T(8,128)(2,1)S(1)} %copy-done.25, ...), custom_call_target="tpu_custom_call" | custom-call | flops 6442450944 | bytes 5242880 | tf_op jit(solution)/shard_map/attend/pallas_call | solution.py:151
  140.6 12.2 %attend.9.refs_8_.refs_0_.refs_3_ = bf16[2,528,512]{2,1,0:T(8,128)(2,1)S(1)} custom-call(s32[3]{0:T(128)S(1)} %pad_add_fusion.table_ref, s32[16,12]{1,0:T(8,128)S(1)} %fusion.kept_ref, bf16[512,512]{1,0:T(8,128)(2,1)} %collective-permute-done.14.refs_0_.refs_2_, bf16[512,512]{1,0:T(8,128)(2,1)} %regroup.2.refs_5_.refs_1_.refs_3_, ...), custom_call_target="tpu_custom_call" | custom-call | flops 6442450944 | bytes 5242880 | tf_op jit(solution)/shard_map/attend/pallas_call | solution.py:151
  153.1 10.7 %attend.10.refs_2_.refs_0_ = bf16[2,528,512]{2,1,0:T(8,128)(2,1)S(1)} custom-call(s32[3]{0:T(128)S(1)} %pad_add_fusion.1.table_ref, s32[16,12]{1,0:T(8,128)S(1)} %fusion.kept_ref, bf16[512,512]{1,0:T(8,128)(2,1)S(1)} %collective-permute-done.20.refs_0_, bf16[512,512]{1,0:T(8,128)(2,1)S(1)} %collective-permute-done.21.refs_1_, ...), custom_call_target="tpu_custom_call" | custom-call | flops 6442450944 | bytes 5242880 | tf_op jit(solution)/shard_map/attend/pallas_call | solution.py:151
  163.9 7.7 %collective-permute-start.25 = (bf16[2,528,512]{2,1,0:T(8,128)(2,1)S(1)}, bf16[2,528,512]{2,1,0:T(8,128)(2,1)S(1)}, u32[]{:S(2)}, u32[]{:S(2)}) collective-permute-start(bf16[2,528,512]{2,1,0:T(8,128)(2,1)S(1)} %attend.10.refs_2_.refs_0_), channel_id=1, source_target_pairs={{0,4},{12,8},{1,5},{13,9},{2,6},{14,10},{3,7},{15,11},{16,20},{28,... | collective-permute-start | bytes 3244040 | tf_op jit(solution)/shard_map/ppermute | solution.py:372
  172.4 10.7 %attend.11.refs_2_.refs_0_.refs_3_ = bf16[2,528,512]{2,1,0:T(8,128)(2,1)S(1)} custom-call(s32[3]{0:T(128)S(1)} %pad_add_fusion.table_ref, s32[16,12]{1,0:T(8,128)S(1)} %fusion.kept_ref, bf16[512,512]{1,0:T(8,128)(2,1)S(1)} %collective-permute-done.19.refs_0_.refs_2_, bf16[512,512]{1,0:T(8,128)(2,1)S(1)} %regroup.3.refs_4_.refs_1_.refs_3_, ...), custom_call_target="tpu_custom_call" | custom-call | flops 6442450944 | bytes 5242880 | tf_op jit(solution)/shard_map/attend/pallas_call | solution.py:151
  183.2 9.9 %collective-permute-done.25.refs_1_ = bf16[2,528,512]{2,1,0:T(8,128)(2,1)S(1)} collective-permute-done((bf16[2,528,512]{2,1,0:T(8,128)(2,1)S(1)}, bf16[2,528,512]{2,1,0:T(8,128)(2,1)S(1)}, u32[]{:S(2)}, u32[]{:S(2)}) %collective-permute-start.25) | collective-permute-done | bytes 1081376 | tf_op jit(solution)/shard_map/ppermute | solution.py:372
  193.8 7.0 %collective-permute-start.12 = (bf16[1,528,512]{2,1,0:T(8,128)(2,1)S(1)}, bf16[1,528,512]{2,1,0:T(8,128)(2,1)S(1)}, u32[]{:S(2)}, u32[]{:S(2)}) collective-permute-start(bf16[1,528,512]{2,1,0:T(8,128)(2,1)S(1)} %slice.28), channel_id=1, source_target_pairs={{0,4},{12,8},{1,5},{13,9},{2,6},{14,10},{3,7},{15,11},{16,20},{28,... | collective-permute-start | bytes 1622024 | tf_op jit(solution)/shard_map/ppermute | solution.py:372
  203.0 5.4 %collective-permute-start.27 = (bf16[1,528,512]{2,1,0:T(8,128)(2,1)}, bf16[1,528,512]{2,1,0:T(8,128)(2,1)}, u32[]{:S(2)}, u32[]{:S(2)}) collective-permute-start(bf16[1,528,512]{2,1,0:T(8,128)(2,1)} %slice.29), channel_id=1, source_target_pairs={{0,4},{12,8},{1,5},{13,9},{2,6},{14,10},{3,7},{15,11},{16,20},{28,... | collective-permute-start | bytes 1622024 | tf_op jit(solution)/shard_map/ppermute | solution.py:372
  209.2 4.3 %collective-permute-done.12.refs_1_ = bf16[1,528,512]{2,1,0:T(8,128)(2,1)S(1)} collective-permute-done((bf16[1,528,512]{2,1,0:T(8,128)(2,1)S(1)}, bf16[1,528,512]{2,1,0:T(8,128)(2,1)S(1)}, u32[]{:S(2)}, u32[]{:S(2)}) %collective-permute-start.12) | collective-permute-done | bytes 540704 | tf_op jit(solution)/shard_map/ppermute | solution.py:372
  213.5 5.2 %collective-permute-start.31 = (bf16[1,528,512]{2,1,0:T(8,128)(2,1)}, bf16[1,528,512]{2,1,0:T(8,128)(2,1)}, u32[]{:S(2)}, u32[]{:S(2)}) collective-permute-start(bf16[1,528,512]{2,1,0:T(8,128)(2,1)} %slice.30), channel_id=1, source_target_pairs={{0,4},{12,8},{1,5},{13,9},{2,6},{14,10},{3,7},{15,11},{16,20},{28,... | collective-permute-start | bytes 1622024 | tf_op jit(solution)/shard_map/ppermute | solution.py:372
  224.5 4.2 %all-to-all-start.1 = ((bf16[4,128,512]{2,1,0:T(8,128)(2,1)}), bf16[4,128,512]{2,1,0:T(8,128)(2,1)}, u32[]{:S(2)}, u32[]{:S(2)}) async-start(bf16[4,128,512]{2,1,0:T(8,128)(2,1)} %bitcast.12), calls=%async_computation.1 | async-start | bytes 1048576 | tf_op jit(solution)/shard_map/all_to_all | solution.py:427
  228.6 6.7 %collective-permute-done.29.refs_4_ = bf16[1,528,512]{2,1,0:T(8,128)(2,1)} collective-permute-done((bf16[1,528,512]{2,1,0:T(8,128)(2,1)S(1)}, bf16[1,528,512]{2,1,0:T(8,128)(2,1)}, u32[]{:S(2)}, u32[]{:S(2)}) %collective-permute-start.29) | collective-permute-done | bytes 540704 | tf_op jit(solution)/shard_map/ppermute | solution.py:372
  242.7 11.2 %all_to_all.21 = bf16[4,128,512]{2,1,0:T(8,128)(2,1)S(1)} all-to-all(bf16[4,128,512]{2,1,0:T(8,128)(2,1)S(1)} %bitcast.35), channel_id=1, replica_groups=mesh['cfg'=2,'blk'=4,'uly'=4] {'uly'}, dimensions={0} | all-to-all | bytes 1048576 | tf_op jit(solution)/shard_map/all_to_all | solution.py:427
  254.0 11.2 %all_to_all.22 = bf16[4,128,512]{2,1,0:T(8,128)(2,1)S(1)} all-to-all(bf16[4,128,512]{2,1,0:T(8,128)(2,1)S(1)} %bitcast.23), channel_id=1, replica_groups=mesh['cfg'=2,'blk'=4,'uly'=4] {'uly'}, dimensions={0} | all-to-all | bytes 1048576 | tf_op jit(solution)/shard_map/all_to_all | solution.py:427
  (139 shorter events, 60.1 us)
Async XLA Ops:
  31.1 25.0 %collective-permute-start.5 = (bf16[256,1536]{1,0:T(8,128)(2,1)S(1)}, bf16[256,1536]{1,0:T(8,128)(2,1)S(1)}, u32[]{:S(2)}, u32[]{:S(2)}) collective-permute-start(bf16[256,1536]{1,0:T(8,128)(2,1)S(1)} %get-tuple-element.20), channel_id=1, source_target_pairs={{0,1},{1,0},{2,3},{3,2},{4,5},{5,4},{6,7},{7,6},{8,9},{9,8},{10,11... | collective-permute-start | bytes 2359304 | tf_op jit(solution)/shard_map/ppermute | solution.py:369
  34.3 20.6 %collective-permute-start.9 = (bf16[512,512]{1,0:T(8,128)(2,1)}, bf16[512,512]{1,0:T(8,128)(2,1)}, u32[]{:S(2)}, u32[]{:S(2)}) collective-permute-start(bf16[512,512]{1,0:T(8,128)(2,1)} %collective-permute-done.refs_0_.refs_2_), channel_id=1, source_target_pairs={{4,8},{8,4},{5,9},{9,5},{6,10},{10,6},{7,11},{11,7},{20,24},{24,20... | collective-permute-start | bytes 1572872 | tf_op jit(solution)/shard_map/ppermute | solution.py:372
  35.9 30.1 %collective-permute-start.6 = (bf16[256,1536]{1,0:T(8,128)(2,1)}, bf16[256,1536]{1,0:T(8,128)(2,1)}, u32[]{:S(2)}, u32[]{:S(2)}) collective-permute-start(bf16[256,1536]{1,0:T(8,128)(2,1)} %get-tuple-element.21), channel_id=1, source_target_pairs={{0,2},{1,3},{2,0},{3,1},{4,6},{5,7},{6,4},{7,5},{8,10},{9,11},{10,... | collective-permute-start | bytes 2359304 | tf_op jit(solution)/shard_map/ppermute | solution.py:369
  36.3 41.0 %collective-permute-start.7 = (bf16[256,1536]{1,0:T(8,128)(2,1)}, bf16[256,1536]{1,0:T(8,128)(2,1)}, u32[]{:S(2)}, u32[]{:S(2)}) collective-permute-start(bf16[256,1536]{1,0:T(8,128)(2,1)} %get-tuple-element.22), channel_id=1, source_target_pairs={{0,3},{1,2},{2,1},{3,0},{4,7},{5,6},{6,5},{7,4},{8,11},{9,10},{10,... | collective-permute-start | bytes 2359304 | tf_op jit(solution)/shard_map/ppermute | solution.py:369
  38.2 43.0 %collective-permute-start.14 = (bf16[512,512]{1,0:T(8,128)(2,1)}, bf16[512,512]{1,0:T(8,128)(2,1)}, u32[]{:S(2)}, u32[]{:S(2)}) collective-permute-start(bf16[512,512]{1,0:T(8,128)(2,1)} %regroup.2.refs_5_.refs_1_.refs_3_), channel_id=1, source_target_pairs={{0,4},{4,0},{8,12},{12,8},{1,5},{5,1},{9,13},{13,9},{2,6},{6,2},{1... | collective-permute-start | bytes 1572872 | tf_op jit(solution)/shard_map/ppermute | solution.py:372
  54.9 25.0 %collective-permute-start.11 = (bf16[512,512]{1,0:T(8,128)(2,1)}, bf16[512,512]{1,0:T(8,128)(2,1)}, u32[]{:S(2)}, u32[]{:S(2)}) collective-permute-start(bf16[512,512]{1,0:T(8,128)(2,1)} %collective-permute-done.4.refs_12_.refs_4_.refs_1_), channel_id=1, source_target_pairs={{4,0},{8,12},{5,1},{9,13},{6,2},{10,14},{7,3},{11,15},{20,16},{24,... | collective-permute-start | bytes 1572872 | tf_op jit(solution)/shard_map/ppermute | solution.py:372
  57.0 33.1 %collective-permute-start.10 = (bf16[512,512]{1,0:T(8,128)(2,1)}, bf16[512,512]{1,0:T(8,128)(2,1)}, u32[]{:S(2)}, u32[]{:S(2)}) collective-permute-start(bf16[512,512]{1,0:T(8,128)(2,1)} %collective-permute-done.9.refs_0_), channel_id=1, source_target_pairs={{4,0},{8,12},{5,1},{9,13},{6,2},{10,14},{7,3},{11,15},{20,16},{24,... | collective-permute-start | bytes 1572872 | tf_op jit(solution)/shard_map/ppermute | solution.py:372
  66.0 39.1 %collective-permute-start.19 = (bf16[512,512]{1,0:T(8,128)(2,1)S(1)}, bf16[512,512]{1,0:T(8,128)(2,1)S(1)}, u32[]{:S(2)}, u32[]{:S(2)}) collective-permute-start(bf16[512,512]{1,0:T(8,128)(2,1)S(1)} %regroup.3.refs_4_.refs_1_.refs_3_), channel_id=1, source_target_pairs={{0,4},{4,0},{8,12},{12,8},{1,5},{5,1},{9,13},{13,9},{2,6},{6,2},{1... | collective-permute-start | bytes 1572872 | tf_op jit(solution)/shard_map/ppermute | solution.py:372
  77.2 28.6 %collective-permute-start.21 = (bf16[512,512]{1,0:T(8,128)(2,1)S(1)}, bf16[512,512]{1,0:T(8,128)(2,1)S(1)}, u32[]{:S(2)}, u32[]{:S(2)}) collective-permute-start(bf16[512,512]{1,0:T(8,128)(2,1)S(1)} %regroup.3.refs_4_.refs_1_.refs_3_), channel_id=1, source_target_pairs={{4,8},{8,4},{5,9},{9,5},{6,10},{10,6},{7,11},{11,7},{20,24},{24,20... | collective-permute-start | bytes 1572872 | tf_op jit(solution)/shard_map/ppermute | solution.py:372
  79.9 39.1 %collective-permute-start.17 = (bf16[512,512]{1,0:T(8,128)(2,1)S(1)}, bf16[512,512]{1,0:T(8,128)(2,1)S(1)}, u32[]{:S(2)}, u32[]{:S(2)}) collective-permute-start(bf16[512,512]{1,0:T(8,128)(2,1)S(1)} %copy-done.25), channel_id=1, source_target_pairs={{4,0},{8,12},{5,1},{9,13},{6,2},{10,14},{7,3},{11,15},{20,16},{24,... | collective-permute-start | bytes 1572872 | tf_op jit(solution)/shard_map/ppermute | solution.py:372
  81.2 22.6 %collective-permute-start.15 = (bf16[512,512]{1,0:T(8,128)(2,1)}, bf16[512,512]{1,0:T(8,128)(2,1)S(1)}, u32[]{:S(2)}, u32[]{:S(2)}) collective-permute-start(bf16[512,512]{1,0:T(8,128)(2,1)} %collective-permute-done.14.refs_0_.refs_2_), channel_id=1, source_target_pairs={{4,8},{8,4},{5,9},{9,5},{6,10},{10,6},{7,11},{11,7},{20,24},{24,20... | collective-permute-start | bytes 1572872 | tf_op jit(solution)/shard_map/ppermute | solution.py:372
  102.3 37.5 %collective-permute-start.13 = (bf16[2,528,512]{2,1,0:T(8,128)(2,1)S(1)}, bf16[2,528,512]{2,1,0:T(8,128)(2,1)S(1)}, u32[]{:S(2)}, u32[]{:S(2)}) collective-permute-start(bf16[2,528,512]{2,1,0:T(8,128)(2,1)S(1)} %attend.6.refs_8_.refs_0_), channel_id=1, source_target_pairs={{0,4},{12,8},{1,5},{13,9},{2,6},{14,10},{3,7},{15,11},{16,20},{28,... | collective-permute-start | bytes 3244040 | tf_op jit(solution)/shard_map/ppermute | solution.py:372
  103.8 19.9 %collective-permute-start.16 = (bf16[512,512]{1,0:T(8,128)(2,1)S(1)}, bf16[512,512]{1,0:T(8,128)(2,1)S(1)}, u32[]{:S(2)}, u32[]{:S(2)}) collective-permute-start(bf16[512,512]{1,0:T(8,128)(2,1)S(1)} %collective-permute-done.15.refs_0_), channel_id=1, source_target_pairs={{4,0},{8,12},{5,1},{9,13},{6,2},{10,14},{7,3},{11,15},{20,16},{24,... | collective-permute-start | bytes 1572872 | tf_op jit(solution)/shard_map/ppermute | solution.py:372
  105.1 33.1 %collective-permute-start.20 = (bf16[512,512]{1,0:T(8,128)(2,1)S(1)}, bf16[512,512]{1,0:T(8,128)(2,1)S(1)}, u32[]{:S(2)}, u32[]{:S(2)}) collective-permute-start(bf16[512,512]{1,0:T(8,128)(2,1)S(1)} %collective-permute-done.19.refs_0_.refs_2_), channel_id=1, source_target_pairs={{4,8},{8,4},{5,9},{9,5},{6,10},{10,6},{7,11},{11,7},{20,24},{24,20... | collective-permute-start | bytes 1572872 | tf_op jit(solution)/shard_map/ppermute | solution.py:372
  105.8 46.9 %collective-permute-start.23 = (bf16[512,512]{1,0:T(8,128)(2,1)S(1)}, bf16[512,512]{1,0:T(8,128)(2,1)S(1)}, u32[]{:S(2)}, u32[]{:S(2)}) collective-permute-start(bf16[512,512]{1,0:T(8,128)(2,1)S(1)} %collective-permute-done.21.refs_1_), channel_id=1, source_target_pairs={{4,0},{8,12},{5,1},{9,13},{6,2},{10,14},{7,3},{11,15},{20,16},{24,... | collective-permute-start | bytes 1572872 | tf_op jit(solution)/shard_map/ppermute | solution.py:372
  136.4 35.2 %collective-permute-start.26 = (bf16[2,528,512]{2,1,0:T(8,128)(2,1)S(1)}, bf16[2,528,512]{2,1,0:T(8,128)(2,1)S(1)}, u32[]{:S(2)}, u32[]{:S(2)}) collective-permute-start(bf16[2,528,512]{2,1,0:T(8,128)(2,1)S(1)} %attend.8.refs_2_.refs_0_), channel_id=1, source_target_pairs={{0,4},{12,8},{1,5},{13,9},{2,6},{14,10},{3,7},{15,11},{16,20},{28,... | collective-permute-start | bytes 3244040 | tf_op jit(solution)/shard_map/ppermute | solution.py:372
  139.8 31.8 %collective-permute-start.18 = (bf16[2,528,512]{2,1,0:T(8,128)(2,1)S(1)}, bf16[2,528,512]{2,1,0:T(8,128)(2,1)S(1)}, u32[]{:S(2)}, u32[]{:S(2)}) collective-permute-start(bf16[2,528,512]{2,1,0:T(8,128)(2,1)S(1)} %merge.6.refs_8_), channel_id=1, source_target_pairs={{4,8},{8,4},{5,9},{9,5},{6,10},{10,6},{7,11},{11,7},{20,24},{24,20... | collective-permute-start | bytes 3244040 | tf_op jit(solution)/shard_map/ppermute | solution.py:372
  163.9 29.2 %collective-permute-start.25 = (bf16[2,528,512]{2,1,0:T(8,128)(2,1)S(1)}, bf16[2,528,512]{2,1,0:T(8,128)(2,1)S(1)}, u32[]{:S(2)}, u32[]{:S(2)}) collective-permute-start(bf16[2,528,512]{2,1,0:T(8,128)(2,1)S(1)} %attend.10.refs_2_.refs_0_), channel_id=1, source_target_pairs={{0,4},{12,8},{1,5},{13,9},{2,6},{14,10},{3,7},{15,11},{16,20},{28,... | collective-permute-start | bytes 3244040 | tf_op jit(solution)/shard_map/ppermute | solution.py:372
  171.7 48.2 %collective-permute-start.28 = (bf16[2,528,512]{2,1,0:T(8,128)(2,1)S(1)}, bf16[2,528,512]{2,1,0:T(8,128)(2,1)S(1)}, u32[]{:S(2)}, u32[]{:S(2)}) collective-permute-start(bf16[2,528,512]{2,1,0:T(8,128)(2,1)S(1)} %merge.8.refs_8_), channel_id=1, source_target_pairs={{4,8},{8,4},{5,9},{9,5},{6,10},{10,6},{7,11},{11,7},{20,24},{24,20... | collective-permute-start | bytes 3244040 | tf_op jit(solution)/shard_map/ppermute | solution.py:372
  193.1 29.1 %collective-permute-start.30 = (bf16[2,528,512]{2,1,0:T(8,128)(2,1)S(1)}, bf16[2,528,512]{2,1,0:T(8,128)(2,1)S(1)}, u32[]{:S(2)}, u32[]{:S(2)}) collective-permute-start(bf16[2,528,512]{2,1,0:T(8,128)(2,1)S(1)} %merge.9.refs_5_), channel_id=1, source_target_pairs={{4,8},{8,4},{5,9},{9,5},{6,10},{10,6},{7,11},{11,7},{20,24},{24,20... | collective-permute-start | bytes 3244040 | tf_op jit(solution)/shard_map/ppermute | solution.py:372
  193.8 19.7 %collective-permute-start.12 = (bf16[1,528,512]{2,1,0:T(8,128)(2,1)S(1)}, bf16[1,528,512]{2,1,0:T(8,128)(2,1)S(1)}, u32[]{:S(2)}, u32[]{:S(2)}) collective-permute-start(bf16[1,528,512]{2,1,0:T(8,128)(2,1)S(1)} %slice.28), channel_id=1, source_target_pairs={{0,4},{12,8},{1,5},{13,9},{2,6},{14,10},{3,7},{15,11},{16,20},{28,... | collective-permute-start | bytes 1622024 | tf_op jit(solution)/shard_map/ppermute | solution.py:372
  203.0 25.6 %collective-permute-start.27 = (bf16[1,528,512]{2,1,0:T(8,128)(2,1)}, bf16[1,528,512]{2,1,0:T(8,128)(2,1)}, u32[]{:S(2)}, u32[]{:S(2)}) collective-permute-start(bf16[1,528,512]{2,1,0:T(8,128)(2,1)} %slice.29), channel_id=1, source_target_pairs={{0,4},{12,8},{1,5},{13,9},{2,6},{14,10},{3,7},{15,11},{16,20},{28,... | collective-permute-start | bytes 1622024 | tf_op jit(solution)/shard_map/ppermute | solution.py:372
  213.5 24.7 %collective-permute-start.31 = (bf16[1,528,512]{2,1,0:T(8,128)(2,1)}, bf16[1,528,512]{2,1,0:T(8,128)(2,1)}, u32[]{:S(2)}, u32[]{:S(2)}) collective-permute-start(bf16[1,528,512]{2,1,0:T(8,128)(2,1)} %slice.30), channel_id=1, source_target_pairs={{0,4},{12,8},{1,5},{13,9},{2,6},{14,10},{3,7},{15,11},{16,20},{28,... | collective-permute-start | bytes 1622024 | tf_op jit(solution)/shard_map/ppermute | solution.py:372
  224.5 18.3 %all-to-all-start.1 = ((bf16[4,128,512]{2,1,0:T(8,128)(2,1)}), bf16[4,128,512]{2,1,0:T(8,128)(2,1)}, u32[]{:S(2)}, u32[]{:S(2)}) async-start(bf16[4,128,512]{2,1,0:T(8,128)(2,1)} %bitcast.12), calls=%async_computation.1 | async-start | bytes 1048576 | tf_op jit(solution)/shard_map/all_to_all | solution.py:427
  (37 other events, 372.3 us)

commit v5 on v4

--- a/solution.py
+++ b/solution.py
@@ -257,30 +257,33 @@
     )(table, *[array for array, _ in parts], dep)
 
 
-def part_kernel(peers, count, start, peer_ref, *refs):
-    rows = refs[0].shape[0]
+def part_kernel(peers, starts, peer_ref, *refs):
     outs = refs[-peers:]
-    for i, ref in enumerate(refs[: count * peers]):
-        outs[i % peers][i // peers * rows : (i // peers + 1) * rows, :] = ref[:, start:]
-
-
-def parts_for_peers(peer, arrays, start, peers, deps):
+    at = 0
+    for i, start in enumerate(starts):
+        for k in range(peers):
+            ref = refs[i * peers + k]
+            outs[k][:, at : at + ref.shape[1] - start] = ref[:, start:]
+        at += ref.shape[1] - start
+
+
+def parts_for_peers(peer, arrays, starts, peers, dep):
     rows, group = arrays[0].shape[0], arrays[0].shape[1] // peers
     specs = [pl.BlockSpec((rows, group), functools.partial(lambda k, i, t: (0, t[0] ^ k), k)) for k in range(peers)]
-    shape = (len(arrays) * rows, group - start)
+    shape = (rows, len(arrays) * group - sum(starts))
     return pl.pallas_call(
-        functools.partial(part_kernel, peers, len(arrays), start),
+        functools.partial(part_kernel, peers, starts),
         out_shape=[jax.ShapeDtypeStruct(shape, jnp.bfloat16)] * peers,
         grid_spec=pltpu.PrefetchScalarGridSpec(
             num_scalar_prefetch=1,
             grid=(1,),
-            in_specs=specs * len(arrays) + [pl.BlockSpec(memory_space=pl.ANY)] * len(deps),
+            in_specs=specs * len(arrays) + [pl.BlockSpec(memory_space=pl.ANY)],
             out_specs=[pl.BlockSpec(shape, lambda i, t: (0, 0))] * peers,
         ),
         compiler_params=pltpu.CompilerParams(vmem_limit_bytes=28 * MIB),
         cost_estimate=QUICK,
         name="parts",
-    )(peer.reshape(1), *[a for a in arrays for _ in range(peers)], *deps)
+    )(peer.reshape(1), *[a for a in arrays for _ in range(peers)], dep)
 
 
 def regroup_kernel(peers, start, peer_ref, *refs):
@@ -312,16 +315,16 @@
 
 def join_kernel(*refs):
     pieces, (k_ref, v_ref, v_s) = refs[:-4], refs[-3:]
-    rows = pieces[0].shape[0] // 2
+    rows, group = pieces[0].shape[0], k_ref.shape[1]
     for i, piece in enumerate(pieces):
-        k_ref[i * rows : (i + 1) * rows, :] = piece[:rows, :]
-        v_s[i * rows : (i + 1) * rows, :] = piece[rows:, :]
+        k_ref[i * rows : (i + 1) * rows, :] = piece[:, :group]
+        v_s[i * rows : (i + 1) * rows, :] = piece[:, group : 2 * group]
     for at in range(0, v_s.shape[0], TILE):
         v_ref[:, at : at + TILE] = jnp.transpose(v_s[at : at + TILE, :])
 
 
-def joined(pieces, dep):
-    rows, group = pieces[0].shape[0] // 2 * len(pieces), pieces[0].shape[1]
+def joined(pieces, group, dep):
+    rows = pieces[0].shape[0] * len(pieces)
     return pl.pallas_call(
         join_kernel,
         out_shape=[
@@ -392,19 +395,14 @@
     early = widths[0]
     first_span = to_heads(jnp.stack([new_queries[:, p * group : p * group + early] for p in range(peers)]))
     found = [spread(first_span)]
-    parts_q = parts_for_peers(peer, [new_queries], early, peers, [first_span])
-    later = to_peers(parts_q)
-    parts_kv = parts_for_peers(peer, [new_keys, new_values], 0, peers, [*later, found[0]["early"]])
+    moved = to_peers(parts_for_peers(peer, [new_keys, new_values, new_queries], [0, 0, early], peers, first_span))
 
     def run_spread(c, deps):
-        span = regrouped(peer, later, PIECES[c][0] * unit - early, widths[c], deps)
+        span = regrouped(peer, moved, 2 * group + PIECES[c][0] * unit - early, widths[c], deps)
         found.append(spread(span))
         return span
 
-    latest = parts_kv[0]
-    for c in range(1, count):
-        latest = run_spread(c, [found[c - 1]["early"], latest])
-    span_k, span_v_t = joined(to_peers(parts_kv), latest)
+    span_k, span_v_t = joined(moved, group, run_spread(1, [first_span]))
     context_values_t = context_values.T
     last = [span_k]
     outer = ((place == 0) | (place == n - 1)).astype(jnp.int32)
@@ -423,8 +421,15 @@
         return last[0]
 
     def run_back(c, choices):
-        done = run_join(c, choices, True).reshape(peers, own_rows, widths[c])
-        backs[c] = lax.all_to_all(done, "uly", split_axis=0, concat_axis=0, tiled=False)
+        backs[c] = run_join(c, choices, True).reshape(peers, own_rows, widths[c])
+
+    def run_return(first, last_one):
+        those = range(first, last_one + 1)
+        moved = lax.all_to_all(jnp.concatenate([backs[c] for c in those], axis=2), "uly", split_axis=0, concat_axis=0, tiled=False)
+        at = 0
+        for c in those:
+            backs[c] = moved[:, :, at : at + widths[c]]
+            at += widths[c]
 
     state = [dict() for _ in range(count)]
 
@@ -451,6 +456,7 @@
 
     if line:
         run_sent(0)
+        last[0] = run_spread(2, [found[1]["early"], last[0]])
         run_kept(0)
         run_sent(1)
         run_cross(0)
@@ -461,12 +467,16 @@
         run_kept(2)
         run_cross(2)
         run_finish(0)
+        run_return(0, 0)
         run_outward(1)
         run_outward(2)
         run_finish(1)
         run_finish(2)
+        run_return(1, 2)
     else:
         for c in range(count):
+            if c > 1:
+                last[0] = run_spread(c, [last[0]])
             parts = {d: [] for d in range(n)}
             for distances in (range(1, n, 2), range(0, n, 2)):
                 blocks = [found[c]["found"][d] for d in distances]
@@ -474,14 +484,15 @@
                 for slot, d in enumerate(distances):
                     parts[d].append((mine, slot))
                 if 1 in distances:
-                    moved = send(mine, *[(i, i ^ 1) for i in range(n)])
+                    swapped = send(mine, *[(i, i ^ 1) for i in range(n)])
             for slot, d in enumerate(range(0, n, 2)):
-                parts[d].append((moved, slot))
+                parts[d].append((swapped, slot))
             for bit in bits[1:]:
                 for d in range(bit, n, 2 * bit):
                     joint = run_join(c, [parts[d], parts[d]])
                     parts[d ^ bit].append((send(joint, *[(i, i ^ bit) for i in range(n)]), 0))
             run_back(c, [parts[0], parts[0]])
+            run_return(c, c)
 
     in_order = [backs[c] for c in sorted(range(count), key=lambda c: PIECES[c][0])]
     together = jnp.concatenate(in_order, axis=2)

time: 269 us -> 291 us (1.082)
  waiting for transfers between devices: 45.5 us -> 102 us
  blocking collectives: 35.4 us -> 16.9 us
  starting transfers between devices: 88 us -> 71.6 us
    ppermute x27, waiting for transfers between devices: 37.1 us -> 64.6 us  [send(): return lax.ppermute(x, 'blk', pairs)]
    ppermute x6 -> x3, waiting for transfers between devices: 8.39 us -> 27.9 us  [to_peers(): lax.ppermute(p, 'uly', [(i, i ^ k) for i in range(peers)])]
    ppermute x27, starting transfers between devices: 79.9 us -> 61.3 us  [send(): return lax.ppermute(x, 'blk', pairs)]
    all_to_all x3 -> x1, blocking collectives: 35.4 us -> 16.9 us  [run_return(): lax.all_to_all(jnp.concatenate([backs[c] for c in those], axis=2), 'uly',...]
    all_to_all x1 -> x2, waiting for transfers between devices: 0.01 us -> 9.46 us  [the longest x1 9.45 us: to_heads(): lax.all_to_all(pieces, 'uly', split_axis=0, concat_axis=0, tiled=False)]
    all_to_all x1 -> x2, starting transfers between devices: 4.15 us -> 8.4 us  [the longest x1 4.24 us: to_heads(): lax.all_to_all(pieces, 'uly', split_axis=0, concat_axis=0, tiled=False)]
    unnamed x55 -> x31, local copies, waits for them, and re-layouts: 14.8 us -> 12.2 us
  transfers between devices with their start and end apart: 34 -> 32, of which waited for: 9 -> 11; matrix products, arithmetic and copies ran while one was open for 2% -> 3% of each run, Pallas kernels for 29% -> 27%
where the time goes in v5:
time: 291 us; the launch traced here: 289 us
  waiting for transfers between devices  102 us (35%)
  Pallas kernels  79.1 us (27%)
  starting transfers between devices  71.6 us (25%)
  blocking collectives  16.9 us (6%)
  local copies, waits for them, and re-layouts  16.8 us (6%)
    pallas_call x6, Pallas kernels, attend(): pl.pallas_call(functools.partial(attend_kernel, [[None] * len(c) for c in...  69.7 us
    ppermute x27, waiting for transfers between devices, send(): return lax.ppermute(x, 'blk', pairs)  64.6 us
    ppermute x27, starting transfers between devices, send(): return lax.ppermute(x, 'blk', pairs)  61.3 us
    ppermute x3, waiting for transfers between devices, to_peers(): lax.ppermute(p, 'uly', [(i, i ^ k) for i in range(peers)])  27.9 us
    all_to_all x1, blocking collectives, run_return(): lax.all_to_all(jnp.concatenate([backs[c] for c in those], axis=2), 'uly',...  16.9 us
    unnamed x31, local copies, waits for them, and re-layouts  12.2 us
    all_to_all x1, waiting for transfers between devices, to_heads(): lax.all_to_all(pieces, 'uly', split_axis=0, concat_axis=0, tiled=False)  9.45 us
    pallas_call x9, Pallas kernels, join_parts(): pl.pallas_call(functools.partial(join_kernel_of, [len(c) for c in choices...  6.06 us
  transfers between devices with their start and end apart: 32, of which 11 were waited for; matrix products, arithmetic and copies ran while one was open for 3% of the time, Pallas kernels for 27%

profile of v5, /device:TPU:0, one launch (start us, length us, event | category | flops | bytes accessed | tf_op | source)
XLA Modules:
  0.0 289.3 jit_solution(1358347275697923199)
XLA Ops:
  2.2 4.2 %all-to-all-start = ((bf16[4,128,512]{2,1,0:T(8,128)(2,1)}), bf16[4,128,512]{2,1,0:T(8,128)(2,1)}, u32[]{:S(2)}, u32[]{:S(2)}) async-start(bf16[4,128,512]{2,1,0:T(8,128)(2,1)} %pad_maximum_fusion.1), calls=%async_computation | async-start | bytes 1048576 | tf_op jit(solution)/shard_map/all_to_all | solution.py:368
  6.4 9.5 %all-to-all-done = bf16[4,128,512]{2,1,0:T(8,128)(2,1)} async-done(((bf16[4,128,512]{2,1,0:T(8,128)(2,1)}), bf16[4,128,512]{2,1,0:T(8,128)(2,1)}, u32[]{:S(2)}, u32[]{:S(2)}) %all-to-all-start) | async-done | bytes 524320 | tf_op jit(solution)/shard_map/all_to_all | solution.py:368
  25.8 11.2 %collective-permute-done.refs_0_.refs_2_ = bf16[512,512]{1,0:T(8,128)(2,1)} collective-permute-done((bf16[512,512]{1,0:T(8,128)(2,1)}, bf16[512,512]{1,0:T(8,128)(2,1)}, u32[]{:S(2)}, u32[]{:S(2)}) %collective-permute-start) | collective-permute-done | bytes 524320 | tf_op jit(solution)/shard_map/ppermute | solution.py:375
  40.1 6.2 %collective-permute-done.2.refs_2_ = bf16[128,4096]{1,0:T(8,128)(2,1)S(1)} collective-permute-done((bf16[128,4096]{1,0:T(8,128)(2,1)}, bf16[128,4096]{1,0:T(8,128)(2,1)S(1)}, u32[]{:S(2)}, u32[]{:S(2)}) %collective-permute-start.2) | collective-permute-done | bytes 1048608 | tf_op jit(solution)/shard_map/ppermute | solution.py:372
  46.3 21.7 %collective-permute-done.3.refs_3_ = bf16[128,4096]{1,0:T(8,128)(2,1)S(1)} collective-permute-done((bf16[128,4096]{1,0:T(8,128)(2,1)}, bf16[128,4096]{1,0:T(8,128)(2,1)S(1)}, u32[]{:S(2)}, u32[]{:S(2)}) %collective-permute-start.3) | collective-permute-done | bytes 1048608 | tf_op jit(solution)/shard_map/ppermute | solution.py:372
  71.9 4.4 %collective-permute-start.11 = (bf16[512,512]{1,0:T(8,128)(2,1)}, bf16[512,512]{1,0:T(8,128)(2,1)}, u32[]{:S(2)}, u32[]{:S(2)}) collective-permute-start(bf16[512,512]{1,0:T(8,128)(2,1)} %regroup.2.refs_4_.refs_1_.refs_3_), channel_id=1, source_target_pairs={{0,4},{4,0},{8,12},{12,8},{1,5},{5,1},{9,13},{13,9},{2,6},{6,2},{1... | collective-permute-start | bytes 1572872 | tf_op jit(solution)/shard_map/ppermute | solution.py:375
  77.8 4.7 %copy.11 = bf16[1024,1536]{0,1:T(8,128)(2,1)} copy(bf16[1024,1536]{1,0:T(8,128)(2,1)} %param.10) | data formatting | bytes 6291456 | tf_op args[4]
  84.6 4.8 %collective-permute-done.11.refs_0_.refs_2_ = bf16[512,512]{1,0:T(8,128)(2,1)} collective-permute-done((bf16[512,512]{1,0:T(8,128)(2,1)}, bf16[512,512]{1,0:T(8,128)(2,1)}, u32[]{:S(2)}, u32[]{:S(2)}) %collective-permute-start.11) | collective-permute-done | bytes 524320 | tf_op jit(solution)/shard_map/ppermute | solution.py:375
  91.4 9.2 %collective-permute-done.7.refs_2_ = bf16[512,512]{1,0:T(8,128)(2,1)} collective-permute-done((bf16[512,512]{1,0:T(8,128)(2,1)}, bf16[512,512]{1,0:T(8,128)(2,1)}, u32[]{:S(2)}, u32[]{:S(2)}) %collective-permute-start.7) | collective-permute-done | bytes 524320 | tf_op jit(solution)/shard_map/ppermute | solution.py:375
  102.5 12.2 %attend.6.refs_5_.refs_0_ = bf16[2,528,512]{2,1,0:T(8,128)(2,1)S(1)} custom-call(s32[3]{0:T(128)S(1)} %pad_add_fusion.1.table_ref, s32[16,12]{1,0:T(8,128)S(1)} %fusion.kept_ref, bf16[512,512]{1,0:T(8,128)(2,1)} %collective-permute-done.5.refs_0_, bf16[512,512]{1,0:T(8,128)(2,1)} %collective-permute-done.6.refs_1_, ...), custom_call_target="tpu_custom_call" | custom-call | flops 6442450944 | bytes 5242880 | tf_op jit(solution)/shard_map/attend/pallas_call | solution.py:151
  118.7 12.2 %attend.7.refs_8_.refs_0_.refs_3_ = bf16[2,528,512]{2,1,0:T(8,128)(2,1)S(1)} custom-call(s32[3]{0:T(128)S(1)} %pad_add_fusion.table_ref, s32[16,12]{1,0:T(8,128)S(1)} %fusion.kept_ref, bf16[512,512]{1,0:T(8,128)(2,1)} %collective-permute-done.refs_0_.refs_2_, bf16[512,512]{1,0:T(8,128)(2,1)} %bitcast.7.refs_12_.refs_4_.refs_1_.refs_3_, ...), custom_call_target="tpu_custom_call" | custom-call | flops 6442450944 | bytes 5242880 | tf_op jit(solution)/shard_map/attend/pallas_call | solution.py:151
  130.9 18.9 %collective-permute-done.16.refs_0_.refs_2_ = bf16[512,512]{1,0:T(8,128)(2,1)S(1)} collective-permute-done((bf16[512,512]{1,0:T(8,128)(2,1)S(1)}, bf16[512,512]{1,0:T(8,128)(2,1)S(1)}, u32[]{:S(2)}, u32[]{:S(2)}) %collective-permute-start.16) | collective-permute-done | bytes 524320 | tf_op jit(solution)/shard_map/ppermute | solution.py:375
  151.8 11.7 %attend.8.refs_2_.refs_0_ = bf16[2,528,512]{2,1,0:T(8,128)(2,1)S(1)} custom-call(s32[3]{0:T(128)S(1)} %pad_add_fusion.1.table_ref, s32[16,12]{1,0:T(8,128)S(1)} %fusion.kept_ref, bf16[512,512]{1,0:T(8,128)(2,1)S(1)} %collective-permute-done.12.refs_0_, bf16[512,512]{1,0:T(8,128)(2,1)} %collective-permute-done.4.refs_4_.refs_1_, ...), custom_call_target="tpu_custom_call" | custom-call | flops 6442450944 | bytes 5242880 | tf_op jit(solution)/shard_map/attend/pallas_call | solution.py:151
  163.5 6.8 %collective-permute-start.23 = (bf16[2,528,512]{2,1,0:T(8,128)(2,1)S(1)}, bf16[2,528,512]{2,1,0:T(8,128)(2,1)S(1)}, u32[]{:S(2)}, u32[]{:S(2)}) collective-permute-start(bf16[2,528,512]{2,1,0:T(8,128)(2,1)S(1)} %attend.8.refs_2_.refs_0_), channel_id=1, source_target_pairs={{0,4},{12,8},{1,5},{13,9},{2,6},{14,10},{3,7},{15,11},{16,20},{28,... | collective-permute-start | bytes 3244040 | tf_op jit(solution)/shard_map/ppermute | solution.py:375
  172.6 12.2 %attend.9.refs_8_.refs_0_.refs_3_ = bf16[2,528,512]{2,1,0:T(8,128)(2,1)S(1)} custom-call(s32[3]{0:T(128)S(1)} %pad_add_fusion.table_ref, s32[16,12]{1,0:T(8,128)S(1)} %fusion.kept_ref, bf16[512,512]{1,0:T(8,128)(2,1)} %collective-permute-done.11.refs_0_.refs_2_, bf16[512,512]{1,0:T(8,128)(2,1)} %regroup.2.refs_4_.refs_1_.refs_3_, ...), custom_call_target="tpu_custom_call" | custom-call | flops 6442450944 | bytes 5242880 | tf_op jit(solution)/shard_map/attend/pallas_call | solution.py:151
  184.8 10.8 %attend.10.refs_2_.refs_0_ = bf16[2,528,512]{2,1,0:T(8,128)(2,1)S(1)} custom-call(s32[3]{0:T(128)S(1)} %pad_add_fusion.1.table_ref, s32[16,12]{1,0:T(8,128)S(1)} %fusion.kept_ref, bf16[512,512]{1,0:T(8,128)(2,1)S(1)} %collective-permute-done.17.refs_0_, bf16[512,512]{1,0:T(8,128)(2,1)S(1)} %collective-permute-done.18.refs_1_, ...), custom_call_target="tpu_custom_call" | custom-call | flops 6442450944 | bytes 5242880 | tf_op jit(solution)/shard_map/attend/pallas_call | solution.py:151
  195.6 7.4 %collective-permute-start.22 = (bf16[2,528,512]{2,1,0:T(8,128)(2,1)S(1)}, bf16[2,528,512]{2,1,0:T(8,128)(2,1)S(1)}, u32[]{:S(2)}, u32[]{:S(2)}) collective-permute-start(bf16[2,528,512]{2,1,0:T(8,128)(2,1)S(1)} %attend.10.refs_2_.refs_0_), channel_id=1, source_target_pairs={{0,4},{12,8},{1,5},{13,9},{2,6},{14,10},{3,7},{15,11},{16,20},{28,... | collective-permute-start | bytes 3244040 | tf_op jit(solution)/shard_map/ppermute | solution.py:375
  203.8 10.8 %attend.11.refs_2_.refs_0_.refs_3_ = bf16[2,528,512]{2,1,0:T(8,128)(2,1)S(1)} custom-call(s32[3]{0:T(128)S(1)} %pad_add_fusion.table_ref, s32[16,12]{1,0:T(8,128)S(1)} %fusion.kept_ref, bf16[512,512]{1,0:T(8,128)(2,1)S(1)} %collective-permute-done.16.refs_0_.refs_2_, bf16[512,512]{1,0:T(8,128)(2,1)S(1)} %regroup.3.refs_8_.refs_1_.refs_3_, ...), custom_call_target="tpu_custom_call" | custom-call | flops 6442450944 | bytes 5242880 | tf_op jit(solution)/shard_map/attend/pallas_call | solution.py:151
  214.6 8.3 %collective-permute-done.22.refs_1_ = bf16[2,528,512]{2,1,0:T(8,128)(2,1)S(1)} collective-permute-done((bf16[2,528,512]{2,1,0:T(8,128)(2,1)S(1)}, bf16[2,528,512]{2,1,0:T(8,128)(2,1)S(1)}, u32[]{:S(2)}, u32[]{:S(2)}) %collective-permute-start.22) | collective-permute-done | bytes 1081376 | tf_op jit(solution)/shard_map/ppermute | solution.py:375
  223.7 7.4 %collective-permute-start.9 = (bf16[1,528,512]{2,1,0:T(8,128)(2,1)S(1)}, bf16[1,528,512]{2,1,0:T(8,128)(2,1)S(1)}, u32[]{:S(2)}, u32[]{:S(2)}) collective-permute-start(bf16[1,528,512]{2,1,0:T(8,128)(2,1)S(1)} %slice.31), channel_id=1, source_target_pairs={{0,4},{12,8},{1,5},{13,9},{2,6},{14,10},{3,7},{15,11},{16,20},{28,... | collective-permute-start | bytes 1622024 | tf_op jit(solution)/shard_map/ppermute | solution.py:375
  233.2 5.4 %collective-permute-start.24 = (bf16[1,528,512]{2,1,0:T(8,128)(2,1)}, bf16[1,528,512]{2,1,0:T(8,128)(2,1)}, u32[]{:S(2)}, u32[]{:S(2)}) collective-permute-start(bf16[1,528,512]{2,1,0:T(8,128)(2,1)} %slice.32), channel_id=1, source_target_pairs={{0,4},{12,8},{1,5},{13,9},{2,6},{14,10},{3,7},{15,11},{16,20},{28,... | collective-permute-start | bytes 1622024 | tf_op jit(solution)/shard_map/ppermute | solution.py:375
  243.5 5.2 %collective-permute-start.28 = (bf16[1,528,512]{2,1,0:T(8,128)(2,1)}, bf16[1,528,512]{2,1,0:T(8,128)(2,1)}, u32[]{:S(2)}, u32[]{:S(2)}) collective-permute-start(bf16[1,528,512]{2,1,0:T(8,128)(2,1)} %slice.33), channel_id=1, source_target_pairs={{0,4},{12,8},{1,5},{13,9},{2,6},{14,10},{3,7},{15,11},{16,20},{28,... | collective-permute-start | bytes 1622024 | tf_op jit(solution)/shard_map/ppermute | solution.py:375
  264.1 4.2 %collective-permute-done.29.refs_4_ = bf16[1,528,512]{2,1,0:T(8,128)(2,1)} collective-permute-done((bf16[1,528,512]{2,1,0:T(8,128)(2,1)}, bf16[1,528,512]{2,1,0:T(8,128)(2,1)}, u32[]{:S(2)}, u32[]{:S(2)}) %collective-permute-start.29) | collective-permute-done | bytes 540704 | tf_op jit(solution)/shard_map/ppermute | solution.py:375
  270.0 16.9 %all_to_all.15 = bf16[4,128,1024]{2,1,0:T(8,128)(2,1)S(1)} all-to-all(bf16[4,128,1024]{2,1,0:T(8,128)(2,1)S(1)} %pad_maximum_fusion), channel_id=1, replica_groups=mesh['cfg'=2,'blk'=4,'uly'=4] {'uly'}, dimensions={0} | all-to-all | bytes 2097152 | tf_op jit(solution)/shard_map/all_to_all | solution.py:428
  (109 shorter events, 62.6 us)
Async XLA Ops:
  20.1 19.9 %collective-permute-start.1 = (bf16[128,4096]{1,0:T(8,128)(2,1)}, bf16[128,4096]{1,0:T(8,128)(2,1)S(1)}, u32[]{:S(2)}, u32[]{:S(2)}) collective-permute-start(bf16[128,4096]{1,0:T(8,128)(2,1)} %get-tuple-element.12), channel_id=1, source_target_pairs={{0,1},{1,0},{2,3},{3,2},{4,5},{5,4},{6,7},{7,6},{8,9},{9,8},{10,11... | collective-permute-start | bytes 3145736 | tf_op jit(solution)/shard_map/ppermute | solution.py:372
  20.1 26.2 %collective-permute-start.2 = (bf16[128,4096]{1,0:T(8,128)(2,1)}, bf16[128,4096]{1,0:T(8,128)(2,1)S(1)}, u32[]{:S(2)}, u32[]{:S(2)}) collective-permute-start(bf16[128,4096]{1,0:T(8,128)(2,1)} %get-tuple-element.13), channel_id=1, source_target_pairs={{0,2},{1,3},{2,0},{3,1},{4,6},{5,7},{6,4},{7,5},{8,10},{9,11},{10,... | collective-permute-start | bytes 3145736 | tf_op jit(solution)/shard_map/ppermute | solution.py:372
  20.1 47.9 %collective-permute-start.3 = (bf16[128,4096]{1,0:T(8,128)(2,1)}, bf16[128,4096]{1,0:T(8,128)(2,1)S(1)}, u32[]{:S(2)}, u32[]{:S(2)}) collective-permute-start(bf16[128,4096]{1,0:T(8,128)(2,1)} %get-tuple-element.14), channel_id=1, source_target_pairs={{0,3},{1,2},{2,1},{3,0},{4,7},{5,6},{6,5},{7,4},{8,11},{9,10},{10,... | collective-permute-start | bytes 3145736 | tf_op jit(solution)/shard_map/ppermute | solution.py:372
  37.1 39.3 %collective-permute-start.5 = (bf16[512,512]{1,0:T(8,128)(2,1)}, bf16[512,512]{1,0:T(8,128)(2,1)}, u32[]{:S(2)}, u32[]{:S(2)}) collective-permute-start(bf16[512,512]{1,0:T(8,128)(2,1)} %collective-permute-done.refs_0_.refs_2_), channel_id=1, source_target_pairs={{4,8},{8,4},{5,9},{9,5},{6,10},{10,6},{7,11},{11,7},{20,24},{24,20... | collective-permute-start | bytes 1572872 | tf_op jit(solution)/shard_map/ppermute | solution.py:375
  38.8 52.6 %collective-permute-start.8 = (bf16[512,512]{1,0:T(8,128)(2,1)}, bf16[512,512]{1,0:T(8,128)(2,1)}, u32[]{:S(2)}, u32[]{:S(2)}) collective-permute-start(bf16[512,512]{1,0:T(8,128)(2,1)} %collective-permute-done.6.refs_1_), channel_id=1, source_target_pairs={{4,0},{8,12},{5,1},{9,13},{6,2},{10,14},{7,3},{11,15},{20,16},{24,... | collective-permute-start | bytes 1572872 | tf_op jit(solution)/shard_map/ppermute | solution.py:375
  70.4 19.7 %collective-permute-start.4 = (bf16[512,512]{1,0:T(8,128)(2,1)}, bf16[512,512]{1,0:T(8,128)(2,1)}, u32[]{:S(2)}, u32[]{:S(2)}) collective-permute-start(bf16[512,512]{1,0:T(8,128)(2,1)} %regroup.2.refs_4_.refs_1_.refs_3_), channel_id=1, source_target_pairs={{4,8},{8,4},{5,9},{9,5},{6,10},{10,6},{7,11},{11,7},{20,24},{24,20... | collective-permute-start | bytes 1572872 | tf_op jit(solution)/shard_map/ppermute | solution.py:375
  76.4 24.3 %collective-permute-start.7 = (bf16[512,512]{1,0:T(8,128)(2,1)}, bf16[512,512]{1,0:T(8,128)(2,1)}, u32[]{:S(2)}, u32[]{:S(2)}) collective-permute-start(bf16[512,512]{1,0:T(8,128)(2,1)} %collective-permute-done.5.refs_0_), channel_id=1, source_target_pairs={{4,0},{8,12},{5,1},{9,13},{6,2},{10,14},{7,3},{11,15},{20,16},{24,... | collective-permute-start | bytes 1572872 | tf_op jit(solution)/shard_map/ppermute | solution.py:375
  89.4 28.0 %collective-permute-start.12 = (bf16[512,512]{1,0:T(8,128)(2,1)}, bf16[512,512]{1,0:T(8,128)(2,1)S(1)}, u32[]{:S(2)}, u32[]{:S(2)}) collective-permute-start(bf16[512,512]{1,0:T(8,128)(2,1)} %collective-permute-done.11.refs_0_.refs_2_), channel_id=1, source_target_pairs={{4,8},{8,4},{5,9},{9,5},{6,10},{10,6},{7,11},{11,7},{20,24},{24,20... | collective-permute-start | bytes 1572872 | tf_op jit(solution)/shard_map/ppermute | solution.py:375
  90.1 61.6 %collective-permute-start.14 = (bf16[512,512]{1,0:T(8,128)(2,1)}, bf16[512,512]{1,0:T(8,128)(2,1)S(1)}, u32[]{:S(2)}, u32[]{:S(2)}) collective-permute-start(bf16[512,512]{1,0:T(8,128)(2,1)} %collective-permute-done.4.refs_4_.refs_1_), channel_id=1, source_target_pairs={{4,0},{8,12},{5,1},{9,13},{6,2},{10,14},{7,3},{11,15},{20,16},{24,... | collective-permute-start | bytes 1572872 | tf_op jit(solution)/shard_map/ppermute | solution.py:375
  114.7 56.9 %collective-permute-start.10 = (bf16[2,528,512]{2,1,0:T(8,128)(2,1)S(1)}, bf16[2,528,512]{2,1,0:T(8,128)(2,1)S(1)}, u32[]{:S(2)}, u32[]{:S(2)}) collective-permute-start(bf16[2,528,512]{2,1,0:T(8,128)(2,1)S(1)} %attend.6.refs_5_.refs_0_), channel_id=1, source_target_pairs={{0,4},{12,8},{1,5},{13,9},{2,6},{14,10},{3,7},{15,11},{16,20},{28,... | collective-permute-start | bytes 3244040 | tf_op jit(solution)/shard_map/ppermute | solution.py:375
  116.6 33.2 %collective-permute-start.16 = (bf16[512,512]{1,0:T(8,128)(2,1)S(1)}, bf16[512,512]{1,0:T(8,128)(2,1)S(1)}, u32[]{:S(2)}, u32[]{:S(2)}) collective-permute-start(bf16[512,512]{1,0:T(8,128)(2,1)S(1)} %regroup.3.refs_8_.refs_1_.refs_3_), channel_id=1, source_target_pairs={{0,4},{4,0},{8,12},{12,8},{1,5},{5,1},{9,13},{13,9},{2,6},{6,2},{1... | collective-permute-start | bytes 1572872 | tf_op jit(solution)/shard_map/ppermute | solution.py:375
  116.7 33.8 %collective-permute-start.18 = (bf16[512,512]{1,0:T(8,128)(2,1)S(1)}, bf16[512,512]{1,0:T(8,128)(2,1)S(1)}, u32[]{:S(2)}, u32[]{:S(2)}) collective-permute-start(bf16[512,512]{1,0:T(8,128)(2,1)S(1)} %regroup.3.refs_8_.refs_1_.refs_3_), channel_id=1, source_target_pairs={{4,8},{8,4},{5,9},{9,5},{6,10},{10,6},{7,11},{11,7},{20,24},{24,20... | collective-permute-start | bytes 1572872 | tf_op jit(solution)/shard_map/ppermute | solution.py:375
  117.4 34.4 %collective-permute-start.13 = (bf16[512,512]{1,0:T(8,128)(2,1)S(1)}, bf16[512,512]{1,0:T(8,128)(2,1)S(1)}, u32[]{:S(2)}, u32[]{:S(2)}) collective-permute-start(bf16[512,512]{1,0:T(8,128)(2,1)S(1)} %collective-permute-done.12.refs_0_), channel_id=1, source_target_pairs={{4,0},{8,12},{5,1},{9,13},{6,2},{10,14},{7,3},{11,15},{20,16},{24,... | collective-permute-start | bytes 1572872 | tf_op jit(solution)/shard_map/ppermute | solution.py:375
  149.8 20.5 %collective-permute-start.17 = (bf16[512,512]{1,0:T(8,128)(2,1)S(1)}, bf16[512,512]{1,0:T(8,128)(2,1)S(1)}, u32[]{:S(2)}, u32[]{:S(2)}) collective-permute-start(bf16[512,512]{1,0:T(8,128)(2,1)S(1)} %collective-permute-done.16.refs_0_.refs_2_), channel_id=1, source_target_pairs={{4,8},{8,4},{5,9},{9,5},{6,10},{10,6},{7,11},{11,7},{20,24},{24,20... | collective-permute-start | bytes 1572872 | tf_op jit(solution)/shard_map/ppermute | solution.py:375
  150.5 34.3 %collective-permute-start.20 = (bf16[512,512]{1,0:T(8,128)(2,1)S(1)}, bf16[512,512]{1,0:T(8,128)(2,1)S(1)}, u32[]{:S(2)}, u32[]{:S(2)}) collective-permute-start(bf16[512,512]{1,0:T(8,128)(2,1)S(1)} %collective-permute-done.18.refs_1_), channel_id=1, source_target_pairs={{4,0},{8,12},{5,1},{9,13},{6,2},{10,14},{7,3},{11,15},{20,16},{24,... | collective-permute-start | bytes 1572872 | tf_op jit(solution)/shard_map/ppermute | solution.py:375
  163.5 39.5 %collective-permute-start.23 = (bf16[2,528,512]{2,1,0:T(8,128)(2,1)S(1)}, bf16[2,528,512]{2,1,0:T(8,128)(2,1)S(1)}, u32[]{:S(2)}, u32[]{:S(2)}) collective-permute-start(bf16[2,528,512]{2,1,0:T(8,128)(2,1)S(1)} %attend.8.refs_2_.refs_0_), channel_id=1, source_target_pairs={{0,4},{12,8},{1,5},{13,9},{2,6},{14,10},{3,7},{15,11},{16,20},{28,... | collective-permute-start | bytes 3244040 | tf_op jit(solution)/shard_map/ppermute | solution.py:375
  171.7 31.3 %collective-permute-start.15 = (bf16[2,528,512]{2,1,0:T(8,128)(2,1)S(1)}, bf16[2,528,512]{2,1,0:T(8,128)(2,1)S(1)}, u32[]{:S(2)}, u32[]{:S(2)}) collective-permute-start(bf16[2,528,512]{2,1,0:T(8,128)(2,1)S(1)} %merge.6.refs_8_), channel_id=1, source_target_pairs={{4,8},{8,4},{5,9},{9,5},{6,10},{10,6},{7,11},{11,7},{20,24},{24,20... | collective-permute-start | bytes 3244040 | tf_op jit(solution)/shard_map/ppermute | solution.py:375
  195.6 27.3 %collective-permute-start.22 = (bf16[2,528,512]{2,1,0:T(8,128)(2,1)S(1)}, bf16[2,528,512]{2,1,0:T(8,128)(2,1)S(1)}, u32[]{:S(2)}, u32[]{:S(2)}) collective-permute-start(bf16[2,528,512]{2,1,0:T(8,128)(2,1)S(1)} %attend.10.refs_2_.refs_0_), channel_id=1, source_target_pairs={{0,4},{12,8},{1,5},{13,9},{2,6},{14,10},{3,7},{15,11},{16,20},{28,... | collective-permute-start | bytes 3244040 | tf_op jit(solution)/shard_map/ppermute | solution.py:375
  203.1 46.8 %collective-permute-start.25 = (bf16[2,528,512]{2,1,0:T(8,128)(2,1)S(1)}, bf16[2,528,512]{2,1,0:T(8,128)(2,1)S(1)}, u32[]{:S(2)}, u32[]{:S(2)}) collective-permute-start(bf16[2,528,512]{2,1,0:T(8,128)(2,1)S(1)} %merge.8.refs_8_), channel_id=1, source_target_pairs={{4,8},{8,4},{5,9},{9,5},{6,10},{10,6},{7,11},{11,7},{20,24},{24,20... | collective-permute-start | bytes 3244040 | tf_op jit(solution)/shard_map/ppermute | solution.py:375
  222.9 29.0 %collective-permute-start.27 = (bf16[2,528,512]{2,1,0:T(8,128)(2,1)S(1)}, bf16[2,528,512]{2,1,0:T(8,128)(2,1)S(1)}, u32[]{:S(2)}, u32[]{:S(2)}) collective-permute-start(bf16[2,528,512]{2,1,0:T(8,128)(2,1)S(1)} %merge.9.refs_5_), channel_id=1, source_target_pairs={{4,8},{8,4},{5,9},{9,5},{6,10},{10,6},{7,11},{11,7},{20,24},{24,20... | collective-permute-start | bytes 3244040 | tf_op jit(solution)/shard_map/ppermute | solution.py:375
  223.7 19.8 %collective-permute-start.9 = (bf16[1,528,512]{2,1,0:T(8,128)(2,1)S(1)}, bf16[1,528,512]{2,1,0:T(8,128)(2,1)S(1)}, u32[]{:S(2)}, u32[]{:S(2)}) collective-permute-start(bf16[1,528,512]{2,1,0:T(8,128)(2,1)S(1)} %slice.31), channel_id=1, source_target_pairs={{0,4},{12,8},{1,5},{13,9},{2,6},{14,10},{3,7},{15,11},{16,20},{28,... | collective-permute-start | bytes 1622024 | tf_op jit(solution)/shard_map/ppermute | solution.py:375
  231.1 17.6 %collective-permute-start.21 = (bf16[1,528,512]{2,1,0:T(8,128)(2,1)S(1)}, bf16[1,528,512]{2,1,0:T(8,128)(2,1)S(1)}, u32[]{:S(2)}, u32[]{:S(2)}) collective-permute-start(bf16[1,528,512]{2,1,0:T(8,128)(2,1)S(1)} %merge.7.refs_2_), channel_id=1, source_target_pairs={{4,0},{8,12},{5,1},{9,13},{6,2},{10,14},{7,3},{11,15},{20,16},{24,... | collective-permute-start | bytes 1622024 | tf_op jit(solution)/shard_map/ppermute | solution.py:375
  233.2 25.3 %collective-permute-start.24 = (bf16[1,528,512]{2,1,0:T(8,128)(2,1)}, bf16[1,528,512]{2,1,0:T(8,128)(2,1)}, u32[]{:S(2)}, u32[]{:S(2)}) collective-permute-start(bf16[1,528,512]{2,1,0:T(8,128)(2,1)} %slice.32), channel_id=1, source_target_pairs={{0,4},{12,8},{1,5},{13,9},{2,6},{14,10},{3,7},{15,11},{16,20},{28,... | collective-permute-start | bytes 1622024 | tf_op jit(solution)/shard_map/ppermute | solution.py:375
  243.5 20.6 %collective-permute-start.28 = (bf16[1,528,512]{2,1,0:T(8,128)(2,1)}, bf16[1,528,512]{2,1,0:T(8,128)(2,1)}, u32[]{:S(2)}, u32[]{:S(2)}) collective-permute-start(bf16[1,528,512]{2,1,0:T(8,128)(2,1)} %slice.33), channel_id=1, source_target_pairs={{0,4},{12,8},{1,5},{13,9},{2,6},{14,10},{3,7},{15,11},{16,20},{28,... | collective-permute-start | bytes 1622024 | tf_op jit(solution)/shard_map/ppermute | solution.py:375
  (23 other events, 248.0 us)

commit v6 on v5

--- a/solution.py
+++ b/solution.py
@@ -174,7 +174,7 @@
         ),
         compiler_params=pltpu.CompilerParams(vmem_limit_bytes=28 * MIB),
         cost_estimate=pl.CostEstimate(
-            flops=8 * blocks * rows * keys * DH * heads,
+            flops=16 * blocks * rows * keys * DH * heads,
             bytes_accessed=4 * blocks * rows * width + 4 * keys * width,
             transcendentals=blocks * rows * keys * heads,
         ),
@@ -380,14 +380,14 @@
         far = send(near, (1, 2), (2, 1))
         third_out = send(third, (1, 0), (2, 3))
         far_out = send(far, (1, 0), (2, 3))
-        return dict(own=span, near=near, sent=[[far, third], [far_out, third_out]], early=third, mid=third_out)
+        return dict(own=span, near=near, sent=[[far, third], [far_out, third_out]], early=third, end=far_out)
 
     def spread_cube(span):
         found = {0: span}
         for bit in reversed(bits):
             for d in list(found):
                 found[d ^ bit] = send(found[d], *[(i, i ^ bit) for i in range(n)])
-        return dict(found=found, early=found[n // 2], mid=found[n // 2])
+        return dict(found=found, early=found[n // 2], end=found[n - 1])
 
     bits = [1 << k for k in range((n - 1).bit_length())]
     line = n == 4
@@ -402,7 +402,7 @@
         found.append(spread(span))
         return span
 
-    span_k, span_v_t = joined(moved, group, run_spread(1, [first_span]))
+    span_k, span_v_t = joined(moved, group, run_spread(1, [found[0]["end"]]))
     context_values_t = context_values.T
     last = [span_k]
     outer = ((place == 0) | (place == n - 1)).astype(jnp.int32)

time: 291 us -> 278 us (0.955)
  waiting for transfers between devices: 102 us -> 88.3 us
  blocking collectives: 16.9 us -> 29.9 us
  starting transfers between devices: 71.6 us -> 61.7 us
    all_to_all x0 -> x1, blocking collectives: none -> 13 us  [to_heads(): lax.all_to_all(pieces, 'uly', split_axis=0, concat_axis=0, tiled=False)]
    ppermute x27, waiting for transfers between devices: 64.6 us -> 53.9 us  [send(): return lax.ppermute(x, 'blk', pairs)]
    all_to_all x1 -> x0, waiting for transfers between devices: 9.45 us -> none  [to_heads(): lax.all_to_all(pieces, 'uly', split_axis=0, concat_axis=0, tiled=False)]
    ppermute x3, waiting for transfers between devices: 27.9 us -> 34.5 us  [to_peers(): lax.ppermute(p, 'uly', [(i, i ^ k) for i in range(peers)])]
    all_to_all x1 -> x0, starting transfers between devices: 4.24 us -> none  [to_heads(): lax.all_to_all(pieces, 'uly', split_axis=0, concat_axis=0, tiled=False)]
    ppermute x27, starting transfers between devices: 61.3 us -> 57.2 us  [send(): return lax.ppermute(x, 'blk', pairs)]
  transfers between devices with their start and end apart: 32 -> 31, of which waited for: 11 -> 10; matrix products, arithmetic and copies ran while one was open for 3% -> 3% of each run, Pallas kernels for 27% -> 28%
where the time goes in v6:
time: 278 us; the launch traced here: 277 us
  waiting for transfers between devices  88.3 us (32%)
  Pallas kernels  78.2 us (28%)
  starting transfers between devices  61.7 us (22%)
  blocking collectives  29.9 us (11%)
  local copies, waits for them, and re-layouts  16.8 us (6%)
    pallas_call x6, Pallas kernels, attend(): pl.pallas_call(functools.partial(attend_kernel, [[None] * len(c) for c in...  68.8 us
    ppermute x27, starting transfers between devices, send(): return lax.ppermute(x, 'blk', pairs)  57.2 us
    ppermute x27, waiting for transfers between devices, send(): return lax.ppermute(x, 'blk', pairs)  53.9 us
    ppermute x3, waiting for transfers between devices, to_peers(): lax.ppermute(p, 'uly', [(i, i ^ k) for i in range(peers)])  34.5 us
    all_to_all x1, blocking collectives, run_return(): lax.all_to_all(jnp.concatenate([backs[c] for c in those], axis=2), 'uly',...  16.9 us
    all_to_all x1, blocking collectives, to_heads(): lax.all_to_all(pieces, 'uly', split_axis=0, concat_axis=0, tiled=False)  13 us
    unnamed x31, local copies, waits for them, and re-layouts  12.2 us
    pallas_call x9, Pallas kernels, join_parts(): pl.pallas_call(functools.partial(join_kernel_of, [len(c) for c in choices...  6.04 us
  transfers between devices with their start and end apart: 31, of which 10 were waited for; matrix products, arithmetic and copies ran while one was open for 3% of the time, Pallas kernels for 28%

profile of v6, /device:TPU:0, one launch (start us, length us, event | category | flops | bytes accessed | tf_op | source)
XLA Modules:
  0.0 277.2 jit_solution(3184950568760152633)
XLA Ops:
  1.4 13.0 %all_to_all.15 = bf16[4,128,512]{2,1,0:T(8,128)(2,1)} all-to-all(bf16[4,128,512]{2,1,0:T(8,128)(2,1)S(1)} %pad_maximum_fusion.1), channel_id=1, replica_groups=mesh['cfg'=2,'blk'=4,'uly'=4] {'uly'}, dimensions={0} | all-to-all | bytes 1048576 | tf_op jit(solution)/shard_map/all_to_all | solution.py:368
  21.0 7.2 %collective-permute-done.refs_0_.refs_2_ = bf16[512,512]{1,0:T(8,128)(2,1)} collective-permute-done((bf16[512,512]{1,0:T(8,128)(2,1)}, bf16[512,512]{1,0:T(8,128)(2,1)}, u32[]{:S(2)}, u32[]{:S(2)}) %collective-permute-start) | collective-permute-done | bytes 524320 | tf_op jit(solution)/shard_map/ppermute | solution.py:375
  34.0 12.8 %collective-permute-done.2.refs_2_ = bf16[128,4096]{1,0:T(8,128)(2,1)S(1)} collective-permute-done((bf16[128,4096]{1,0:T(8,128)(2,1)}, bf16[128,4096]{1,0:T(8,128)(2,1)S(1)}, u32[]{:S(2)}, u32[]{:S(2)}) %collective-permute-start.2) | collective-permute-done | bytes 1048608 | tf_op jit(solution)/shard_map/ppermute | solution.py:372
  46.8 21.7 %collective-permute-done.3.refs_3_ = bf16[128,4096]{1,0:T(8,128)(2,1)S(1)} collective-permute-done((bf16[128,4096]{1,0:T(8,128)(2,1)}, bf16[128,4096]{1,0:T(8,128)(2,1)S(1)}, u32[]{:S(2)}, u32[]{:S(2)}) %collective-permute-start.3) | collective-permute-done | bytes 1048608 | tf_op jit(solution)/shard_map/ppermute | solution.py:372
  71.2 4.7 %copy.11 = bf16[1024,1536]{0,1:T(8,128)(2,1)} copy(bf16[1024,1536]{1,0:T(8,128)(2,1)} %param.10) | data formatting | bytes 6291456 | tf_op args[4]
  78.7 6.6 %collective-permute-done.11.refs_0_.refs_2_ = bf16[512,512]{1,0:T(8,128)(2,1)} collective-permute-done((bf16[512,512]{1,0:T(8,128)(2,1)}, bf16[512,512]{1,0:T(8,128)(2,1)}, u32[]{:S(2)}, u32[]{:S(2)}) %collective-permute-start.11) | collective-permute-done | bytes 524320 | tf_op jit(solution)/shard_map/ppermute | solution.py:375
  87.9 12.1 %attend.6.refs_5_.refs_0_ = bf16[2,528,512]{2,1,0:T(8,128)(2,1)S(1)} custom-call(s32[3]{0:T(128)S(1)} %pad_add_fusion.1.table_ref, s32[16,12]{1,0:T(8,128)S(1)} %fusion.kept_ref, bf16[512,512]{1,0:T(8,128)(2,1)} %collective-permute-done.4.refs_0_, bf16[512,512]{1,0:T(8,128)(2,1)} %collective-permute-done.7.refs_1_, ...), custom_call_target="tpu_custom_call" | custom-call | flops 12884901888 | bytes 5242880 | tf_op jit(solution)/shard_map/attend/pallas_call | solution.py:151
  100.1 6.6 %collective-permute-start.10 = (bf16[2,528,512]{2,1,0:T(8,128)(2,1)S(1)}, bf16[2,528,512]{2,1,0:T(8,128)(2,1)S(1)}, u32[]{:S(2)}, u32[]{:S(2)}) collective-permute-start(bf16[2,528,512]{2,1,0:T(8,128)(2,1)S(1)} %attend.6.refs_5_.refs_0_), channel_id=1, source_target_pairs={{0,4},{12,8},{1,5},{13,9},{2,6},{14,10},{3,7},{15,11},{16,20},{28,... | collective-permute-start | bytes 3244040 | tf_op jit(solution)/shard_map/ppermute | solution.py:375
  110.2 12.2 %attend.7.refs_8_.refs_0_.refs_3_ = bf16[2,528,512]{2,1,0:T(8,128)(2,1)S(1)} custom-call(s32[3]{0:T(128)S(1)} %pad_add_fusion.table_ref, s32[16,12]{1,0:T(8,128)S(1)} %fusion.kept_ref, bf16[512,512]{1,0:T(8,128)(2,1)} %collective-permute-done.refs_0_.refs_2_, bf16[512,512]{1,0:T(8,128)(2,1)} %bitcast.7.refs_12_.refs_1_.refs_3_, ...), custom_call_target="tpu_custom_call" | custom-call | flops 12884901888 | bytes 5242880 | tf_op jit(solution)/shard_map/attend/pallas_call | solution.py:151
  122.3 17.9 %collective-permute-done.16.refs_0_.refs_2_ = bf16[512,512]{1,0:T(8,128)(2,1)S(1)} collective-permute-done((bf16[512,512]{1,0:T(8,128)(2,1)S(1)}, bf16[512,512]{1,0:T(8,128)(2,1)S(1)}, u32[]{:S(2)}, u32[]{:S(2)}) %collective-permute-start.16) | collective-permute-done | bytes 524320 | tf_op jit(solution)/shard_map/ppermute | solution.py:375
  142.2 10.8 %attend.8.refs_2_.refs_0_ = bf16[2,528,512]{2,1,0:T(8,128)(2,1)S(1)} custom-call(s32[3]{0:T(128)S(1)} %pad_add_fusion.1.table_ref, s32[16,12]{1,0:T(8,128)S(1)} %fusion.kept_ref, bf16[512,512]{1,0:T(8,128)(2,1)S(1)} %collective-permute-done.12.refs_0_, bf16[512,512]{1,0:T(8,128)(2,1)S(1)} %collective-permute-done.6.refs_4_.refs_1_, ...), custom_call_target="tpu_custom_call" | custom-call | flops 12884901888 | bytes 5242880 | tf_op jit(solution)/shard_map/attend/pallas_call | solution.py:151
  153.0 6.0 %collective-permute-start.23 = (bf16[2,528,512]{2,1,0:T(8,128)(2,1)S(1)}, bf16[2,528,512]{2,1,0:T(8,128)(2,1)S(1)}, u32[]{:S(2)}, u32[]{:S(2)}) collective-permute-start(bf16[2,528,512]{2,1,0:T(8,128)(2,1)S(1)} %attend.8.refs_2_.refs_0_), channel_id=1, source_target_pairs={{0,4},{12,8},{1,5},{13,9},{2,6},{14,10},{3,7},{15,11},{16,20},{28,... | collective-permute-start | bytes 3244040 | tf_op jit(solution)/shard_map/ppermute | solution.py:375
  161.3 12.3 %attend.9.refs_8_.refs_0_.refs_3_ = bf16[2,528,512]{2,1,0:T(8,128)(2,1)S(1)} custom-call(s32[3]{0:T(128)S(1)} %pad_add_fusion.table_ref, s32[16,12]{1,0:T(8,128)S(1)} %fusion.kept_ref, bf16[512,512]{1,0:T(8,128)(2,1)} %collective-permute-done.11.refs_0_.refs_2_, bf16[512,512]{1,0:T(8,128)(2,1)} %regroup.2.refs_4_.refs_1_.refs_3_, ...), custom_call_target="tpu_custom_call" | custom-call | flops 12884901888 | bytes 5242880 | tf_op jit(solution)/shard_map/attend/pallas_call | solution.py:151
  173.7 10.8 %attend.10.refs_2_.refs_0_ = bf16[2,528,512]{2,1,0:T(8,128)(2,1)S(1)} custom-call(s32[3]{0:T(128)S(1)} %pad_add_fusion.1.table_ref, s32[16,12]{1,0:T(8,128)S(1)} %fusion.kept_ref, bf16[512,512]{1,0:T(8,128)(2,1)S(1)} %collective-permute-done.17.refs_0_, bf16[512,512]{1,0:T(8,128)(2,1)S(1)} %collective-permute-done.18.refs_1_, ...), custom_call_target="tpu_custom_call" | custom-call | flops 12884901888 | bytes 5242880 | tf_op jit(solution)/shard_map/attend/pallas_call | solution.py:151
  184.4 4.8 %collective-permute-start.22 = (bf16[2,528,512]{2,1,0:T(8,128)(2,1)S(1)}, bf16[2,528,512]{2,1,0:T(8,128)(2,1)S(1)}, u32[]{:S(2)}, u32[]{:S(2)}) collective-permute-start(bf16[2,528,512]{2,1,0:T(8,128)(2,1)S(1)} %attend.10.refs_2_.refs_0_), channel_id=1, source_target_pairs={{0,4},{12,8},{1,5},{13,9},{2,6},{14,10},{3,7},{15,11},{16,20},{28,... | collective-permute-start | bytes 3244040 | tf_op jit(solution)/shard_map/ppermute | solution.py:375
  190.1 10.8 %attend.11.refs_2_.refs_0_.refs_3_ = bf16[2,528,512]{2,1,0:T(8,128)(2,1)S(1)} custom-call(s32[3]{0:T(128)S(1)} %pad_add_fusion.table_ref, s32[16,12]{1,0:T(8,128)S(1)} %fusion.kept_ref, bf16[512,512]{1,0:T(8,128)(2,1)S(1)} %collective-permute-done.16.refs_0_.refs_2_, bf16[512,512]{1,0:T(8,128)(2,1)S(1)} %regroup.3.refs_8_.refs_1_.refs_3_, ...), custom_call_target="tpu_custom_call" | custom-call | flops 12884901888 | bytes 5242880 | tf_op jit(solution)/shard_map/attend/pallas_call | solution.py:151
  200.9 9.2 %collective-permute-done.22.refs_1_ = bf16[2,528,512]{2,1,0:T(8,128)(2,1)S(1)} collective-permute-done((bf16[2,528,512]{2,1,0:T(8,128)(2,1)S(1)}, bf16[2,528,512]{2,1,0:T(8,128)(2,1)S(1)}, u32[]{:S(2)}, u32[]{:S(2)}) %collective-permute-start.22) | collective-permute-done | bytes 1081376 | tf_op jit(solution)/shard_map/ppermute | solution.py:375
  210.9 7.5 %collective-permute-start.9 = (bf16[1,528,512]{2,1,0:T(8,128)(2,1)S(1)}, bf16[1,528,512]{2,1,0:T(8,128)(2,1)S(1)}, u32[]{:S(2)}, u32[]{:S(2)}) collective-permute-start(bf16[1,528,512]{2,1,0:T(8,128)(2,1)S(1)} %slice.31), channel_id=1, source_target_pairs={{0,4},{12,8},{1,5},{13,9},{2,6},{14,10},{3,7},{15,11},{16,20},{28,... | collective-permute-start | bytes 1622024 | tf_op jit(solution)/shard_map/ppermute | solution.py:375
  220.5 5.4 %collective-permute-start.24 = (bf16[1,528,512]{2,1,0:T(8,128)(2,1)}, bf16[1,528,512]{2,1,0:T(8,128)(2,1)}, u32[]{:S(2)}, u32[]{:S(2)}) collective-permute-start(bf16[1,528,512]{2,1,0:T(8,128)(2,1)} %slice.32), channel_id=1, source_target_pairs={{0,4},{12,8},{1,5},{13,9},{2,6},{14,10},{3,7},{15,11},{16,20},{28,... | collective-permute-start | bytes 1622024 | tf_op jit(solution)/shard_map/ppermute | solution.py:375
  226.7 4.3 %collective-permute-done.9.refs_1_ = bf16[1,528,512]{2,1,0:T(8,128)(2,1)S(1)} collective-permute-done((bf16[1,528,512]{2,1,0:T(8,128)(2,1)S(1)}, bf16[1,528,512]{2,1,0:T(8,128)(2,1)S(1)}, u32[]{:S(2)}, u32[]{:S(2)}) %collective-permute-start.9) | collective-permute-done | bytes 540704 | tf_op jit(solution)/shard_map/ppermute | solution.py:375
  231.0 5.2 %collective-permute-start.28 = (bf16[1,528,512]{2,1,0:T(8,128)(2,1)}, bf16[1,528,512]{2,1,0:T(8,128)(2,1)}, u32[]{:S(2)}, u32[]{:S(2)}) collective-permute-start(bf16[1,528,512]{2,1,0:T(8,128)(2,1)} %slice.33), channel_id=1, source_target_pairs={{0,4},{12,8},{1,5},{13,9},{2,6},{14,10},{3,7},{15,11},{16,20},{28,... | collective-permute-start | bytes 1622024 | tf_op jit(solution)/shard_map/ppermute | solution.py:375
  246.1 4.3 %collective-permute-done.26.refs_4_ = bf16[1,528,512]{2,1,0:T(8,128)(2,1)} collective-permute-done((bf16[1,528,512]{2,1,0:T(8,128)(2,1)}, bf16[1,528,512]{2,1,0:T(8,128)(2,1)}, u32[]{:S(2)}, u32[]{:S(2)}) %collective-permute-start.26) | collective-permute-done | bytes 540704 | tf_op jit(solution)/shard_map/ppermute | solution.py:375
  252.0 4.2 %collective-permute-done.29.refs_4_ = bf16[1,528,512]{2,1,0:T(8,128)(2,1)} collective-permute-done((bf16[1,528,512]{2,1,0:T(8,128)(2,1)}, bf16[1,528,512]{2,1,0:T(8,128)(2,1)}, u32[]{:S(2)}, u32[]{:S(2)}) %collective-permute-start.29) | collective-permute-done | bytes 540704 | tf_op jit(solution)/shard_map/ppermute | solution.py:375
  257.9 16.9 %all_to_all.16 = bf16[4,128,1024]{2,1,0:T(8,128)(2,1)S(1)} all-to-all(bf16[4,128,1024]{2,1,0:T(8,128)(2,1)S(1)} %pad_maximum_fusion), channel_id=1, replica_groups=mesh['cfg'=2,'blk'=4,'uly'=4] {'uly'}, dimensions={0} | all-to-all | bytes 2097152 | tf_op jit(solution)/shard_map/all_to_all | solution.py:428
  (108 shorter events, 49.5 us)
Async XLA Ops:
  20.6 26.2 %collective-permute-start.2 = (bf16[128,4096]{1,0:T(8,128)(2,1)}, bf16[128,4096]{1,0:T(8,128)(2,1)S(1)}, u32[]{:S(2)}, u32[]{:S(2)}) collective-permute-start(bf16[128,4096]{1,0:T(8,128)(2,1)} %get-tuple-element.13), channel_id=1, source_target_pairs={{0,2},{1,3},{2,0},{3,1},{4,6},{5,7},{6,4},{7,5},{8,10},{9,11},{10,... | collective-permute-start | bytes 3145736 | tf_op jit(solution)/shard_map/ppermute | solution.py:372
  29.7 38.8 %collective-permute-start.3 = (bf16[128,4096]{1,0:T(8,128)(2,1)}, bf16[128,4096]{1,0:T(8,128)(2,1)S(1)}, u32[]{:S(2)}, u32[]{:S(2)}) collective-permute-start(bf16[128,4096]{1,0:T(8,128)(2,1)} %get-tuple-element.14), channel_id=1, source_target_pairs={{0,3},{1,2},{2,1},{3,0},{4,7},{5,6},{6,5},{7,4},{8,11},{9,10},{10,... | collective-permute-start | bytes 3145736 | tf_op jit(solution)/shard_map/ppermute | solution.py:372
  31.1 37.4 %collective-permute-start.5 = (bf16[512,512]{1,0:T(8,128)(2,1)}, bf16[512,512]{1,0:T(8,128)(2,1)}, u32[]{:S(2)}, u32[]{:S(2)}) collective-permute-start(bf16[512,512]{1,0:T(8,128)(2,1)} %collective-permute-done.4.refs_0_), channel_id=1, source_target_pairs={{4,0},{8,12},{5,1},{9,13},{6,2},{10,14},{7,3},{11,15},{20,16},{24,... | collective-permute-start | bytes 1572872 | tf_op jit(solution)/shard_map/ppermute | solution.py:375
  32.7 53.3 %collective-permute-start.8 = (bf16[512,512]{1,0:T(8,128)(2,1)}, bf16[512,512]{1,0:T(8,128)(2,1)}, u32[]{:S(2)}, u32[]{:S(2)}) collective-permute-start(bf16[512,512]{1,0:T(8,128)(2,1)} %collective-permute-done.7.refs_1_), channel_id=1, source_target_pairs={{4,0},{8,12},{5,1},{9,13},{6,2},{10,14},{7,3},{11,15},{20,16},{24,... | collective-permute-start | bytes 1572872 | tf_op jit(solution)/shard_map/ppermute | solution.py:375
  76.2 30.5 %collective-permute-start.6 = (bf16[512,512]{1,0:T(8,128)(2,1)}, bf16[512,512]{1,0:T(8,128)(2,1)S(1)}, u32[]{:S(2)}, u32[]{:S(2)}) collective-permute-start(bf16[512,512]{1,0:T(8,128)(2,1)} %regroup.2.refs_4_.refs_1_.refs_3_), channel_id=1, source_target_pairs={{4,8},{8,4},{5,9},{9,5},{6,10},{10,6},{7,11},{11,7},{20,24},{24,20... | collective-permute-start | bytes 1572872 | tf_op jit(solution)/shard_map/ppermute | solution.py:375
  85.3 23.6 %collective-permute-start.12 = (bf16[512,512]{1,0:T(8,128)(2,1)}, bf16[512,512]{1,0:T(8,128)(2,1)S(1)}, u32[]{:S(2)}, u32[]{:S(2)}) collective-permute-start(bf16[512,512]{1,0:T(8,128)(2,1)} %collective-permute-done.11.refs_0_.refs_2_), channel_id=1, source_target_pairs={{4,8},{8,4},{5,9},{9,5},{6,10},{10,6},{7,11},{11,7},{20,24},{24,20... | collective-permute-start | bytes 1572872 | tf_op jit(solution)/shard_map/ppermute | solution.py:375
  100.1 58.9 %collective-permute-start.10 = (bf16[2,528,512]{2,1,0:T(8,128)(2,1)S(1)}, bf16[2,528,512]{2,1,0:T(8,128)(2,1)S(1)}, u32[]{:S(2)}, u32[]{:S(2)}) collective-permute-start(bf16[2,528,512]{2,1,0:T(8,128)(2,1)S(1)} %attend.6.refs_5_.refs_0_), channel_id=1, source_target_pairs={{0,4},{12,8},{1,5},{13,9},{2,6},{14,10},{3,7},{15,11},{16,20},{28,... | collective-permute-start | bytes 3244040 | tf_op jit(solution)/shard_map/ppermute | solution.py:375
  106.8 33.5 %collective-permute-start.16 = (bf16[512,512]{1,0:T(8,128)(2,1)S(1)}, bf16[512,512]{1,0:T(8,128)(2,1)S(1)}, u32[]{:S(2)}, u32[]{:S(2)}) collective-permute-start(bf16[512,512]{1,0:T(8,128)(2,1)S(1)} %regroup.3.refs_8_.refs_1_.refs_3_), channel_id=1, source_target_pairs={{0,4},{4,0},{8,12},{12,8},{1,5},{5,1},{9,13},{13,9},{2,6},{6,2},{1... | collective-permute-start | bytes 1572872 | tf_op jit(solution)/shard_map/ppermute | solution.py:375
  106.8 34.1 %collective-permute-start.18 = (bf16[512,512]{1,0:T(8,128)(2,1)S(1)}, bf16[512,512]{1,0:T(8,128)(2,1)S(1)}, u32[]{:S(2)}, u32[]{:S(2)}) collective-permute-start(bf16[512,512]{1,0:T(8,128)(2,1)S(1)} %regroup.3.refs_8_.refs_1_.refs_3_), channel_id=1, source_target_pairs={{4,8},{8,4},{5,9},{9,5},{6,10},{10,6},{7,11},{11,7},{20,24},{24,20... | collective-permute-start | bytes 1572872 | tf_op jit(solution)/shard_map/ppermute | solution.py:375
  107.5 34.7 %collective-permute-start.14 = (bf16[512,512]{1,0:T(8,128)(2,1)S(1)}, bf16[512,512]{1,0:T(8,128)(2,1)S(1)}, u32[]{:S(2)}, u32[]{:S(2)}) collective-permute-start(bf16[512,512]{1,0:T(8,128)(2,1)S(1)} %collective-permute-done.6.refs_4_.refs_1_), channel_id=1, source_target_pairs={{4,0},{8,12},{5,1},{9,13},{6,2},{10,14},{7,3},{11,15},{20,16},{24,... | collective-permute-start | bytes 1572872 | tf_op jit(solution)/shard_map/ppermute | solution.py:375
  108.9 33.4 %collective-permute-start.13 = (bf16[512,512]{1,0:T(8,128)(2,1)S(1)}, bf16[512,512]{1,0:T(8,128)(2,1)S(1)}, u32[]{:S(2)}, u32[]{:S(2)}) collective-permute-start(bf16[512,512]{1,0:T(8,128)(2,1)S(1)} %collective-permute-done.12.refs_0_), channel_id=1, source_target_pairs={{4,0},{8,12},{5,1},{9,13},{6,2},{10,14},{7,3},{11,15},{20,16},{24,... | collective-permute-start | bytes 1572872 | tf_op jit(solution)/shard_map/ppermute | solution.py:375
  140.2 19.6 %collective-permute-start.17 = (bf16[512,512]{1,0:T(8,128)(2,1)S(1)}, bf16[512,512]{1,0:T(8,128)(2,1)S(1)}, u32[]{:S(2)}, u32[]{:S(2)}) collective-permute-start(bf16[512,512]{1,0:T(8,128)(2,1)S(1)} %collective-permute-done.16.refs_0_.refs_2_), channel_id=1, source_target_pairs={{4,8},{8,4},{5,9},{9,5},{6,10},{10,6},{7,11},{11,7},{20,24},{24,20... | collective-permute-start | bytes 1572872 | tf_op jit(solution)/shard_map/ppermute | solution.py:375
  140.9 32.7 %collective-permute-start.20 = (bf16[512,512]{1,0:T(8,128)(2,1)S(1)}, bf16[512,512]{1,0:T(8,128)(2,1)S(1)}, u32[]{:S(2)}, u32[]{:S(2)}) collective-permute-start(bf16[512,512]{1,0:T(8,128)(2,1)S(1)} %collective-permute-done.18.refs_1_), channel_id=1, source_target_pairs={{4,0},{8,12},{5,1},{9,13},{6,2},{10,14},{7,3},{11,15},{20,16},{24,... | collective-permute-start | bytes 1572872 | tf_op jit(solution)/shard_map/ppermute | solution.py:375
  153.0 36.3 %collective-permute-start.23 = (bf16[2,528,512]{2,1,0:T(8,128)(2,1)S(1)}, bf16[2,528,512]{2,1,0:T(8,128)(2,1)S(1)}, u32[]{:S(2)}, u32[]{:S(2)}) collective-permute-start(bf16[2,528,512]{2,1,0:T(8,128)(2,1)S(1)} %attend.8.refs_2_.refs_0_), channel_id=1, source_target_pairs={{0,4},{12,8},{1,5},{13,9},{2,6},{14,10},{3,7},{15,11},{16,20},{28,... | collective-permute-start | bytes 3244040 | tf_op jit(solution)/shard_map/ppermute | solution.py:375
  159.1 30.2 %collective-permute-start.15 = (bf16[2,528,512]{2,1,0:T(8,128)(2,1)S(1)}, bf16[2,528,512]{2,1,0:T(8,128)(2,1)S(1)}, u32[]{:S(2)}, u32[]{:S(2)}) collective-permute-start(bf16[2,528,512]{2,1,0:T(8,128)(2,1)S(1)} %merge.6.refs_8_), channel_id=1, source_target_pairs={{4,8},{8,4},{5,9},{9,5},{6,10},{10,6},{7,11},{11,7},{20,24},{24,20... | collective-permute-start | bytes 3244040 | tf_op jit(solution)/shard_map/ppermute | solution.py:375
  184.4 25.6 %collective-permute-start.22 = (bf16[2,528,512]{2,1,0:T(8,128)(2,1)S(1)}, bf16[2,528,512]{2,1,0:T(8,128)(2,1)S(1)}, u32[]{:S(2)}, u32[]{:S(2)}) collective-permute-start(bf16[2,528,512]{2,1,0:T(8,128)(2,1)S(1)} %attend.10.refs_2_.refs_0_), channel_id=1, source_target_pairs={{0,4},{12,8},{1,5},{13,9},{2,6},{14,10},{3,7},{15,11},{16,20},{28,... | collective-permute-start | bytes 3244040 | tf_op jit(solution)/shard_map/ppermute | solution.py:375
  189.4 48.0 %collective-permute-start.25 = (bf16[2,528,512]{2,1,0:T(8,128)(2,1)S(1)}, bf16[2,528,512]{2,1,0:T(8,128)(2,1)S(1)}, u32[]{:S(2)}, u32[]{:S(2)}) collective-permute-start(bf16[2,528,512]{2,1,0:T(8,128)(2,1)S(1)} %merge.8.refs_8_), channel_id=1, source_target_pairs={{4,8},{8,4},{5,9},{9,5},{6,10},{10,6},{7,11},{11,7},{20,24},{24,20... | collective-permute-start | bytes 3244040 | tf_op jit(solution)/shard_map/ppermute | solution.py:375
  210.1 29.4 %collective-permute-start.27 = (bf16[2,528,512]{2,1,0:T(8,128)(2,1)S(1)}, bf16[2,528,512]{2,1,0:T(8,128)(2,1)S(1)}, u32[]{:S(2)}, u32[]{:S(2)}) collective-permute-start(bf16[2,528,512]{2,1,0:T(8,128)(2,1)S(1)} %merge.9.refs_5_), channel_id=1, source_target_pairs={{4,8},{8,4},{5,9},{9,5},{6,10},{10,6},{7,11},{11,7},{20,24},{24,20... | collective-permute-start | bytes 3244040 | tf_op jit(solution)/shard_map/ppermute | solution.py:375
  210.9 20.2 %collective-permute-start.9 = (bf16[1,528,512]{2,1,0:T(8,128)(2,1)S(1)}, bf16[1,528,512]{2,1,0:T(8,128)(2,1)S(1)}, u32[]{:S(2)}, u32[]{:S(2)}) collective-permute-start(bf16[1,528,512]{2,1,0:T(8,128)(2,1)S(1)} %slice.31), channel_id=1, source_target_pairs={{0,4},{12,8},{1,5},{13,9},{2,6},{14,10},{3,7},{15,11},{16,20},{28,... | collective-permute-start | bytes 1622024 | tf_op jit(solution)/shard_map/ppermute | solution.py:375
  218.4 17.9 %collective-permute-start.21 = (bf16[1,528,512]{2,1,0:T(8,128)(2,1)S(1)}, bf16[1,528,512]{2,1,0:T(8,128)(2,1)S(1)}, u32[]{:S(2)}, u32[]{:S(2)}) collective-permute-start(bf16[1,528,512]{2,1,0:T(8,128)(2,1)S(1)} %merge.7.refs_2_), channel_id=1, source_target_pairs={{4,0},{8,12},{5,1},{9,13},{6,2},{10,14},{7,3},{11,15},{20,16},{24,... | collective-permute-start | bytes 1622024 | tf_op jit(solution)/shard_map/ppermute | solution.py:375
  220.5 25.6 %collective-permute-start.24 = (bf16[1,528,512]{2,1,0:T(8,128)(2,1)}, bf16[1,528,512]{2,1,0:T(8,128)(2,1)}, u32[]{:S(2)}, u32[]{:S(2)}) collective-permute-start(bf16[1,528,512]{2,1,0:T(8,128)(2,1)} %slice.32), channel_id=1, source_target_pairs={{0,4},{12,8},{1,5},{13,9},{2,6},{14,10},{3,7},{15,11},{16,20},{28,... | collective-permute-start | bytes 1622024 | tf_op jit(solution)/shard_map/ppermute | solution.py:375
  231.0 20.9 %collective-permute-start.28 = (bf16[1,528,512]{2,1,0:T(8,128)(2,1)}, bf16[1,528,512]{2,1,0:T(8,128)(2,1)}, u32[]{:S(2)}, u32[]{:S(2)}) collective-permute-start(bf16[1,528,512]{2,1,0:T(8,128)(2,1)} %slice.33), channel_id=1, source_target_pairs={{0,4},{12,8},{1,5},{13,9},{2,6},{14,10},{3,7},{15,11},{16,20},{28,... | collective-permute-start | bytes 1622024 | tf_op jit(solution)/shard_map/ppermute | solution.py:375
  240.6 15.5 %collective-permute-start.29 = (bf16[1,528,512]{2,1,0:T(8,128)(2,1)}, bf16[1,528,512]{2,1,0:T(8,128)(2,1)}, u32[]{:S(2)}, u32[]{:S(2)}) collective-permute-start(bf16[1,528,512]{2,1,0:T(8,128)(2,1)} %merge.11.refs_5_), channel_id=1, source_target_pairs={{4,0},{8,12},{5,1},{9,13},{6,2},{10,14},{7,3},{11,15},{20,16},{24,... | collective-permute-start | bytes 1622024 | tf_op jit(solution)/shard_map/ppermute | solution.py:375
  241.9 16.0 %all-to-all-start.1 = ((bf16[4,128,512]{2,1,0:T(8,128)(2,1)}), bf16[4,128,512]{2,1,0:T(8,128)(2,1)}, u32[]{:S(2)}, u32[]{:S(2)}) async-start(bf16[4,128,512]{2,1,0:T(8,128)(2,1)} %bitcast.12), calls=%async_computation.1 | async-start | bytes 1048576 | tf_op jit(solution)/shard_map/all_to_all | solution.py:428
  (22 other events, 202.0 us)

commit v7 on v4

--- a/solution.py
+++ b/solution.py
@@ -423,8 +423,15 @@
         return last[0]
 
     def run_back(c, choices):
-        done = run_join(c, choices, True).reshape(peers, own_rows, widths[c])
-        backs[c] = lax.all_to_all(done, "uly", split_axis=0, concat_axis=0, tiled=False)
+        backs[c] = run_join(c, choices, True).reshape(peers, own_rows, widths[c])
+
+    def run_return(*those):
+        joint = jnp.concatenate([backs[c] for c in those], axis=2)
+        joint = lax.all_to_all(joint, "uly", split_axis=0, concat_axis=0, tiled=False)
+        at = 0
+        for c in those:
+            backs[c] = joint[:, :, at : at + widths[c]]
+            at += widths[c]
 
     state = [dict() for _ in range(count)]
 
@@ -448,6 +455,23 @@
     def run_finish(c):
         inner = [(state[c]["kept"], 1), (state[c]["edge_near"], 0), (state[c]["cross"], 1)]
         run_back(c, [inner, [(state[c]["kept"], 1), (state[c]["outward"], 0)]])
+
+    def run_halves(c):
+        inner, outer_ones = found[c]["sent"]
+        near, own = found[c]["near"], found[c]["own"]
+        mine = run_attend(c, [[near, inner[1]], [near, outer_ones[0]]], [place ^ 1, place ^ 3])
+        state[c].update(swap=send(mine, (0, 1), (1, 0), (2, 3), (3, 2)), rest=[[own, inner[0]], [own, outer_ones[1]]])
+
+    def run_halves_kept(c):
+        state[c]["kept"] = run_attend(c, state[c]["rest"], [place, place ^ 2])
+
+    def run_halves_join(c):
+        pair = [(state[c]["kept"], 1), (state[c]["swap"], 1)]
+        state[c]["across"] = send(run_join(c, [pair, pair]), (0, 2), (2, 0), (1, 3), (3, 1))
+
+    def run_halves_finish(c):
+        three = [(state[c]["kept"], 0), (state[c]["swap"], 0), (state[c]["across"], 0)]
+        run_back(c, [three, three])
 
     if line:
         run_sent(0)
@@ -455,16 +479,17 @@
         run_sent(1)
         run_cross(0)
         run_kept(1)
-        run_sent(2)
+        run_halves(2)
         run_outward(0)
         run_cross(1)
-        run_kept(2)
-        run_cross(2)
+        run_halves_kept(2)
+        run_halves_join(2)
+        run_outward(1)
         run_finish(0)
-        run_outward(1)
-        run_outward(2)
+        run_return(0)
         run_finish(1)
-        run_finish(2)
+        run_halves_finish(2)
+        run_return(1, 2)
     else:
         for c in range(count):
             parts = {d: [] for d in range(n)}
@@ -482,6 +507,7 @@
                     joint = run_join(c, [parts[d], parts[d]])
                     parts[d ^ bit].append((send(joint, *[(i, i ^ bit) for i in range(n)]), 0))
             run_back(c, [parts[0], parts[0]])
+            run_return(c)
 
     in_order = [backs[c] for c in sorted(range(count), key=lambda c: PIECES[c][0])]
     together = jnp.concatenate(in_order, axis=2)

time: 269 us -> 256 us (0.952)
  starting transfers between devices: 88 us -> 76.6 us
  waiting for transfers between devices: 45.5 us -> 36.4 us
  Pallas kernels: 77.1 us -> 83.5 us
  local copies, waits for them, and re-layouts: 19.4 us -> 25.5 us
  blocking collectives: 35.4 us -> 29.8 us
    ppermute x27 -> x25, waiting for transfers between devices: 37.1 us -> 24.4 us  [send(): return lax.ppermute(x, 'blk', pairs)]
    ppermute x27 -> x25, starting transfers between devices: 79.9 us -> 68.6 us  [send(): return lax.ppermute(x, 'blk', pairs)]
    unnamed x55 -> x83, local copies, waits for them, and re-layouts: 14.8 us -> 21.7 us
    all_to_all x2 -> x1, blocking collectives: 22.5 us -> 16.9 us  [run_return(): lax.all_to_all(joint, 'uly', split_axis=0, concat_axis=0, tiled=False)]
    ppermute x6, waiting for transfers between devices: 8.39 us -> 12 us  [to_peers(): lax.ppermute(p, 'uly', [(i, i ^ k) for i in range(peers)])]
    pallas_call x9 -> x8, Pallas kernels: 4.52 us -> 7.95 us  [join_parts(): pl.pallas_call(functools.partial(join_kernel_of, [len(c) for c in choices...]
  transfers between devices with their start and end apart: 34 -> 32, of which waited for: 9 -> 7; matrix products, arithmetic and copies ran while one was open for 2% -> 2% of each run, Pallas kernels for 29% -> 33%
where the time goes in v7:
time: 256 us; the launch traced here: 254 us
  Pallas kernels  83.5 us (33%)
  starting transfers between devices  76.6 us (30%)
  waiting for transfers between devices  36.4 us (14%)
  blocking collectives  29.8 us (12%)
  local copies, waits for them, and re-layouts  25.5 us (10%)
    pallas_call x6, Pallas kernels, attend(): pl.pallas_call(functools.partial(attend_kernel, [[None] * len(c) for c in...  71 us
    ppermute x25, starting transfers between devices, send(): return lax.ppermute(x, 'blk', pairs)  68.6 us
    ppermute x25, waiting for transfers between devices, send(): return lax.ppermute(x, 'blk', pairs)  24.4 us
    unnamed x83, local copies, waits for them, and re-layouts  21.7 us
    all_to_all x1, blocking collectives, run_return(): lax.all_to_all(joint, 'uly', split_axis=0, concat_axis=0, tiled=False)  16.9 us
    all_to_all x1, blocking collectives, to_heads(): lax.all_to_all(pieces, 'uly', split_axis=0, concat_axis=0, tiled=False)  12.9 us
    ppermute x6, waiting for transfers between devices, to_peers(): lax.ppermute(p, 'uly', [(i, i ^ k) for i in range(peers)])  12 us
    pallas_call x8, Pallas kernels, join_parts(): pl.pallas_call(functools.partial(join_kernel_of, [len(c) for c in choices...  7.95 us
  transfers between devices with their start and end apart: 32, of which 7 were waited for; matrix products, arithmetic and copies ran while one was open for 2% of the time, Pallas kernels for 33%

profile of v7, /device:TPU:0, one launch (start us, length us, event | category | flops | bytes accessed | tf_op | source)
XLA Modules:
  0.0 254.2 jit_solution(6821044756535791556)
XLA Ops:
  1.3 12.9 %all_to_all.15 = bf16[4,128,512]{2,1,0:T(8,128)(2,1)S(1)} all-to-all(bf16[4,128,512]{2,1,0:T(8,128)(2,1)S(1)} %pad_maximum_fusion.1), channel_id=1, replica_groups=mesh['cfg'=2,'blk'=4,'uly'=4] {'uly'}, dimensions={0} | all-to-all | bytes 1048576 | tf_op jit(solution)/shard_map/all_to_all | solution.py:365
  15.7 3.7 %collective-permute-start = (bf16[512,512]{1,0:T(8,128)(2,1)S(1)}, bf16[512,512]{1,0:T(8,128)(2,1)}, u32[]{:S(2)}, u32[]{:S(2)}) collective-permute-start(bf16[512,512]{1,0:T(8,128)(2,1)S(1)} %bitcast.35), channel_id=1, source_target_pairs={{0,4},{4,0},{8,12},{12,8},{1,5},{5,1},{9,13},{13,9},{2,6},{6,2},{1... | collective-permute-start | bytes 1572872 | tf_op jit(solution)/shard_map/ppermute | solution.py:372
  21.4 7.3 %collective-permute-done.2.refs_10_.refs_2_ = bf16[128,1024]{1,0:T(8,128)(2,1)S(1)} collective-permute-done((bf16[128,1024]{1,0:T(8,128)(2,1)S(1)}, bf16[128,1024]{1,0:T(8,128)(2,1)S(1)}, u32[]{:S(2)}, u32[]{:S(2)}) %collective-permute-start.2) | collective-permute-done | bytes 262176 | tf_op jit(solution)/shard_map/ppermute | solution.py:369
  28.7 4.7 %collective-permute-done.3.refs_11_.refs_3_ = bf16[128,1024]{1,0:T(8,128)(2,1)S(1)} collective-permute-done((bf16[128,1024]{1,0:T(8,128)(2,1)S(1)}, bf16[128,1024]{1,0:T(8,128)(2,1)S(1)}, u32[]{:S(2)}, u32[]{:S(2)}) %collective-permute-start.3) | collective-permute-done | bytes 262176 | tf_op jit(solution)/shard_map/ppermute | solution.py:369
  41.2 12.7 %collective-permute-start.14 = (bf16[512,512]{1,0:T(8,128)(2,1)}, bf16[512,512]{1,0:T(8,128)(2,1)}, u32[]{:S(2)}, u32[]{:S(2)}) collective-permute-start(bf16[512,512]{1,0:T(8,128)(2,1)} %regroup.2.refs_5_.refs_1_.refs_3_), channel_id=1, source_target_pairs={{0,4},{4,0},{8,12},{12,8},{1,5},{5,1},{9,13},{13,9},{2,6},{6,2},{1... | collective-permute-start | bytes 1572872 | tf_op jit(solution)/shard_map/ppermute | solution.py:372
  57.7 3.2 %copy.11 = bf16[1024,1536]{0,1:T(8,128)(2,1)S(1)} copy(bf16[1024,1536]{1,0:T(8,128)(2,1)} %param.10) | data formatting | bytes 6291456 | tf_op args[4]
  64.9 11.5 %collective-permute-start.19 = (bf16[512,512]{1,0:T(8,128)(2,1)S(1)}, bf16[512,512]{1,0:T(8,128)(2,1)S(1)}, u32[]{:S(2)}, u32[]{:S(2)}) collective-permute-start(bf16[512,512]{1,0:T(8,128)(2,1)S(1)} %regroup.3.refs_4_.refs_0_.refs_2_), channel_id=1, source_target_pairs={{0,4},{4,0},{8,12},{12,8},{1,5},{5,1},{9,13},{13,9},{2,6},{6,2},{1... | collective-permute-start | bytes 1572872 | tf_op jit(solution)/shard_map/ppermute | solution.py:372
  81.8 7.5 %collective-permute-done.10.refs_2_ = bf16[512,512]{1,0:T(8,128)(2,1)} collective-permute-done((bf16[512,512]{1,0:T(8,128)(2,1)}, bf16[512,512]{1,0:T(8,128)(2,1)}, u32[]{:S(2)}, u32[]{:S(2)}) %collective-permute-start.10) | collective-permute-done | bytes 524320 | tf_op jit(solution)/shard_map/ppermute | solution.py:372
  89.3 12.1 %attend.6.refs_8_.refs_0_ = bf16[2,528,512]{2,1,0:T(8,128)(2,1)S(1)} custom-call(s32[3]{0:T(128)S(1)} %pad_add_fusion.2.table_ref, s32[16,12]{1,0:T(8,128)S(1)} %fusion.kept_ref, bf16[512,512]{1,0:T(8,128)(2,1)} %collective-permute-done.9.refs_0_, bf16[512,512]{1,0:T(8,128)(2,1)} %collective-permute-done.4.refs_12_.refs_4_.refs_1_, ...), custom_call_target="tpu_custom_call" | custom-call | flops 6442450944 | bytes 5242880 | tf_op jit(solution)/shard_map/attend/pallas_call | solution.py:151
  108.3 11.9 %attend.7.refs_8_.refs_0_.refs_3_ = bf16[2,528,512]{2,1,0:T(8,128)(2,1)S(1)} custom-call(s32[3]{0:T(128)S(1)} %pad_add_fusion.table_ref, s32[16,12]{1,0:T(8,128)S(1)} %fusion.kept_ref, bf16[512,512]{1,0:T(8,128)(2,1)} %collective-permute-done.refs_0_.refs_2_, bf16[512,512]{1,0:T(8,128)(2,1)S(1)} %bitcast.37, ...), custom_call_target="tpu_custom_call" | custom-call | flops 6442450944 | bytes 5242880 | tf_op jit(solution)/shard_map/attend/pallas_call | solution.py:151
  120.1 2.8 %collective-permute-done.16.refs_2_ = bf16[512,512]{1,0:T(8,128)(2,1)S(1)} collective-permute-done((bf16[512,512]{1,0:T(8,128)(2,1)S(1)}, bf16[512,512]{1,0:T(8,128)(2,1)S(1)}, u32[]{:S(2)}, u32[]{:S(2)}) %collective-permute-start.16) | collective-permute-done | bytes 524320 | tf_op jit(solution)/shard_map/ppermute | solution.py:372
  122.9 10.8 %attend.8.refs_2_.refs_0_ = bf16[2,528,512]{2,1,0:T(8,128)(2,1)S(1)} custom-call(s32[3]{0:T(128)S(1)} %pad_add_fusion.2.table_ref, s32[16,12]{1,0:T(8,128)S(1)} %fusion.kept_ref, bf16[512,512]{1,0:T(8,128)(2,1)S(1)} %collective-permute-done.15.refs_0_, bf16[512,512]{1,0:T(8,128)(2,1)S(1)} %copy-done.32, ...), custom_call_target="tpu_custom_call" | custom-call | flops 6442450944 | bytes 5242880 | tf_op jit(solution)/shard_map/attend/pallas_call | solution.py:151
  133.7 4.9 %collective-permute-start.24 = (bf16[2,528,512]{2,1,0:T(8,128)(2,1)S(1)}, bf16[2,528,512]{2,1,0:T(8,128)(2,1)S(1)}, u32[]{:S(2)}, u32[]{:S(2)}) collective-permute-start(bf16[2,528,512]{2,1,0:T(8,128)(2,1)S(1)} %attend.8.refs_2_.refs_0_), channel_id=1, source_target_pairs={{0,4},{12,8},{1,5},{13,9},{2,6},{14,10},{3,7},{15,11},{16,20},{28,... | collective-permute-start | bytes 3244040 | tf_op jit(solution)/shard_map/ppermute | solution.py:372
  140.9 12.2 %attend.9.refs_8_.refs_0_.refs_3_ = bf16[2,528,512]{2,1,0:T(8,128)(2,1)S(1)} custom-call(s32[3]{0:T(128)S(1)} %pad_add_fusion.table_ref, s32[16,12]{1,0:T(8,128)S(1)} %fusion.kept_ref, bf16[512,512]{1,0:T(8,128)(2,1)} %collective-permute-done.14.refs_0_.refs_2_, bf16[512,512]{1,0:T(8,128)(2,1)} %regroup.2.refs_5_.refs_1_.refs_3_, ...), custom_call_target="tpu_custom_call" | custom-call | flops 6442450944 | bytes 5242880 | tf_op jit(solution)/shard_map/attend/pallas_call | solution.py:151
  153.4 12.5 %attend.10.refs_2_ = bf16[2,528,512]{2,1,0:T(8,128)(2,1)} custom-call(s32[3]{0:T(128)S(1)} %pad_add_fusion.3.table_ref, s32[16,12]{1,0:T(8,128)S(1)} %fusion.kept_ref, bf16[512,512]{1,0:T(8,128)(2,1)S(1)} %collective-permute-done.19.refs_0_.refs_2_, bf16[512,512]{1,0:T(8,128)(2,1)} %collective-permute-done.20.refs_1_, ...), custom_call_target="tpu_custom_call" | custom-call | flops 6442450944 | bytes 5242880 | tf_op jit(solution)/shard_map/attend/pallas_call | solution.py:151
  165.9 5.0 %collective-permute-start.27 = (bf16[2,528,512]{2,1,0:T(8,128)(2,1)}, bf16[2,528,512]{2,1,0:T(8,128)(2,1)S(1)}, u32[]{:S(2)}, u32[]{:S(2)}) collective-permute-start(bf16[2,528,512]{2,1,0:T(8,128)(2,1)} %attend.10.refs_2_), channel_id=1, source_target_pairs={{0,4},{4,0},{8,12},{12,8},{1,5},{5,1},{9,13},{13,9},{2,6},{6,2},{1... | collective-permute-start | bytes 3244040 | tf_op jit(solution)/shard_map/ppermute | solution.py:372
  174.9 3.7 %collective-permute-start.12 = (bf16[1,528,512]{2,1,0:T(8,128)(2,1)S(1)}, bf16[1,528,512]{2,1,0:T(8,128)(2,1)S(1)}, u32[]{:S(2)}, u32[]{:S(2)}) collective-permute-start(bf16[1,528,512]{2,1,0:T(8,128)(2,1)S(1)} %slice.27), channel_id=1, source_target_pairs={{0,4},{12,8},{1,5},{13,9},{2,6},{14,10},{3,7},{15,11},{16,20},{28,... | collective-permute-start | bytes 1622024 | tf_op jit(solution)/shard_map/ppermute | solution.py:372
  179.5 2.1 collective-permute-start.28
  189.5 11.6 %attend.11.refs_0_.refs_2_.refs_4_.refs_3_ = bf16[2,528,512]{2,1,0:T(8,128)(2,1)S(1)} custom-call(s32[3]{0:T(128)S(1)} %pad_add_fusion.4.table_ref, s32[16,12]{1,0:T(8,128)S(1)} %fusion.kept_ref, bf16[512,512]{1,0:T(8,128)(2,1)S(1)} %copy-done.25, bf16[512,512]{1,0:T(8,128)(2,1)S(1)} %copy-done.40, bf16[512,512]{1,0:T(8,128)(2,1)S(1)} %copy-done.25, ...), custom_call_target="tpu_custom_call" | custom-call | flops 6442450944 | bytes 5242880 | tf_op jit(solution)/shard_map/attend/pallas_call | solution.py:151
  205.6 4.2 %collective-permute-start.30 = (bf16[1,528,512]{2,1,0:T(8,128)(2,1)}, bf16[1,528,512]{2,1,0:T(8,128)(2,1)}, u32[]{:S(2)}, u32[]{:S(2)}) collective-permute-start(bf16[1,528,512]{2,1,0:T(8,128)(2,1)} %merge.8.refs_2_), channel_id=1, source_target_pairs={{0,8},{8,0},{4,12},{12,4},{1,9},{9,1},{5,13},{13,5},{2,10},{10,2},... | collective-permute-start | bytes 1622024 | tf_op jit(solution)/shard_map/ppermute | solution.py:372
  211.1 4.1 %all-to-all-start.1 = ((bf16[4,128,512]{2,1,0:T(8,128)(2,1)}), bf16[4,128,512]{2,1,0:T(8,128)(2,1)}, u32[]{:S(2)}, u32[]{:S(2)}) async-start(bf16[4,128,512]{2,1,0:T(8,128)(2,1)} %bitcast.26), calls=%async_computation.1 | async-start | bytes 1048576 | tf_op jit(solution)/shard_map/all_to_all | solution.py:430
  215.2 3.5 %collective-permute-done.28.refs_1_ = bf16[1,528,512]{2,1,0:T(8,128)(2,1)} collective-permute-done((bf16[1,528,512]{2,1,0:T(8,128)(2,1)}, bf16[1,528,512]{2,1,0:T(8,128)(2,1)}, u32[]{:S(2)}, u32[]{:S(2)}) %collective-permute-start.28) | collective-permute-done | bytes 540704 | tf_op jit(solution)/shard_map/ppermute | solution.py:372
  218.7 10.2 %collective-permute-done.29.refs_4_ = bf16[1,528,512]{2,1,0:T(8,128)(2,1)} collective-permute-done((bf16[1,528,512]{2,1,0:T(8,128)(2,1)}, bf16[1,528,512]{2,1,0:T(8,128)(2,1)}, u32[]{:S(2)}, u32[]{:S(2)}) %collective-permute-start.29) | collective-permute-done | bytes 540704 | tf_op jit(solution)/shard_map/ppermute | solution.py:372
  234.8 16.9 %all_to_all.16 = bf16[4,128,1024]{2,1,0:T(8,128)(2,1)S(1)} all-to-all(bf16[4,128,1024]{2,1,0:T(8,128)(2,1)S(1)} %pad_maximum_fusion), channel_id=1, replica_groups=mesh['cfg'=2,'blk'=4,'uly'=4] {'uly'}, dimensions={0} | all-to-all | bytes 2097152 | tf_op jit(solution)/shard_map/all_to_all | solution.py:430
  (163 shorter events, 61.6 us)
Async XLA Ops:
  15.7 21.2 %collective-permute-start = (bf16[512,512]{1,0:T(8,128)(2,1)S(1)}, bf16[512,512]{1,0:T(8,128)(2,1)}, u32[]{:S(2)}, u32[]{:S(2)}) collective-permute-start(bf16[512,512]{1,0:T(8,128)(2,1)S(1)} %bitcast.35), channel_id=1, source_target_pairs={{0,4},{4,0},{8,12},{12,8},{1,5},{5,1},{9,13},{13,9},{2,6},{6,2},{1... | collective-permute-start | bytes 1572872 | tf_op jit(solution)/shard_map/ppermute | solution.py:372
  35.0 20.1 %collective-permute-start.5 = (bf16[256,1536]{1,0:T(8,128)(2,1)}, bf16[256,1536]{1,0:T(8,128)(2,1)S(1)}, u32[]{:S(2)}, u32[]{:S(2)}) collective-permute-start(bf16[256,1536]{1,0:T(8,128)(2,1)} %get-tuple-element.20), channel_id=1, source_target_pairs={{0,1},{1,0},{2,3},{3,2},{4,5},{5,4},{6,7},{7,6},{8,9},{9,8},{10,11... | collective-permute-start | bytes 2359304 | tf_op jit(solution)/shard_map/ppermute | solution.py:369
  38.4 26.5 %collective-permute-start.6 = (bf16[256,1536]{1,0:T(8,128)(2,1)}, bf16[256,1536]{1,0:T(8,128)(2,1)}, u32[]{:S(2)}, u32[]{:S(2)}) collective-permute-start(bf16[256,1536]{1,0:T(8,128)(2,1)} %get-tuple-element.21), channel_id=1, source_target_pairs={{0,2},{1,3},{2,0},{3,1},{4,6},{5,7},{6,4},{7,5},{8,10},{9,11},{10,... | collective-permute-start | bytes 2359304 | tf_op jit(solution)/shard_map/ppermute | solution.py:369
  38.8 37.6 %collective-permute-start.7 = (bf16[256,1536]{1,0:T(8,128)(2,1)}, bf16[256,1536]{1,0:T(8,128)(2,1)}, u32[]{:S(2)}, u32[]{:S(2)}) collective-permute-start(bf16[256,1536]{1,0:T(8,128)(2,1)} %get-tuple-element.22), channel_id=1, source_target_pairs={{0,3},{1,2},{2,1},{3,0},{4,7},{5,6},{6,5},{7,4},{8,11},{9,10},{10,... | collective-permute-start | bytes 2359304 | tf_op jit(solution)/shard_map/ppermute | solution.py:369
  41.2 40.0 %collective-permute-start.14 = (bf16[512,512]{1,0:T(8,128)(2,1)}, bf16[512,512]{1,0:T(8,128)(2,1)}, u32[]{:S(2)}, u32[]{:S(2)}) collective-permute-start(bf16[512,512]{1,0:T(8,128)(2,1)} %regroup.2.refs_5_.refs_1_.refs_3_), channel_id=1, source_target_pairs={{0,4},{4,0},{8,12},{12,8},{1,5},{5,1},{9,13},{13,9},{2,6},{6,2},{1... | collective-permute-start | bytes 1572872 | tf_op jit(solution)/shard_map/ppermute | solution.py:372
  53.9 25.9 %collective-permute-start.11 = (bf16[512,512]{1,0:T(8,128)(2,1)}, bf16[512,512]{1,0:T(8,128)(2,1)}, u32[]{:S(2)}, u32[]{:S(2)}) collective-permute-start(bf16[512,512]{1,0:T(8,128)(2,1)} %collective-permute-done.4.refs_12_.refs_4_.refs_1_), channel_id=1, source_target_pairs={{4,0},{8,12},{5,1},{9,13},{6,2},{10,14},{7,3},{11,15},{20,16},{24,... | collective-permute-start | bytes 1572872 | tf_op jit(solution)/shard_map/ppermute | solution.py:372
  56.1 33.3 %collective-permute-start.10 = (bf16[512,512]{1,0:T(8,128)(2,1)}, bf16[512,512]{1,0:T(8,128)(2,1)}, u32[]{:S(2)}, u32[]{:S(2)}) collective-permute-start(bf16[512,512]{1,0:T(8,128)(2,1)} %collective-permute-done.9.refs_0_), channel_id=1, source_target_pairs={{4,0},{8,12},{5,1},{9,13},{6,2},{10,14},{7,3},{11,15},{20,16},{24,... | collective-permute-start | bytes 1572872 | tf_op jit(solution)/shard_map/ppermute | solution.py:372
  64.9 39.4 %collective-permute-start.19 = (bf16[512,512]{1,0:T(8,128)(2,1)S(1)}, bf16[512,512]{1,0:T(8,128)(2,1)S(1)}, u32[]{:S(2)}, u32[]{:S(2)}) collective-permute-start(bf16[512,512]{1,0:T(8,128)(2,1)S(1)} %regroup.3.refs_4_.refs_0_.refs_2_), channel_id=1, source_target_pairs={{0,4},{4,0},{8,12},{12,8},{1,5},{5,1},{9,13},{13,9},{2,6},{6,2},{1... | collective-permute-start | bytes 1572872 | tf_op jit(solution)/shard_map/ppermute | solution.py:372
  76.4 28.7 %collective-permute-start.20 = (bf16[512,512]{1,0:T(8,128)(2,1)S(1)}, bf16[512,512]{1,0:T(8,128)(2,1)}, u32[]{:S(2)}, u32[]{:S(2)}) collective-permute-start(bf16[512,512]{1,0:T(8,128)(2,1)S(1)} %regroup.3.refs_4_.refs_0_.refs_2_), channel_id=1, source_target_pairs={{4,8},{8,4},{5,9},{9,5},{6,10},{10,6},{7,11},{11,7},{20,24},{24,20... | collective-permute-start | bytes 1572872 | tf_op jit(solution)/shard_map/ppermute | solution.py:372
  79.8 40.3 %collective-permute-start.17 = (bf16[512,512]{1,0:T(8,128)(2,1)S(1)}, bf16[512,512]{1,0:T(8,128)(2,1)S(1)}, u32[]{:S(2)}, u32[]{:S(2)}) collective-permute-start(bf16[512,512]{1,0:T(8,128)(2,1)S(1)} %copy-done.32), channel_id=1, source_target_pairs={{4,0},{8,12},{5,1},{9,13},{6,2},{10,14},{7,3},{11,15},{20,16},{24,... | collective-permute-start | bytes 1572872 | tf_op jit(solution)/shard_map/ppermute | solution.py:372
  81.1 21.9 %collective-permute-start.15 = (bf16[512,512]{1,0:T(8,128)(2,1)}, bf16[512,512]{1,0:T(8,128)(2,1)S(1)}, u32[]{:S(2)}, u32[]{:S(2)}) collective-permute-start(bf16[512,512]{1,0:T(8,128)(2,1)} %collective-permute-done.14.refs_0_.refs_2_), channel_id=1, source_target_pairs={{4,8},{8,4},{5,9},{9,5},{6,10},{10,6},{7,11},{11,7},{20,24},{24,20... | collective-permute-start | bytes 1572872 | tf_op jit(solution)/shard_map/ppermute | solution.py:372
  101.5 38.4 %collective-permute-start.13 = (bf16[2,528,512]{2,1,0:T(8,128)(2,1)S(1)}, bf16[2,528,512]{2,1,0:T(8,128)(2,1)S(1)}, u32[]{:S(2)}, u32[]{:S(2)}) collective-permute-start(bf16[2,528,512]{2,1,0:T(8,128)(2,1)S(1)} %attend.6.refs_8_.refs_0_), channel_id=1, source_target_pairs={{0,4},{12,8},{1,5},{13,9},{2,6},{14,10},{3,7},{15,11},{16,20},{28,... | collective-permute-start | bytes 3244040 | tf_op jit(solution)/shard_map/ppermute | solution.py:372
  104.3 34.3 %collective-permute-start.21 = (bf16[512,512]{1,0:T(8,128)(2,1)S(1)}, bf16[512,512]{1,0:T(8,128)(2,1)S(1)}, u32[]{:S(2)}, u32[]{:S(2)}) collective-permute-start(bf16[512,512]{1,0:T(8,128)(2,1)S(1)} %collective-permute-done.19.refs_0_.refs_2_), channel_id=1, source_target_pairs={{4,8},{8,4},{5,9},{9,5},{6,10},{10,6},{7,11},{11,7},{20,24},{24,20... | collective-permute-start | bytes 1572872 | tf_op jit(solution)/shard_map/ppermute | solution.py:372
  105.1 76.6 %collective-permute-start.26 = (bf16[512,512]{1,0:T(8,128)(2,1)}, bf16[512,512]{1,0:T(8,128)(2,1)}, u32[]{:S(2)}, u32[]{:S(2)}) collective-permute-start(bf16[512,512]{1,0:T(8,128)(2,1)} %collective-permute-done.20.refs_1_), channel_id=1, source_target_pairs={{4,0},{8,12},{5,1},{9,13},{6,2},{10,14},{7,3},{11,15},{20,16},{24,... | collective-permute-start | bytes 1572872 | tf_op jit(solution)/shard_map/ppermute | solution.py:372
  133.7 38.3 %collective-permute-start.24 = (bf16[2,528,512]{2,1,0:T(8,128)(2,1)S(1)}, bf16[2,528,512]{2,1,0:T(8,128)(2,1)S(1)}, u32[]{:S(2)}, u32[]{:S(2)}) collective-permute-start(bf16[2,528,512]{2,1,0:T(8,128)(2,1)S(1)} %attend.8.refs_2_.refs_0_), channel_id=1, source_target_pairs={{0,4},{12,8},{1,5},{13,9},{2,6},{14,10},{3,7},{15,11},{16,20},{28,... | collective-permute-start | bytes 3244040 | tf_op jit(solution)/shard_map/ppermute | solution.py:372
  140.0 30.9 %collective-permute-start.18 = (bf16[2,528,512]{2,1,0:T(8,128)(2,1)S(1)}, bf16[2,528,512]{2,1,0:T(8,128)(2,1)S(1)}, u32[]{:S(2)}, u32[]{:S(2)}) collective-permute-start(bf16[2,528,512]{2,1,0:T(8,128)(2,1)S(1)} %merge.5.refs_8_), channel_id=1, source_target_pairs={{4,8},{8,4},{5,9},{9,5},{6,10},{10,6},{7,11},{11,7},{20,24},{24,20... | collective-permute-start | bytes 3244040 | tf_op jit(solution)/shard_map/ppermute | solution.py:372
  165.9 35.3 %collective-permute-start.27 = (bf16[2,528,512]{2,1,0:T(8,128)(2,1)}, bf16[2,528,512]{2,1,0:T(8,128)(2,1)S(1)}, u32[]{:S(2)}, u32[]{:S(2)}) collective-permute-start(bf16[2,528,512]{2,1,0:T(8,128)(2,1)} %attend.10.refs_2_), channel_id=1, source_target_pairs={{0,4},{4,0},{8,12},{12,8},{1,5},{5,1},{9,13},{13,9},{2,6},{6,2},{1... | collective-permute-start | bytes 3244040 | tf_op jit(solution)/shard_map/ppermute | solution.py:372
  173.2 29.2 %collective-permute-start.25 = (bf16[2,528,512]{2,1,0:T(8,128)(2,1)}, bf16[2,528,512]{2,1,0:T(8,128)(2,1)}, u32[]{:S(2)}, u32[]{:S(2)}) collective-permute-start(bf16[2,528,512]{2,1,0:T(8,128)(2,1)} %merge.7.refs_8_), channel_id=1, source_target_pairs={{4,8},{8,4},{5,9},{9,5},{6,10},{10,6},{7,11},{11,7},{20,24},{24,20... | collective-permute-start | bytes 3244040 | tf_op jit(solution)/shard_map/ppermute | solution.py:372
  174.9 34.9 %collective-permute-start.12 = (bf16[1,528,512]{2,1,0:T(8,128)(2,1)S(1)}, bf16[1,528,512]{2,1,0:T(8,128)(2,1)S(1)}, u32[]{:S(2)}, u32[]{:S(2)}) collective-permute-start(bf16[1,528,512]{2,1,0:T(8,128)(2,1)S(1)} %slice.27), channel_id=1, source_target_pairs={{0,4},{12,8},{1,5},{13,9},{2,6},{14,10},{3,7},{15,11},{16,20},{28,... | collective-permute-start | bytes 1622024 | tf_op jit(solution)/shard_map/ppermute | solution.py:372
  179.5 39.2 %collective-permute-start.28 = (bf16[1,528,512]{2,1,0:T(8,128)(2,1)}, bf16[1,528,512]{2,1,0:T(8,128)(2,1)}, u32[]{:S(2)}, u32[]{:S(2)}) collective-permute-start(bf16[1,528,512]{2,1,0:T(8,128)(2,1)} %slice.28), channel_id=1, source_target_pairs={{0,4},{12,8},{1,5},{13,9},{2,6},{14,10},{3,7},{15,11},{16,20},{28,... | collective-permute-start | bytes 1622024 | tf_op jit(solution)/shard_map/ppermute | solution.py:372
  181.6 28.2 %collective-permute-start.23 = (bf16[1,528,512]{2,1,0:T(8,128)(2,1)S(1)}, bf16[1,528,512]{2,1,0:T(8,128)(2,1)S(1)}, u32[]{:S(2)}, u32[]{:S(2)}) collective-permute-start(bf16[1,528,512]{2,1,0:T(8,128)(2,1)S(1)} %copy-done.23), channel_id=1, source_target_pairs={{4,0},{8,12},{5,1},{9,13},{6,2},{10,14},{7,3},{11,15},{20,16},{24,... | collective-permute-start | bytes 1622024 | tf_op jit(solution)/shard_map/ppermute | solution.py:372
  204.4 24.6 %collective-permute-start.29 = (bf16[1,528,512]{2,1,0:T(8,128)(2,1)}, bf16[1,528,512]{2,1,0:T(8,128)(2,1)}, u32[]{:S(2)}, u32[]{:S(2)}) collective-permute-start(bf16[1,528,512]{2,1,0:T(8,128)(2,1)} %merge.9.refs_5_), channel_id=1, source_target_pairs={{4,0},{8,12},{5,1},{9,13},{6,2},{10,14},{7,3},{11,15},{20,16},{24,... | collective-permute-start | bytes 1622024 | tf_op jit(solution)/shard_map/ppermute | solution.py:372
  205.6 27.3 %collective-permute-start.30 = (bf16[1,528,512]{2,1,0:T(8,128)(2,1)}, bf16[1,528,512]{2,1,0:T(8,128)(2,1)}, u32[]{:S(2)}, u32[]{:S(2)}) collective-permute-start(bf16[1,528,512]{2,1,0:T(8,128)(2,1)} %merge.8.refs_2_), channel_id=1, source_target_pairs={{0,8},{8,0},{4,12},{12,4},{1,9},{9,1},{5,13},{13,5},{2,10},{10,2},... | collective-permute-start | bytes 1622024 | tf_op jit(solution)/shard_map/ppermute | solution.py:372
  211.1 23.7 %all-to-all-start.1 = ((bf16[4,128,512]{2,1,0:T(8,128)(2,1)}), bf16[4,128,512]{2,1,0:T(8,128)(2,1)}, u32[]{:S(2)}, u32[]{:S(2)}) async-start(bf16[4,128,512]{2,1,0:T(8,128)(2,1)} %bitcast.26), calls=%async_computation.1 | async-start | bytes 1048576 | tf_op jit(solution)/shard_map/all_to_all | solution.py:430
  (49 other events, 584.7 us)

commit v8 on v7

--- a/solution.py
+++ b/solution.py
@@ -172,7 +172,7 @@
                 pltpu.VMEM((stat_rows(width), rows), jnp.float32),
             ],
         ),
-        compiler_params=pltpu.CompilerParams(vmem_limit_bytes=28 * MIB),
+        compiler_params=pltpu.CompilerParams(vmem_limit_bytes=22 * MIB),
         cost_estimate=pl.CostEstimate(
             flops=8 * blocks * rows * keys * DH * heads,
             bytes_accessed=4 * blocks * rows * width + 4 * keys * width,
@@ -394,7 +394,10 @@
     found = [spread(first_span)]
     parts_q = parts_for_peers(peer, [new_queries], early, peers, [first_span])
     later = to_peers(parts_q)
-    parts_kv = parts_for_peers(peer, [new_keys, new_values], 0, peers, [*later, found[0]["early"]])
+    context_values_t = context_values.T
+    parts_kv = parts_for_peers(
+        peer, [new_keys, new_values], 0, peers, [*later, found[0]["early"], context_values_t]
+    )
 
     def run_spread(c, deps):
         span = regrouped(peer, later, PIECES[c][0] * unit - early, widths[c], deps)
@@ -405,7 +408,6 @@
     for c in range(1, count):
         latest = run_spread(c, [found[c - 1]["early"], latest])
     span_k, span_v_t = joined(to_peers(parts_kv), latest)
-    context_values_t = context_values.T
     last = [span_k]
     outer = ((place == 0) | (place == n - 1)).astype(jnp.int32)
     low = place < n // 2

time: 256 us -> 259 us (1.012)
  waiting for transfers between devices: 36.4 us -> 40.3 us
    ppermute x6, waiting for transfers between devices: 12 us -> 16.7 us  [to_peers(): lax.ppermute(p, 'uly', [(i, i ^ k) for i in range(peers)])]
    unnamed x83 -> x63, local copies, waits for them, and re-layouts: 21.7 us -> 21.6 us
  transfers between devices with their start and end apart: 32 -> 32, of which waited for: 7 -> 8; matrix products, arithmetic and copies ran while one was open for 2% -> 3% of each run, Pallas kernels for 33% -> 33%
where the time goes in v8:
time: 259 us; the launch traced here: 257 us
  Pallas kernels  84.5 us (33%)
  starting transfers between devices  74.7 us (29%)
  waiting for transfers between devices  40.3 us (16%)
  blocking collectives  29.9 us (12%)
  local copies, waits for them, and re-layouts  25.3 us (10%)
    pallas_call x6, Pallas kernels, attend(): pl.pallas_call(functools.partial(attend_kernel, [[None] * len(c) for c in...  69.8 us
    ppermute x25, starting transfers between devices, send(): return lax.ppermute(x, 'blk', pairs)  66.8 us
    ppermute x25, waiting for transfers between devices, send(): return lax.ppermute(x, 'blk', pairs)  23.5 us
    unnamed x63, local copies, waits for them, and re-layouts  21.6 us
    all_to_all x1, blocking collectives, run_return(): lax.all_to_all(joint, 'uly', split_axis=0, concat_axis=0, tiled=False)  16.9 us
    ppermute x6, waiting for transfers between devices, to_peers(): lax.ppermute(p, 'uly', [(i, i ^ k) for i in range(peers)])  16.7 us
    all_to_all x1, blocking collectives, to_heads(): lax.all_to_all(pieces, 'uly', split_axis=0, concat_axis=0, tiled=False)  13 us
    pallas_call x8, Pallas kernels, join_parts(): pl.pallas_call(functools.partial(join_kernel_of, [len(c) for c in choices...  7.98 us
  transfers between devices with their start and end apart: 32, of which 8 were waited for; matrix products, arithmetic and copies ran while one was open for 3% of the time, Pallas kernels for 33%

profile of v8, /device:TPU:0, one launch (start us, length us, event | category | flops | bytes accessed | tf_op | source)
XLA Modules:
  0.0 257.2 jit_solution(7024925252511966750)
XLA Ops:
  1.3 13.0 %all_to_all.15 = bf16[4,128,512]{2,1,0:T(8,128)(2,1)} all-to-all(bf16[4,128,512]{2,1,0:T(8,128)(2,1)S(1)} %pad_maximum_fusion.1), channel_id=1, replica_groups=mesh['cfg'=2,'blk'=4,'uly'=4] {'uly'}, dimensions={0} | all-to-all | bytes 1048576 | tf_op jit(solution)/shard_map/all_to_all | solution.py:365
  15.8 4.0 %collective-permute-start = (bf16[512,512]{1,0:T(8,128)(2,1)}, bf16[512,512]{1,0:T(8,128)(2,1)}, u32[]{:S(2)}, u32[]{:S(2)}) collective-permute-start(bf16[512,512]{1,0:T(8,128)(2,1)} %bitcast.7.refs_4_.refs_1_.refs_3_), channel_id=1, source_target_pairs={{0,4},{4,0},{8,12},{12,8},{1,5},{5,1},{9,13},{13,9},{2,6},{6,2},{1... | collective-permute-start | bytes 1572872 | tf_op jit(solution)/shard_map/ppermute | solution.py:372
  22.7 4.7 %copy.11 = bf16[1024,1536]{0,1:T(8,128)(2,1)} copy(bf16[1024,1536]{1,0:T(8,128)(2,1)} %param.10) | data formatting | bytes 6291456 | tf_op args[4]
  27.3 2.9 %collective-permute-done.2.refs_10_.refs_2_ = bf16[128,1024]{1,0:T(8,128)(2,1)} collective-permute-done((bf16[128,1024]{1,0:T(8,128)(2,1)}, bf16[128,1024]{1,0:T(8,128)(2,1)}, u32[]{:S(2)}, u32[]{:S(2)}) %collective-permute-start.2) | collective-permute-done | bytes 262176 | tf_op jit(solution)/shard_map/ppermute | solution.py:369
  30.2 4.8 %collective-permute-done.3.refs_11_.refs_3_ = bf16[128,1024]{1,0:T(8,128)(2,1)} collective-permute-done((bf16[128,1024]{1,0:T(8,128)(2,1)}, bf16[128,1024]{1,0:T(8,128)(2,1)}, u32[]{:S(2)}, u32[]{:S(2)}) %collective-permute-start.3) | collective-permute-done | bytes 262176 | tf_op jit(solution)/shard_map/ppermute | solution.py:369
  46.3 12.4 %collective-permute-start.14 = (bf16[512,512]{1,0:T(8,128)(2,1)S(1)}, bf16[512,512]{1,0:T(8,128)(2,1)S(1)}, u32[]{:S(2)}, u32[]{:S(2)}) collective-permute-start(bf16[512,512]{1,0:T(8,128)(2,1)S(1)} %regroup.2.refs_5_.refs_1_.refs_3_), channel_id=1, source_target_pairs={{0,4},{4,0},{8,12},{12,8},{1,5},{5,1},{9,13},{13,9},{2,6},{6,2},{1... | collective-permute-start | bytes 1572872 | tf_op jit(solution)/shard_map/ppermute | solution.py:372
  65.0 8.7 %collective-permute-start.19 = (bf16[512,512]{1,0:T(8,128)(2,1)S(1)}, bf16[512,512]{1,0:T(8,128)(2,1)S(1)}, u32[]{:S(2)}, u32[]{:S(2)}) collective-permute-start(bf16[512,512]{1,0:T(8,128)(2,1)S(1)} %regroup.3.refs_4_.refs_0_.refs_2_), channel_id=1, source_target_pairs={{0,4},{4,0},{8,12},{12,8},{1,5},{5,1},{9,13},{13,9},{2,6},{6,2},{1... | collective-permute-start | bytes 1572872 | tf_op jit(solution)/shard_map/ppermute | solution.py:372
  73.7 6.9 %collective-permute-done.7.refs_3_ = bf16[256,1536]{1,0:T(8,128)(2,1)} collective-permute-done((bf16[256,1536]{1,0:T(8,128)(2,1)}, bf16[256,1536]{1,0:T(8,128)(2,1)}, u32[]{:S(2)}, u32[]{:S(2)}) %collective-permute-start.7) | collective-permute-done | bytes 786464 | tf_op jit(solution)/shard_map/ppermute | solution.py:369
  86.1 8.9 %collective-permute-done.10.refs_2_ = bf16[512,512]{1,0:T(8,128)(2,1)S(1)} collective-permute-done((bf16[512,512]{1,0:T(8,128)(2,1)}, bf16[512,512]{1,0:T(8,128)(2,1)S(1)}, u32[]{:S(2)}, u32[]{:S(2)}) %collective-permute-start.10) | collective-permute-done | bytes 524320 | tf_op jit(solution)/shard_map/ppermute | solution.py:372
  96.8 11.8 %attend.6.refs_8_.refs_0_ = bf16[2,528,512]{2,1,0:T(8,128)(2,1)S(1)} custom-call(s32[3]{0:T(128)S(1)} %pad_add_fusion.2.table_ref, s32[16,12]{1,0:T(8,128)S(1)} %fusion.kept_ref, bf16[512,512]{1,0:T(8,128)(2,1)} %collective-permute-done.9.refs_0_, bf16[512,512]{1,0:T(8,128)(2,1)} %collective-permute-done.4.refs_12_.refs_4_.refs_1_, ...), custom_call_target="tpu_custom_call" | custom-call | flops 6442450944 | bytes 5242880 | tf_op jit(solution)/shard_map/attend/pallas_call | solution.py:151
  113.7 12.3 %attend.7.refs_8_.refs_0_.refs_3_ = bf16[2,528,512]{2,1,0:T(8,128)(2,1)S(1)} custom-call(s32[3]{0:T(128)S(1)} %pad_add_fusion.table_ref, s32[16,12]{1,0:T(8,128)S(1)} %fusion.kept_ref, bf16[512,512]{1,0:T(8,128)(2,1)} %collective-permute-done.refs_0_.refs_2_, bf16[512,512]{1,0:T(8,128)(2,1)} %bitcast.7.refs_4_.refs_1_.refs_3_, ...), custom_call_target="tpu_custom_call" | custom-call | flops 6442450944 | bytes 5242880 | tf_op jit(solution)/shard_map/attend/pallas_call | solution.py:151
  126.0 2.7 %collective-permute-done.16.refs_2_ = bf16[512,512]{1,0:T(8,128)(2,1)S(1)} collective-permute-done((bf16[512,512]{1,0:T(8,128)(2,1)S(1)}, bf16[512,512]{1,0:T(8,128)(2,1)S(1)}, u32[]{:S(2)}, u32[]{:S(2)}) %collective-permute-start.16) | collective-permute-done | bytes 524320 | tf_op jit(solution)/shard_map/ppermute | solution.py:372
  128.7 10.8 %attend.8.refs_2_.refs_0_ = bf16[2,528,512]{2,1,0:T(8,128)(2,1)S(1)} custom-call(s32[3]{0:T(128)S(1)} %pad_add_fusion.2.table_ref, s32[16,12]{1,0:T(8,128)S(1)} %fusion.kept_ref, bf16[512,512]{1,0:T(8,128)(2,1)S(1)} %collective-permute-done.15.refs_0_, bf16[512,512]{1,0:T(8,128)(2,1)S(1)} %collective-permute-done.8.refs_4_.refs_1_, ...), custom_call_target="tpu_custom_call" | custom-call | flops 6442450944 | bytes 5242880 | tf_op jit(solution)/shard_map/attend/pallas_call | solution.py:151
  139.4 5.2 %collective-permute-start.24 = (bf16[2,528,512]{2,1,0:T(8,128)(2,1)S(1)}, bf16[2,528,512]{2,1,0:T(8,128)(2,1)S(1)}, u32[]{:S(2)}, u32[]{:S(2)}) collective-permute-start(bf16[2,528,512]{2,1,0:T(8,128)(2,1)S(1)} %attend.8.refs_2_.refs_0_), channel_id=1, source_target_pairs={{0,4},{12,8},{1,5},{13,9},{2,6},{14,10},{3,7},{15,11},{16,20},{28,... | collective-permute-start | bytes 3244040 | tf_op jit(solution)/shard_map/ppermute | solution.py:372
  147.0 10.8 %attend.9.refs_8_.refs_0_.refs_3_ = bf16[2,528,512]{2,1,0:T(8,128)(2,1)S(1)} custom-call(s32[3]{0:T(128)S(1)} %pad_add_fusion.table_ref, s32[16,12]{1,0:T(8,128)S(1)} %fusion.kept_ref, bf16[512,512]{1,0:T(8,128)(2,1)S(1)} %collective-permute-done.14.refs_0_.refs_2_, bf16[512,512]{1,0:T(8,128)(2,1)S(1)} %copy-done.22, ...), custom_call_target="tpu_custom_call" | custom-call | flops 6442450944 | bytes 5242880 | tf_op jit(solution)/shard_map/attend/pallas_call | solution.py:151
  157.8 12.5 %attend.10.refs_2_ = bf16[2,528,512]{2,1,0:T(8,128)(2,1)} custom-call(s32[3]{0:T(128)S(1)} %pad_add_fusion.3.table_ref, s32[16,12]{1,0:T(8,128)S(1)} %fusion.kept_ref, bf16[512,512]{1,0:T(8,128)(2,1)S(1)} %collective-permute-done.19.refs_0_.refs_2_, bf16[512,512]{1,0:T(8,128)(2,1)} %collective-permute-done.20.refs_1_, ...), custom_call_target="tpu_custom_call" | custom-call | flops 6442450944 | bytes 5242880 | tf_op jit(solution)/shard_map/attend/pallas_call | solution.py:151
  170.3 5.3 %collective-permute-start.27 = (bf16[2,528,512]{2,1,0:T(8,128)(2,1)}, bf16[2,528,512]{2,1,0:T(8,128)(2,1)S(1)}, u32[]{:S(2)}, u32[]{:S(2)}) collective-permute-start(bf16[2,528,512]{2,1,0:T(8,128)(2,1)} %attend.10.refs_2_), channel_id=1, source_target_pairs={{0,4},{4,0},{8,12},{12,8},{1,5},{5,1},{9,13},{13,9},{2,6},{6,2},{1... | collective-permute-start | bytes 3244040 | tf_op jit(solution)/shard_map/ppermute | solution.py:372
  179.6 3.8 %collective-permute-start.12 = (bf16[1,528,512]{2,1,0:T(8,128)(2,1)S(1)}, bf16[1,528,512]{2,1,0:T(8,128)(2,1)S(1)}, u32[]{:S(2)}, u32[]{:S(2)}) collective-permute-start(bf16[1,528,512]{2,1,0:T(8,128)(2,1)S(1)} %slice.27), channel_id=1, source_target_pairs={{0,4},{12,8},{1,5},{13,9},{2,6},{14,10},{3,7},{15,11},{16,20},{28,... | collective-permute-start | bytes 1622024 | tf_op jit(solution)/shard_map/ppermute | solution.py:372
  194.2 11.6 %attend.11.refs_0_.refs_2_.refs_4_.refs_3_ = bf16[2,528,512]{2,1,0:T(8,128)(2,1)S(1)} custom-call(s32[3]{0:T(128)S(1)} %pad_add_fusion.4.table_ref, s32[16,12]{1,0:T(8,128)S(1)} %fusion.kept_ref, bf16[512,512]{1,0:T(8,128)(2,1)S(1)} %copy-done.20, bf16[512,512]{1,0:T(8,128)(2,1)S(1)} %copy-done.30, bf16[512,512]{1,0:T(8,128)(2,1)S(1)} %copy-done.20, ...), custom_call_target="tpu_custom_call" | custom-call | flops 6442450944 | bytes 5242880 | tf_op jit(solution)/shard_map/attend/pallas_call | solution.py:151
  210.4 4.2 %collective-permute-start.30 = (bf16[1,528,512]{2,1,0:T(8,128)(2,1)}, bf16[1,528,512]{2,1,0:T(8,128)(2,1)}, u32[]{:S(2)}, u32[]{:S(2)}) collective-permute-start(bf16[1,528,512]{2,1,0:T(8,128)(2,1)} %merge.8.refs_2_), channel_id=1, source_target_pairs={{0,8},{8,0},{4,12},{12,4},{1,9},{9,1},{5,13},{13,5},{2,10},{10,2},... | collective-permute-start | bytes 1622024 | tf_op jit(solution)/shard_map/ppermute | solution.py:372
  215.8 4.2 %all-to-all-start.1 = ((bf16[4,128,512]{2,1,0:T(8,128)(2,1)}), bf16[4,128,512]{2,1,0:T(8,128)(2,1)}, u32[]{:S(2)}, u32[]{:S(2)}) async-start(bf16[4,128,512]{2,1,0:T(8,128)(2,1)} %bitcast.33), calls=%async_computation.1 | async-start | bytes 1048576 | tf_op jit(solution)/shard_map/all_to_all | solution.py:432
  220.0 3.4 %collective-permute-done.28.refs_1_ = bf16[1,528,512]{2,1,0:T(8,128)(2,1)} collective-permute-done((bf16[1,528,512]{2,1,0:T(8,128)(2,1)}, bf16[1,528,512]{2,1,0:T(8,128)(2,1)}, u32[]{:S(2)}, u32[]{:S(2)}) %collective-permute-start.28) | collective-permute-done | bytes 540704 | tf_op jit(solution)/shard_map/ppermute | solution.py:372
  223.4 8.5 %collective-permute-done.29.refs_4_ = bf16[1,528,512]{2,1,0:T(8,128)(2,1)} collective-permute-done((bf16[1,528,512]{2,1,0:T(8,128)(2,1)}, bf16[1,528,512]{2,1,0:T(8,128)(2,1)}, u32[]{:S(2)}, u32[]{:S(2)}) %collective-permute-start.29) | collective-permute-done | bytes 540704 | tf_op jit(solution)/shard_map/ppermute | solution.py:372
  237.8 16.9 %all_to_all.16 = bf16[4,128,1024]{2,1,0:T(8,128)(2,1)S(1)} all-to-all(bf16[4,128,1024]{2,1,0:T(8,128)(2,1)S(1)} %pad_maximum_fusion), channel_id=1, replica_groups=mesh['cfg'=2,'blk'=4,'uly'=4] {'uly'}, dimensions={0} | all-to-all | bytes 2097152 | tf_op jit(solution)/shard_map/all_to_all | solution.py:432
  (143 shorter events, 66.4 us)
Async XLA Ops:
  14.3 20.7 %collective-permute-start.4 = (bf16[512,512]{1,0:T(8,128)(2,1)}, bf16[512,512]{1,0:T(8,128)(2,1)}, u32[]{:S(2)}, u32[]{:S(2)}) collective-permute-start(bf16[512,512]{1,0:T(8,128)(2,1)} %bitcast.7.refs_4_.refs_1_.refs_3_), channel_id=1, source_target_pairs={{4,8},{8,4},{5,9},{9,5},{6,10},{10,6},{7,11},{11,7},{20,24},{24,20... | collective-permute-start | bytes 1572872 | tf_op jit(solution)/shard_map/ppermute | solution.py:372
  15.8 27.0 %collective-permute-start = (bf16[512,512]{1,0:T(8,128)(2,1)}, bf16[512,512]{1,0:T(8,128)(2,1)}, u32[]{:S(2)}, u32[]{:S(2)}) collective-permute-start(bf16[512,512]{1,0:T(8,128)(2,1)} %bitcast.7.refs_4_.refs_1_.refs_3_), channel_id=1, source_target_pairs={{0,4},{4,0},{8,12},{12,8},{1,5},{5,1},{9,13},{13,9},{2,6},{6,2},{1... | collective-permute-start | bytes 1572872 | tf_op jit(solution)/shard_map/ppermute | solution.py:372
  44.3 20.7 %collective-permute-start.6 = (bf16[256,1536]{1,0:T(8,128)(2,1)}, bf16[256,1536]{1,0:T(8,128)(2,1)}, u32[]{:S(2)}, u32[]{:S(2)}) collective-permute-start(bf16[256,1536]{1,0:T(8,128)(2,1)} %get-tuple-element.21), channel_id=1, source_target_pairs={{0,2},{1,3},{2,0},{3,1},{4,6},{5,7},{6,4},{7,5},{8,10},{9,11},{10,... | collective-permute-start | bytes 2359304 | tf_op jit(solution)/shard_map/ppermute | solution.py:369
  44.7 35.9 %collective-permute-start.7 = (bf16[256,1536]{1,0:T(8,128)(2,1)}, bf16[256,1536]{1,0:T(8,128)(2,1)}, u32[]{:S(2)}, u32[]{:S(2)}) collective-permute-start(bf16[256,1536]{1,0:T(8,128)(2,1)} %get-tuple-element.22), channel_id=1, source_target_pairs={{0,3},{1,2},{2,1},{3,0},{4,7},{5,6},{6,5},{7,4},{8,11},{9,10},{10,... | collective-permute-start | bytes 2359304 | tf_op jit(solution)/shard_map/ppermute | solution.py:369
  46.3 39.0 %collective-permute-start.14 = (bf16[512,512]{1,0:T(8,128)(2,1)S(1)}, bf16[512,512]{1,0:T(8,128)(2,1)S(1)}, u32[]{:S(2)}, u32[]{:S(2)}) collective-permute-start(bf16[512,512]{1,0:T(8,128)(2,1)S(1)} %regroup.2.refs_5_.refs_1_.refs_3_), channel_id=1, source_target_pairs={{0,4},{4,0},{8,12},{12,8},{1,5},{5,1},{9,13},{13,9},{2,6},{6,2},{1... | collective-permute-start | bytes 1572872 | tf_op jit(solution)/shard_map/ppermute | solution.py:372
  58.7 25.3 %collective-permute-start.11 = (bf16[512,512]{1,0:T(8,128)(2,1)}, bf16[512,512]{1,0:T(8,128)(2,1)S(1)}, u32[]{:S(2)}, u32[]{:S(2)}) collective-permute-start(bf16[512,512]{1,0:T(8,128)(2,1)} %collective-permute-done.4.refs_12_.refs_4_.refs_1_), channel_id=1, source_target_pairs={{4,0},{8,12},{5,1},{9,13},{6,2},{10,14},{7,3},{11,15},{20,16},{24,... | collective-permute-start | bytes 1572872 | tf_op jit(solution)/shard_map/ppermute | solution.py:372
  60.0 34.9 %collective-permute-start.10 = (bf16[512,512]{1,0:T(8,128)(2,1)}, bf16[512,512]{1,0:T(8,128)(2,1)S(1)}, u32[]{:S(2)}, u32[]{:S(2)}) collective-permute-start(bf16[512,512]{1,0:T(8,128)(2,1)} %collective-permute-done.9.refs_0_), channel_id=1, source_target_pairs={{4,0},{8,12},{5,1},{9,13},{6,2},{10,14},{7,3},{11,15},{20,16},{24,... | collective-permute-start | bytes 1572872 | tf_op jit(solution)/shard_map/ppermute | solution.py:372
  65.0 46.6 %collective-permute-start.19 = (bf16[512,512]{1,0:T(8,128)(2,1)S(1)}, bf16[512,512]{1,0:T(8,128)(2,1)S(1)}, u32[]{:S(2)}, u32[]{:S(2)}) collective-permute-start(bf16[512,512]{1,0:T(8,128)(2,1)S(1)} %regroup.3.refs_4_.refs_0_.refs_2_), channel_id=1, source_target_pairs={{0,4},{4,0},{8,12},{12,8},{1,5},{5,1},{9,13},{13,9},{2,6},{6,2},{1... | collective-permute-start | bytes 1572872 | tf_op jit(solution)/shard_map/ppermute | solution.py:372
  80.6 31.8 %collective-permute-start.20 = (bf16[512,512]{1,0:T(8,128)(2,1)S(1)}, bf16[512,512]{1,0:T(8,128)(2,1)}, u32[]{:S(2)}, u32[]{:S(2)}) collective-permute-start(bf16[512,512]{1,0:T(8,128)(2,1)S(1)} %regroup.3.refs_4_.refs_0_.refs_2_), channel_id=1, source_target_pairs={{4,8},{8,4},{5,9},{9,5},{6,10},{10,6},{7,11},{11,7},{20,24},{24,20... | collective-permute-start | bytes 1572872 | tf_op jit(solution)/shard_map/ppermute | solution.py:372
  84.1 41.9 %collective-permute-start.17 = (bf16[512,512]{1,0:T(8,128)(2,1)S(1)}, bf16[512,512]{1,0:T(8,128)(2,1)S(1)}, u32[]{:S(2)}, u32[]{:S(2)}) collective-permute-start(bf16[512,512]{1,0:T(8,128)(2,1)S(1)} %collective-permute-done.8.refs_4_.refs_1_), channel_id=1, source_target_pairs={{4,0},{8,12},{5,1},{9,13},{6,2},{10,14},{7,3},{11,15},{20,16},{24,... | collective-permute-start | bytes 1572872 | tf_op jit(solution)/shard_map/ppermute | solution.py:372
  85.4 25.0 %collective-permute-start.15 = (bf16[512,512]{1,0:T(8,128)(2,1)S(1)}, bf16[512,512]{1,0:T(8,128)(2,1)S(1)}, u32[]{:S(2)}, u32[]{:S(2)}) collective-permute-start(bf16[512,512]{1,0:T(8,128)(2,1)S(1)} %collective-permute-done.14.refs_0_.refs_2_), channel_id=1, source_target_pairs={{4,8},{8,4},{5,9},{9,5},{6,10},{10,6},{7,11},{11,7},{20,24},{24,20... | collective-permute-start | bytes 1572872 | tf_op jit(solution)/shard_map/ppermute | solution.py:372
  108.7 37.3 %collective-permute-start.13 = (bf16[2,528,512]{2,1,0:T(8,128)(2,1)S(1)}, bf16[2,528,512]{2,1,0:T(8,128)(2,1)S(1)}, u32[]{:S(2)}, u32[]{:S(2)}) collective-permute-start(bf16[2,528,512]{2,1,0:T(8,128)(2,1)S(1)} %attend.6.refs_8_.refs_0_), channel_id=1, source_target_pairs={{0,4},{12,8},{1,5},{13,9},{2,6},{14,10},{3,7},{15,11},{16,20},{28,... | collective-permute-start | bytes 3244040 | tf_op jit(solution)/shard_map/ppermute | solution.py:372
  111.6 33.0 %collective-permute-start.21 = (bf16[512,512]{1,0:T(8,128)(2,1)S(1)}, bf16[512,512]{1,0:T(8,128)(2,1)S(1)}, u32[]{:S(2)}, u32[]{:S(2)}) collective-permute-start(bf16[512,512]{1,0:T(8,128)(2,1)S(1)} %collective-permute-done.19.refs_0_.refs_2_), channel_id=1, source_target_pairs={{4,8},{8,4},{5,9},{9,5},{6,10},{10,6},{7,11},{11,7},{20,24},{24,20... | collective-permute-start | bytes 1572872 | tf_op jit(solution)/shard_map/ppermute | solution.py:372
  112.4 74.0 %collective-permute-start.26 = (bf16[512,512]{1,0:T(8,128)(2,1)}, bf16[512,512]{1,0:T(8,128)(2,1)}, u32[]{:S(2)}, u32[]{:S(2)}) collective-permute-start(bf16[512,512]{1,0:T(8,128)(2,1)} %collective-permute-done.20.refs_1_), channel_id=1, source_target_pairs={{4,0},{8,12},{5,1},{9,13},{6,2},{10,14},{7,3},{11,15},{20,16},{24,... | collective-permute-start | bytes 1572872 | tf_op jit(solution)/shard_map/ppermute | solution.py:372
  139.4 37.3 %collective-permute-start.24 = (bf16[2,528,512]{2,1,0:T(8,128)(2,1)S(1)}, bf16[2,528,512]{2,1,0:T(8,128)(2,1)S(1)}, u32[]{:S(2)}, u32[]{:S(2)}) collective-permute-start(bf16[2,528,512]{2,1,0:T(8,128)(2,1)S(1)} %attend.8.refs_2_.refs_0_), channel_id=1, source_target_pairs={{0,4},{12,8},{1,5},{13,9},{2,6},{14,10},{3,7},{15,11},{16,20},{28,... | collective-permute-start | bytes 3244040 | tf_op jit(solution)/shard_map/ppermute | solution.py:372
  146.1 29.5 %collective-permute-start.18 = (bf16[2,528,512]{2,1,0:T(8,128)(2,1)S(1)}, bf16[2,528,512]{2,1,0:T(8,128)(2,1)S(1)}, u32[]{:S(2)}, u32[]{:S(2)}) collective-permute-start(bf16[2,528,512]{2,1,0:T(8,128)(2,1)S(1)} %merge.5.refs_8_), channel_id=1, source_target_pairs={{4,8},{8,4},{5,9},{9,5},{6,10},{10,6},{7,11},{11,7},{20,24},{24,20... | collective-permute-start | bytes 3244040 | tf_op jit(solution)/shard_map/ppermute | solution.py:372
  170.3 35.6 %collective-permute-start.27 = (bf16[2,528,512]{2,1,0:T(8,128)(2,1)}, bf16[2,528,512]{2,1,0:T(8,128)(2,1)S(1)}, u32[]{:S(2)}, u32[]{:S(2)}) collective-permute-start(bf16[2,528,512]{2,1,0:T(8,128)(2,1)} %attend.10.refs_2_), channel_id=1, source_target_pairs={{0,4},{4,0},{8,12},{12,8},{1,5},{5,1},{9,13},{13,9},{2,6},{6,2},{1... | collective-permute-start | bytes 3244040 | tf_op jit(solution)/shard_map/ppermute | solution.py:372
  177.9 29.2 %collective-permute-start.25 = (bf16[2,528,512]{2,1,0:T(8,128)(2,1)}, bf16[2,528,512]{2,1,0:T(8,128)(2,1)}, u32[]{:S(2)}, u32[]{:S(2)}) collective-permute-start(bf16[2,528,512]{2,1,0:T(8,128)(2,1)} %merge.7.refs_8_), channel_id=1, source_target_pairs={{4,8},{8,4},{5,9},{9,5},{6,10},{10,6},{7,11},{11,7},{20,24},{24,20... | collective-permute-start | bytes 3244040 | tf_op jit(solution)/shard_map/ppermute | solution.py:372
  179.6 35.0 %collective-permute-start.12 = (bf16[1,528,512]{2,1,0:T(8,128)(2,1)S(1)}, bf16[1,528,512]{2,1,0:T(8,128)(2,1)S(1)}, u32[]{:S(2)}, u32[]{:S(2)}) collective-permute-start(bf16[1,528,512]{2,1,0:T(8,128)(2,1)S(1)} %slice.27), channel_id=1, source_target_pairs={{0,4},{12,8},{1,5},{13,9},{2,6},{14,10},{3,7},{15,11},{16,20},{28,... | collective-permute-start | bytes 1622024 | tf_op jit(solution)/shard_map/ppermute | solution.py:372
  184.2 39.2 %collective-permute-start.28 = (bf16[1,528,512]{2,1,0:T(8,128)(2,1)}, bf16[1,528,512]{2,1,0:T(8,128)(2,1)}, u32[]{:S(2)}, u32[]{:S(2)}) collective-permute-start(bf16[1,528,512]{2,1,0:T(8,128)(2,1)} %slice.28), channel_id=1, source_target_pairs={{0,4},{12,8},{1,5},{13,9},{2,6},{14,10},{3,7},{15,11},{16,20},{28,... | collective-permute-start | bytes 1622024 | tf_op jit(solution)/shard_map/ppermute | solution.py:372
  186.3 28.3 %collective-permute-start.23 = (bf16[1,528,512]{2,1,0:T(8,128)(2,1)S(1)}, bf16[1,528,512]{2,1,0:T(8,128)(2,1)S(1)}, u32[]{:S(2)}, u32[]{:S(2)}) collective-permute-start(bf16[1,528,512]{2,1,0:T(8,128)(2,1)S(1)} %copy-done.18), channel_id=1, source_target_pairs={{4,0},{8,12},{5,1},{9,13},{6,2},{10,14},{7,3},{11,15},{20,16},{24,... | collective-permute-start | bytes 1622024 | tf_op jit(solution)/shard_map/ppermute | solution.py:372
  209.1 22.9 %collective-permute-start.29 = (bf16[1,528,512]{2,1,0:T(8,128)(2,1)}, bf16[1,528,512]{2,1,0:T(8,128)(2,1)}, u32[]{:S(2)}, u32[]{:S(2)}) collective-permute-start(bf16[1,528,512]{2,1,0:T(8,128)(2,1)} %merge.9.refs_5_), channel_id=1, source_target_pairs={{4,0},{8,12},{5,1},{9,13},{6,2},{10,14},{7,3},{11,15},{20,16},{24,... | collective-permute-start | bytes 1622024 | tf_op jit(solution)/shard_map/ppermute | solution.py:372
  210.4 25.6 %collective-permute-start.30 = (bf16[1,528,512]{2,1,0:T(8,128)(2,1)}, bf16[1,528,512]{2,1,0:T(8,128)(2,1)}, u32[]{:S(2)}, u32[]{:S(2)}) collective-permute-start(bf16[1,528,512]{2,1,0:T(8,128)(2,1)} %merge.8.refs_2_), channel_id=1, source_target_pairs={{0,8},{8,0},{4,12},{12,4},{1,9},{9,1},{5,13},{13,5},{2,10},{10,2},... | collective-permute-start | bytes 1622024 | tf_op jit(solution)/shard_map/ppermute | solution.py:372
  215.8 22.0 %all-to-all-start.1 = ((bf16[4,128,512]{2,1,0:T(8,128)(2,1)}), bf16[4,128,512]{2,1,0:T(8,128)(2,1)}, u32[]{:S(2)}, u32[]{:S(2)}) async-start(bf16[4,128,512]{2,1,0:T(8,128)(2,1)} %bitcast.33), calls=%async_computation.1 | async-start | bytes 1048576 | tf_op jit(solution)/shard_map/all_to_all | solution.py:432
  (39 other events, 563.2 us)

commit v9 on v7

--- a/solution.py
+++ b/solution.py
@@ -172,7 +172,7 @@
                 pltpu.VMEM((stat_rows(width), rows), jnp.float32),
             ],
         ),
-        compiler_params=pltpu.CompilerParams(vmem_limit_bytes=28 * MIB),
+        compiler_params=pltpu.CompilerParams(vmem_limit_bytes=22 * MIB),
         cost_estimate=pl.CostEstimate(
             flops=8 * blocks * rows * keys * DH * heads,
             bytes_accessed=4 * blocks * rows * width + 4 * keys * width,
@@ -366,7 +366,10 @@
         return moved.reshape(span_rows, pieces.shape[2])
 
     def to_peers(pieces):
-        return [lax.ppermute(p, "uly", [(i, i ^ k) for i in range(peers)]) if k else p for k, p in enumerate(pieces)]
+        got = {0: pieces[0]}
+        for k in reversed(range(1, peers)):
+            got[k] = lax.ppermute(pieces[k], "uly", [(i, i ^ k) for i in range(peers)])
+        return [got[k] for k in range(peers)]
 
     def send(x, *pairs):
         return lax.ppermute(x, "blk", pairs)
@@ -377,14 +380,14 @@
         far = send(near, (1, 2), (2, 1))
         third_out = send(third, (1, 0), (2, 3))
         far_out = send(far, (1, 0), (2, 3))
-        return dict(own=span, near=near, sent=[[far, third], [far_out, third_out]], early=third, mid=third_out)
+        return dict(own=span, near=near, sent=[[far, third], [far_out, third_out]], early=third, after=near)
 
     def spread_cube(span):
         found = {0: span}
         for bit in reversed(bits):
             for d in list(found):
                 found[d ^ bit] = send(found[d], *[(i, i ^ bit) for i in range(n)])
-        return dict(found=found, early=found[n // 2], mid=found[n // 2])
+        return dict(found=found, early=found[n // 2], after=found[n // 2])
 
     bits = [1 << k for k in range((n - 1).bit_length())]
     line = n == 4
@@ -403,7 +406,7 @@
 
     latest = parts_kv[0]
     for c in range(1, count):
-        latest = run_spread(c, [found[c - 1]["early"], latest])
+        latest = run_spread(c, [found[c - 1]["after"], latest])
     span_k, span_v_t = joined(to_peers(parts_kv), latest)
     context_values_t = context_values.T
     last = [span_k]

time: 256 us -> 256 us (level)
  starting transfers between devices: 76.6 us -> 64.3 us
  waiting for transfers between devices: 36.4 us -> 48.1 us
    ppermute x25, starting transfers between devices: 68.6 us -> 56.5 us  [send(): return lax.ppermute(x, 'blk', pairs)]
    ppermute x25, waiting for transfers between devices: 24.4 us -> 30.3 us  [send(): return lax.ppermute(x, 'blk', pairs)]
    ppermute x6, waiting for transfers between devices: 12 us -> 17.8 us  [to_peers(): got[k] = lax.ppermute(pieces[k], 'uly', [(i, i ^ k) for i in range(peers)])]
  transfers between devices with their start and end apart: 32 -> 32, of which waited for: 7 -> 9; matrix products, arithmetic and copies ran while one was open for 2% -> 2% of each run, Pallas kernels for 33% -> 33%
where the time goes in v9:
time: 256 us; the launch traced here: 254 us
  Pallas kernels  84.1 us (33%)
  starting transfers between devices  64.3 us (25%)
  waiting for transfers between devices  48.1 us (19%)
  blocking collectives  29.8 us (12%)
  local copies, waits for them, and re-layouts  25.5 us (10%)
    pallas_call x6, Pallas kernels, attend(): pl.pallas_call(functools.partial(attend_kernel, [[None] * len(c) for c in...  71.7 us
    ppermute x25, starting transfers between devices, send(): return lax.ppermute(x, 'blk', pairs)  56.5 us
    ppermute x25, waiting for transfers between devices, send(): return lax.ppermute(x, 'blk', pairs)  30.3 us
    unnamed x83, local copies, waits for them, and re-layouts  21.7 us
    ppermute x6, waiting for transfers between devices, to_peers(): got[k] = lax.ppermute(pieces[k], 'uly', [(i, i ^ k) for i in range(peers)])  17.8 us
    all_to_all x1, blocking collectives, run_return(): lax.all_to_all(joint, 'uly', split_axis=0, concat_axis=0, tiled=False)  16.9 us
    all_to_all x1, blocking collectives, to_heads(): lax.all_to_all(pieces, 'uly', split_axis=0, concat_axis=0, tiled=False)  12.9 us
    pallas_call x8, Pallas kernels, join_parts(): pl.pallas_call(functools.partial(join_kernel_of, [len(c) for c in choices...  7.95 us
  transfers between devices with their start and end apart: 32, of which 9 were waited for; matrix products, arithmetic and copies ran while one was open for 2% of the time, Pallas kernels for 33%

profile of v9, /device:TPU:0, one launch (start us, length us, event | category | flops | bytes accessed | tf_op | source)
XLA Modules:
  0.0 254.3 jit_solution(6167604224970808882)
XLA Ops:
  1.3 12.9 %all_to_all.15 = bf16[4,128,512]{2,1,0:T(8,128)(2,1)S(1)} all-to-all(bf16[4,128,512]{2,1,0:T(8,128)(2,1)S(1)} %pad_maximum_fusion.1), channel_id=1, replica_groups=mesh['cfg'=2,'blk'=4,'uly'=4] {'uly'}, dimensions={0} | all-to-all | bytes 1048576 | tf_op jit(solution)/shard_map/all_to_all | solution.py:365
  15.7 3.7 %collective-permute-start = (bf16[512,512]{1,0:T(8,128)(2,1)S(1)}, bf16[512,512]{1,0:T(8,128)(2,1)}, u32[]{:S(2)}, u32[]{:S(2)}) collective-permute-start(bf16[512,512]{1,0:T(8,128)(2,1)S(1)} %bitcast.35), channel_id=1, source_target_pairs={{0,4},{4,0},{8,12},{12,8},{1,5},{5,1},{9,13},{13,9},{2,6},{6,2},{1... | collective-permute-start | bytes 1572872 | tf_op jit(solution)/shard_map/ppermute | solution.py:375
  21.4 7.3 %collective-permute-done.2.refs_10_.refs_2_ = bf16[128,1024]{1,0:T(8,128)(2,1)S(1)} collective-permute-done((bf16[128,1024]{1,0:T(8,128)(2,1)S(1)}, bf16[128,1024]{1,0:T(8,128)(2,1)S(1)}, u32[]{:S(2)}, u32[]{:S(2)}) %collective-permute-start.2) | collective-permute-done | bytes 262176 | tf_op jit(solution)/shard_map/ppermute | solution.py:371
  28.7 4.7 %collective-permute-done.3.refs_11_.refs_3_ = bf16[128,1024]{1,0:T(8,128)(2,1)S(1)} collective-permute-done((bf16[128,1024]{1,0:T(8,128)(2,1)S(1)}, bf16[128,1024]{1,0:T(8,128)(2,1)S(1)}, u32[]{:S(2)}, u32[]{:S(2)}) %collective-permute-start.3) | collective-permute-done | bytes 262176 | tf_op jit(solution)/shard_map/ppermute | solution.py:371
  39.6 10.8 %collective-permute-done.8.refs_4_.refs_0_.refs_2_ = bf16[512,512]{1,0:T(8,128)(2,1)S(1)} collective-permute-done((bf16[512,512]{1,0:T(8,128)(2,1)}, bf16[512,512]{1,0:T(8,128)(2,1)S(1)}, u32[]{:S(2)}, u32[]{:S(2)}) %collective-permute-start.8) | collective-permute-done | bytes 524320 | tf_op jit(solution)/shard_map/ppermute | solution.py:375
  56.6 3.2 %copy.11 = bf16[1024,1536]{0,1:T(8,128)(2,1)S(1)} copy(bf16[1024,1536]{1,0:T(8,128)(2,1)} %param.10) | data formatting | bytes 6291456 | tf_op args[4]
  63.8 4.3 %collective-permute-start.19 = (bf16[512,512]{1,0:T(8,128)(2,1)S(1)}, bf16[512,512]{1,0:T(8,128)(2,1)S(1)}, u32[]{:S(2)}, u32[]{:S(2)}) collective-permute-start(bf16[512,512]{1,0:T(8,128)(2,1)S(1)} %regroup.3.refs_4_.refs_0_.refs_2_), channel_id=1, source_target_pairs={{0,4},{4,0},{8,12},{12,8},{1,5},{5,1},{9,13},{13,9},{2,6},{6,2},{1... | collective-permute-start | bytes 1572872 | tf_op jit(solution)/shard_map/ppermute | solution.py:375
  68.0 5.8 %collective-permute-done.7.refs_3_ = bf16[256,1536]{1,0:T(8,128)(2,1)} collective-permute-done((bf16[256,1536]{1,0:T(8,128)(2,1)}, bf16[256,1536]{1,0:T(8,128)(2,1)}, u32[]{:S(2)}, u32[]{:S(2)}) %collective-permute-start.7) | collective-permute-done | bytes 786464 | tf_op jit(solution)/shard_map/ppermute | solution.py:371
  81.0 12.2 %attend.6.refs_8_.refs_0_ = bf16[2,528,512]{2,1,0:T(8,128)(2,1)S(1)} custom-call(s32[3]{0:T(128)S(1)} %pad_add_fusion.2.table_ref, s32[16,12]{1,0:T(8,128)S(1)} %fusion.kept_ref, bf16[512,512]{1,0:T(8,128)(2,1)} %collective-permute-done.9.refs_0_, bf16[512,512]{1,0:T(8,128)(2,1)} %collective-permute-done.4.refs_12_.refs_1_, ...), custom_call_target="tpu_custom_call" | custom-call | flops 6442450944 | bytes 5242880 | tf_op jit(solution)/shard_map/attend/pallas_call | solution.py:151
  93.2 5.8 %collective-permute-start.13 = (bf16[2,528,512]{2,1,0:T(8,128)(2,1)S(1)}, bf16[2,528,512]{2,1,0:T(8,128)(2,1)S(1)}, u32[]{:S(2)}, u32[]{:S(2)}) collective-permute-start(bf16[2,528,512]{2,1,0:T(8,128)(2,1)S(1)} %attend.6.refs_8_.refs_0_), channel_id=1, source_target_pairs={{0,4},{12,8},{1,5},{13,9},{2,6},{14,10},{3,7},{15,11},{16,20},{28,... | collective-permute-start | bytes 3244040 | tf_op jit(solution)/shard_map/ppermute | solution.py:375
  104.2 11.9 %attend.7.refs_8_.refs_0_.refs_3_ = bf16[2,528,512]{2,1,0:T(8,128)(2,1)S(1)} custom-call(s32[3]{0:T(128)S(1)} %pad_add_fusion.table_ref, s32[16,12]{1,0:T(8,128)S(1)} %fusion.kept_ref, bf16[512,512]{1,0:T(8,128)(2,1)} %collective-permute-done.refs_4_.refs_0_.refs_2_, bf16[512,512]{1,0:T(8,128)(2,1)S(1)} %bitcast.37, ...), custom_call_target="tpu_custom_call" | custom-call | flops 6442450944 | bytes 5242880 | tf_op jit(solution)/shard_map/attend/pallas_call | solution.py:151
  117.3 11.7 %attend.8.refs_2_.refs_0_ = bf16[2,528,512]{2,1,0:T(8,128)(2,1)S(1)} custom-call(s32[3]{0:T(128)S(1)} %pad_add_fusion.2.table_ref, s32[16,12]{1,0:T(8,128)S(1)} %fusion.kept_ref, bf16[512,512]{1,0:T(8,128)(2,1)S(1)} %collective-permute-done.14.refs_0_, bf16[512,512]{1,0:T(8,128)(2,1)} %collective-permute-done.15.refs_1_, ...), custom_call_target="tpu_custom_call" | custom-call | flops 6442450944 | bytes 5242880 | tf_op jit(solution)/shard_map/attend/pallas_call | solution.py:151
  128.9 8.7 %collective-permute-start.24 = (bf16[2,528,512]{2,1,0:T(8,128)(2,1)S(1)}, bf16[2,528,512]{2,1,0:T(8,128)(2,1)S(1)}, u32[]{:S(2)}, u32[]{:S(2)}) collective-permute-start(bf16[2,528,512]{2,1,0:T(8,128)(2,1)S(1)} %attend.8.refs_2_.refs_0_), channel_id=1, source_target_pairs={{0,4},{12,8},{1,5},{13,9},{2,6},{14,10},{3,7},{15,11},{16,20},{28,... | collective-permute-start | bytes 3244040 | tf_op jit(solution)/shard_map/ppermute | solution.py:375
  140.0 11.8 %attend.9.refs_8_.refs_0_.refs_3_ = bf16[2,528,512]{2,1,0:T(8,128)(2,1)S(1)} custom-call(s32[3]{0:T(128)S(1)} %pad_add_fusion.table_ref, s32[16,12]{1,0:T(8,128)S(1)} %fusion.kept_ref, bf16[512,512]{1,0:T(8,128)(2,1)S(1)} %copy-done.32, bf16[512,512]{1,0:T(8,128)(2,1)} %regroup.2.refs_5_.refs_1_.refs_3_, bf16[512,512]{1,0:T(8,128)(2,1)S(1)} %copy-done.32, ...), custom_call_target="tpu_custom_call" | custom-call | flops 6442450944 | bytes 5242880 | tf_op jit(solution)/shard_map/attend/pallas_call | solution.py:151
  153.3 12.5 %attend.10.refs_2_ = bf16[2,528,512]{2,1,0:T(8,128)(2,1)} custom-call(s32[3]{0:T(128)S(1)} %pad_add_fusion.3.table_ref, s32[16,12]{1,0:T(8,128)S(1)} %fusion.kept_ref, bf16[512,512]{1,0:T(8,128)(2,1)S(1)} %collective-permute-done.19.refs_0_.refs_2_, bf16[512,512]{1,0:T(8,128)(2,1)} %collective-permute-done.20.refs_1_, ...), custom_call_target="tpu_custom_call" | custom-call | flops 6442450944 | bytes 5242880 | tf_op jit(solution)/shard_map/attend/pallas_call | solution.py:151
  165.8 3.4 %collective-permute-start.27 = (bf16[2,528,512]{2,1,0:T(8,128)(2,1)}, bf16[2,528,512]{2,1,0:T(8,128)(2,1)S(1)}, u32[]{:S(2)}, u32[]{:S(2)}) collective-permute-start(bf16[2,528,512]{2,1,0:T(8,128)(2,1)} %attend.10.refs_2_), channel_id=1, source_target_pairs={{0,4},{4,0},{8,12},{12,8},{1,5},{5,1},{9,13},{13,9},{2,6},{6,2},{1... | collective-permute-start | bytes 3244040 | tf_op jit(solution)/shard_map/ppermute | solution.py:375
  173.2 4.2 %collective-permute-start.12 = (bf16[1,528,512]{2,1,0:T(8,128)(2,1)S(1)}, bf16[1,528,512]{2,1,0:T(8,128)(2,1)S(1)}, u32[]{:S(2)}, u32[]{:S(2)}) collective-permute-start(bf16[1,528,512]{2,1,0:T(8,128)(2,1)S(1)} %slice.27), channel_id=1, source_target_pairs={{0,4},{12,8},{1,5},{13,9},{2,6},{14,10},{3,7},{15,11},{16,20},{28,... | collective-permute-start | bytes 1622024 | tf_op jit(solution)/shard_map/ppermute | solution.py:375
  178.3 2.1 collective-permute-start.28
  188.3 11.7 %attend.11.refs_0_.refs_2_.refs_4_.refs_3_ = bf16[2,528,512]{2,1,0:T(8,128)(2,1)S(1)} custom-call(s32[3]{0:T(128)S(1)} %pad_add_fusion.4.table_ref, s32[16,12]{1,0:T(8,128)S(1)} %fusion.kept_ref, bf16[512,512]{1,0:T(8,128)(2,1)S(1)} %copy-done.25, bf16[512,512]{1,0:T(8,128)(2,1)S(1)} %copy-done.40, bf16[512,512]{1,0:T(8,128)(2,1)S(1)} %copy-done.25, ...), custom_call_target="tpu_custom_call" | custom-call | flops 6442450944 | bytes 5242880 | tf_op jit(solution)/shard_map/attend/pallas_call | solution.py:151
  204.4 4.2 %collective-permute-start.30 = (bf16[1,528,512]{2,1,0:T(8,128)(2,1)}, bf16[1,528,512]{2,1,0:T(8,128)(2,1)}, u32[]{:S(2)}, u32[]{:S(2)}) collective-permute-start(bf16[1,528,512]{2,1,0:T(8,128)(2,1)} %merge.8.refs_2_), channel_id=1, source_target_pairs={{0,8},{8,0},{4,12},{12,4},{1,9},{9,1},{5,13},{13,5},{2,10},{10,2},... | collective-permute-start | bytes 1622024 | tf_op jit(solution)/shard_map/ppermute | solution.py:375
  209.8 4.1 %all-to-all-start.1 = ((bf16[4,128,512]{2,1,0:T(8,128)(2,1)}), bf16[4,128,512]{2,1,0:T(8,128)(2,1)}, u32[]{:S(2)}, u32[]{:S(2)}) async-start(bf16[4,128,512]{2,1,0:T(8,128)(2,1)} %bitcast.26), calls=%async_computation.1 | async-start | bytes 1048576 | tf_op jit(solution)/shard_map/all_to_all | solution.py:433
  214.0 3.0 %collective-permute-done.28.refs_1_ = bf16[1,528,512]{2,1,0:T(8,128)(2,1)} collective-permute-done((bf16[1,528,512]{2,1,0:T(8,128)(2,1)}, bf16[1,528,512]{2,1,0:T(8,128)(2,1)}, u32[]{:S(2)}, u32[]{:S(2)}) %collective-permute-start.28) | collective-permute-done | bytes 540704 | tf_op jit(solution)/shard_map/ppermute | solution.py:375
  217.0 12.1 %collective-permute-done.29.refs_4_ = bf16[1,528,512]{2,1,0:T(8,128)(2,1)} collective-permute-done((bf16[1,528,512]{2,1,0:T(8,128)(2,1)}, bf16[1,528,512]{2,1,0:T(8,128)(2,1)}, u32[]{:S(2)}, u32[]{:S(2)}) %collective-permute-start.29) | collective-permute-done | bytes 540704 | tf_op jit(solution)/shard_map/ppermute | solution.py:375
  234.9 16.9 %all_to_all.16 = bf16[4,128,1024]{2,1,0:T(8,128)(2,1)S(1)} all-to-all(bf16[4,128,1024]{2,1,0:T(8,128)(2,1)S(1)} %pad_maximum_fusion), channel_id=1, replica_groups=mesh['cfg'=2,'blk'=4,'uly'=4] {'uly'}, dimensions={0} | all-to-all | bytes 2097152 | tf_op jit(solution)/shard_map/all_to_all | solution.py:433
  (163 shorter events, 64.8 us)
Async XLA Ops:
  14.2 19.2 %collective-permute-start.4 = (bf16[512,512]{1,0:T(8,128)(2,1)S(1)}, bf16[512,512]{1,0:T(8,128)(2,1)}, u32[]{:S(2)}, u32[]{:S(2)}) collective-permute-start(bf16[512,512]{1,0:T(8,128)(2,1)S(1)} %bitcast.34), channel_id=1, source_target_pairs={{4,8},{8,4},{5,9},{9,5},{6,10},{10,6},{7,11},{11,7},{20,24},{24,20... | collective-permute-start | bytes 1572872 | tf_op jit(solution)/shard_map/ppermute | solution.py:375
  15.7 19.6 %collective-permute-start = (bf16[512,512]{1,0:T(8,128)(2,1)S(1)}, bf16[512,512]{1,0:T(8,128)(2,1)}, u32[]{:S(2)}, u32[]{:S(2)}) collective-permute-start(bf16[512,512]{1,0:T(8,128)(2,1)S(1)} %bitcast.35), channel_id=1, source_target_pairs={{0,4},{4,0},{8,12},{12,8},{1,5},{5,1},{9,13},{13,9},{2,6},{6,2},{1... | collective-permute-start | bytes 1572872 | tf_op jit(solution)/shard_map/ppermute | solution.py:375
  37.8 26.0 %collective-permute-start.6 = (bf16[256,1536]{1,0:T(8,128)(2,1)}, bf16[256,1536]{1,0:T(8,128)(2,1)}, u32[]{:S(2)}, u32[]{:S(2)}) collective-permute-start(bf16[256,1536]{1,0:T(8,128)(2,1)} %get-tuple-element.21), channel_id=1, source_target_pairs={{0,2},{1,3},{2,0},{3,1},{4,6},{5,7},{6,4},{7,5},{8,10},{9,11},{10,... | collective-permute-start | bytes 2359304 | tf_op jit(solution)/shard_map/ppermute | solution.py:371
  38.1 35.7 %collective-permute-start.7 = (bf16[256,1536]{1,0:T(8,128)(2,1)}, bf16[256,1536]{1,0:T(8,128)(2,1)}, u32[]{:S(2)}, u32[]{:S(2)}) collective-permute-start(bf16[256,1536]{1,0:T(8,128)(2,1)} %get-tuple-element.22), channel_id=1, source_target_pairs={{0,3},{1,2},{2,1},{3,0},{4,7},{5,6},{6,5},{7,4},{8,11},{9,10},{10,... | collective-permute-start | bytes 2359304 | tf_op jit(solution)/shard_map/ppermute | solution.py:371
  51.3 26.7 %collective-permute-start.15 = (bf16[512,512]{1,0:T(8,128)(2,1)}, bf16[512,512]{1,0:T(8,128)(2,1)}, u32[]{:S(2)}, u32[]{:S(2)}) collective-permute-start(bf16[512,512]{1,0:T(8,128)(2,1)} %regroup.2.refs_5_.refs_1_.refs_3_), channel_id=1, source_target_pairs={{4,8},{8,4},{5,9},{9,5},{6,10},{10,6},{7,11},{11,7},{20,24},{24,20... | collective-permute-start | bytes 1572872 | tf_op jit(solution)/shard_map/ppermute | solution.py:375
  52.7 24.5 %collective-permute-start.11 = (bf16[512,512]{1,0:T(8,128)(2,1)}, bf16[512,512]{1,0:T(8,128)(2,1)}, u32[]{:S(2)}, u32[]{:S(2)}) collective-permute-start(bf16[512,512]{1,0:T(8,128)(2,1)} %collective-permute-done.4.refs_12_.refs_1_), channel_id=1, source_target_pairs={{4,0},{8,12},{5,1},{9,13},{6,2},{10,14},{7,3},{11,15},{20,16},{24,... | collective-permute-start | bytes 1572872 | tf_op jit(solution)/shard_map/ppermute | solution.py:375
  54.9 26.1 %collective-permute-start.10 = (bf16[512,512]{1,0:T(8,128)(2,1)}, bf16[512,512]{1,0:T(8,128)(2,1)}, u32[]{:S(2)}, u32[]{:S(2)}) collective-permute-start(bf16[512,512]{1,0:T(8,128)(2,1)} %collective-permute-done.9.refs_0_), channel_id=1, source_target_pairs={{4,0},{8,12},{5,1},{9,13},{6,2},{10,14},{7,3},{11,15},{20,16},{24,... | collective-permute-start | bytes 1572872 | tf_op jit(solution)/shard_map/ppermute | solution.py:375
  63.8 36.5 %collective-permute-start.19 = (bf16[512,512]{1,0:T(8,128)(2,1)S(1)}, bf16[512,512]{1,0:T(8,128)(2,1)S(1)}, u32[]{:S(2)}, u32[]{:S(2)}) collective-permute-start(bf16[512,512]{1,0:T(8,128)(2,1)S(1)} %regroup.3.refs_4_.refs_0_.refs_2_), channel_id=1, source_target_pairs={{0,4},{4,0},{8,12},{12,8},{1,5},{5,1},{9,13},{13,9},{2,6},{6,2},{1... | collective-permute-start | bytes 1572872 | tf_op jit(solution)/shard_map/ppermute | solution.py:375
  73.8 27.2 %collective-permute-start.20 = (bf16[512,512]{1,0:T(8,128)(2,1)S(1)}, bf16[512,512]{1,0:T(8,128)(2,1)}, u32[]{:S(2)}, u32[]{:S(2)}) collective-permute-start(bf16[512,512]{1,0:T(8,128)(2,1)S(1)} %regroup.3.refs_4_.refs_0_.refs_2_), channel_id=1, source_target_pairs={{4,8},{8,4},{5,9},{9,5},{6,10},{10,6},{7,11},{11,7},{20,24},{24,20... | collective-permute-start | bytes 1572872 | tf_op jit(solution)/shard_map/ppermute | solution.py:375
  77.2 21.8 %collective-permute-start.14 = (bf16[512,512]{1,0:T(8,128)(2,1)S(1)}, bf16[512,512]{1,0:T(8,128)(2,1)S(1)}, u32[]{:S(2)}, u32[]{:S(2)}) collective-permute-start(bf16[512,512]{1,0:T(8,128)(2,1)S(1)} %copy-done.32), channel_id=1, source_target_pairs={{4,8},{8,4},{5,9},{9,5},{6,10},{10,6},{7,11},{11,7},{20,24},{24,20... | collective-permute-start | bytes 1572872 | tf_op jit(solution)/shard_map/ppermute | solution.py:375
  78.0 38.2 %collective-permute-start.17 = (bf16[512,512]{1,0:T(8,128)(2,1)}, bf16[512,512]{1,0:T(8,128)(2,1)S(1)}, u32[]{:S(2)}, u32[]{:S(2)}) collective-permute-start(bf16[512,512]{1,0:T(8,128)(2,1)} %collective-permute-done.15.refs_1_), channel_id=1, source_target_pairs={{4,0},{8,12},{5,1},{9,13},{6,2},{10,14},{7,3},{11,15},{20,16},{24,... | collective-permute-start | bytes 1572872 | tf_op jit(solution)/shard_map/ppermute | solution.py:375
  93.2 45.8 %collective-permute-start.13 = (bf16[2,528,512]{2,1,0:T(8,128)(2,1)S(1)}, bf16[2,528,512]{2,1,0:T(8,128)(2,1)S(1)}, u32[]{:S(2)}, u32[]{:S(2)}) collective-permute-start(bf16[2,528,512]{2,1,0:T(8,128)(2,1)S(1)} %attend.6.refs_8_.refs_0_), channel_id=1, source_target_pairs={{0,4},{12,8},{1,5},{13,9},{2,6},{14,10},{3,7},{15,11},{16,20},{28,... | collective-permute-start | bytes 3244040 | tf_op jit(solution)/shard_map/ppermute | solution.py:375
  100.3 37.4 %collective-permute-start.21 = (bf16[512,512]{1,0:T(8,128)(2,1)S(1)}, bf16[512,512]{1,0:T(8,128)(2,1)S(1)}, u32[]{:S(2)}, u32[]{:S(2)}) collective-permute-start(bf16[512,512]{1,0:T(8,128)(2,1)S(1)} %collective-permute-done.19.refs_0_.refs_2_), channel_id=1, source_target_pairs={{4,8},{8,4},{5,9},{9,5},{6,10},{10,6},{7,11},{11,7},{20,24},{24,20... | collective-permute-start | bytes 1572872 | tf_op jit(solution)/shard_map/ppermute | solution.py:375
  101.0 79.3 %collective-permute-start.26 = (bf16[512,512]{1,0:T(8,128)(2,1)}, bf16[512,512]{1,0:T(8,128)(2,1)}, u32[]{:S(2)}, u32[]{:S(2)}) collective-permute-start(bf16[512,512]{1,0:T(8,128)(2,1)} %collective-permute-done.20.refs_1_), channel_id=1, source_target_pairs={{4,0},{8,12},{5,1},{9,13},{6,2},{10,14},{7,3},{11,15},{20,16},{24,... | collective-permute-start | bytes 1572872 | tf_op jit(solution)/shard_map/ppermute | solution.py:375
  128.9 41.3 %collective-permute-start.24 = (bf16[2,528,512]{2,1,0:T(8,128)(2,1)S(1)}, bf16[2,528,512]{2,1,0:T(8,128)(2,1)S(1)}, u32[]{:S(2)}, u32[]{:S(2)}) collective-permute-start(bf16[2,528,512]{2,1,0:T(8,128)(2,1)S(1)} %attend.8.refs_2_.refs_0_), channel_id=1, source_target_pairs={{0,4},{12,8},{1,5},{13,9},{2,6},{14,10},{3,7},{15,11},{16,20},{28,... | collective-permute-start | bytes 3244040 | tf_op jit(solution)/shard_map/ppermute | solution.py:375
  139.1 30.1 %collective-permute-start.18 = (bf16[2,528,512]{2,1,0:T(8,128)(2,1)S(1)}, bf16[2,528,512]{2,1,0:T(8,128)(2,1)S(1)}, u32[]{:S(2)}, u32[]{:S(2)}) collective-permute-start(bf16[2,528,512]{2,1,0:T(8,128)(2,1)S(1)} %merge.5.refs_8_), channel_id=1, source_target_pairs={{4,8},{8,4},{5,9},{9,5},{6,10},{10,6},{7,11},{11,7},{20,24},{24,20... | collective-permute-start | bytes 3244040 | tf_op jit(solution)/shard_map/ppermute | solution.py:375
  165.8 34.2 %collective-permute-start.27 = (bf16[2,528,512]{2,1,0:T(8,128)(2,1)}, bf16[2,528,512]{2,1,0:T(8,128)(2,1)S(1)}, u32[]{:S(2)}, u32[]{:S(2)}) collective-permute-start(bf16[2,528,512]{2,1,0:T(8,128)(2,1)} %attend.10.refs_2_), channel_id=1, source_target_pairs={{0,4},{4,0},{8,12},{12,8},{1,5},{5,1},{9,13},{13,9},{2,6},{6,2},{1... | collective-permute-start | bytes 3244040 | tf_op jit(solution)/shard_map/ppermute | solution.py:375
  171.4 29.7 %collective-permute-start.25 = (bf16[2,528,512]{2,1,0:T(8,128)(2,1)}, bf16[2,528,512]{2,1,0:T(8,128)(2,1)}, u32[]{:S(2)}, u32[]{:S(2)}) collective-permute-start(bf16[2,528,512]{2,1,0:T(8,128)(2,1)} %merge.7.refs_8_), channel_id=1, source_target_pairs={{4,8},{8,4},{5,9},{9,5},{6,10},{10,6},{7,11},{11,7},{20,24},{24,20... | collective-permute-start | bytes 3244040 | tf_op jit(solution)/shard_map/ppermute | solution.py:375
  173.2 35.4 %collective-permute-start.12 = (bf16[1,528,512]{2,1,0:T(8,128)(2,1)S(1)}, bf16[1,528,512]{2,1,0:T(8,128)(2,1)S(1)}, u32[]{:S(2)}, u32[]{:S(2)}) collective-permute-start(bf16[1,528,512]{2,1,0:T(8,128)(2,1)S(1)} %slice.27), channel_id=1, source_target_pairs={{0,4},{12,8},{1,5},{13,9},{2,6},{14,10},{3,7},{15,11},{16,20},{28,... | collective-permute-start | bytes 1622024 | tf_op jit(solution)/shard_map/ppermute | solution.py:375
  178.3 38.7 %collective-permute-start.28 = (bf16[1,528,512]{2,1,0:T(8,128)(2,1)}, bf16[1,528,512]{2,1,0:T(8,128)(2,1)}, u32[]{:S(2)}, u32[]{:S(2)}) collective-permute-start(bf16[1,528,512]{2,1,0:T(8,128)(2,1)} %slice.28), channel_id=1, source_target_pairs={{0,4},{12,8},{1,5},{13,9},{2,6},{14,10},{3,7},{15,11},{16,20},{28,... | collective-permute-start | bytes 1622024 | tf_op jit(solution)/shard_map/ppermute | solution.py:375
  180.4 28.2 %collective-permute-start.23 = (bf16[1,528,512]{2,1,0:T(8,128)(2,1)S(1)}, bf16[1,528,512]{2,1,0:T(8,128)(2,1)S(1)}, u32[]{:S(2)}, u32[]{:S(2)}) collective-permute-start(bf16[1,528,512]{2,1,0:T(8,128)(2,1)S(1)} %copy-done.23), channel_id=1, source_target_pairs={{4,0},{8,12},{5,1},{9,13},{6,2},{10,14},{7,3},{11,15},{20,16},{24,... | collective-permute-start | bytes 1622024 | tf_op jit(solution)/shard_map/ppermute | solution.py:375
  203.1 25.9 %collective-permute-start.29 = (bf16[1,528,512]{2,1,0:T(8,128)(2,1)}, bf16[1,528,512]{2,1,0:T(8,128)(2,1)}, u32[]{:S(2)}, u32[]{:S(2)}) collective-permute-start(bf16[1,528,512]{2,1,0:T(8,128)(2,1)} %merge.9.refs_5_), channel_id=1, source_target_pairs={{4,0},{8,12},{5,1},{9,13},{6,2},{10,14},{7,3},{11,15},{20,16},{24,... | collective-permute-start | bytes 1622024 | tf_op jit(solution)/shard_map/ppermute | solution.py:375
  204.4 28.7 %collective-permute-start.30 = (bf16[1,528,512]{2,1,0:T(8,128)(2,1)}, bf16[1,528,512]{2,1,0:T(8,128)(2,1)}, u32[]{:S(2)}, u32[]{:S(2)}) collective-permute-start(bf16[1,528,512]{2,1,0:T(8,128)(2,1)} %merge.8.refs_2_), channel_id=1, source_target_pairs={{0,8},{8,0},{4,12},{12,4},{1,9},{9,1},{5,13},{13,5},{2,10},{10,2},... | collective-permute-start | bytes 1622024 | tf_op jit(solution)/shard_map/ppermute | solution.py:375
  209.8 25.1 %all-to-all-start.1 = ((bf16[4,128,512]{2,1,0:T(8,128)(2,1)}), bf16[4,128,512]{2,1,0:T(8,128)(2,1)}, u32[]{:S(2)}, u32[]{:S(2)}) async-start(bf16[4,128,512]{2,1,0:T(8,128)(2,1)} %bitcast.26), calls=%async_computation.1 | async-start | bytes 1048576 | tf_op jit(solution)/shard_map/all_to_all | solution.py:433
  (49 other events, 582.0 us)

commit v10 on v7

--- a/solution.py
+++ b/solution.py
@@ -479,17 +479,17 @@
         run_sent(1)
         run_cross(0)
         run_kept(1)
+        run_cross(1)
         run_halves(2)
         run_outward(0)
-        run_cross(1)
         run_halves_kept(2)
+        run_outward(1)
         run_halves_join(2)
-        run_outward(1)
         run_finish(0)
-        run_return(0)
         run_finish(1)
+        run_return(0, 1)
         run_halves_finish(2)
-        run_return(1, 2)
+        run_return(2)
     else:
         for c in range(count):
             parts = {d: [] for d in range(n)}

time: 256 us -> 278 us (1.086)
  waiting for transfers between devices: 36.4 us -> 52.2 us
  Pallas kernels: 83.5 us -> 88.8 us
  starting transfers between devices: 76.6 us -> 81.4 us
  local copies, waits for them, and re-layouts: 25.5 us -> 22.5 us
    ppermute x25, waiting for transfers between devices: 24.4 us -> 35.2 us  [send(): return lax.ppermute(x, 'blk', pairs)]
    all_to_all x1, waiting for transfers between devices: 0.01 us -> 8.66 us  [run_return(): lax.all_to_all(joint, 'uly', split_axis=0, concat_axis=0, tiled=False)]
    ppermute x25, starting transfers between devices: 68.6 us -> 74 us  [send(): return lax.ppermute(x, 'blk', pairs)]
    ppermute x6, waiting for transfers between devices: 12 us -> 8.39 us  [to_peers(): lax.ppermute(p, 'uly', [(i, i ^ k) for i in range(peers)])]
    pallas_call x8, Pallas kernels: 7.95 us -> 10.8 us  [join_parts(): pl.pallas_call(functools.partial(join_kernel_of, [len(c) for c in choices...]
    unnamed x83 -> x73, local copies, waits for them, and re-layouts: 21.7 us -> 19.6 us
  transfers between devices with their start and end apart: 32 -> 32, of which waited for: 7 -> 9; matrix products, arithmetic and copies ran while one was open for 2% -> 2% of each run, Pallas kernels for 33% -> 32%
where the time goes in v10:
time: 278 us; the launch traced here: 276 us
  Pallas kernels  88.8 us (32%)
  starting transfers between devices  81.4 us (29%)
  waiting for transfers between devices  52.2 us (19%)
  blocking collectives  29.8 us (11%)
  local copies, waits for them, and re-layouts  22.5 us (8%)
    ppermute x25, starting transfers between devices, send(): return lax.ppermute(x, 'blk', pairs)  74 us
    pallas_call x6, Pallas kernels, attend(): pl.pallas_call(functools.partial(attend_kernel, [[None] * len(c) for c in...  72.9 us
    ppermute x25, waiting for transfers between devices, send(): return lax.ppermute(x, 'blk', pairs)  35.2 us
    unnamed x73, local copies, waits for them, and re-layouts  19.6 us
    all_to_all x1, blocking collectives, run_return(): lax.all_to_all(joint, 'uly', split_axis=0, concat_axis=0, tiled=False)  16.9 us
    all_to_all x1, blocking collectives, to_heads(): lax.all_to_all(pieces, 'uly', split_axis=0, concat_axis=0, tiled=False)  12.9 us
    pallas_call x8, Pallas kernels, join_parts(): pl.pallas_call(functools.partial(join_kernel_of, [len(c) for c in choices...  10.8 us
    all_to_all x1, waiting for transfers between devices, run_return(): lax.all_to_all(joint, 'uly', split_axis=0, concat_axis=0, tiled=False)  8.66 us
  transfers between devices with their start and end apart: 32, of which 9 were waited for; matrix products, arithmetic and copies ran while one was open for 2% of the time, Pallas kernels for 32%

profile of v10, /device:TPU:0, one launch (start us, length us, event | category | flops | bytes accessed | tf_op | source)
XLA Modules:
  0.0 276.1 jit_solution(12252535850055038105)
XLA Ops:
  1.3 12.9 %all_to_all.15 = bf16[4,128,512]{2,1,0:T(8,128)(2,1)S(1)} all-to-all(bf16[4,128,512]{2,1,0:T(8,128)(2,1)S(1)} %pad_maximum_fusion.1), channel_id=1, replica_groups=mesh['cfg'=2,'blk'=4,'uly'=4] {'uly'}, dimensions={0} | all-to-all | bytes 1048576 | tf_op jit(solution)/shard_map/all_to_all | solution.py:365
  17.7 3.6 %collective-permute-start = (bf16[512,512]{1,0:T(8,128)(2,1)S(1)}, bf16[512,512]{1,0:T(8,128)(2,1)}, u32[]{:S(2)}, u32[]{:S(2)}) collective-permute-start(bf16[512,512]{1,0:T(8,128)(2,1)S(1)} %bitcast.35), channel_id=1, source_target_pairs={{0,4},{4,0},{8,12},{12,8},{1,5},{5,1},{9,13},{13,9},{2,6},{6,2},{1... | collective-permute-start | bytes 1572872 | tf_op jit(solution)/shard_map/ppermute | solution.py:372
  21.4 3.7 %collective-permute-done.2.refs_10_.refs_2_ = bf16[128,1024]{1,0:T(8,128)(2,1)S(1)} collective-permute-done((bf16[128,1024]{1,0:T(8,128)(2,1)S(1)}, bf16[128,1024]{1,0:T(8,128)(2,1)S(1)}, u32[]{:S(2)}, u32[]{:S(2)}) %collective-permute-start.2) | collective-permute-done | bytes 262176 | tf_op jit(solution)/shard_map/ppermute | solution.py:369
  25.0 4.7 %collective-permute-done.3.refs_11_.refs_3_ = bf16[128,1024]{1,0:T(8,128)(2,1)S(1)} collective-permute-done((bf16[128,1024]{1,0:T(8,128)(2,1)S(1)}, bf16[128,1024]{1,0:T(8,128)(2,1)S(1)}, u32[]{:S(2)}, u32[]{:S(2)}) %collective-permute-start.3) | collective-permute-done | bytes 262176 | tf_op jit(solution)/shard_map/ppermute | solution.py:369
  38.2 16.7 %collective-permute-start.14 = (bf16[512,512]{1,0:T(8,128)(2,1)}, bf16[512,512]{1,0:T(8,128)(2,1)}, u32[]{:S(2)}, u32[]{:S(2)}) collective-permute-start(bf16[512,512]{1,0:T(8,128)(2,1)} %regroup.2.refs_5_.refs_1_.refs_3_), channel_id=1, source_target_pairs={{0,4},{4,0},{8,12},{12,8},{1,5},{5,1},{9,13},{13,9},{2,6},{6,2},{1... | collective-permute-start | bytes 1572872 | tf_op jit(solution)/shard_map/ppermute | solution.py:372
  58.8 3.2 %copy.11 = bf16[1024,1536]{0,1:T(8,128)(2,1)S(1)} copy(bf16[1024,1536]{1,0:T(8,128)(2,1)} %param.10) | data formatting | bytes 6291456 | tf_op args[4]
  66.8 11.2 %collective-permute-start.19 = (bf16[512,512]{1,0:T(8,128)(2,1)}, bf16[512,512]{1,0:T(8,128)(2,1)}, u32[]{:S(2)}, u32[]{:S(2)}) collective-permute-start(bf16[512,512]{1,0:T(8,128)(2,1)} %regroup.3.refs_4_.refs_0_.refs_2_), channel_id=1, source_target_pairs={{0,4},{4,0},{8,12},{12,8},{1,5},{5,1},{9,13},{13,9},{2,6},{6,2},{1... | collective-permute-start | bytes 1572872 | tf_op jit(solution)/shard_map/ppermute | solution.py:372
  83.4 6.7 %collective-permute-done.10.refs_2_ = bf16[512,512]{1,0:T(8,128)(2,1)} collective-permute-done((bf16[512,512]{1,0:T(8,128)(2,1)}, bf16[512,512]{1,0:T(8,128)(2,1)}, u32[]{:S(2)}, u32[]{:S(2)}) %collective-permute-start.10) | collective-permute-done | bytes 524320 | tf_op jit(solution)/shard_map/ppermute | solution.py:372
  90.2 13.0 %attend.6.refs_8_.refs_0_ = bf16[2,528,512]{2,1,0:T(8,128)(2,1)} custom-call(s32[3]{0:T(128)S(1)} %pad_add_fusion.2.table_ref, s32[16,12]{1,0:T(8,128)S(1)} %fusion.kept_ref, bf16[512,512]{1,0:T(8,128)(2,1)} %collective-permute-done.9.refs_0_, bf16[512,512]{1,0:T(8,128)(2,1)} %collective-permute-done.4.refs_12_.refs_4_.refs_1_, ...), custom_call_target="tpu_custom_call" | custom-call | flops 6442450944 | bytes 5242880 | tf_op jit(solution)/shard_map/attend/pallas_call | solution.py:151
  107.9 12.1 %attend.7.refs_8_.refs_0_.refs_3_ = bf16[2,528,512]{2,1,0:T(8,128)(2,1)S(1)} custom-call(s32[3]{0:T(128)S(1)} %pad_add_fusion.table_ref, s32[16,12]{1,0:T(8,128)S(1)} %fusion.kept_ref, bf16[512,512]{1,0:T(8,128)(2,1)} %collective-permute-done.refs_0_.refs_2_, bf16[512,512]{1,0:T(8,128)(2,1)S(1)} %bitcast.36, ...), custom_call_target="tpu_custom_call" | custom-call | flops 6442450944 | bytes 5242880 | tf_op jit(solution)/shard_map/attend/pallas_call | solution.py:151
  122.2 10.7 %attend.8.refs_2_.refs_0_ = bf16[2,528,512]{2,1,0:T(8,128)(2,1)S(1)} custom-call(s32[3]{0:T(128)S(1)} %pad_add_fusion.2.table_ref, s32[16,12]{1,0:T(8,128)S(1)} %fusion.kept_ref, bf16[512,512]{1,0:T(8,128)(2,1)S(1)} %collective-permute-done.15.refs_0_, bf16[512,512]{1,0:T(8,128)(2,1)S(1)} %copy-done.25, ...), custom_call_target="tpu_custom_call" | custom-call | flops 6442450944 | bytes 5242880 | tf_op jit(solution)/shard_map/attend/pallas_call | solution.py:151
  132.9 5.8 %collective-permute-start.23 = (bf16[2,528,512]{2,1,0:T(8,128)(2,1)S(1)}, bf16[2,528,512]{2,1,0:T(8,128)(2,1)}, u32[]{:S(2)}, u32[]{:S(2)}) collective-permute-start(bf16[2,528,512]{2,1,0:T(8,128)(2,1)S(1)} %attend.8.refs_2_.refs_0_), channel_id=1, source_target_pairs={{0,4},{12,8},{1,5},{13,9},{2,6},{14,10},{3,7},{15,11},{16,20},{28,... | collective-permute-start | bytes 3244040 | tf_op jit(solution)/shard_map/ppermute | solution.py:372
  150.1 12.1 %attend.9.refs_2_.refs_0_.refs_3_ = bf16[2,528,512]{2,1,0:T(8,128)(2,1)S(1)} custom-call(s32[3]{0:T(128)S(1)} %pad_add_fusion.table_ref, s32[16,12]{1,0:T(8,128)S(1)} %fusion.kept_ref, bf16[512,512]{1,0:T(8,128)(2,1)} %collective-permute-done.14.refs_0_.refs_2_, bf16[512,512]{1,0:T(8,128)(2,1)} %regroup.2.refs_5_.refs_1_.refs_3_, ...), custom_call_target="tpu_custom_call" | custom-call | flops 6442450944 | bytes 5242880 | tf_op jit(solution)/shard_map/attend/pallas_call | solution.py:151
  162.3 2.2 merge.6.refs_8_
  166.2 12.8 %attend.10.refs_2_ = bf16[2,528,512]{2,1,0:T(8,128)(2,1)} custom-call(s32[3]{0:T(128)S(1)} %pad_add_fusion.3.table_ref, s32[16,12]{1,0:T(8,128)S(1)} %fusion.kept_ref, bf16[512,512]{1,0:T(8,128)(2,1)} %collective-permute-done.19.refs_0_.refs_2_, bf16[512,512]{1,0:T(8,128)(2,1)} %collective-permute-done.20.refs_1_, ...), custom_call_target="tpu_custom_call" | custom-call | flops 6442450944 | bytes 5242880 | tf_op jit(solution)/shard_map/attend/pallas_call | solution.py:151
  178.9 7.1 %collective-permute-start.26 = (bf16[2,528,512]{2,1,0:T(8,128)(2,1)}, bf16[2,528,512]{2,1,0:T(8,128)(2,1)S(1)}, u32[]{:S(2)}, u32[]{:S(2)}) collective-permute-start(bf16[2,528,512]{2,1,0:T(8,128)(2,1)} %attend.10.refs_2_), channel_id=1, source_target_pairs={{0,4},{4,0},{8,12},{12,8},{1,5},{5,1},{9,13},{13,9},{2,6},{6,2},{1... | collective-permute-start | bytes 3244040 | tf_op jit(solution)/shard_map/ppermute | solution.py:372
  195.6 12.2 %attend.11.refs_2_.refs_0_.refs_3_ = bf16[2,528,512]{2,1,0:T(8,128)(2,1)S(1)} custom-call(s32[3]{0:T(128)S(1)} %pad_add_fusion.4.table_ref, s32[16,12]{1,0:T(8,128)S(1)} %fusion.kept_ref, bf16[512,512]{1,0:T(8,128)(2,1)} %regroup.3.refs_4_.refs_0_.refs_2_, bf16[512,512]{1,0:T(8,128)(2,1)} %collective-permute-done.21.refs_1_, ...), custom_call_target="tpu_custom_call" | custom-call | flops 6442450944 | bytes 5242880 | tf_op jit(solution)/shard_map/attend/pallas_call | solution.py:151
  211.4 3.2 %collective-permute-start.30 = (bf16[1,528,512]{2,1,0:T(8,128)(2,1)S(1)}, bf16[1,528,512]{2,1,0:T(8,128)(2,1)S(1)}, u32[]{:S(2)}, u32[]{:S(2)}) collective-permute-start(bf16[1,528,512]{2,1,0:T(8,128)(2,1)S(1)} %merge.9.refs_5_), channel_id=1, source_target_pairs={{0,8},{8,0},{4,12},{12,4},{1,9},{9,1},{5,13},{13,5},{2,10},{10,2},... | collective-permute-start | bytes 1622024 | tf_op jit(solution)/shard_map/ppermute | solution.py:372
  214.7 7.5 %collective-permute-done.12.refs_1_ = bf16[1,528,512]{2,1,0:T(8,128)(2,1)S(1)} collective-permute-done((bf16[1,528,512]{2,1,0:T(8,128)(2,1)S(1)}, bf16[1,528,512]{2,1,0:T(8,128)(2,1)S(1)}, u32[]{:S(2)}, u32[]{:S(2)}) %collective-permute-start.12) | collective-permute-done | bytes 540704 | tf_op jit(solution)/shard_map/ppermute | solution.py:372
  222.2 12.0 %collective-permute-done.24.refs_4_ = bf16[1,528,512]{2,1,0:T(8,128)(2,1)S(1)} collective-permute-done((bf16[1,528,512]{2,1,0:T(8,128)(2,1)S(1)}, bf16[1,528,512]{2,1,0:T(8,128)(2,1)S(1)}, u32[]{:S(2)}, u32[]{:S(2)}) %collective-permute-start.24) | collective-permute-done | bytes 540704 | tf_op jit(solution)/shard_map/ppermute | solution.py:372
  235.7 7.2 %collective-permute-done.29.refs_4_ = bf16[1,528,512]{2,1,0:T(8,128)(2,1)S(1)} collective-permute-done((bf16[1,528,512]{2,1,0:T(8,128)(2,1)S(1)}, bf16[1,528,512]{2,1,0:T(8,128)(2,1)S(1)}, u32[]{:S(2)}, u32[]{:S(2)}) %collective-permute-start.29) | collective-permute-done | bytes 540704 | tf_op jit(solution)/shard_map/ppermute | solution.py:372
  245.6 3.5 %all-to-all-start.2 = ((bf16[4,128,512]{2,1,0:T(8,128)(2,1)}), bf16[4,128,512]{2,1,0:T(8,128)(2,1)S(1)}, u32[]{:S(2)}, u32[]{:S(2)}) async-start(bf16[4,128,512]{2,1,0:T(8,128)(2,1)} %bitcast.16), calls=%async_computation.2 | async-start | bytes 1048576 | tf_op jit(solution)/shard_map/all_to_all | solution.py:430
  249.2 8.7 %all-to-all-done.2 = bf16[4,128,512]{2,1,0:T(8,128)(2,1)S(1)} async-done(((bf16[4,128,512]{2,1,0:T(8,128)(2,1)}), bf16[4,128,512]{2,1,0:T(8,128)(2,1)S(1)}, u32[]{:S(2)}, u32[]{:S(2)}) %all-to-all-start.2) | async-done | bytes 524320 | tf_op jit(solution)/shard_map/all_to_all | solution.py:430
  257.9 16.9 %all_to_all.16 = bf16[4,128,1024]{2,1,0:T(8,128)(2,1)S(1)} all-to-all(bf16[4,128,1024]{2,1,0:T(8,128)(2,1)S(1)} %pad_maximum_fusion), channel_id=1, replica_groups=mesh['cfg'=2,'blk'=4,'uly'=4] {'uly'}, dimensions={0} | all-to-all | bytes 2097152 | tf_op jit(solution)/shard_map/all_to_all | solution.py:430
  (153 shorter events, 65.9 us)
Async XLA Ops:
  31.2 25.0 %collective-permute-start.5 = (bf16[256,1536]{1,0:T(8,128)(2,1)S(1)}, bf16[256,1536]{1,0:T(8,128)(2,1)S(1)}, u32[]{:S(2)}, u32[]{:S(2)}) collective-permute-start(bf16[256,1536]{1,0:T(8,128)(2,1)S(1)} %get-tuple-element.20), channel_id=1, source_target_pairs={{0,1},{1,0},{2,3},{3,2},{4,5},{5,4},{6,7},{7,6},{8,9},{9,8},{10,11... | collective-permute-start | bytes 2359304 | tf_op jit(solution)/shard_map/ppermute | solution.py:369
  34.3 20.6 %collective-permute-start.9 = (bf16[512,512]{1,0:T(8,128)(2,1)}, bf16[512,512]{1,0:T(8,128)(2,1)}, u32[]{:S(2)}, u32[]{:S(2)}) collective-permute-start(bf16[512,512]{1,0:T(8,128)(2,1)} %collective-permute-done.refs_0_.refs_2_), channel_id=1, source_target_pairs={{4,8},{8,4},{5,9},{9,5},{6,10},{10,6},{7,11},{11,7},{20,24},{24,20... | collective-permute-start | bytes 1572872 | tf_op jit(solution)/shard_map/ppermute | solution.py:372
  36.0 30.8 %collective-permute-start.6 = (bf16[256,1536]{1,0:T(8,128)(2,1)}, bf16[256,1536]{1,0:T(8,128)(2,1)}, u32[]{:S(2)}, u32[]{:S(2)}) collective-permute-start(bf16[256,1536]{1,0:T(8,128)(2,1)} %get-tuple-element.21), channel_id=1, source_target_pairs={{0,2},{1,3},{2,0},{3,1},{4,6},{5,7},{6,4},{7,5},{8,10},{9,11},{10,... | collective-permute-start | bytes 2359304 | tf_op jit(solution)/shard_map/ppermute | solution.py:369
  36.3 41.7 %collective-permute-start.7 = (bf16[256,1536]{1,0:T(8,128)(2,1)}, bf16[256,1536]{1,0:T(8,128)(2,1)}, u32[]{:S(2)}, u32[]{:S(2)}) collective-permute-start(bf16[256,1536]{1,0:T(8,128)(2,1)} %get-tuple-element.22), channel_id=1, source_target_pairs={{0,3},{1,2},{2,1},{3,0},{4,7},{5,6},{6,5},{7,4},{8,11},{9,10},{10,... | collective-permute-start | bytes 2359304 | tf_op jit(solution)/shard_map/ppermute | solution.py:369
  38.2 44.5 %collective-permute-start.14 = (bf16[512,512]{1,0:T(8,128)(2,1)}, bf16[512,512]{1,0:T(8,128)(2,1)}, u32[]{:S(2)}, u32[]{:S(2)}) collective-permute-start(bf16[512,512]{1,0:T(8,128)(2,1)} %regroup.2.refs_5_.refs_1_.refs_3_), channel_id=1, source_target_pairs={{0,4},{4,0},{8,12},{12,8},{1,5},{5,1},{9,13},{13,9},{2,6},{6,2},{1... | collective-permute-start | bytes 1572872 | tf_op jit(solution)/shard_map/ppermute | solution.py:372
  54.9 26.5 %collective-permute-start.11 = (bf16[512,512]{1,0:T(8,128)(2,1)}, bf16[512,512]{1,0:T(8,128)(2,1)}, u32[]{:S(2)}, u32[]{:S(2)}) collective-permute-start(bf16[512,512]{1,0:T(8,128)(2,1)} %collective-permute-done.4.refs_12_.refs_4_.refs_1_), channel_id=1, source_target_pairs={{4,0},{8,12},{5,1},{9,13},{6,2},{10,14},{7,3},{11,15},{20,16},{24,... | collective-permute-start | bytes 1572872 | tf_op jit(solution)/shard_map/ppermute | solution.py:372
  57.1 33.1 %collective-permute-start.10 = (bf16[512,512]{1,0:T(8,128)(2,1)}, bf16[512,512]{1,0:T(8,128)(2,1)}, u32[]{:S(2)}, u32[]{:S(2)}) collective-permute-start(bf16[512,512]{1,0:T(8,128)(2,1)} %collective-permute-done.9.refs_0_), channel_id=1, source_target_pairs={{4,0},{8,12},{5,1},{9,13},{6,2},{10,14},{7,3},{11,15},{20,16},{24,... | collective-permute-start | bytes 1572872 | tf_op jit(solution)/shard_map/ppermute | solution.py:372
  66.8 53.2 %collective-permute-start.19 = (bf16[512,512]{1,0:T(8,128)(2,1)}, bf16[512,512]{1,0:T(8,128)(2,1)}, u32[]{:S(2)}, u32[]{:S(2)}) collective-permute-start(bf16[512,512]{1,0:T(8,128)(2,1)} %regroup.3.refs_4_.refs_0_.refs_2_), channel_id=1, source_target_pairs={{0,4},{4,0},{8,12},{12,8},{1,5},{5,1},{9,13},{13,9},{2,6},{6,2},{1... | collective-permute-start | bytes 1572872 | tf_op jit(solution)/shard_map/ppermute | solution.py:372
  78.0 60.8 %collective-permute-start.20 = (bf16[512,512]{1,0:T(8,128)(2,1)}, bf16[512,512]{1,0:T(8,128)(2,1)}, u32[]{:S(2)}, u32[]{:S(2)}) collective-permute-start(bf16[512,512]{1,0:T(8,128)(2,1)} %regroup.3.refs_4_.refs_0_.refs_2_), channel_id=1, source_target_pairs={{4,8},{8,4},{5,9},{9,5},{6,10},{10,6},{7,11},{11,7},{20,24},{24,20... | collective-permute-start | bytes 1572872 | tf_op jit(solution)/shard_map/ppermute | solution.py:372
  81.4 40.0 %collective-permute-start.17 = (bf16[512,512]{1,0:T(8,128)(2,1)S(1)}, bf16[512,512]{1,0:T(8,128)(2,1)S(1)}, u32[]{:S(2)}, u32[]{:S(2)}) collective-permute-start(bf16[512,512]{1,0:T(8,128)(2,1)S(1)} %copy-done.25), channel_id=1, source_target_pairs={{4,0},{8,12},{5,1},{9,13},{6,2},{10,14},{7,3},{11,15},{20,16},{24,... | collective-permute-start | bytes 1572872 | tf_op jit(solution)/shard_map/ppermute | solution.py:372
  82.7 21.9 %collective-permute-start.15 = (bf16[512,512]{1,0:T(8,128)(2,1)}, bf16[512,512]{1,0:T(8,128)(2,1)S(1)}, u32[]{:S(2)}, u32[]{:S(2)}) collective-permute-start(bf16[512,512]{1,0:T(8,128)(2,1)} %collective-permute-done.14.refs_0_.refs_2_), channel_id=1, source_target_pairs={{4,8},{8,4},{5,9},{9,5},{6,10},{10,6},{7,11},{11,7},{20,24},{24,20... | collective-permute-start | bytes 1572872 | tf_op jit(solution)/shard_map/ppermute | solution.py:372
  103.1 38.5 %collective-permute-start.13 = (bf16[2,528,512]{2,1,0:T(8,128)(2,1)}, bf16[2,528,512]{2,1,0:T(8,128)(2,1)S(1)}, u32[]{:S(2)}, u32[]{:S(2)}) collective-permute-start(bf16[2,528,512]{2,1,0:T(8,128)(2,1)} %attend.6.refs_8_.refs_0_), channel_id=1, source_target_pairs={{0,4},{12,8},{1,5},{13,9},{2,6},{14,10},{3,7},{15,11},{16,20},{28,... | collective-permute-start | bytes 3244040 | tf_op jit(solution)/shard_map/ppermute | solution.py:372
  120.0 20.4 %collective-permute-start.21 = (bf16[512,512]{1,0:T(8,128)(2,1)}, bf16[512,512]{1,0:T(8,128)(2,1)}, u32[]{:S(2)}, u32[]{:S(2)}) collective-permute-start(bf16[512,512]{1,0:T(8,128)(2,1)} %collective-permute-done.19.refs_0_.refs_2_), channel_id=1, source_target_pairs={{4,8},{8,4},{5,9},{9,5},{6,10},{10,6},{7,11},{11,7},{20,24},{24,20... | collective-permute-start | bytes 1572872 | tf_op jit(solution)/shard_map/ppermute | solution.py:372
  132.9 29.4 %collective-permute-start.23 = (bf16[2,528,512]{2,1,0:T(8,128)(2,1)S(1)}, bf16[2,528,512]{2,1,0:T(8,128)(2,1)}, u32[]{:S(2)}, u32[]{:S(2)}) collective-permute-start(bf16[2,528,512]{2,1,0:T(8,128)(2,1)S(1)} %attend.8.refs_2_.refs_0_), channel_id=1, source_target_pairs={{0,4},{12,8},{1,5},{13,9},{2,6},{14,10},{3,7},{15,11},{16,20},{28,... | collective-permute-start | bytes 3244040 | tf_op jit(solution)/shard_map/ppermute | solution.py:372
  138.8 52.2 %collective-permute-start.25 = (bf16[512,512]{1,0:T(8,128)(2,1)}, bf16[512,512]{1,0:T(8,128)(2,1)}, u32[]{:S(2)}, u32[]{:S(2)}) collective-permute-start(bf16[512,512]{1,0:T(8,128)(2,1)} %collective-permute-done.20.refs_1_), channel_id=1, source_target_pairs={{4,0},{8,12},{5,1},{9,13},{6,2},{10,14},{7,3},{11,15},{20,16},{24,... | collective-permute-start | bytes 1572872 | tf_op jit(solution)/shard_map/ppermute | solution.py:372
  140.3 25.8 %collective-permute-start.22 = (bf16[512,512]{1,0:T(8,128)(2,1)}, bf16[512,512]{1,0:T(8,128)(2,1)S(1)}, u32[]{:S(2)}, u32[]{:S(2)}) collective-permute-start(bf16[512,512]{1,0:T(8,128)(2,1)} %collective-permute-done.21.refs_1_), channel_id=1, source_target_pairs={{4,0},{8,12},{5,1},{9,13},{6,2},{10,14},{7,3},{11,15},{20,16},{24,... | collective-permute-start | bytes 1572872 | tf_op jit(solution)/shard_map/ppermute | solution.py:372
  143.8 44.4 %collective-permute-start.18 = (bf16[2,528,512]{2,1,0:T(8,128)(2,1)}, bf16[2,528,512]{2,1,0:T(8,128)(2,1)}, u32[]{:S(2)}, u32[]{:S(2)}) collective-permute-start(bf16[2,528,512]{2,1,0:T(8,128)(2,1)} %merge.5.refs_8_), channel_id=1, source_target_pairs={{4,8},{8,4},{5,9},{9,5},{6,10},{10,6},{7,11},{11,7},{20,24},{24,20... | collective-permute-start | bytes 3244040 | tf_op jit(solution)/shard_map/ppermute | solution.py:372
  164.5 43.3 %collective-permute-start.27 = (bf16[2,528,512]{2,1,0:T(8,128)(2,1)}, bf16[2,528,512]{2,1,0:T(8,128)(2,1)}, u32[]{:S(2)}, u32[]{:S(2)}) collective-permute-start(bf16[2,528,512]{2,1,0:T(8,128)(2,1)} %merge.6.refs_8_), channel_id=1, source_target_pairs={{4,8},{8,4},{5,9},{9,5},{6,10},{10,6},{7,11},{11,7},{20,24},{24,20... | collective-permute-start | bytes 3244040 | tf_op jit(solution)/shard_map/ppermute | solution.py:372
  178.9 32.1 %collective-permute-start.26 = (bf16[2,528,512]{2,1,0:T(8,128)(2,1)}, bf16[2,528,512]{2,1,0:T(8,128)(2,1)S(1)}, u32[]{:S(2)}, u32[]{:S(2)}) collective-permute-start(bf16[2,528,512]{2,1,0:T(8,128)(2,1)} %attend.10.refs_2_), channel_id=1, source_target_pairs={{0,4},{4,0},{8,12},{12,8},{1,5},{5,1},{9,13},{13,9},{2,6},{6,2},{1... | collective-permute-start | bytes 3244040 | tf_op jit(solution)/shard_map/ppermute | solution.py:372
  186.2 36.0 %collective-permute-start.12 = (bf16[1,528,512]{2,1,0:T(8,128)(2,1)S(1)}, bf16[1,528,512]{2,1,0:T(8,128)(2,1)S(1)}, u32[]{:S(2)}, u32[]{:S(2)}) collective-permute-start(bf16[1,528,512]{2,1,0:T(8,128)(2,1)S(1)} %slice.27), channel_id=1, source_target_pairs={{0,4},{12,8},{1,5},{13,9},{2,6},{14,10},{3,7},{15,11},{16,20},{28,... | collective-permute-start | bytes 1622024 | tf_op jit(solution)/shard_map/ppermute | solution.py:372
  188.2 47.4 %collective-permute-start.28 = (bf16[1,528,512]{2,1,0:T(8,128)(2,1)S(1)}, bf16[1,528,512]{2,1,0:T(8,128)(2,1)S(1)}, u32[]{:S(2)}, u32[]{:S(2)}) collective-permute-start(bf16[1,528,512]{2,1,0:T(8,128)(2,1)S(1)} %slice.28), channel_id=1, source_target_pairs={{0,4},{12,8},{1,5},{13,9},{2,6},{14,10},{3,7},{15,11},{16,20},{28,... | collective-permute-start | bytes 1622024 | tf_op jit(solution)/shard_map/ppermute | solution.py:372
  191.0 43.3 %collective-permute-start.24 = (bf16[1,528,512]{2,1,0:T(8,128)(2,1)S(1)}, bf16[1,528,512]{2,1,0:T(8,128)(2,1)S(1)}, u32[]{:S(2)}, u32[]{:S(2)}) collective-permute-start(bf16[1,528,512]{2,1,0:T(8,128)(2,1)S(1)} %merge.7.refs_8_), channel_id=1, source_target_pairs={{4,0},{8,12},{5,1},{9,13},{6,2},{10,14},{7,3},{11,15},{20,16},{24,... | collective-permute-start | bytes 1622024 | tf_op jit(solution)/shard_map/ppermute | solution.py:372
  208.9 34.0 %collective-permute-start.29 = (bf16[1,528,512]{2,1,0:T(8,128)(2,1)S(1)}, bf16[1,528,512]{2,1,0:T(8,128)(2,1)S(1)}, u32[]{:S(2)}, u32[]{:S(2)}) collective-permute-start(bf16[1,528,512]{2,1,0:T(8,128)(2,1)S(1)} %merge.8.refs_4_), channel_id=1, source_target_pairs={{4,0},{8,12},{5,1},{9,13},{6,2},{10,14},{7,3},{11,15},{20,16},{24,... | collective-permute-start | bytes 1622024 | tf_op jit(solution)/shard_map/ppermute | solution.py:372
  211.4 32.8 %collective-permute-start.30 = (bf16[1,528,512]{2,1,0:T(8,128)(2,1)S(1)}, bf16[1,528,512]{2,1,0:T(8,128)(2,1)S(1)}, u32[]{:S(2)}, u32[]{:S(2)}) collective-permute-start(bf16[1,528,512]{2,1,0:T(8,128)(2,1)S(1)} %merge.9.refs_5_), channel_id=1, source_target_pairs={{0,8},{8,0},{4,12},{12,4},{1,9},{9,1},{5,13},{13,5},{2,10},{10,2},... | collective-permute-start | bytes 1622024 | tf_op jit(solution)/shard_map/ppermute | solution.py:372
  (44 other events, 445.8 us)

commit v11 on v7

--- a/solution.py
+++ b/solution.py
@@ -172,7 +172,7 @@
                 pltpu.VMEM((stat_rows(width), rows), jnp.float32),
             ],
         ),
-        compiler_params=pltpu.CompilerParams(vmem_limit_bytes=28 * MIB),
+        compiler_params=pltpu.CompilerParams(vmem_limit_bytes=22 * MIB),
         cost_estimate=pl.CostEstimate(
             flops=8 * blocks * rows * keys * DH * heads,
             bytes_accessed=4 * blocks * rows * width + 4 * keys * width,
@@ -277,7 +277,7 @@
             in_specs=specs * len(arrays) + [pl.BlockSpec(memory_space=pl.ANY)] * len(deps),
             out_specs=[pl.BlockSpec(shape, lambda i, t: (0, 0))] * peers,
         ),
-        compiler_params=pltpu.CompilerParams(vmem_limit_bytes=28 * MIB),
+        compiler_params=pltpu.CompilerParams(vmem_limit_bytes=22 * MIB),
         cost_estimate=QUICK,
         name="parts",
     )(peer.reshape(1), *[a for a in arrays for _ in range(peers)], *deps)

time: 256 us -> 256 us (level)
  no operation moved by 1% of the time
where the time goes in v11:
time: 256 us; the launch traced here: 254 us
  Pallas kernels  83.6 us (33%)
  starting transfers between devices  76.7 us (30%)
  waiting for transfers between devices  36.3 us (14%)
  blocking collectives  29.8 us (12%)
  local copies, waits for them, and re-layouts  25.5 us (10%)
    pallas_call x6, Pallas kernels, attend(): pl.pallas_call(functools.partial(attend_kernel, [[None] * len(c) for c in...  71.1 us
    ppermute x25, starting transfers between devices, send(): return lax.ppermute(x, 'blk', pairs)  68.7 us
    ppermute x25, waiting for transfers between devices, send(): return lax.ppermute(x, 'blk', pairs)  24.3 us
    unnamed x83, local copies, waits for them, and re-layouts  21.7 us
    all_to_all x1, blocking collectives, run_return(): lax.all_to_all(joint, 'uly', split_axis=0, concat_axis=0, tiled=False)  16.9 us
    all_to_all x1, blocking collectives, to_heads(): lax.all_to_all(pieces, 'uly', split_axis=0, concat_axis=0, tiled=False)  12.9 us
    ppermute x6, waiting for transfers between devices, to_peers(): lax.ppermute(p, 'uly', [(i, i ^ k) for i in range(peers)])  12 us
    pallas_call x8, Pallas kernels, join_parts(): pl.pallas_call(functools.partial(join_kernel_of, [len(c) for c in choices...  7.95 us
  transfers between devices with their start and end apart: 32, of which 7 were waited for; matrix products, arithmetic and copies ran while one was open for 2% of the time, Pallas kernels for 33%

profile of v11, /device:TPU:0, one launch (start us, length us, event | category | flops | bytes accessed | tf_op | source)
XLA Modules:
  0.0 254.3 jit_solution(1391016746510666477)
XLA Ops:
  1.3 12.9 %all_to_all.15 = bf16[4,128,512]{2,1,0:T(8,128)(2,1)S(1)} all-to-all(bf16[4,128,512]{2,1,0:T(8,128)(2,1)S(1)} %pad_maximum_fusion.1), channel_id=1, replica_groups=mesh['cfg'=2,'blk'=4,'uly'=4] {'uly'}, dimensions={0} | all-to-all | bytes 1048576 | tf_op jit(solution)/shard_map/all_to_all | solution.py:365
  15.7 3.7 %collective-permute-start = (bf16[512,512]{1,0:T(8,128)(2,1)S(1)}, bf16[512,512]{1,0:T(8,128)(2,1)}, u32[]{:S(2)}, u32[]{:S(2)}) collective-permute-start(bf16[512,512]{1,0:T(8,128)(2,1)S(1)} %bitcast.35), channel_id=1, source_target_pairs={{0,4},{4,0},{8,12},{12,8},{1,5},{5,1},{9,13},{13,9},{2,6},{6,2},{1... | collective-permute-start | bytes 1572872 | tf_op jit(solution)/shard_map/ppermute | solution.py:372
  21.4 7.3 %collective-permute-done.2.refs_10_.refs_2_ = bf16[128,1024]{1,0:T(8,128)(2,1)S(1)} collective-permute-done((bf16[128,1024]{1,0:T(8,128)(2,1)S(1)}, bf16[128,1024]{1,0:T(8,128)(2,1)S(1)}, u32[]{:S(2)}, u32[]{:S(2)}) %collective-permute-start.2) | collective-permute-done | bytes 262176 | tf_op jit(solution)/shard_map/ppermute | solution.py:369
  28.7 4.7 %collective-permute-done.3.refs_11_.refs_3_ = bf16[128,1024]{1,0:T(8,128)(2,1)S(1)} collective-permute-done((bf16[128,1024]{1,0:T(8,128)(2,1)S(1)}, bf16[128,1024]{1,0:T(8,128)(2,1)S(1)}, u32[]{:S(2)}, u32[]{:S(2)}) %collective-permute-start.3) | collective-permute-done | bytes 262176 | tf_op jit(solution)/shard_map/ppermute | solution.py:369
  41.2 12.7 %collective-permute-start.14 = (bf16[512,512]{1,0:T(8,128)(2,1)}, bf16[512,512]{1,0:T(8,128)(2,1)}, u32[]{:S(2)}, u32[]{:S(2)}) collective-permute-start(bf16[512,512]{1,0:T(8,128)(2,1)} %regroup.2.refs_5_.refs_1_.refs_3_), channel_id=1, source_target_pairs={{0,4},{4,0},{8,12},{12,8},{1,5},{5,1},{9,13},{13,9},{2,6},{6,2},{1... | collective-permute-start | bytes 1572872 | tf_op jit(solution)/shard_map/ppermute | solution.py:372
  57.7 3.2 %copy.11 = bf16[1024,1536]{0,1:T(8,128)(2,1)S(1)} copy(bf16[1024,1536]{1,0:T(8,128)(2,1)} %param.10) | data formatting | bytes 6291456 | tf_op args[4]
  64.9 11.5 %collective-permute-start.19 = (bf16[512,512]{1,0:T(8,128)(2,1)S(1)}, bf16[512,512]{1,0:T(8,128)(2,1)S(1)}, u32[]{:S(2)}, u32[]{:S(2)}) collective-permute-start(bf16[512,512]{1,0:T(8,128)(2,1)S(1)} %regroup.3.refs_4_.refs_0_.refs_2_), channel_id=1, source_target_pairs={{0,4},{4,0},{8,12},{12,8},{1,5},{5,1},{9,13},{13,9},{2,6},{6,2},{1... | collective-permute-start | bytes 1572872 | tf_op jit(solution)/shard_map/ppermute | solution.py:372
  81.8 7.5 %collective-permute-done.10.refs_2_ = bf16[512,512]{1,0:T(8,128)(2,1)} collective-permute-done((bf16[512,512]{1,0:T(8,128)(2,1)}, bf16[512,512]{1,0:T(8,128)(2,1)}, u32[]{:S(2)}, u32[]{:S(2)}) %collective-permute-start.10) | collective-permute-done | bytes 524320 | tf_op jit(solution)/shard_map/ppermute | solution.py:372
  89.3 12.1 %attend.6.refs_8_.refs_0_ = bf16[2,528,512]{2,1,0:T(8,128)(2,1)S(1)} custom-call(s32[3]{0:T(128)S(1)} %pad_add_fusion.2.table_ref, s32[16,12]{1,0:T(8,128)S(1)} %fusion.kept_ref, bf16[512,512]{1,0:T(8,128)(2,1)} %collective-permute-done.9.refs_0_, bf16[512,512]{1,0:T(8,128)(2,1)} %collective-permute-done.4.refs_12_.refs_4_.refs_1_, ...), custom_call_target="tpu_custom_call" | custom-call | flops 6442450944 | bytes 5242880 | tf_op jit(solution)/shard_map/attend/pallas_call | solution.py:151
  108.3 11.9 %attend.7.refs_8_.refs_0_.refs_3_ = bf16[2,528,512]{2,1,0:T(8,128)(2,1)S(1)} custom-call(s32[3]{0:T(128)S(1)} %pad_add_fusion.table_ref, s32[16,12]{1,0:T(8,128)S(1)} %fusion.kept_ref, bf16[512,512]{1,0:T(8,128)(2,1)} %collective-permute-done.refs_0_.refs_2_, bf16[512,512]{1,0:T(8,128)(2,1)S(1)} %bitcast.37, ...), custom_call_target="tpu_custom_call" | custom-call | flops 6442450944 | bytes 5242880 | tf_op jit(solution)/shard_map/attend/pallas_call | solution.py:151
  120.2 2.8 %collective-permute-done.16.refs_2_ = bf16[512,512]{1,0:T(8,128)(2,1)S(1)} collective-permute-done((bf16[512,512]{1,0:T(8,128)(2,1)S(1)}, bf16[512,512]{1,0:T(8,128)(2,1)S(1)}, u32[]{:S(2)}, u32[]{:S(2)}) %collective-permute-start.16) | collective-permute-done | bytes 524320 | tf_op jit(solution)/shard_map/ppermute | solution.py:372
  122.9 10.8 %attend.8.refs_2_.refs_0_ = bf16[2,528,512]{2,1,0:T(8,128)(2,1)S(1)} custom-call(s32[3]{0:T(128)S(1)} %pad_add_fusion.2.table_ref, s32[16,12]{1,0:T(8,128)S(1)} %fusion.kept_ref, bf16[512,512]{1,0:T(8,128)(2,1)S(1)} %collective-permute-done.15.refs_0_, bf16[512,512]{1,0:T(8,128)(2,1)S(1)} %copy-done.32, ...), custom_call_target="tpu_custom_call" | custom-call | flops 6442450944 | bytes 5242880 | tf_op jit(solution)/shard_map/attend/pallas_call | solution.py:151
  133.7 4.9 %collective-permute-start.24 = (bf16[2,528,512]{2,1,0:T(8,128)(2,1)S(1)}, bf16[2,528,512]{2,1,0:T(8,128)(2,1)S(1)}, u32[]{:S(2)}, u32[]{:S(2)}) collective-permute-start(bf16[2,528,512]{2,1,0:T(8,128)(2,1)S(1)} %attend.8.refs_2_.refs_0_), channel_id=1, source_target_pairs={{0,4},{12,8},{1,5},{13,9},{2,6},{14,10},{3,7},{15,11},{16,20},{28,... | collective-permute-start | bytes 3244040 | tf_op jit(solution)/shard_map/ppermute | solution.py:372
  140.9 12.2 %attend.9.refs_8_.refs_0_.refs_3_ = bf16[2,528,512]{2,1,0:T(8,128)(2,1)S(1)} custom-call(s32[3]{0:T(128)S(1)} %pad_add_fusion.table_ref, s32[16,12]{1,0:T(8,128)S(1)} %fusion.kept_ref, bf16[512,512]{1,0:T(8,128)(2,1)} %collective-permute-done.14.refs_0_.refs_2_, bf16[512,512]{1,0:T(8,128)(2,1)} %regroup.2.refs_5_.refs_1_.refs_3_, ...), custom_call_target="tpu_custom_call" | custom-call | flops 6442450944 | bytes 5242880 | tf_op jit(solution)/shard_map/attend/pallas_call | solution.py:151
  153.5 12.5 %attend.10.refs_2_ = bf16[2,528,512]{2,1,0:T(8,128)(2,1)} custom-call(s32[3]{0:T(128)S(1)} %pad_add_fusion.3.table_ref, s32[16,12]{1,0:T(8,128)S(1)} %fusion.kept_ref, bf16[512,512]{1,0:T(8,128)(2,1)S(1)} %collective-permute-done.19.refs_0_.refs_2_, bf16[512,512]{1,0:T(8,128)(2,1)} %collective-permute-done.20.refs_1_, ...), custom_call_target="tpu_custom_call" | custom-call | flops 6442450944 | bytes 5242880 | tf_op jit(solution)/shard_map/attend/pallas_call | solution.py:151
  166.0 5.1 %collective-permute-start.27 = (bf16[2,528,512]{2,1,0:T(8,128)(2,1)}, bf16[2,528,512]{2,1,0:T(8,128)(2,1)S(1)}, u32[]{:S(2)}, u32[]{:S(2)}) collective-permute-start(bf16[2,528,512]{2,1,0:T(8,128)(2,1)} %attend.10.refs_2_), channel_id=1, source_target_pairs={{0,4},{4,0},{8,12},{12,8},{1,5},{5,1},{9,13},{13,9},{2,6},{6,2},{1... | collective-permute-start | bytes 3244040 | tf_op jit(solution)/shard_map/ppermute | solution.py:372
  175.1 3.7 %collective-permute-start.12 = (bf16[1,528,512]{2,1,0:T(8,128)(2,1)S(1)}, bf16[1,528,512]{2,1,0:T(8,128)(2,1)S(1)}, u32[]{:S(2)}, u32[]{:S(2)}) collective-permute-start(bf16[1,528,512]{2,1,0:T(8,128)(2,1)S(1)} %slice.27), channel_id=1, source_target_pairs={{0,4},{12,8},{1,5},{13,9},{2,6},{14,10},{3,7},{15,11},{16,20},{28,... | collective-permute-start | bytes 1622024 | tf_op jit(solution)/shard_map/ppermute | solution.py:372
  179.6 2.1 collective-permute-start.28
  189.6 11.7 %attend.11.refs_0_.refs_2_.refs_4_.refs_3_ = bf16[2,528,512]{2,1,0:T(8,128)(2,1)S(1)} custom-call(s32[3]{0:T(128)S(1)} %pad_add_fusion.4.table_ref, s32[16,12]{1,0:T(8,128)S(1)} %fusion.kept_ref, bf16[512,512]{1,0:T(8,128)(2,1)S(1)} %copy-done.25, bf16[512,512]{1,0:T(8,128)(2,1)S(1)} %copy-done.40, bf16[512,512]{1,0:T(8,128)(2,1)S(1)} %copy-done.25, ...), custom_call_target="tpu_custom_call" | custom-call | flops 6442450944 | bytes 5242880 | tf_op jit(solution)/shard_map/attend/pallas_call | solution.py:151
  205.8 4.3 %collective-permute-start.30 = (bf16[1,528,512]{2,1,0:T(8,128)(2,1)}, bf16[1,528,512]{2,1,0:T(8,128)(2,1)}, u32[]{:S(2)}, u32[]{:S(2)}) collective-permute-start(bf16[1,528,512]{2,1,0:T(8,128)(2,1)} %merge.8.refs_2_), channel_id=1, source_target_pairs={{0,8},{8,0},{4,12},{12,4},{1,9},{9,1},{5,13},{13,5},{2,10},{10,2},... | collective-permute-start | bytes 1622024 | tf_op jit(solution)/shard_map/ppermute | solution.py:372
  211.3 4.1 %all-to-all-start.1 = ((bf16[4,128,512]{2,1,0:T(8,128)(2,1)}), bf16[4,128,512]{2,1,0:T(8,128)(2,1)}, u32[]{:S(2)}, u32[]{:S(2)}) async-start(bf16[4,128,512]{2,1,0:T(8,128)(2,1)} %bitcast.26), calls=%async_computation.1 | async-start | bytes 1048576 | tf_op jit(solution)/shard_map/all_to_all | solution.py:430
  215.4 3.4 %collective-permute-done.28.refs_1_ = bf16[1,528,512]{2,1,0:T(8,128)(2,1)} collective-permute-done((bf16[1,528,512]{2,1,0:T(8,128)(2,1)}, bf16[1,528,512]{2,1,0:T(8,128)(2,1)}, u32[]{:S(2)}, u32[]{:S(2)}) %collective-permute-start.28) | collective-permute-done | bytes 540704 | tf_op jit(solution)/shard_map/ppermute | solution.py:372
  218.9 10.2 %collective-permute-done.29.refs_4_ = bf16[1,528,512]{2,1,0:T(8,128)(2,1)} collective-permute-done((bf16[1,528,512]{2,1,0:T(8,128)(2,1)}, bf16[1,528,512]{2,1,0:T(8,128)(2,1)}, u32[]{:S(2)}, u32[]{:S(2)}) %collective-permute-start.29) | collective-permute-done | bytes 540704 | tf_op jit(solution)/shard_map/ppermute | solution.py:372
  234.9 16.9 %all_to_all.16 = bf16[4,128,1024]{2,1,0:T(8,128)(2,1)S(1)} all-to-all(bf16[4,128,1024]{2,1,0:T(8,128)(2,1)S(1)} %pad_maximum_fusion), channel_id=1, replica_groups=mesh['cfg'=2,'blk'=4,'uly'=4] {'uly'}, dimensions={0} | all-to-all | bytes 2097152 | tf_op jit(solution)/shard_map/all_to_all | solution.py:430
  (163 shorter events, 61.6 us)
Async XLA Ops:
  15.7 21.2 %collective-permute-start = (bf16[512,512]{1,0:T(8,128)(2,1)S(1)}, bf16[512,512]{1,0:T(8,128)(2,1)}, u32[]{:S(2)}, u32[]{:S(2)}) collective-permute-start(bf16[512,512]{1,0:T(8,128)(2,1)S(1)} %bitcast.35), channel_id=1, source_target_pairs={{0,4},{4,0},{8,12},{12,8},{1,5},{5,1},{9,13},{13,9},{2,6},{6,2},{1... | collective-permute-start | bytes 1572872 | tf_op jit(solution)/shard_map/ppermute | solution.py:372
  35.0 20.1 %collective-permute-start.5 = (bf16[256,1536]{1,0:T(8,128)(2,1)}, bf16[256,1536]{1,0:T(8,128)(2,1)S(1)}, u32[]{:S(2)}, u32[]{:S(2)}) collective-permute-start(bf16[256,1536]{1,0:T(8,128)(2,1)} %get-tuple-element.20), channel_id=1, source_target_pairs={{0,1},{1,0},{2,3},{3,2},{4,5},{5,4},{6,7},{7,6},{8,9},{9,8},{10,11... | collective-permute-start | bytes 2359304 | tf_op jit(solution)/shard_map/ppermute | solution.py:369
  38.4 26.5 %collective-permute-start.6 = (bf16[256,1536]{1,0:T(8,128)(2,1)}, bf16[256,1536]{1,0:T(8,128)(2,1)}, u32[]{:S(2)}, u32[]{:S(2)}) collective-permute-start(bf16[256,1536]{1,0:T(8,128)(2,1)} %get-tuple-element.21), channel_id=1, source_target_pairs={{0,2},{1,3},{2,0},{3,1},{4,6},{5,7},{6,4},{7,5},{8,10},{9,11},{10,... | collective-permute-start | bytes 2359304 | tf_op jit(solution)/shard_map/ppermute | solution.py:369
  38.8 37.6 %collective-permute-start.7 = (bf16[256,1536]{1,0:T(8,128)(2,1)}, bf16[256,1536]{1,0:T(8,128)(2,1)}, u32[]{:S(2)}, u32[]{:S(2)}) collective-permute-start(bf16[256,1536]{1,0:T(8,128)(2,1)} %get-tuple-element.22), channel_id=1, source_target_pairs={{0,3},{1,2},{2,1},{3,0},{4,7},{5,6},{6,5},{7,4},{8,11},{9,10},{10,... | collective-permute-start | bytes 2359304 | tf_op jit(solution)/shard_map/ppermute | solution.py:369
  41.2 40.0 %collective-permute-start.14 = (bf16[512,512]{1,0:T(8,128)(2,1)}, bf16[512,512]{1,0:T(8,128)(2,1)}, u32[]{:S(2)}, u32[]{:S(2)}) collective-permute-start(bf16[512,512]{1,0:T(8,128)(2,1)} %regroup.2.refs_5_.refs_1_.refs_3_), channel_id=1, source_target_pairs={{0,4},{4,0},{8,12},{12,8},{1,5},{5,1},{9,13},{13,9},{2,6},{6,2},{1... | collective-permute-start | bytes 1572872 | tf_op jit(solution)/shard_map/ppermute | solution.py:372
  53.9 25.9 %collective-permute-start.11 = (bf16[512,512]{1,0:T(8,128)(2,1)}, bf16[512,512]{1,0:T(8,128)(2,1)}, u32[]{:S(2)}, u32[]{:S(2)}) collective-permute-start(bf16[512,512]{1,0:T(8,128)(2,1)} %collective-permute-done.4.refs_12_.refs_4_.refs_1_), channel_id=1, source_target_pairs={{4,0},{8,12},{5,1},{9,13},{6,2},{10,14},{7,3},{11,15},{20,16},{24,... | collective-permute-start | bytes 1572872 | tf_op jit(solution)/shard_map/ppermute | solution.py:372
  56.1 33.3 %collective-permute-start.10 = (bf16[512,512]{1,0:T(8,128)(2,1)}, bf16[512,512]{1,0:T(8,128)(2,1)}, u32[]{:S(2)}, u32[]{:S(2)}) collective-permute-start(bf16[512,512]{1,0:T(8,128)(2,1)} %collective-permute-done.9.refs_0_), channel_id=1, source_target_pairs={{4,0},{8,12},{5,1},{9,13},{6,2},{10,14},{7,3},{11,15},{20,16},{24,... | collective-permute-start | bytes 1572872 | tf_op jit(solution)/shard_map/ppermute | solution.py:372
  64.9 39.4 %collective-permute-start.19 = (bf16[512,512]{1,0:T(8,128)(2,1)S(1)}, bf16[512,512]{1,0:T(8,128)(2,1)S(1)}, u32[]{:S(2)}, u32[]{:S(2)}) collective-permute-start(bf16[512,512]{1,0:T(8,128)(2,1)S(1)} %regroup.3.refs_4_.refs_0_.refs_2_), channel_id=1, source_target_pairs={{0,4},{4,0},{8,12},{12,8},{1,5},{5,1},{9,13},{13,9},{2,6},{6,2},{1... | collective-permute-start | bytes 1572872 | tf_op jit(solution)/shard_map/ppermute | solution.py:372
  76.4 28.7 %collective-permute-start.20 = (bf16[512,512]{1,0:T(8,128)(2,1)S(1)}, bf16[512,512]{1,0:T(8,128)(2,1)}, u32[]{:S(2)}, u32[]{:S(2)}) collective-permute-start(bf16[512,512]{1,0:T(8,128)(2,1)S(1)} %regroup.3.refs_4_.refs_0_.refs_2_), channel_id=1, source_target_pairs={{4,8},{8,4},{5,9},{9,5},{6,10},{10,6},{7,11},{11,7},{20,24},{24,20... | collective-permute-start | bytes 1572872 | tf_op jit(solution)/shard_map/ppermute | solution.py:372
  79.8 40.3 %collective-permute-start.17 = (bf16[512,512]{1,0:T(8,128)(2,1)S(1)}, bf16[512,512]{1,0:T(8,128)(2,1)S(1)}, u32[]{:S(2)}, u32[]{:S(2)}) collective-permute-start(bf16[512,512]{1,0:T(8,128)(2,1)S(1)} %copy-done.32), channel_id=1, source_target_pairs={{4,0},{8,12},{5,1},{9,13},{6,2},{10,14},{7,3},{11,15},{20,16},{24,... | collective-permute-start | bytes 1572872 | tf_op jit(solution)/shard_map/ppermute | solution.py:372
  81.1 21.9 %collective-permute-start.15 = (bf16[512,512]{1,0:T(8,128)(2,1)}, bf16[512,512]{1,0:T(8,128)(2,1)S(1)}, u32[]{:S(2)}, u32[]{:S(2)}) collective-permute-start(bf16[512,512]{1,0:T(8,128)(2,1)} %collective-permute-done.14.refs_0_.refs_2_), channel_id=1, source_target_pairs={{4,8},{8,4},{5,9},{9,5},{6,10},{10,6},{7,11},{11,7},{20,24},{24,20... | collective-permute-start | bytes 1572872 | tf_op jit(solution)/shard_map/ppermute | solution.py:372
  101.5 38.4 %collective-permute-start.13 = (bf16[2,528,512]{2,1,0:T(8,128)(2,1)S(1)}, bf16[2,528,512]{2,1,0:T(8,128)(2,1)S(1)}, u32[]{:S(2)}, u32[]{:S(2)}) collective-permute-start(bf16[2,528,512]{2,1,0:T(8,128)(2,1)S(1)} %attend.6.refs_8_.refs_0_), channel_id=1, source_target_pairs={{0,4},{12,8},{1,5},{13,9},{2,6},{14,10},{3,7},{15,11},{16,20},{28,... | collective-permute-start | bytes 3244040 | tf_op jit(solution)/shard_map/ppermute | solution.py:372
  104.4 34.3 %collective-permute-start.21 = (bf16[512,512]{1,0:T(8,128)(2,1)S(1)}, bf16[512,512]{1,0:T(8,128)(2,1)S(1)}, u32[]{:S(2)}, u32[]{:S(2)}) collective-permute-start(bf16[512,512]{1,0:T(8,128)(2,1)S(1)} %collective-permute-done.19.refs_0_.refs_2_), channel_id=1, source_target_pairs={{4,8},{8,4},{5,9},{9,5},{6,10},{10,6},{7,11},{11,7},{20,24},{24,20... | collective-permute-start | bytes 1572872 | tf_op jit(solution)/shard_map/ppermute | solution.py:372
  105.1 76.6 %collective-permute-start.26 = (bf16[512,512]{1,0:T(8,128)(2,1)}, bf16[512,512]{1,0:T(8,128)(2,1)}, u32[]{:S(2)}, u32[]{:S(2)}) collective-permute-start(bf16[512,512]{1,0:T(8,128)(2,1)} %collective-permute-done.20.refs_1_), channel_id=1, source_target_pairs={{4,0},{8,12},{5,1},{9,13},{6,2},{10,14},{7,3},{11,15},{20,16},{24,... | collective-permute-start | bytes 1572872 | tf_op jit(solution)/shard_map/ppermute | solution.py:372
  133.7 38.4 %collective-permute-start.24 = (bf16[2,528,512]{2,1,0:T(8,128)(2,1)S(1)}, bf16[2,528,512]{2,1,0:T(8,128)(2,1)S(1)}, u32[]{:S(2)}, u32[]{:S(2)}) collective-permute-start(bf16[2,528,512]{2,1,0:T(8,128)(2,1)S(1)} %attend.8.refs_2_.refs_0_), channel_id=1, source_target_pairs={{0,4},{12,8},{1,5},{13,9},{2,6},{14,10},{3,7},{15,11},{16,20},{28,... | collective-permute-start | bytes 3244040 | tf_op jit(solution)/shard_map/ppermute | solution.py:372
  140.0 31.0 %collective-permute-start.18 = (bf16[2,528,512]{2,1,0:T(8,128)(2,1)S(1)}, bf16[2,528,512]{2,1,0:T(8,128)(2,1)S(1)}, u32[]{:S(2)}, u32[]{:S(2)}) collective-permute-start(bf16[2,528,512]{2,1,0:T(8,128)(2,1)S(1)} %merge.5.refs_8_), channel_id=1, source_target_pairs={{4,8},{8,4},{5,9},{9,5},{6,10},{10,6},{7,11},{11,7},{20,24},{24,20... | collective-permute-start | bytes 3244040 | tf_op jit(solution)/shard_map/ppermute | solution.py:372
  166.0 35.3 %collective-permute-start.27 = (bf16[2,528,512]{2,1,0:T(8,128)(2,1)}, bf16[2,528,512]{2,1,0:T(8,128)(2,1)S(1)}, u32[]{:S(2)}, u32[]{:S(2)}) collective-permute-start(bf16[2,528,512]{2,1,0:T(8,128)(2,1)} %attend.10.refs_2_), channel_id=1, source_target_pairs={{0,4},{4,0},{8,12},{12,8},{1,5},{5,1},{9,13},{13,9},{2,6},{6,2},{1... | collective-permute-start | bytes 3244040 | tf_op jit(solution)/shard_map/ppermute | solution.py:372
  173.3 29.2 %collective-permute-start.25 = (bf16[2,528,512]{2,1,0:T(8,128)(2,1)}, bf16[2,528,512]{2,1,0:T(8,128)(2,1)}, u32[]{:S(2)}, u32[]{:S(2)}) collective-permute-start(bf16[2,528,512]{2,1,0:T(8,128)(2,1)} %merge.7.refs_8_), channel_id=1, source_target_pairs={{4,8},{8,4},{5,9},{9,5},{6,10},{10,6},{7,11},{11,7},{20,24},{24,20... | collective-permute-start | bytes 3244040 | tf_op jit(solution)/shard_map/ppermute | solution.py:372
  175.1 35.0 %collective-permute-start.12 = (bf16[1,528,512]{2,1,0:T(8,128)(2,1)S(1)}, bf16[1,528,512]{2,1,0:T(8,128)(2,1)S(1)}, u32[]{:S(2)}, u32[]{:S(2)}) collective-permute-start(bf16[1,528,512]{2,1,0:T(8,128)(2,1)S(1)} %slice.27), channel_id=1, source_target_pairs={{0,4},{12,8},{1,5},{13,9},{2,6},{14,10},{3,7},{15,11},{16,20},{28,... | collective-permute-start | bytes 1622024 | tf_op jit(solution)/shard_map/ppermute | solution.py:372
  179.6 39.3 %collective-permute-start.28 = (bf16[1,528,512]{2,1,0:T(8,128)(2,1)}, bf16[1,528,512]{2,1,0:T(8,128)(2,1)}, u32[]{:S(2)}, u32[]{:S(2)}) collective-permute-start(bf16[1,528,512]{2,1,0:T(8,128)(2,1)} %slice.28), channel_id=1, source_target_pairs={{0,4},{12,8},{1,5},{13,9},{2,6},{14,10},{3,7},{15,11},{16,20},{28,... | collective-permute-start | bytes 1622024 | tf_op jit(solution)/shard_map/ppermute | solution.py:372
  181.7 28.3 %collective-permute-start.23 = (bf16[1,528,512]{2,1,0:T(8,128)(2,1)S(1)}, bf16[1,528,512]{2,1,0:T(8,128)(2,1)S(1)}, u32[]{:S(2)}, u32[]{:S(2)}) collective-permute-start(bf16[1,528,512]{2,1,0:T(8,128)(2,1)S(1)} %copy-done.23), channel_id=1, source_target_pairs={{4,0},{8,12},{5,1},{9,13},{6,2},{10,14},{7,3},{11,15},{20,16},{24,... | collective-permute-start | bytes 1622024 | tf_op jit(solution)/shard_map/ppermute | solution.py:372
  204.5 24.6 %collective-permute-start.29 = (bf16[1,528,512]{2,1,0:T(8,128)(2,1)}, bf16[1,528,512]{2,1,0:T(8,128)(2,1)}, u32[]{:S(2)}, u32[]{:S(2)}) collective-permute-start(bf16[1,528,512]{2,1,0:T(8,128)(2,1)} %merge.9.refs_5_), channel_id=1, source_target_pairs={{4,0},{8,12},{5,1},{9,13},{6,2},{10,14},{7,3},{11,15},{20,16},{24,... | collective-permute-start | bytes 1622024 | tf_op jit(solution)/shard_map/ppermute | solution.py:372
  205.8 27.3 %collective-permute-start.30 = (bf16[1,528,512]{2,1,0:T(8,128)(2,1)}, bf16[1,528,512]{2,1,0:T(8,128)(2,1)}, u32[]{:S(2)}, u32[]{:S(2)}) collective-permute-start(bf16[1,528,512]{2,1,0:T(8,128)(2,1)} %merge.8.refs_2_), channel_id=1, source_target_pairs={{0,8},{8,0},{4,12},{12,4},{1,9},{9,1},{5,13},{13,5},{2,10},{10,2},... | collective-permute-start | bytes 1622024 | tf_op jit(solution)/shard_map/ppermute | solution.py:372
  211.3 23.6 %all-to-all-start.1 = ((bf16[4,128,512]{2,1,0:T(8,128)(2,1)}), bf16[4,128,512]{2,1,0:T(8,128)(2,1)}, u32[]{:S(2)}, u32[]{:S(2)}) async-start(bf16[4,128,512]{2,1,0:T(8,128)(2,1)} %bitcast.26), calls=%async_computation.1 | async-start | bytes 1048576 | tf_op jit(solution)/shard_map/all_to_all | solution.py:430
  (49 other events, 584.8 us)
